TPU v7x, 256 devices: a whole 4x4x8 slice. The times are simulated.
256 devices in a mesh: slot: 8 (over x, core), seq: 32 (over z, y).
Axes of the slice: x: 4, y: 4, z: 8, core: 2. Of those that a mesh axis runs over, the one named last changes fastest.
Arguments:
- latent: bfloat16 [8, 1024, 3072], P('slot', 'seq'), may hold values from -6 to 6
- noise_frame: bfloat16 [512, 3072], replicated, may hold values from -6 to 6
- frame_pos: int32 [8, 2], P('slot'), may hold values from 0 to 15
- t_index: int32 [8], P('slot'), may hold values from 0 to 49
- pos_table: bfloat16 [16, 3072], replicated, may hold values from -6 to 6
- mod_table: bfloat16 [50, 2, 3, 3072], replicated, may hold values from -5 to 5
- w_qkv: bfloat16 [2, 3072, 32, 192], P(None, None, 'seq'), may hold values from -0.109375 to 0.109375
- qk_gain: bfloat16 [2, 32, 128], P(None, 'seq'), may hold values from 0.5 to 3
- w_out: bfloat16 [2, 2048, 3072], P(None, 'seq'), may hold values from -0.25 to 0.25
Outputs:
- denoised: bfloat16 [8, 1024, 3072], P('slot', 'seq')
- queue_next: bfloat16 [8, 1024, 3072], P('slot', 'seq')
All inputs are finite; a program needn't handle non-finite values.
Results may differ from a plain program's by a relative error of at most 0.039.
Values may be sent and summed in bfloat16 or wider, within the bound.
No kernel may reach another device: no remote copies, remote signals or barrier semaphores. Data moves between devices by JAX's collectives and lax.ppermute only.
A program may use at most 128 MiB of HBM per device.

v0:
```python
import jax
import jax.numpy as jnp
from jax import lax
from jax.sharding import PartitionSpec as P


def shifted(block, axis, distance):
    devices = range(lax.axis_size(axis))
    route = [(i - distance, i) for i in devices if i - distance in devices]
    return lax.ppermute(block, axis, route)


def layer_norm(value):
    center = value - jnp.mean(value, axis=-1, keepdims=True)
    spread = jnp.mean(center * center, axis=-1, keepdims=True)
    return center * lax.rsqrt(spread + 1e-06)


def per_device(
    latent, noise_frame, frame_pos, t_index, pos_table, mod_table, w_qkv, qk_gain, w_out
):
    seq_count = lax.axis_size("seq")
    rank = lax.axis_index("seq")
    slot_count = lax.axis_size("slot")
    slot = lax.axis_index("slot")
    rows = latent.shape[1]
    width = latent.shape[2]
    half = seq_count // 2
    layers = w_qkv.shape[0]
    heads = w_qkv.shape[2]
    head_dim = qk_gain.shape[2] // 2
    inv = 1.0 / jnp.sqrt(jnp.float32(head_dim))
    second = rank >= half
    frame_id = jnp.where(second, frame_pos[0, 1], frame_pos[0, 0])
    frame_pick = (jnp.arange(pos_table.shape[0]) == frame_id).astype(jnp.bfloat16)[None, :]
    pos_row = jnp.dot(frame_pick, pos_table, preferred_element_type=jnp.float32)
    stream = (latent[0].astype(jnp.float32) + pos_row).astype(jnp.bfloat16)
    steps_count = mod_table.shape[0]
    time_pick = (jnp.arange(steps_count) == t_index[0]).astype(jnp.bfloat16)[None, :]
    mods = jnp.dot(
        time_pick, mod_table.reshape(steps_count, -1), preferred_element_type=jnp.float32
    )
    mods = mods.reshape(layers, 3, width)
    mask_prev = (slot > 0).astype(jnp.float32)
    mask_next = (slot < slot_count - 1).astype(jnp.float32)
    for layer in range(layers):
        normed = (
            layer_norm(stream.astype(jnp.float32)) * (1.0 + mods[layer, 1]) + mods[layer, 0]
        ).astype(jnp.bfloat16)
        w_layer = w_qkv[layer].reshape(width, -1)
        qkv = jnp.dot(
            lax.all_gather(normed, "seq", axis=0, tiled=True),
            w_layer,
            preferred_element_type=jnp.float32,
        )
        full_len = qkv.shape[0]
        parts = qkv.reshape(full_len, heads, 3, head_dim)
        gains = qk_gain[layer].astype(jnp.float32)
        query = (layer_norm(parts[:, :, 0]) * gains[:, :head_dim]).astype(jnp.bfloat16)
        keyed = (layer_norm(parts[:, :, 1]) * gains[:, head_dim:]).astype(jnp.bfloat16)
        valued = parts[:, :, 2].astype(jnp.bfloat16)
        own_kv = jnp.concatenate([keyed, valued], axis=-1).reshape(full_len, heads * 2 * head_dim)
        lower = shifted(own_kv, "slot", 1)
        upper = shifted(own_kv, "slot", -1)
        block = min(512, full_len)
        query_blocks = query.reshape(full_len // block, block, heads, head_dim)

        def contribution(qblk, kv_rows, mask_value):
            kv_rows = kv_rows.reshape(kv_rows.shape[0], heads, 2 * head_dim)
            scores = (
                jnp.einsum(
                    "qhd,khd->hqk",
                    qblk,
                    kv_rows[:, :, :head_dim],
                    preferred_element_type=jnp.float32,
                )
                * inv
            )
            weights = jnp.exp(scores) * mask_value
            denom = jnp.sum(weights, axis=-1)
            numer = jnp.einsum(
                "hqk,khd->qhd",
                weights.astype(jnp.bfloat16),
                kv_rows[:, :, head_dim:],
                preferred_element_type=jnp.float32,
            )
            return (numer, denom)

        all_kv = jnp.concatenate([lower, own_kv, upper], axis=0)
        ones_row = jnp.ones((full_len,), jnp.float32)
        mask_row = jnp.concatenate([ones_row * mask_prev, ones_row, ones_row * mask_next])

        def one_block(qblk):
            numer, denom = contribution(qblk, all_kv, mask_row)
            return numer / jnp.transpose(denom)[:, :, None]

        attended = lax.map(one_block, query_blocks)
        outputs = attended.astype(jnp.bfloat16).reshape(full_len, heads * head_dim)
        head_w_layer = w_out[layer]
        attn = lax.psum_scatter(
            jnp.dot(outputs, head_w_layer, preferred_element_type=jnp.float32).astype(jnp.bfloat16),
            "seq",
            scatter_dimension=0,
            tiled=True,
        ).astype(jnp.float32)
        stream = (stream.astype(jnp.float32) + mods[layer, 2] * attn).astype(jnp.bfloat16)
    moved = shifted(stream, ("slot", "seq"), -half)
    start_row = jnp.maximum(rank - half, 0) * rows
    fresh = lax.dynamic_slice_in_dim(noise_frame, start_row, rows, 0)
    at_tail = jnp.logical_and(slot == slot_count - 1, second)
    queue_rows = jnp.where(at_tail, fresh, moved)
    return (stream[None], queue_rows[None])


def solution(mesh):
    placed = (
        P("slot", "seq", None),
        P(),
        P("slot", None),
        P("slot"),
        P(),
        P(),
        P(None, None, "seq", None),
        P(None, "seq", None),
        P(None, "seq", None),
    )
    return jax.shard_map(
        per_device,
        mesh=mesh,
        in_specs=placed,
        out_specs=(P("slot", "seq", None), P("slot", "seq", None)),
        check_vma=False,
    )
```

profile of v0, /device:TPU:4, one launch (start us, length us, event | category | flops | bytes accessed | tf_op | source)
XLA Modules:
  0.0 728.4 jit_solution(1093540729877104308)
XLA Ops:
  7.2 1.3 fusion.97
  10.0 1.1 convert_reduce_fusion.1
  11.1 1.1 fusion.62
  12.2 2.7 copy.15
  15.0 3.8 reshape.709
  18.8 5.5 dot_general.52
  25.0 2.2 fusion.46
  27.3 0.8 fusion.65
  28.3 1.8 fusion.95
  30.1 89.8 %all-gather.3.cloned.1.call-done = bf16[1024,3072]{1,0:T(8,128)(2,1)} async-done(((bf16[32,3072]{1,0:T(8,128)(2,1)}), bf16[1024,3072]{1,0:T(8,128)(2,1)}) %all-gather.3.cloned.1.call-update) | async-done | bytes 6291472 | tf_op jit(solution)/shard_map/all_gather | solution.py:52
  119.9 5.0 fusion.48
  125.2 1.9 collective-permute-start
  127.2 3.8 collective-permute-start.1
  131.0 0.2 squeeze.44
  131.3 1.7 collective-permute-done
  133.0 1.7 collective-permute-done.1
  134.7 1.1 pad_maximum_fusion
  135.8 0.4 copy.17
  136.2 5.7 while.20
  136.2 1.4 fusion.110
  137.6 1.4 fusion.111
  139.0 1.4 fusion.110
  140.4 1.4 fusion.111
  141.9 0.1 copy.18
  142.1 4.5 convolution_convert_fusion.1
  146.6 221.8 %reduce-scatter.3.cloned.1.call-done = bf16[32,3072]{1,0:T(8,128)(2,1)} async-done(((bf16[1024,3072]{1,0:T(8,128)(2,1)}), bf16[32,3072]{1,0:T(8,128)(2,1)}) %reduce-scatter.3.cloned.1.call-update) | async-done | bytes 196624 | tf_op jit(solution)/shard_map/reduce_scatter | solution.py:100
  368.4 1.1 convert_reduce_fusion
  369.5 0.2 fusion.58
  369.8 0.8 fusion.61
  370.8 88.1 %all-gather.5.cloned.1.call-done = bf16[1024,3072]{1,0:T(8,128)(2,1)} async-done(((bf16[32,3072]{1,0:T(8,128)(2,1)}), bf16[1024,3072]{1,0:T(8,128)(2,1)}) %all-gather.5.cloned.1.call-update) | async-done | bytes 6291472 | tf_op jit(solution)/shard_map/all_gather | solution.py:52
  458.8 5.0 fusion.51
  464.1 1.9 collective-permute-start.2
  466.1 3.9 collective-permute-start.3
  470.0 0.2 squeeze.48
  470.3 1.5 collective-permute-done.2
  471.8 1.8 collective-permute-done.3
  473.6 0.4 copy.20
  474.0 5.7 while.21
  474.1 1.4 fusion.113
  475.5 1.4 fusion.114
  476.9 1.4 fusion.113
  478.3 1.4 fusion.114
  479.9 4.5 convolution_convert_fusion
  484.4 221.9 %reduce-scatter.5.cloned.1.call-done = bf16[32,3072]{1,0:T(8,128)(2,1)} async-done(((bf16[1024,3072]{1,0:T(8,128)(2,1)}), bf16[32,3072]{1,0:T(8,128)(2,1)}) %reduce-scatter.5.cloned.1.call-update) | async-done | bytes 196624 | tf_op jit(solution)/shard_map/reduce_scatter | solution.py:100
  706.4 1.0 fusion.67
  707.4 1.9 collective-permute-start.4
  709.3 10.9 %collective-permute-done.4 = bf16[32,3072]{1,0:T(8,128)(2,1)S(1)} collective-permute-done((bf16[32,3072]{1,0:T(8,128)(2,1)S(1)}, bf16[32,3072]{1,0:T(8,128)(2,1)S(1)}, u32[]{:S(2)}, u32[]{:S(2)}) %collective-permute-start.4) | collective-permute-done | bytes 196640 | tf_op jit(solution)/shard_map/ppermute | solution.py:10
  720.2 1.7 select_bitcast_fusion
  (63 shorter events, 1.6 us)
Async XLA Ops:
  7.2 2.7 copy-start
  7.2 112.7 %all-gather.3.cloned.1.call-start = ((), (), s32[]{:S(2)}) async-start(), calls=%async_computation.2 | async-start | bytes 6488064 | tf_op jit(solution)/shard_map/all_gather | solution.py:52
  15.0 12.3 %copy-start.1 = (bf16[1,32,3072]{2,1,0:T(8,128)(2,1)S(1)}, bf16[1,32,3072]{2,1,0:T(8,128)(2,1)}, u32[]{:S(2)}) copy-start(bf16[1,32,3072]{2,1,0:T(8,128)(2,1)} %param.13) | copy-start | bytes 589828
  15.0 13.2 %copy-start.5 = (bf16[2,1,128]{2,0,1:T(2,128)(2,1)S(1)}, bf16[2,1,128]{2,0,1:T(2,128)(2,1)}, u32[]{:S(2)}) copy-start(bf16[2,1,128]{2,0,1:T(2,128)(2,1)} %param.20) | copy-start | bytes 1540
  28.1 340.3 %reduce-scatter.3.cloned.1.call-start = ((), (), s32[]{:S(2)}) async-start(), calls=%async_computation.3 | async-start | bytes 6488064 | tf_op jit(solution)/shard_map/reduce_scatter | solution.py:100
  125.2 7.8 %collective-permute-start = (bf16[1024,128]{0,1:T(8,128)(2,1)S(1)}, bf16[1024,128]{0,1:T(8,128)(2,1)}, u32[]{:S(2)}, u32[]{:S(2)}) collective-permute-start(bf16[1024,128]{0,1:T(8,128)(2,1)S(1)} %maximum_bitcast_fusion), channel_id=1, source_target_pairs={{0,32},{32,64},{64,96},{96,128},{128,160},{160,192},{192,224},{1,3... | collective-permute-start | bytes 786440 | tf_op jit(solution)/shard_map/ppermute | solution.py:10
  127.2 7.5 %collective-permute-start.1 = (bf16[1024,128]{0,1:T(8,128)(2,1)S(1)}, bf16[1024,128]{0,1:T(8,128)(2,1)}, u32[]{:S(2)}, u32[]{:S(2)}) collective-permute-start(bf16[1024,128]{0,1:T(8,128)(2,1)S(1)} %maximum_bitcast_fusion), channel_id=1, source_target_pairs={{32,0},{64,32},{96,64},{128,96},{160,128},{192,160},{224,192},{33,... | collective-permute-start | bytes 786440 | tf_op jit(solution)/shard_map/ppermute | solution.py:10
  136.2 5.9 copy-start.2
  146.6 312.3 %all-gather.5.cloned.1.call-start = ((), (), s32[]{:S(2)}) async-start(), calls=%async_computation.4 | async-start | bytes 6488064 | tf_op jit(solution)/shard_map/all_gather | solution.py:52
  370.6 335.7 %reduce-scatter.5.cloned.1.call-start = ((), (), s32[]{:S(2)}) async-start(), calls=%async_computation.5 | async-start | bytes 6488064 | tf_op jit(solution)/shard_map/reduce_scatter | solution.py:100
  464.1 7.7 %collective-permute-start.2 = (bf16[1024,128]{0,1:T(8,128)(2,1)S(1)}, bf16[1024,128]{0,1:T(8,128)(2,1)S(1)}, u32[]{:S(2)}, u32[]{:S(2)}) collective-permute-start(bf16[1024,128]{0,1:T(8,128)(2,1)S(1)} %maximum_bitcast_fusion.1), channel_id=1, source_target_pairs={{0,32},{32,64},{64,96},{96,128},{128,160},{160,192},{192,224},{1,3... | collective-permute-start | bytes 786440 | tf_op jit(solution)/shard_map/ppermute | solution.py:10
  466.1 7.5 %collective-permute-start.3 = (bf16[1024,128]{0,1:T(8,128)(2,1)S(1)}, bf16[1024,128]{0,1:T(8,128)(2,1)S(1)}, u32[]{:S(2)}, u32[]{:S(2)}) collective-permute-start(bf16[1024,128]{0,1:T(8,128)(2,1)S(1)} %maximum_bitcast_fusion.1), channel_id=1, source_target_pairs={{32,0},{64,32},{96,64},{128,96},{160,128},{192,160},{224,192},{33,... | collective-permute-start | bytes 786440 | tf_op jit(solution)/shard_map/ppermute | solution.py:10
  474.0 5.9 copy-start.3
  707.4 14.5 %copy-start.4 = (bf16[32,3072]{1,0:T(8,128)(2,1)}, bf16[32,3072]{1,0:T(8,128)(2,1)S(1)}, u32[]{:S(2)}) copy-start(bf16[32,3072]{1,0:T(8,128)(2,1)S(1)} %fusion.67) | copy-start | bytes 589828
  707.4 12.8 %collective-permute-start.4 = (bf16[32,3072]{1,0:T(8,128)(2,1)S(1)}, bf16[32,3072]{1,0:T(8,128)(2,1)S(1)}, u32[]{:S(2)}, u32[]{:S(2)}) collective-permute-start(bf16[32,3072]{1,0:T(8,128)(2,1)S(1)} %fusion.67), channel_id=1, source_target_pairs={{16,0},{17,1},{18,2},{19,3},{20,4},{21,5},{22,6},{23,7},{24,8},{25... | collective-permute-start | bytes 589832 | tf_op jit(solution)/shard_map/ppermute | solution.py:10
Sparse Core Ops, SparseCore 0:
  28.2 91.6 all-gather.2
  146.7 221.6 reduce-scatter.2
  371.9 86.8 all-gather.4
  484.6 221.7 reduce-scatter.4
where the time goes:
time: 729 us; the launch traced here: 728 us
  waiting for transfers between devices  639 us (88%)
  matrix products  32.6 us (4%)
  local copies, waits for them, and re-layouts  17 us (2%)
  between operations  16.2 us (2%)
  starting transfers between devices  13.6 us (2%)
  other arithmetic  9.74 us (1%)
    reduce_scatter x2, waiting for transfers between devices, per_device(): lax.psum_scatter(jnp.dot(outputs, head_w_layer, preferred_element_type=jn...  444 us
    all_gather x2, waiting for transfers between devices, per_device(): lax.all_gather(normed, 'seq', axis=0, tiled=True)  178 us
    ppermute x5, waiting for transfers between devices, shifted(): return lax.ppermute(block, axis, route)  17.5 us
  transfers between devices with their start and end apart: 9, of which 9 were waited for; matrix products, arithmetic and copies ran while one was open for 0% of the time, Pallas kernels for 0%

commit v1 on v0

v1 whole, which is shorter than its diff:
```python
import functools

import jax
import jax.numpy as jnp
from jax import lax
from jax.experimental import pallas as pl
from jax.experimental.pallas import tpu as pltpu
from jax.sharding import Mesh, PartitionSpec as P

BF = jnp.bfloat16
F32 = jnp.float32
EPS = 1e-6
NX, NC, NZ, NY = 4, 2, 8, 4
D = 3072
HD = 64
ROWS = 32
QUARTER = D // NY
EIGHTH = QUARTER // 2
VMEM_LIMIT = 48 * 1024 * 1024

VM = pl.BlockSpec(memory_space=pltpu.VMEM)
SM = pl.BlockSpec(memory_space=pltpu.SMEM)


def params():
    return pltpu.CompilerParams(vmem_limit_bytes=VMEM_LIMIT)


def normalized(blocks):
    mean = sum(jnp.sum(b, axis=-1, keepdims=True) for b in blocks) / D
    centers = [b - mean for b in blocks]
    spread = sum(jnp.sum(c * c, axis=-1, keepdims=True) for c in centers) / D
    inv = lax.rsqrt(spread + EPS)
    return [c * inv for c in centers]


def head_rows(value):
    center = value - jnp.mean(value, axis=0, keepdims=True)
    spread = jnp.mean(center * center, axis=0, keepdims=True)
    return center * lax.rsqrt(spread + EPS)


def store_head(out, result):
    out[0:HD, :] = head_rows(result[0:HD]).astype(BF)
    out[HD : 2 * HD, :] = head_rows(result[HD : 2 * HD]).astype(BF)
    out[2 * HD :, :] = result[2 * HD :].astype(BF)


def times(weight, h):
    return lax.dot_general(weight, h, (((1,), (1,)), ((), ())), preferred_element_type=F32)


def qkv_first_kernel(idx, *refs):
    shards = refs[0:8]
    shift, scale, own = refs[8:11]
    mine, other = refs[11:14], refs[14:17]
    out, h = refs[17:19]
    z, y, core = idx[0], idx[1], idx[2]
    for k in range(NZ):
        value = shards[k][...].astype(F32)
        at = lax.rem(z + k, NZ)
        (norm,) = normalized([value])
        for b in range(NY):
            cols = slice(b * QUARTER, (b + 1) * QUARTER)
            part = norm[:, cols] * (1.0 + scale[b : b + 1, :]) + shift[b : b + 1, :]
            h[b, at] = part.astype(BF)

    def tokens(b):
        return h[b].reshape(NZ * ROWS, QUARTER)

    for j in range(NY):
        if j == 0:
            total = sum(times(own[:, b * QUARTER : (b + 1) * QUARTER], tokens(b)) for b in range(NY))
        else:
            total = None
            for weight, side in ((mine[j - 1], core), (other[j - 1], 1 - core)):
                for t in range(2):
                    term = times(weight[:, t * QUARTER : (t + 1) * QUARTER], tokens(2 * side + t))
                    total = term if total is None else total + term
        store_head(out.at[lax.rem(y + j, NY)], total)


def qkv_first(idx, shards, shift, scale, own, mine, other):
    return pl.pallas_call(
        qkv_first_kernel,
        out_shape=jax.ShapeDtypeStruct((NY, 3 * HD, NZ * ROWS), BF),
        in_specs=[SM] + [VM] * 17,
        out_specs=VM,
        scratch_shapes=[pltpu.VMEM((NY, NZ, ROWS, QUARTER), BF)],
        compiler_params=params(),
        cost_estimate=pl.CostEstimate(flops=1_200_000_000, bytes_accessed=7_000_000, transcendentals=0),
        name="qkv_first",
    )(idx, *shards, shift, scale, own, *mine, *other)


def qkv_second_kernel(idx, x0, x1, x2, x3, shift, scale, mine, other, out, h):
    y, core = idx[1], idx[2]

    @pl.when(pl.program_id(0) == 0)
    def _():
        for r in range(NY):
            rows = slice(r * ROWS, (r + 1) * ROWS)
            blocks = [x[s, rows, :].astype(F32) for x in (x0, x1, x2, x3) for s in range(2)]
            norms = normalized(blocks)
            for j in range(NY):
                b = lax.rem(y + j, NY)
                for s in range(2):
                    cols = slice(s * EIGHTH, (s + 1) * EIGHTH)
                    part = norms[2 * j + s] * (1.0 + scale[b, :, cols]) + shift[b, :, cols]
                    h[b, rows, cols] = part.astype(BF)

    total = None
    for weight, side in ((mine, core), (other, 1 - core)):
        for t in range(2):
            term = times(weight[0, :, t * QUARTER : (t + 1) * QUARTER], h[2 * side + t])
            total = term if total is None else total + term
    store_head(out.at[0], total)


def qkv_second(idx, tiles, shift, scale, mine, other):
    tile = pl.BlockSpec((2, NY * ROWS, EIGHTH), lambda i: (0, 0, 0))
    mods = pl.BlockSpec((NY, 1, QUARTER), lambda i: (0, 0, 0))
    weight = pl.BlockSpec((1, 3 * HD, D // 2), lambda i: (i, 0, 0))
    return pl.pallas_call(
        qkv_second_kernel,
        grid=(NZ,),
        out_shape=jax.ShapeDtypeStruct((NZ, 3 * HD, NY * ROWS), BF),
        in_specs=[SM] + [tile] * 4 + [mods] * 2 + [weight] * 2,
        out_specs=pl.BlockSpec((1, 3 * HD, NY * ROWS), lambda i: (i, 0, 0)),
        scratch_shapes=[pltpu.VMEM((NY, NY * ROWS, QUARTER), BF)],
        compiler_params=params(),
        cost_estimate=pl.CostEstimate(flops=1_200_000_000, bytes_accessed=10_500_000, transcendentals=0),
        name="qkv_second",
    )(idx, *tiles, shift, scale, mine, other)


def attention_kernel(groups, idx, own, lower, upper, gain, out, acc, den, queries):
    length = 1024 // groups
    per = 256 // length
    g = gain[0:HD, :] * gain[HD:, :] * 0.125

    def wide(ref, n, lo, hi):
        if per == 1:
            return ref[n, lo:hi, :]
        return jnp.concatenate([ref[n * per + i, lo:hi, :] for i in range(per)], axis=1)

    for n in range(4):
        queries[n] = (wide(own, n, 0, HD).astype(F32) * g).astype(BF)
    acc[...] = jnp.zeros_like(acc)
    den[...] = jnp.zeros_like(den)

    def source(ref, first):
        def body(m, carry):
            q = queries[m]
            total = acc[m]
            norm = den[m]
            for n in range(4):
                keys = wide(ref, n, first, first + HD)
                values = wide(ref, n, first + HD, first + 2 * HD)
                score = lax.dot_general(keys, q, (((0,), (0,)), ((), ())), preferred_element_type=F32)
                e = jnp.exp(score)
                norm = norm + jnp.sum(e, axis=0, keepdims=True)
                total = total + jnp.dot(values, e.astype(BF), preferred_element_type=F32)
            acc[m] = total
            den[m] = norm
            return carry

        lax.fori_loop(0, 4, body, 0)

    source(own, HD)

    @pl.when(idx[3] == 1)
    def _():
        source(lower, 0)

    @pl.when(idx[4] == 1)
    def _():
        source(upper, 0)

    if per == 1:
        done = [acc[n] / den[n] for n in range(4)]
        for z in range(NZ):
            cols = slice(z * ROWS, (z + 1) * ROWS)
            out[z] = jnp.concatenate([d[:, cols] for d in done], axis=1).astype(BF)
    else:
        for n in range(4):
            done = (acc[n] / den[n]).astype(BF)
            for i in range(per):
                out[n * per + i] = done[:, i * length : (i + 1) * length]


def attention(idx, own, lower, upper, gain):
    groups = own.shape[0]
    return pl.pallas_call(
        functools.partial(attention_kernel, groups),
        out_shape=jax.ShapeDtypeStruct((NZ, HD, NY * ROWS), BF),
        in_specs=[SM] + [VM] * 4,
        out_specs=VM,
        scratch_shapes=[
            pltpu.VMEM((4, HD, 256), F32),
            pltpu.VMEM((4, 1, 256), F32),
            pltpu.VMEM((4, HD, 256), BF),
        ],
        compiler_params=params(),
        cost_estimate=pl.CostEstimate(flops=3_000_000_000, bytes_accessed=1_200_000, transcendentals=3_000_000),
        name="attention_%d" % groups,
    )(idx, own, lower, upper, gain)


def project_kernel(idx, o0, o1, o2, o3, mine, other, gate, x, out, joined):
    core = idx[2]
    for j, o in enumerate((o0, o1, o2, o3)):
        for z in range(NZ):
            joined[z, j] = o[z]
    rows = joined[...].reshape(NZ * NY * HD, NY * ROWS)
    for weight, side in ((mine, core), (other, 1 - core)):
        w = weight[...].reshape(NZ * NY * HD, EIGHTH)
        attn = lax.dot_general(rows, w, (((0,), (0,)), ((), ())), preferred_element_type=F32)
        out[side] = (x[side].astype(F32) + gate[side] * attn).astype(BF)


def project(idx, parts, mine, other, gate, x):
    return pl.pallas_call(
        project_kernel,
        out_shape=jax.ShapeDtypeStruct((2, NY * ROWS, EIGHTH), BF),
        in_specs=[SM] + [VM] * 8,
        out_specs=VM,
        scratch_shapes=[pltpu.VMEM((NZ, NY, HD, NY * ROWS), BF)],
        compiler_params=params(),
        cost_estimate=pl.CostEstimate(flops=420_000_000, bytes_accessed=4_000_000, transcendentals=0),
        name="project",
    )(idx, *parts, mine, other, gate, x)


def from_ahead(block, axis, size, distance):
    return lax.ppermute(block, axis, [(i, (i - distance) % size) for i in range(size)])


def swap(block):
    return lax.ppermute(block, "core", [(0, 1), (1, 0)])


def shifted(block, axis, distance):
    devices = range(lax.axis_size(axis))
    route = [(i - distance, i) for i in devices if i - distance in devices]
    return lax.ppermute(block, axis, route)


def per_device(
    latent, noise_frame, frame_pos, t_index, pos_table, mod_table, w_qkv, qk_gain, w_out
):
    core, z, y = lax.axis_index("core"), lax.axis_index("z"), lax.axis_index("y")
    slot = lax.axis_index(("x", "core"))
    slots = NX * NC
    has_prev = (slot > 0).astype(jnp.int32)
    has_next = (slot < slots - 1).astype(jnp.int32)
    idx = jnp.stack([z, y, core, has_prev, has_next]).astype(jnp.int32)
    second = z >= NZ // 2

    frame_id = jnp.where(second, frame_pos[0, 1], frame_pos[0, 0])
    pos_row = lax.dynamic_slice_in_dim(pos_table, frame_id, 1, 0)
    x0 = (latent[0].astype(F32) + pos_row.astype(F32)).astype(BF)
    mods = lax.dynamic_slice_in_dim(mod_table, t_index[0], 1, 0)[0].astype(F32)
    gates = lax.dynamic_slice_in_dim(mods[:, 2].reshape(2, NY, 2, 1, EIGHTH), y, 1, 1)[:, 0]
    gains = qk_gain[:, 0].astype(F32)[:, :, None]

    w_t = jnp.transpose(w_qkv[:, :, 0, :], (0, 2, 1))
    half = lax.dynamic_slice_in_dim(w_t, core * (D // 2), D // 2, 2)

    shards = [x0] + [from_ahead(x0, "z", NZ, k) for k in range(1, NZ)]
    mine = [from_ahead(half[0], "y", NY, j) for j in range(1, NY)]
    other = [swap(m) for m in mine]

    def out_columns(layer):
        parts = []
        for j in range(NY):
            start = lax.rem(y - j + NY, NY) * QUARTER + core * EIGHTH
            part = lax.dynamic_slice_in_dim(w_out[layer], start, EIGHTH, 1)
            parts.append(part if j == 0 else from_ahead(part, "y", NY, j))
        return lax.all_gather(jnp.stack(parts), "z", axis=0, tiled=False)

    x_split = jnp.transpose(x0.reshape(ROWS, NY, 2, EIGHTH), (1, 2, 0, 3))
    x_tile = lax.all_to_all(x_split, "y", 0, 0, tiled=True)
    x_tile = jnp.transpose(x_tile, (1, 0, 2, 3)).reshape(2, NY * ROWS, EIGHTH)

    wo_mine = out_columns(0)
    wo_other = swap(wo_mine)
    wq_mine = lax.all_gather(half[1], "z", axis=0, tiled=False)
    wq_other = swap(wq_mine)
    wo1_mine = out_columns(1)
    wo1_other = swap(wo1_mine)

    def attend(heads, axis, layer):
        own = lax.all_to_all(heads, axis, 0, 0, tiled=True)
        kv = own[:, HD:]
        lower = shifted(kv, ("x", "core"), 1)
        upper = shifted(kv, ("x", "core"), -1)
        done = attention(idx, own, lower, upper, gains[layer])
        done = lax.all_to_all(done, "z", 0, 0, tiled=True)
        return [done] + [from_ahead(done, "y", NY, j) for j in range(1, NY)]

    shift, scale = mods[0, 0].reshape(NY, QUARTER), mods[0, 1].reshape(NY, QUARTER)
    heads = qkv_first(idx, shards, shift, scale, w_t[0], mine, other)
    x_tile = project(idx, attend(heads, "y", 0), wo_mine, wo_other, gates[0], x_tile)

    tiles = [x_tile] + [from_ahead(x_tile, "y", NY, j) for j in range(1, NY)]
    shift, scale = mods[1, 0].reshape(NY, 1, QUARTER), mods[1, 1].reshape(NY, 1, QUARTER)
    heads = qkv_second(idx, tiles, shift, scale, wq_mine, wq_other)
    x_tile = project(idx, attend(heads, "z", 1), wo1_mine, wo1_other, gates[1], x_tile)

    split = jnp.transpose(x_tile.reshape(2, NY, ROWS, EIGHTH), (1, 0, 2, 3))
    rows = lax.all_to_all(split, "y", 0, 0, tiled=True)
    stream = jnp.transpose(rows, (2, 0, 1, 3)).reshape(ROWS, D)

    seq_half = NZ * NY // 2
    rank = z * NY + y
    moved = shifted(stream, ("x", "core", "z", "y"), -seq_half)
    start_row = jnp.maximum(rank - seq_half, 0) * ROWS
    fresh = lax.dynamic_slice_in_dim(noise_frame, start_row, ROWS, 0)
    at_tail = jnp.logical_and(slot == slots - 1, second)
    queue_rows = jnp.where(at_tail, fresh, moved)
    return (stream[None], queue_rows[None])


def solution(mesh):
    grid = Mesh(mesh.devices.reshape(NX, NC, NZ, NY), ("x", "core", "z", "y"))
    slot, seq = ("x", "core"), ("z", "y")
    placed = (
        P(slot, seq, None),
        P(),
        P(slot, None),
        P(slot),
        P(),
        P(),
        P(None, None, seq, None),
        P(None, seq, None),
        P(None, seq, None),
    )
    return jax.shard_map(
        per_device,
        mesh=grid,
        in_specs=placed,
        out_specs=(P(slot, seq, None), P(slot, seq, None)),
        check_vma=False,
    )
```

time: 729 us -> 367 us (0.50)
  waiting for transfers between devices: 639 us -> 157 us
  starting transfers between devices: 13.6 us -> 85.3 us
  Pallas kernels: 0 us -> 34.4 us
  blocking collectives: 0 us -> 33.8 us
  matrix products: 32.6 us -> 0 us
  local copies, waits for them, and re-layouts: 17 us -> 25.8 us
    reduce_scatter x2 -> x0, waiting for transfers between devices: 444 us -> none  [per_device(): lax.psum_scatter(jnp.dot(outputs, head_w_layer, preferred_element_type=jn...]
    all_gather x2 -> x3, waiting for transfers between devices: 178 us -> 52.5 us  [the longest x1 52.5 us: per_device(): wq_mine = lax.all_gather(half[1], 'z', axis=0, tiled=False)]
    ppermute x0 -> x31, waiting for transfers between devices: none -> 65.5 us  [the longest x25 65.5 us: from_ahead(): lax.ppermute(block, axis, [(i, (i - distance) % size) for i in range(size)])]
    ppermute x0 -> x31, starting transfers between devices: none -> 55 us  [the longest x25 54.2 us: from_ahead(): lax.ppermute(block, axis, [(i, (i - distance) % size) for i in range(size)])]
    pallas_call x0 -> x6, Pallas kernels: none -> 34.4 us  [the longest x2 17.3 us: attention(): pl.pallas_call(functools.partial(attention_kernel, groups), out_shape=jax...]
    all_to_all x0 -> x3, blocking collectives: none -> 33.8 us  [the longest x1 13 us: attend(): own = lax.all_to_all(heads, axis, 0, 0, tiled=True)]
    dot_general x14 -> x0, matrix products: 32.6 us -> none  [the longest x2 9.99 us: per_device(): jnp.dot(lax.all_gather(normed, 'seq', axis=0, tiled=True), w_layer, prefe...]
    all_to_all x0 -> x3, waiting for transfers between devices: none -> 25.1 us  [the longest x1 14.8 us: attend(): own = lax.all_to_all(heads, axis, 0, 0, tiled=True)]
  transfers between devices with their start and end apart: 9 -> 42, of which waited for: 9 -> 27; matrix products, arithmetic and copies ran while one was open for 0% -> 5% of each run, Pallas kernels for 0% -> 9%
where the time goes in v1:
time: 367 us; the launch traced here: 360 us
  waiting for transfers between devices  157 us (43%)
  starting transfers between devices  85.3 us (23%)
  Pallas kernels  34.4 us (9%)
  blocking collectives  33.8 us (9%)
  local copies, waits for them, and re-layouts  25.8 us (7%)
  between operations  16.1 us (4%)
  other arithmetic  8.34 us (2%)
    ppermute x25, waiting for transfers between devices, from_ahead(): lax.ppermute(block, axis, [(i, (i - distance) % size) for i in range(size)])  65.5 us
    ppermute x25, starting transfers between devices, from_ahead(): lax.ppermute(block, axis, [(i, (i - distance) % size) for i in range(size)])  54.2 us
    all_gather x1, waiting for transfers between devices, per_device(): wq_mine = lax.all_gather(half[1], 'z', axis=0, tiled=False)  52.5 us
    pallas_call x2, Pallas kernels, attention(): pl.pallas_call(functools.partial(attention_kernel, groups), out_shape=jax...  17.3 us
    all_to_all x1, waiting for transfers between devices, attend(): own = lax.all_to_all(heads, axis, 0, 0, tiled=True)  14.8 us
    ppermute x5, starting transfers between devices, shifted(): return lax.ppermute(block, axis, route)  13.9 us
    ppermute x5, waiting for transfers between devices, shifted(): return lax.ppermute(block, axis, route)  13.5 us
    all_to_all x1, blocking collectives, attend(): own = lax.all_to_all(heads, axis, 0, 0, tiled=True)  13 us
  transfers between devices with their start and end apart: 42, of which 27 were waited for; matrix products, arithmetic and copies ran while one was open for 5% of the time, Pallas kernels for 9%

profile of v1, /device:TPU:4, one launch (start us, length us, event | category | flops | bytes accessed | tf_op | source)
XLA Modules:
  0.0 360.3 jit_solution(7135056769322178934)
XLA Ops:
  10.0 3.1 collective-permute-start.18
  14.9 3.8 %collective-permute-done.19 = bf16[64,384]{1,0:T(8,128)(2,1)S(1)} collective-permute-done((bf16[64,384]{1,0:T(8,128)(2,1)S(1)}, bf16[64,384]{1,0:T(8,128)(2,1)S(1)}, u32[]{:S(2)}, u32[]{:S(2)}) %collective-permute-start.19) | collective-permute-done | bytes 49184 | tf_op jit(solution)/shard_map/ppermute | solution.py:236
  20.0 52.5 %all-gather.6.cloned.1.call-done.mine = bf16[8,192,1536]{2,1,0:T(8,128)(2,1)} async-done(((bf16[1,192,1536]{2,1,0:T(8,128)(2,1)}), bf16[8,192,1536]{2,1,0:T(8,128)(2,1)}) %all-gather.6.cloned.1.call-update) | async-done | bytes 4718608 | tf_op jit(solution)/shard_map/all_gather | solution.py:288
  74.9 2.1 fusion.5
  78.5 2.2 collective-permute-start.1
  80.6 2.2 collective-permute-start.2
  82.8 2.8 collective-permute-start.31
  87.4 2.6 collective-permute-start.32
  90.0 3.0 collective-permute-done.32
  94.1 4.5 %collective-permute-done.33 = bf16[64,384]{1,0:T(8,128)(2,1)S(1)} collective-permute-done((bf16[64,384]{1,0:T(8,128)(2,1)S(1)}, bf16[64,384]{1,0:T(8,128)(2,1)S(1)}, u32[]{:S(2)}, u32[]{:S(2)}) %collective-permute-start.33) | collective-permute-done | bytes 49184 | tf_op jit(solution)/shard_map/ppermute | solution.py:236
  98.6 3.0 collective-permute-start.3
  101.6 2.0 collective-permute-start.7
  103.6 8.4 %collective-permute-done.2.refs_3_ = bf16[32,3072]{1,0:T(8,128)(2,1)S(1)} collective-permute-done((bf16[32,3072]{1,0:T(8,128)(2,1)S(1)}, bf16[32,3072]{1,0:T(8,128)(2,1)S(1)}, u32[]{:S(2)}, u32[]{:S(2)}) %collective-permute-start.2) | collective-permute-done | bytes 196640 | tf_op jit(solution)/shard_map/ppermute | solution.py:236
  113.5 13.0 %collective-permute-start.4 = (bf16[32,3072]{1,0:T(8,128)(2,1)S(1)}, bf16[32,3072]{1,0:T(8,128)(2,1)S(1)}, u32[]{:S(2)}, u32[]{:S(2)}) collective-permute-start(bf16[32,3072]{1,0:T(8,128)(2,1)S(1)} %fusion.refs_0_), channel_id=1, source_target_pairs={{0,12},{4,16},{8,20},{12,24},{16,28},{20,0},{24,4},{28,8},{1,13},{... | collective-permute-start | bytes 589832 | tf_op jit(solution)/shard_map/ppermute | solution.py:236
  126.5 15.4 %collective-permute-done.4.refs_5_ = bf16[32,3072]{1,0:T(8,128)(2,1)S(1)} collective-permute-done((bf16[32,3072]{1,0:T(8,128)(2,1)S(1)}, bf16[32,3072]{1,0:T(8,128)(2,1)S(1)}, u32[]{:S(2)}, u32[]{:S(2)}) %collective-permute-start.4) | collective-permute-done | bytes 196640 | tf_op jit(solution)/shard_map/ppermute | solution.py:236
  141.9 4.2 %collective-permute-start.5 = (bf16[32,3072]{1,0:T(8,128)(2,1)S(1)}, bf16[32,3072]{1,0:T(8,128)(2,1)S(1)}, u32[]{:S(2)}, u32[]{:S(2)}) collective-permute-start(bf16[32,3072]{1,0:T(8,128)(2,1)S(1)} %fusion.refs_0_), channel_id=1, source_target_pairs={{0,8},{4,12},{8,16},{12,20},{16,24},{20,28},{24,0},{28,4},{1,9},{5... | collective-permute-start | bytes 589832 | tf_op jit(solution)/shard_map/ppermute | solution.py:236
  146.9 3.9 %collective-permute-done.5.refs_6_ = bf16[32,3072]{1,0:T(8,128)(2,1)S(1)} collective-permute-done((bf16[32,3072]{1,0:T(8,128)(2,1)S(1)}, bf16[32,3072]{1,0:T(8,128)(2,1)S(1)}, u32[]{:S(2)}, u32[]{:S(2)}) %collective-permute-start.5) | collective-permute-done | bytes 196640 | tf_op jit(solution)/shard_map/ppermute | solution.py:236
  150.8 3.7 %collective-permute-start.6 = (bf16[32,3072]{1,0:T(8,128)(2,1)S(1)}, bf16[32,3072]{1,0:T(8,128)(2,1)S(1)}, u32[]{:S(2)}, u32[]{:S(2)}) collective-permute-start(bf16[32,3072]{1,0:T(8,128)(2,1)S(1)} %fusion.refs_0_), channel_id=1, source_target_pairs={{0,4},{4,8},{8,12},{12,16},{16,20},{20,24},{24,28},{28,0},{1,5},{5... | collective-permute-start | bytes 589832 | tf_op jit(solution)/shard_map/ppermute | solution.py:236
  155.1 2.3 slice_bitcast_fusion.refs_10_
  158.1 3.1 collective-permute-done.6.refs_7_
  163.4 2.1 fusion.8
  173.4 5.5 %qkv_first.1 = bf16[4,192,256]{2,1,0:T(8,128)(2,1)S(1)} custom-call(s32[5]{0:T(128)S(1)} %stack.57.idx, bf16[32,3072]{1,0:T(8,128)(2,1)S(1)} %fusion.refs_0_, bf16[32,3072]{1,0:T(8,128)(2,1)S(1)} %collective-permute-done.refs_1_, bf16[32,3072]{1,0:T(8,128)(2,1)S(1)} %collective-permute-done.1.refs_2_, bf16[32,3072]{1,0:T(8,128)(2,1)S(1)} %collective-permute-done.2.refs_3_, ...), custom_call_target="tpu_custom_call" | custom-call | flops 1200000000 | bytes 7000000 | tf_op jit(solution)/shard_map/qkv_first/pallas_call | solution.py:84
  178.9 13.0 %all_to_all.30.own = bf16[4,192,256]{2,1,0:T(8,128)(2,1)S(1)} all-to-all(bf16[4,192,256]{2,1,0:T(8,128)(2,1)S(1)} %qkv_first.1), channel_id=1, replica_groups=mesh['x'=4,'core'=2,'z'=8,'y'=4] {'y'}, dimensions={0} | all-to-all | bytes 786432 | tf_op jit(solution)/shard_map/all_to_all | solution.py:294
  191.9 1.9 collective-permute-start.13
  193.8 3.6 %collective-permute-start.14 = (bf16[4,128,256]{2,1,0:T(8,128)(2,1)S(1)}, bf16[4,128,256]{2,1,0:T(8,128)(2,1)S(1)}, u32[]{:S(2)}, u32[]{:S(2)}) collective-permute-start(bf16[4,128,256]{2,1,0:T(8,128)(2,1)S(1)} %slice.90), channel_id=1, source_target_pairs={{32,0},{64,32},{96,64},{128,96},{160,128},{192,160},{224,192},{33,... | collective-permute-start | bytes 786440 | tf_op jit(solution)/shard_map/ppermute | solution.py:246
  197.4 2.1 reshape.60
  201.3 8.7 %attention_4.1 = bf16[8,64,128]{2,1,0:T(8,128)(2,1)S(1)} custom-call(s32[5]{0:T(128)S(1)} %stack.57.idx, bf16[4,192,256]{2,1,0:T(8,128)(2,1)S(1)} %all_to_all.30.own, bf16[4,128,256]{2,1,0:T(8,128)(2,1)S(1)} %collective-permute-done.13.lower, bf16[4,128,256]{2,1,0:T(8,128)(2,1)S(1)} %collective-permute-done.14.upper, f32[128,1]{1,0:T(8,128)S(1)} %copy.22.gain), custom_call_target="tpu_custom_call" | custom-call | flops 3000000000 | bytes 1200000 | tf_op jit(solution)/shard_map/attention_4/pallas_call | solution.py:194
  210.7 8.8 %all-to-all-start.1 = ((bf16[8,64,128]{2,1,0:T(8,128)(2,1)}), bf16[8,64,128]{2,1,0:T(8,128)(2,1)S(1)}, u32[]{:S(2)}, u32[]{:S(2)}) async-start(bf16[8,64,128]{2,1,0:T(8,128)(2,1)} %copy-done.13), calls=%async_computation.1 | async-start | bytes 262144 | tf_op jit(solution)/shard_map/all_to_all | solution.py:299
  221.3 8.7 %all-to-all-done.1.o0 = bf16[8,64,128]{2,1,0:T(8,128)(2,1)S(1)} async-done(((bf16[8,64,128]{2,1,0:T(8,128)(2,1)}), bf16[8,64,128]{2,1,0:T(8,128)(2,1)S(1)}, u32[]{:S(2)}, u32[]{:S(2)}) %all-to-all-start.1) | async-done | bytes 131104 | tf_op jit(solution)/shard_map/all_to_all | solution.py:299
  229.9 4.0 %all-to-all-start.2 = ((bf16[4,2,32,384]{3,2,1,0:T(8,128)(2,1)}), bf16[4,2,32,384]{3,2,1,0:T(8,128)(2,1)}, u32[]{:S(2)}, u32[]{:S(2)}) async-start(bf16[4,2,32,384]{3,2,1,0:T(8,128)(2,1)} %fusion.2), calls=%async_computation.2 | async-start | bytes 393216 | tf_op jit(solution)/shard_map/all_to_all | solution.py:283
  233.9 3.2 collective-permute-start.15
  251.6 5.5 %collective-permute-done.22.x1 = bf16[2,128,384]{2,1,0:T(8,128)(2,1)S(1)} collective-permute-done((bf16[2,128,384]{2,1,0:T(8,128)(2,1)S(1)}, bf16[2,128,384]{2,1,0:T(8,128)(2,1)S(1)}, u32[]{:S(2)}, u32[]{:S(2)}) %collective-permute-start.22) | collective-permute-done | bytes 196640 | tf_op jit(solution)/shard_map/ppermute | solution.py:236
  257.1 2.4 collective-permute-done.23.x2
  259.5 2.4 collective-permute-done.24.x3
  261.9 2.3 copy-done
  264.3 8.5 %qkv_second.1 = bf16[8,192,128]{2,1,0:T(8,128)(2,1)} custom-call(s32[5]{0:T(128)S(1)} %stack.57.idx, bf16[2,128,384]{2,1,0:T(8,128)(2,1)S(1)} %project.2.x0.x, bf16[2,128,384]{2,1,0:T(8,128)(2,1)S(1)} %collective-permute-done.22.x1, bf16[2,128,384]{2,1,0:T(8,128)(2,1)S(1)} %collective-permute-done.23.x2, ...), custom_call_target="tpu_custom_call" | custom-call | flops 1200000000 | bytes 10500000 | tf_op jit(solution)/shard_map/qkv_second/pallas_call | solution.py:124
  272.8 3.5 all-to-all-start.3
  276.3 14.8 %all-to-all-done.3.own = bf16[8,192,128]{2,1,0:T(8,128)(2,1)S(1)} async-done(((bf16[8,192,128]{2,1,0:T(8,128)(2,1)}), bf16[8,192,128]{2,1,0:T(8,128)(2,1)S(1)}, u32[]{:S(2)}, u32[]{:S(2)}) %all-to-all-start.3) | async-done | bytes 393248 | tf_op jit(solution)/shard_map/all_to_all | solution.py:294
  291.2 1.9 collective-permute-start.26
  293.1 3.6 %collective-permute-start.27 = (bf16[8,128,128]{2,1,0:T(8,128)(2,1)S(1)}, bf16[8,128,128]{2,1,0:T(8,128)(2,1)S(1)}, u32[]{:S(2)}, u32[]{:S(2)}) collective-permute-start(bf16[8,128,128]{2,1,0:T(8,128)(2,1)S(1)} %slice.95), channel_id=1, source_target_pairs={{32,0},{64,32},{96,64},{128,96},{160,128},{192,160},{224,192},{33,... | collective-permute-start | bytes 786440 | tf_op jit(solution)/shard_map/ppermute | solution.py:246
  296.9 2.0 collective-permute-done.26.lower
  300.7 8.6 %attention_8.1 = bf16[8,64,128]{2,1,0:T(8,128)(2,1)S(1)} custom-call(s32[5]{0:T(128)S(1)} %stack.57.idx, bf16[8,192,128]{2,1,0:T(8,128)(2,1)S(1)} %all-to-all-done.3.own, bf16[8,128,128]{2,1,0:T(8,128)(2,1)S(1)} %collective-permute-done.26.lower, bf16[8,128,128]{2,1,0:T(8,128)(2,1)S(1)} %collective-permute-done.27.upper, f32[128,1]{1,0:T(8,128)S(1)} %copy.25.gain), custom_call_target="tpu_custom_call" | custom-call | flops 3000000000 | bytes 1200000 | tf_op jit(solution)/shard_map/attention_8/pallas_call | solution.py:194
  309.2 12.1 %all_to_all.31.o0 = bf16[8,64,128]{2,1,0:T(8,128)(2,1)S(1)} all-to-all(bf16[8,64,128]{2,1,0:T(8,128)(2,1)S(1)} %attention_8.1), channel_id=1, replica_groups=mesh['x'=4,'core'=2,'z'=8,'y'=4] {'z'}, dimensions={0} | all-to-all | bytes 262144 | tf_op jit(solution)/shard_map/all_to_all | solution.py:299
  323.9 3.2 collective-permute-done.28.o1
  327.1 2.0 collective-permute-done.29.o2
  331.4 8.7 %all_to_all.32 = bf16[4,2,32,384]{3,2,1,0:T(8,128)(2,1)S(1)} all-to-all(bf16[4,2,32,384]{3,2,1,0:T(8,128)(2,1)S(1)} %bitcast.82), channel_id=1, replica_groups=mesh['x'=4,'core'=2,'z'=8,'y'=4] {'y'}, dimensions={0} | all-to-all | bytes 393216 | tf_op jit(solution)/shard_map/all_to_all | solution.py:312
  340.4 2.8 collective-permute-start.35
  344.0 8.1 %collective-permute-done.35 = bf16[32,3072]{1,0:T(8,128)(2,1)S(1)} collective-permute-done((bf16[32,3072]{1,0:T(8,128)(2,1)S(1)}, bf16[32,3072]{1,0:T(8,128)(2,1)S(1)}, u32[]{:S(2)}, u32[]{:S(2)}) %collective-permute-start.35) | collective-permute-done | bytes 196640 | tf_op jit(solution)/shard_map/ppermute | solution.py:246
  (128 shorter events, 52.3 us)
Async XLA Ops:
  7.2 65.3 %all-gather.6.cloned.1.call-start = ((), (), s32[]{:S(2)}) async-start(), calls=%async_computation.6 | async-start | bytes 5308416 | tf_op jit(solution)/shard_map/all_gather | solution.py:288
  9.5 63.0 %copy-start.20 = (s32[1,2]{1,0:T(1,128)S(1)}, s32[1,2]{1,0:T(1,128)}, u32[]{:S(2)}) copy-start(s32[1,2]{1,0:T(1,128)} %param.11) | copy-start | bytes 28
  9.5 67.5 %copy-start.18 = (bf16[1,32,3072]{2,1,0:T(8,128)(2,1)S(1)}, bf16[1,32,3072]{2,1,0:T(8,128)(2,1)}, u32[]{:S(2)}) copy-start(bf16[1,32,3072]{2,1,0:T(8,128)(2,1)} %param.9) | copy-start | bytes 589828
  9.5 152.4 %all-gather.8.cloned.1.call-start = ((), (), s32[]{:S(2)}) async-start(), calls=%async_computation.7 | async-start | bytes 1769472 | tf_op jit(solution)/shard_map/all_gather | solution.py:280
  10.0 4.9 %collective-permute-start.18 = (bf16[64,384]{1,0:T(8,128)(2,1)S(1)}, bf16[64,384]{1,0:T(8,128)(2,1)S(1)}, u32[]{:S(2)}, u32[]{:S(2)}) collective-permute-start(bf16[64,384]{1,0:T(8,128)(2,1)S(1)} %get-tuple-element.17), channel_id=1, source_target_pairs={{0,3},{1,0},{2,1},{3,2},{4,7},{5,4},{6,5},{7,6},{8,11},{9,8},{10,9... | collective-permute-start | bytes 147464 | tf_op jit(solution)/shard_map/ppermute | solution.py:236
  13.1 5.6 %collective-permute-start.19 = (bf16[64,384]{1,0:T(8,128)(2,1)S(1)}, bf16[64,384]{1,0:T(8,128)(2,1)S(1)}, u32[]{:S(2)}, u32[]{:S(2)}) collective-permute-start(bf16[64,384]{1,0:T(8,128)(2,1)S(1)} %get-tuple-element.16), channel_id=1, source_target_pairs={{0,2},{1,3},{2,0},{3,1},{4,6},{5,7},{6,4},{7,5},{8,10},{9,11},{10,... | collective-permute-start | bytes 147464 | tf_op jit(solution)/shard_map/ppermute | solution.py:236
  13.7 5.5 %collective-permute-start.20 = (bf16[64,384]{1,0:T(8,128)(2,1)S(1)}, bf16[64,384]{1,0:T(8,128)(2,1)S(1)}, u32[]{:S(2)}, u32[]{:S(2)}) collective-permute-start(bf16[64,384]{1,0:T(8,128)(2,1)S(1)} %get-tuple-element.15), channel_id=1, source_target_pairs={{0,1},{1,2},{2,3},{3,0},{4,5},{5,6},{6,7},{7,4},{8,9},{9,10},{10,1... | collective-permute-start | bytes 147464 | tf_op jit(solution)/shard_map/ppermute | solution.py:236
  20.0 256.3 %all-gather.10.cloned.1.call-start = ((), (), s32[]{:S(2)}) async-start(), calls=%async_computation.8 | async-start | bytes 1769472 | tf_op jit(solution)/shard_map/all_gather | solution.py:280
  72.5 189.5 %collective-permute-start.25 = (bf16[8,192,1536]{2,1,0:T(8,128)(2,1)}, bf16[8,192,1536]{2,1,0:T(8,128)(2,1)}, u32[]{:S(2)}, u32[]{:S(2)}) collective-permute-start(bf16[8,192,1536]{2,1,0:T(8,128)(2,1)} %all-gather.6.cloned.1.call-done.mine), channel_id=1, source_target_pairs={{0,32},{32,0},{1,33},{33,1},{2,34},{34,2},{3,35},{35,3},{4,36},{36... | collective-permute-start | bytes 14155784 | tf_op jit(solution)/shard_map/ppermute | solution.py:240
  77.0 24.6 %collective-permute-start = (bf16[32,3072]{1,0:T(8,128)(2,1)S(1)}, bf16[32,3072]{1,0:T(8,128)(2,1)S(1)}, u32[]{:S(2)}, u32[]{:S(2)}) collective-permute-start(bf16[32,3072]{1,0:T(8,128)(2,1)S(1)} %fusion.refs_0_), channel_id=1, source_target_pairs={{0,28},{4,0},{8,4},{12,8},{16,12},{20,16},{24,20},{28,24},{1,29},{... | collective-permute-start | bytes 589832 | tf_op jit(solution)/shard_map/ppermute | solution.py:236
  78.5 25.1 %collective-permute-start.1 = (bf16[32,3072]{1,0:T(8,128)(2,1)S(1)}, bf16[32,3072]{1,0:T(8,128)(2,1)S(1)}, u32[]{:S(2)}, u32[]{:S(2)}) collective-permute-start(bf16[32,3072]{1,0:T(8,128)(2,1)S(1)} %fusion.refs_0_), channel_id=1, source_target_pairs={{0,24},{4,28},{8,0},{12,4},{16,8},{20,12},{24,16},{28,20},{1,25},{... | collective-permute-start | bytes 589832 | tf_op jit(solution)/shard_map/ppermute | solution.py:236
  80.6 31.4 %collective-permute-start.2 = (bf16[32,3072]{1,0:T(8,128)(2,1)S(1)}, bf16[32,3072]{1,0:T(8,128)(2,1)S(1)}, u32[]{:S(2)}, u32[]{:S(2)}) collective-permute-start(bf16[32,3072]{1,0:T(8,128)(2,1)S(1)} %fusion.refs_0_), channel_id=1, source_target_pairs={{0,20},{4,24},{8,28},{12,0},{16,4},{20,8},{24,12},{28,16},{1,21},{... | collective-permute-start | bytes 589832 | tf_op jit(solution)/shard_map/ppermute | solution.py:236
  82.8 4.6 %collective-permute-start.31 = (bf16[64,384]{1,0:T(8,128)(2,1)S(1)}, bf16[64,384]{1,0:T(8,128)(2,1)S(1)}, u32[]{:S(2)}, u32[]{:S(2)}) collective-permute-start(bf16[64,384]{1,0:T(8,128)(2,1)S(1)} %get-tuple-element.13), channel_id=1, source_target_pairs={{0,3},{1,0},{2,1},{3,2},{4,7},{5,4},{6,5},{7,6},{8,11},{9,8},{10,9... | collective-permute-start | bytes 147464 | tf_op jit(solution)/shard_map/ppermute | solution.py:236
  87.4 5.6 %collective-permute-start.32 = (bf16[64,384]{1,0:T(8,128)(2,1)S(1)}, bf16[64,384]{1,0:T(8,128)(2,1)S(1)}, u32[]{:S(2)}, u32[]{:S(2)}) collective-permute-start(bf16[64,384]{1,0:T(8,128)(2,1)S(1)} %get-tuple-element.12), channel_id=1, source_target_pairs={{0,2},{1,3},{2,0},{3,1},{4,6},{5,7},{6,4},{7,5},{8,10},{9,11},{10,... | collective-permute-start | bytes 147464 | tf_op jit(solution)/shard_map/ppermute | solution.py:236
  93.0 5.6 %collective-permute-start.33 = (bf16[64,384]{1,0:T(8,128)(2,1)S(1)}, bf16[64,384]{1,0:T(8,128)(2,1)S(1)}, u32[]{:S(2)}, u32[]{:S(2)}) collective-permute-start(bf16[64,384]{1,0:T(8,128)(2,1)S(1)} %get-tuple-element.11), channel_id=1, source_target_pairs={{0,1},{1,2},{2,3},{3,0},{4,5},{5,6},{6,7},{7,4},{8,9},{9,10},{10,1... | collective-permute-start | bytes 147464 | tf_op jit(solution)/shard_map/ppermute | solution.py:236
  98.6 14.9 %collective-permute-start.3 = (bf16[32,3072]{1,0:T(8,128)(2,1)S(1)}, bf16[32,3072]{1,0:T(8,128)(2,1)S(1)}, u32[]{:S(2)}, u32[]{:S(2)}) collective-permute-start(bf16[32,3072]{1,0:T(8,128)(2,1)S(1)} %fusion.refs_0_), channel_id=1, source_target_pairs={{0,16},{4,20},{8,24},{12,28},{16,0},{20,4},{24,8},{28,12},{1,17},{... | collective-permute-start | bytes 589832 | tf_op jit(solution)/shard_map/ppermute | solution.py:236
  101.6 52.9 %collective-permute-start.7 = (bf16[192,1536]{1,0:T(8,128)(2,1)S(1)}, bf16[192,1536]{1,0:T(8,128)(2,1)S(1)}, u32[]{:S(2)}, u32[]{:S(2)}) collective-permute-start(bf16[192,1536]{1,0:T(8,128)(2,1)S(1)} %get-tuple-element.7), channel_id=1, source_target_pairs={{0,3},{1,0},{2,1},{3,2},{4,7},{5,4},{6,5},{7,6},{8,11},{9,8},{10,9... | collective-permute-start | bytes 1769480 | tf_op jit(solution)/shard_map/ppermute | solution.py:236
  103.6 50.9 %collective-permute-start.8 = (bf16[192,1536]{1,0:T(8,128)(2,1)S(1)}, bf16[192,1536]{1,0:T(8,128)(2,1)S(1)}, u32[]{:S(2)}, u32[]{:S(2)}) collective-permute-start(bf16[192,1536]{1,0:T(8,128)(2,1)S(1)} %get-tuple-element.7), channel_id=1, source_target_pairs={{0,2},{1,3},{2,0},{3,1},{4,6},{5,7},{6,4},{7,5},{8,10},{9,11},{10,... | collective-permute-start | bytes 1769480 | tf_op jit(solution)/shard_map/ppermute | solution.py:236
  112.0 43.0 %collective-permute-start.9 = (bf16[192,1536]{1,0:T(8,128)(2,1)S(1)}, bf16[192,1536]{1,0:T(8,128)(2,1)}, u32[]{:S(2)}, u32[]{:S(2)}) collective-permute-start(bf16[192,1536]{1,0:T(8,128)(2,1)S(1)} %get-tuple-element.7), channel_id=1, source_target_pairs={{0,1},{1,2},{2,3},{3,0},{4,5},{5,6},{6,7},{7,4},{8,9},{9,10},{10,1... | collective-permute-start | bytes 1769480 | tf_op jit(solution)/shard_map/ppermute | solution.py:236
  113.5 48.4 %copy-start.3 = (bf16[32,3072]{1,0:T(8,128)(2,1)}, bf16[32,3072]{1,0:T(8,128)(2,1)S(1)}, u32[]{:S(2)}) copy-start(bf16[32,3072]{1,0:T(8,128)(2,1)S(1)} %collective-permute-done.3.refs_4_) | copy-start | bytes 589828
  113.5 28.4 %collective-permute-start.4 = (bf16[32,3072]{1,0:T(8,128)(2,1)S(1)}, bf16[32,3072]{1,0:T(8,128)(2,1)S(1)}, u32[]{:S(2)}, u32[]{:S(2)}) collective-permute-start(bf16[32,3072]{1,0:T(8,128)(2,1)S(1)} %fusion.refs_0_), channel_id=1, source_target_pairs={{0,12},{4,16},{8,20},{12,24},{16,28},{20,0},{24,4},{28,8},{1,13},{... | collective-permute-start | bytes 589832 | tf_op jit(solution)/shard_map/ppermute | solution.py:236
  141.9 8.9 %collective-permute-start.5 = (bf16[32,3072]{1,0:T(8,128)(2,1)S(1)}, bf16[32,3072]{1,0:T(8,128)(2,1)S(1)}, u32[]{:S(2)}, u32[]{:S(2)}) collective-permute-start(bf16[32,3072]{1,0:T(8,128)(2,1)S(1)} %fusion.refs_0_), channel_id=1, source_target_pairs={{0,8},{4,12},{8,16},{12,20},{16,24},{20,28},{24,0},{28,4},{1,9},{5... | collective-permute-start | bytes 589832 | tf_op jit(solution)/shard_map/ppermute | solution.py:236
  150.8 10.4 %collective-permute-start.6 = (bf16[32,3072]{1,0:T(8,128)(2,1)S(1)}, bf16[32,3072]{1,0:T(8,128)(2,1)S(1)}, u32[]{:S(2)}, u32[]{:S(2)}) collective-permute-start(bf16[32,3072]{1,0:T(8,128)(2,1)S(1)} %fusion.refs_0_), channel_id=1, source_target_pairs={{0,4},{4,8},{8,12},{12,16},{16,20},{20,24},{24,28},{28,0},{1,5},{5... | collective-permute-start | bytes 589832 | tf_op jit(solution)/shard_map/ppermute | solution.py:236
  154.5 13.7 %collective-permute-start.10 = (bf16[192,1536]{1,0:T(8,128)(2,1)S(1)}, bf16[192,1536]{1,0:T(8,128)(2,1)}, u32[]{:S(2)}, u32[]{:S(2)}) collective-permute-start(bf16[192,1536]{1,0:T(8,128)(2,1)S(1)} %collective-permute-done.7.refs_11_), channel_id=1, source_target_pairs={{0,32},{32,0},{1,33},{33,1},{2,34},{34,2},{3,35},{35,3},{4,36},{36... | collective-permute-start | bytes 1769480 | tf_op jit(solution)/shard_map/ppermute | solution.py:240
  154.5 13.7 %collective-permute-start.11 = (bf16[192,1536]{1,0:T(8,128)(2,1)S(1)}, bf16[192,1536]{1,0:T(8,128)(2,1)}, u32[]{:S(2)}, u32[]{:S(2)}) collective-permute-start(bf16[192,1536]{1,0:T(8,128)(2,1)S(1)} %collective-permute-done.8.refs_12_), channel_id=1, source_target_pairs={{0,32},{32,0},{1,33},{33,1},{2,34},{34,2},{3,35},{35,3},{4,36},{36... | collective-permute-start | bytes 1769480 | tf_op jit(solution)/shard_map/ppermute | solution.py:240
  155.0 13.2 %collective-permute-start.12 = (bf16[192,1536]{1,0:T(8,128)(2,1)}, bf16[192,1536]{1,0:T(8,128)(2,1)}, u32[]{:S(2)}, u32[]{:S(2)}) collective-permute-start(bf16[192,1536]{1,0:T(8,128)(2,1)} %collective-permute-done.9.refs_13_), channel_id=1, source_target_pairs={{0,32},{32,0},{1,33},{33,1},{2,34},{34,2},{3,35},{35,3},{4,36},{36... | collective-permute-start | bytes 1769480 | tf_op jit(solution)/shard_map/ppermute | solution.py:240
  161.9 84.6 %collective-permute-start.21 = (bf16[8,4,64,384]{3,2,1,0:T(8,128)(2,1)}, bf16[8,4,64,384]{3,2,1,0:T(8,128)(2,1)S(1)}, u32[]{:S(2)}, u32[]{:S(2)}) collective-permute-start(bf16[8,4,64,384]{3,2,1,0:T(8,128)(2,1)} %bitcast.73), channel_id=1, source_target_pairs={{0,32},{32,0},{1,33},{33,1},{2,34},{34,2},{3,35},{35,3},{4,36},{36... | collective-permute-start | bytes 4718600 | tf_op jit(solution)/shard_map/ppermute | solution.py:240
  191.9 7.8 %collective-permute-start.13 = (bf16[4,128,256]{2,1,0:T(8,128)(2,1)S(1)}, bf16[4,128,256]{2,1,0:T(8,128)(2,1)S(1)}, u32[]{:S(2)}, u32[]{:S(2)}) collective-permute-start(bf16[4,128,256]{2,1,0:T(8,128)(2,1)S(1)} %slice.90), channel_id=1, source_target_pairs={{0,32},{32,64},{64,96},{96,128},{128,160},{160,192},{192,224},{1,3... | collective-permute-start | bytes 786440 | tf_op jit(solution)/shard_map/ppermute | solution.py:246
  193.8 7.5 %collective-permute-start.14 = (bf16[4,128,256]{2,1,0:T(8,128)(2,1)S(1)}, bf16[4,128,256]{2,1,0:T(8,128)(2,1)S(1)}, u32[]{:S(2)}, u32[]{:S(2)}) collective-permute-start(bf16[4,128,256]{2,1,0:T(8,128)(2,1)S(1)} %slice.90), channel_id=1, source_target_pairs={{32,0},{64,32},{96,64},{128,96},{160,128},{192,160},{224,192},{33,... | collective-permute-start | bytes 786440 | tf_op jit(solution)/shard_map/ppermute | solution.py:246
  199.7 39.2 %slice-start = ((f32[2,3,3072]{2,0,1:T(2,128)}), f32[2,1,3072]{2,0,1:T(2,128)S(1)}, s32[]{:S(2)}) async-start(f32[2,3,3072]{2,0,1:T(2,128)} %bitcast_convert_fusion), calls=%async_computation.9 | async-start | bytes 49152 | tf_op jit(solution)/shard_map/slice | solution.py:264
  210.7 35.8 %copy-start.1 = (bf16[32,64,384]{2,1,0:T(8,128)(2,1)S(1)}, bf16[32,64,384]{2,1,0:T(8,128)(2,1)}, u32[]{:S(2)}) copy-start(bf16[32,64,384]{2,1,0:T(8,128)(2,1)} %all-gather.8.cloned.1.call-done) | copy-start | bytes 4718596
  210.7 19.2 %all-to-all-start.1 = ((bf16[8,64,128]{2,1,0:T(8,128)(2,1)}), bf16[8,64,128]{2,1,0:T(8,128)(2,1)S(1)}, u32[]{:S(2)}, u32[]{:S(2)}) async-start(bf16[8,64,128]{2,1,0:T(8,128)(2,1)} %copy-done.13), calls=%async_computation.1 | async-start | bytes 262144 | tf_op jit(solution)/shard_map/all_to_all | solution.py:299
  229.9 10.6 %all-to-all-start.2 = ((bf16[4,2,32,384]{3,2,1,0:T(8,128)(2,1)}), bf16[4,2,32,384]{3,2,1,0:T(8,128)(2,1)}, u32[]{:S(2)}, u32[]{:S(2)}) async-start(bf16[4,2,32,384]{3,2,1,0:T(8,128)(2,1)} %fusion.2), calls=%async_computation.2 | async-start | bytes 393216 | tf_op jit(solution)/shard_map/all_to_all | solution.py:283
  233.9 8.6 %collective-permute-start.15 = (bf16[8,64,128]{2,1,0:T(8,128)(2,1)S(1)}, bf16[8,64,128]{2,1,0:T(8,128)(2,1)S(1)}, u32[]{:S(2)}, u32[]{:S(2)}) collective-permute-start(bf16[8,64,128]{2,1,0:T(8,128)(2,1)S(1)} %all-to-all-done.1.o0), channel_id=1, source_target_pairs={{0,3},{1,0},{2,1},{3,2},{4,7},{5,4},{6,5},{7,6},{8,11},{9,8},{10,9... | collective-permute-start | bytes 393224 | tf_op jit(solution)/shard_map/ppermute | solution.py:236
  237.1 8.0 %collective-permute-start.16 = (bf16[8,64,128]{2,1,0:T(8,128)(2,1)S(1)}, bf16[8,64,128]{2,1,0:T(8,128)(2,1)}, u32[]{:S(2)}, u32[]{:S(2)}) collective-permute-start(bf16[8,64,128]{2,1,0:T(8,128)(2,1)S(1)} %all-to-all-done.1.o0), channel_id=1, source_target_pairs={{0,2},{1,3},{2,0},{3,1},{4,6},{5,7},{6,4},{7,5},{8,10},{9,11},{10,... | collective-permute-start | bytes 393224 | tf_op jit(solution)/shard_map/ppermute | solution.py:236
  238.0 8.5 %collective-permute-start.17 = (bf16[8,64,128]{2,1,0:T(8,128)(2,1)S(1)}, bf16[8,64,128]{2,1,0:T(8,128)(2,1)}, u32[]{:S(2)}, u32[]{:S(2)}) collective-permute-start(bf16[8,64,128]{2,1,0:T(8,128)(2,1)S(1)} %all-to-all-done.1.o0), channel_id=1, source_target_pairs={{0,1},{1,2},{2,3},{3,0},{4,5},{5,6},{6,7},{7,4},{8,9},{9,10},{10,1... | collective-permute-start | bytes 393224 | tf_op jit(solution)/shard_map/ppermute | solution.py:236
  249.2 7.9 %collective-permute-start.22 = (bf16[2,128,384]{2,1,0:T(8,128)(2,1)S(1)}, bf16[2,128,384]{2,1,0:T(8,128)(2,1)S(1)}, u32[]{:S(2)}, u32[]{:S(2)}) collective-permute-start(bf16[2,128,384]{2,1,0:T(8,128)(2,1)S(1)} %project.2.x0.x), channel_id=1, source_target_pairs={{0,3},{1,0},{2,1},{3,2},{4,7},{5,4},{6,5},{7,6},{8,11},{9,8},{10,9... | collective-permute-start | bytes 589832 | tf_op jit(solution)/shard_map/ppermute | solution.py:236
  250.1 9.4 %collective-permute-start.23 = (bf16[2,128,384]{2,1,0:T(8,128)(2,1)S(1)}, bf16[2,128,384]{2,1,0:T(8,128)(2,1)S(1)}, u32[]{:S(2)}, u32[]{:S(2)}) collective-permute-start(bf16[2,128,384]{2,1,0:T(8,128)(2,1)S(1)} %project.2.x0.x), channel_id=1, source_target_pairs={{0,2},{1,3},{2,0},{3,1},{4,6},{5,7},{6,4},{7,5},{8,10},{9,11},{10,... | collective-permute-start | bytes 589832 | tf_op jit(solution)/shard_map/ppermute | solution.py:236
  251.6 10.4 %collective-permute-start.24 = (bf16[2,128,384]{2,1,0:T(8,128)(2,1)S(1)}, bf16[2,128,384]{2,1,0:T(8,128)(2,1)S(1)}, u32[]{:S(2)}, u32[]{:S(2)}) collective-permute-start(bf16[2,128,384]{2,1,0:T(8,128)(2,1)S(1)} %project.2.x0.x), channel_id=1, source_target_pairs={{0,1},{1,2},{2,3},{3,0},{4,5},{5,6},{6,7},{7,4},{8,9},{9,10},{10,1... | collective-permute-start | bytes 589832 | tf_op jit(solution)/shard_map/ppermute | solution.py:236
  272.8 18.4 %all-to-all-start.3 = ((bf16[8,192,128]{2,1,0:T(8,128)(2,1)}), bf16[8,192,128]{2,1,0:T(8,128)(2,1)S(1)}, u32[]{:S(2)}, u32[]{:S(2)}) async-start(bf16[8,192,128]{2,1,0:T(8,128)(2,1)} %qkv_second.1), calls=%async_computation.3 | async-start | bytes 786432 | tf_op jit(solution)/shard_map/all_to_all | solution.py:294
  276.2 47.6 %collective-permute-start.34 = (bf16[8,4,64,384]{3,2,1,0:T(8,128)(2,1)}, bf16[8,4,64,384]{3,2,1,0:T(8,128)(2,1)S(1)}, u32[]{:S(2)}, u32[]{:S(2)}) collective-permute-start(bf16[8,4,64,384]{3,2,1,0:T(8,128)(2,1)} %bitcast.75), channel_id=1, source_target_pairs={{0,32},{32,0},{1,33},{33,1},{2,34},{34,2},{3,35},{35,3},{4,36},{36... | collective-permute-start | bytes 4718600 | tf_op jit(solution)/shard_map/ppermute | solution.py:240
  291.2 7.7 %collective-permute-start.26 = (bf16[8,128,128]{2,1,0:T(8,128)(2,1)S(1)}, bf16[8,128,128]{2,1,0:T(8,128)(2,1)S(1)}, u32[]{:S(2)}, u32[]{:S(2)}) collective-permute-start(bf16[8,128,128]{2,1,0:T(8,128)(2,1)S(1)} %slice.95), channel_id=1, source_target_pairs={{0,32},{32,64},{64,96},{96,128},{128,160},{160,192},{192,224},{1,3... | collective-permute-start | bytes 786440 | tf_op jit(solution)/shard_map/ppermute | solution.py:246
  293.1 7.5 %collective-permute-start.27 = (bf16[8,128,128]{2,1,0:T(8,128)(2,1)S(1)}, bf16[8,128,128]{2,1,0:T(8,128)(2,1)S(1)}, u32[]{:S(2)}, u32[]{:S(2)}) collective-permute-start(bf16[8,128,128]{2,1,0:T(8,128)(2,1)S(1)} %slice.95), channel_id=1, source_target_pairs={{32,0},{64,32},{96,64},{128,96},{160,128},{192,160},{224,192},{33,... | collective-permute-start | bytes 786440 | tf_op jit(solution)/shard_map/ppermute | solution.py:246
  296.9 33.1 %copy-start.2 = (bf16[32,64,384]{2,1,0:T(8,128)(2,1)S(1)}, bf16[32,64,384]{2,1,0:T(8,128)(2,1)}, u32[]{:S(2)}) copy-start(bf16[32,64,384]{2,1,0:T(8,128)(2,1)} %all-gather.10.cloned.1.call-done) | copy-start | bytes 4718596
  321.3 5.8 %collective-permute-start.28 = (bf16[8,64,128]{2,1,0:T(8,128)(2,1)S(1)}, bf16[8,64,128]{2,1,0:T(8,128)(2,1)S(1)}, u32[]{:S(2)}, u32[]{:S(2)}) collective-permute-start(bf16[8,64,128]{2,1,0:T(8,128)(2,1)S(1)} %all_to_all.31.o0), channel_id=1, source_target_pairs={{0,3},{1,0},{2,1},{3,2},{4,7},{5,4},{6,5},{7,6},{8,11},{9,8},{10,9... | collective-permute-start | bytes 393224 | tf_op jit(solution)/shard_map/ppermute | solution.py:236
  321.3 7.8 %collective-permute-start.29 = (bf16[8,64,128]{2,1,0:T(8,128)(2,1)S(1)}, bf16[8,64,128]{2,1,0:T(8,128)(2,1)S(1)}, u32[]{:S(2)}, u32[]{:S(2)}) collective-permute-start(bf16[8,64,128]{2,1,0:T(8,128)(2,1)S(1)} %all_to_all.31.o0), channel_id=1, source_target_pairs={{0,2},{1,3},{2,0},{3,1},{4,6},{5,7},{6,4},{7,5},{8,10},{9,11},{10,... | collective-permute-start | bytes 393224 | tf_op jit(solution)/shard_map/ppermute | solution.py:236
  322.5 7.5 %collective-permute-start.30 = (bf16[8,64,128]{2,1,0:T(8,128)(2,1)S(1)}, bf16[8,64,128]{2,1,0:T(8,128)(2,1)S(1)}, u32[]{:S(2)}, u32[]{:S(2)}) collective-permute-start(bf16[8,64,128]{2,1,0:T(8,128)(2,1)S(1)} %all_to_all.31.o0), channel_id=1, source_target_pairs={{0,1},{1,2},{2,3},{3,0},{4,5},{5,6},{6,7},{7,4},{8,9},{9,10},{10,1... | collective-permute-start | bytes 393224 | tf_op jit(solution)/shard_map/ppermute | solution.py:236
  340.4 11.7 %collective-permute-start.35 = (bf16[32,3072]{1,0:T(8,128)(2,1)S(1)}, bf16[32,3072]{1,0:T(8,128)(2,1)S(1)}, u32[]{:S(2)}, u32[]{:S(2)}) collective-permute-start(bf16[32,3072]{1,0:T(8,128)(2,1)S(1)} %reshape.55), channel_id=1, source_target_pairs={{16,0},{17,1},{18,2},{19,3},{20,4},{21,5},{22,6},{23,7},{24,8},{25... | collective-permute-start | bytes 589832 | tf_op jit(solution)/shard_map/ppermute | solution.py:246
  (17 other events, 98.7 us)
Sparse Core Ops, SparseCore 0:
  9.8 62.6 all-gather.5
  74.3 58.9 all-gather.7
  147.0 41.3 all-gather.9

commit v2 on v1

v2 whole, which is shorter than its diff:
```python
import functools

import jax
import jax.numpy as jnp
from jax import lax
from jax.experimental import pallas as pl
from jax.experimental.pallas import tpu as pltpu
from jax.sharding import Mesh, PartitionSpec as P

BF = jnp.bfloat16
F32 = jnp.float32
EPS = 1e-6
NX, NC, NZ, NY = 4, 2, 8, 4
D = 3072
HD = 64
ROWS = 32
QUARTER = D // NY
EIGHTH = QUARTER // 2
VMEM_LIMIT = 48 * 1024 * 1024

VM = pl.BlockSpec(memory_space=pltpu.VMEM)
SM = pl.BlockSpec(memory_space=pltpu.SMEM)


def params():
    return pltpu.CompilerParams(vmem_limit_bytes=VMEM_LIMIT)


def normalized(blocks):
    mean = sum(jnp.sum(b, axis=-1, keepdims=True) for b in blocks) / D
    centers = [b - mean for b in blocks]
    spread = sum(jnp.sum(c * c, axis=-1, keepdims=True) for c in centers) / D
    inv = lax.rsqrt(spread + EPS)
    return [c * inv for c in centers]


def head_rows(value):
    center = value - jnp.mean(value, axis=0, keepdims=True)
    spread = jnp.mean(center * center, axis=0, keepdims=True)
    return center * lax.rsqrt(spread + EPS)


def store_head(out, result):
    out[0:HD, :] = head_rows(result[0:HD]).astype(BF)
    out[HD : 2 * HD, :] = head_rows(result[HD : 2 * HD]).astype(BF)
    out[2 * HD :, :] = result[2 * HD :].astype(BF)


def times(weight, h):
    return lax.dot_general(weight, h, (((1,), (1,)), ((), ())), preferred_element_type=F32)


def qkv_first_kernel(idx, *refs):
    shards = refs[0:8]
    mods, own = refs[8:10]
    mine, other = refs[10:13], refs[13:16]
    out, h = refs[16:18]
    core, z, y = idx[1], idx[2], idx[3]
    for k in range(NZ):
        value = shards[k][...].astype(F32)
        at = lax.rem(z + k, NZ)
        (norm,) = normalized([value])
        for b in range(NY):
            cols = slice(b * QUARTER, (b + 1) * QUARTER)
            part = norm[:, cols] * (1.0 + mods[1:2, cols]) + mods[0:1, cols]
            h[b, at] = part.astype(BF)

    def tokens(b):
        return h[b].reshape(NZ * ROWS, QUARTER)

    for j in range(NY):
        if j == 0:
            total = sum(times(own[0, :, b * QUARTER : (b + 1) * QUARTER], tokens(b)) for b in range(NY))
        else:
            total = None
            for weight, side in ((mine[j - 1], core), (other[j - 1], 1 - core)):
                for t in range(2):
                    term = times(weight[:, t * QUARTER : (t + 1) * QUARTER], tokens(2 * side + t))
                    total = term if total is None else total + term
        store_head(out.at[lax.rem(y + j, NY)], total)


def qkv_first(idx, shards, mods, w_t, mine, other):
    return pl.pallas_call(
        qkv_first_kernel,
        out_shape=jax.ShapeDtypeStruct((NY, 3 * HD, NZ * ROWS), BF),
        in_specs=[SM] + [VM] * 16,
        out_specs=VM,
        scratch_shapes=[pltpu.VMEM((NY, NZ, ROWS, QUARTER), BF)],
        compiler_params=params(),
        cost_estimate=pl.CostEstimate(flops=1_200_000_000, bytes_accessed=7_000_000, transcendentals=0),
        name="qkv_first",
    )(idx, *shards, mods, w_t, *mine, *other)


def qkv_second_kernel(idx, x0, x1, x2, x3, mods, weight, out, h):
    y = idx[3]

    @pl.when(pl.program_id(0) == 0)
    def _():
        for r in range(NY):
            rows = slice(r * ROWS, (r + 1) * ROWS)
            blocks = [x[s, rows, :].astype(F32) for x in (x0, x1, x2, x3) for s in range(2)]
            norms = normalized(blocks)
            for j in range(NY):
                b = lax.rem(y + j, NY)
                for s in range(2):
                    cols = pl.ds(pl.multiple_of(b * QUARTER + s * EIGHTH, 128), EIGHTH)
                    part = norms[2 * j + s] * (1.0 + mods[4:5, cols]) + mods[3:4, cols]
                    h[b, rows, s * EIGHTH : (s + 1) * EIGHTH] = part.astype(BF)

    total = None
    for b in range(NY):
        w = jnp.concatenate([weight[2 * b, 0], weight[2 * b + 1, 0]], axis=1)
        term = times(w, h[b])
        total = term if total is None else total + term
    store_head(out.at[0], total)


def qkv_second(idx, tiles, mods, weight):
    tile = pl.BlockSpec((2, NY * ROWS, EIGHTH), lambda i: (0, 0, 0))
    return pl.pallas_call(
        qkv_second_kernel,
        grid=(NZ,),
        out_shape=jax.ShapeDtypeStruct((NZ, 3 * HD, NY * ROWS), BF),
        in_specs=[SM]
        + [tile] * 4
        + [pl.BlockSpec((6, D), lambda i: (0, 0))]
        + [pl.BlockSpec((8, 1, 3 * HD, EIGHTH), lambda i: (0, i, 0, 0))],
        out_specs=pl.BlockSpec((1, 3 * HD, NY * ROWS), lambda i: (i, 0, 0)),
        scratch_shapes=[pltpu.VMEM((NY, NY * ROWS, QUARTER), BF)],
        compiler_params=params(),
        cost_estimate=pl.CostEstimate(flops=1_200_000_000, bytes_accessed=10_500_000, transcendentals=0),
        name="qkv_second",
    )(idx, *tiles, mods, weight)


def attention_kernel(groups, idx, own, lower, upper, gain, out, acc, den, queries):
    length = 1024 // groups
    per = 256 // length
    slot = idx[0] * NC + idx[1]
    column = jnp.transpose(jnp.broadcast_to(gain[...], (8, 2 * HD)))[:, 0:1]
    g = column[0:HD] * column[HD:] * 0.125

    def wide(ref, n, lo, hi):
        if per == 1:
            return ref[n, lo:hi, :]
        return jnp.concatenate([ref[n * per + i, lo:hi, :] for i in range(per)], axis=1)

    for n in range(4):
        queries[n] = (wide(own, n, 0, HD).astype(F32) * g).astype(BF)
    acc[...] = jnp.zeros_like(acc)
    den[...] = jnp.zeros_like(den)

    def source(ref, first):
        def body(m, carry):
            q = queries[m]
            total = acc[m]
            norm = den[m]
            for n in range(4):
                keys = wide(ref, n, first, first + HD)
                values = wide(ref, n, first + HD, first + 2 * HD)
                score = lax.dot_general(keys, q, (((0,), (0,)), ((), ())), preferred_element_type=F32)
                e = jnp.exp(score)
                norm = norm + jnp.sum(e, axis=0, keepdims=True)
                total = total + jnp.dot(values, e.astype(BF), preferred_element_type=F32)
            acc[m] = total
            den[m] = norm
            return carry

        lax.fori_loop(0, 4, body, 0)

    source(own, HD)

    @pl.when(slot > 0)
    def _():
        source(lower, 0)

    @pl.when(slot < NX * NC - 1)
    def _():
        source(upper, 0)

    if per == 1:
        done = [acc[n] / den[n] for n in range(4)]
        for z in range(NZ):
            cols = slice(z * ROWS, (z + 1) * ROWS)
            out[z] = jnp.concatenate([d[:, cols] for d in done], axis=1).astype(BF)
    else:
        for n in range(4):
            done = (acc[n] / den[n]).astype(BF)
            for i in range(per):
                out[n * per + i] = done[:, i * length : (i + 1) * length]


def attention(idx, own, lower, upper, gain):
    groups = own.shape[0]
    return pl.pallas_call(
        functools.partial(attention_kernel, groups),
        out_shape=jax.ShapeDtypeStruct((NZ, HD, NY * ROWS), BF),
        in_specs=[SM] + [VM] * 4,
        out_specs=VM,
        scratch_shapes=[
            pltpu.VMEM((4, HD, 256), F32),
            pltpu.VMEM((4, 1, 256), F32),
            pltpu.VMEM((4, HD, 256), BF),
        ],
        compiler_params=params(),
        cost_estimate=pl.CostEstimate(flops=3_000_000_000, bytes_accessed=1_200_000, transcendentals=3_000_000),
        name="attention_%d" % groups,
    )(idx, own, lower, upper, gain)


def project_kernel(layer, relative, idx, o0, o1, o2, o3, *refs):
    weights = refs[: 2 if relative else 1]
    mods, x, out, absolute = refs[len(weights) :]
    x_pos, core, y = idx[0], idx[1], idx[3]
    for j, o in enumerate((o0, o1, o2, o3)):
        b = lax.rem(y + j, NY)
        for z in range(NZ):
            for half in range(2):
                absolute[b, half, z] = o[z, half * ROWS : (half + 1) * ROWS, :]
    for h in range(2):
        attn = None
        for n, weight in enumerate(weights):
            if relative:
                side = core if n == 0 else 1 - core
                rows = [absolute[lax.rem(x_pos + k, NX), side] for k in range(NX)]
            else:
                rows = [absolute[s // 2, s % 2] for s in range(8)]
            rows = jnp.concatenate([r.reshape(NZ * ROWS, NY * ROWS) for r in rows], axis=0)
            w = weight[:, :, h * ROWS : (h + 1) * ROWS, :].reshape(-1, EIGHTH)
            term = lax.dot_general(rows, w, (((0,), (0,)), ((), ())), preferred_element_type=F32)
            attn = term if attn is None else attn + term
        cols = pl.ds(pl.multiple_of(y * QUARTER + h * EIGHTH, 128), EIGHTH)
        gate = mods[3 * layer + 2 : 3 * layer + 3, cols]
        out[h] = (x[h].astype(F32) + gate * attn).astype(BF)


def project(layer, idx, parts, weights, mods, x):
    relative = len(weights) == 2
    return pl.pallas_call(
        functools.partial(project_kernel, layer, relative),
        out_shape=jax.ShapeDtypeStruct((2, NY * ROWS, EIGHTH), BF),
        in_specs=[SM] + [VM] * (6 + len(weights)),
        out_specs=VM,
        scratch_shapes=[pltpu.VMEM((NY, 2, NZ, ROWS, NY * ROWS), BF)],
        compiler_params=params(),
        cost_estimate=pl.CostEstimate(flops=420_000_000, bytes_accessed=4_000_000, transcendentals=0),
        name="project_%d" % layer,
    )(idx, *parts, *weights, mods, x)


def finish_kernel(idx, rows, q0, q1, q2, q3, fresh, out, queue):
    slot = idx[0] * NC + idx[1]
    z, y = idx[2], idx[3]
    for b in range(NY):
        for h in range(2):
            out[:, b * QUARTER + h * EIGHTH : b * QUARTER + (h + 1) * EIGHTH] = rows[b, h]
    tail = jnp.logical_and(slot == NX * NC - 1, z >= NZ // 2)

    @pl.when(tail)
    def _():
        queue[...] = fresh[...]

    @pl.when(jnp.logical_not(tail))
    def _():
        for j, q in enumerate((q0, q1, q2, q3)):
            b = lax.rem(y - j + NY, NY)
            for h in range(2):
                cols = pl.ds(pl.multiple_of(b * QUARTER + h * EIGHTH, 128), EIGHTH)
                queue[:, cols] = q[h]


def finish(idx, rows, pieces, fresh):
    shape = jax.ShapeDtypeStruct((ROWS, D), BF)
    return pl.pallas_call(
        finish_kernel,
        out_shape=(shape, shape),
        in_specs=[SM] + [VM] * 6,
        out_specs=(VM, VM),
        compiler_params=params(),
        cost_estimate=pl.CostEstimate(flops=0, bytes_accessed=800_000, transcendentals=0),
        name="finish",
    )(idx, rows, *pieces, fresh)


def from_ahead(block, axis, size, distance):
    return lax.ppermute(block, axis, [(i, (i - distance) % size) for i in range(size)])


def swap(block):
    return lax.ppermute(block, "core", [(0, 1), (1, 0)])


def shifted(block, axis, distance):
    devices = range(lax.axis_size(axis))
    route = [(i - distance, i) for i in devices if i - distance in devices]
    return lax.ppermute(block, axis, route)


def after(value, *others):
    return lax.optimization_barrier((value, *others))[0]


ALL = ("x", "core", "z", "y")
SEQ = NZ * NY


def per_device(
    latent, noise_frame, frame_pos, t_index, pos_table, mod_table, w_qkv, qk_gain, w_out
):
    x_pos, core = lax.axis_index("x"), lax.axis_index("core")
    z, y = lax.axis_index("z"), lax.axis_index("y")
    slot = x_pos * NC + core
    idx = jnp.stack([x_pos, core, z, y]).astype(jnp.int32)

    frame_id = jnp.where(z >= NZ // 2, frame_pos[0, 1], frame_pos[0, 0])
    pos_row = lax.dynamic_slice_in_dim(pos_table, frame_id, 1, 0)
    x0 = (latent[0].astype(F32) + pos_row.astype(F32)).astype(BF)
    mods = lax.dynamic_slice_in_dim(mod_table, t_index[0], 1, 0)[0].astype(F32).reshape(6, D)
    gains = qk_gain[:, 0].astype(F32)
    w_t = jnp.transpose(w_qkv[:, :, 0, :], (0, 2, 1))

    half = lax.dynamic_slice_in_dim(w_t[0], core * (D // 2), D // 2, 1)
    mine = [from_ahead(half, "y", NY, j) for j in range(1, NY)]
    ahead, behind = [x0], [x0]
    for _ in range(NZ // 2):
        ahead.append(from_ahead(ahead[-1], "z", NZ, 1))
    for _ in range(NZ // 2 - 1):
        behind.append(from_ahead(behind[-1], "z", NZ, -1))
    shards = ahead + behind[:0:-1]
    other = [swap(m) for m in mine]

    rows_half = lax.dynamic_slice_in_dim(w_out, core * ROWS, ROWS, 1)
    wo = None
    for j in range(NY):
        columns = lax.dynamic_slice_in_dim(rows_half, lax.rem(y + j, NY) * QUARTER, QUARTER, 2)
        if j:
            route = [
                ((s * NZ + c) * NY + s // NC, (s * NZ + c) * NY + (s // NC + j) % NY)
                for s in range(NX * NC)
                for c in range(NZ)
            ]
            columns = lax.ppermute(columns, ALL, route)
        else:
            columns = jnp.where(y == x_pos, columns, jnp.zeros_like(columns))
        wo = columns if wo is None else wo + columns
    wo = jnp.transpose(wo.reshape(2, ROWS, 2, EIGHTH), (0, 2, 1, 3)).reshape(4 * ROWS, EIGHTH)
    wq = lax.dynamic_slice_in_dim(w_t[1], slot * EIGHTH, EIGHTH, 1)
    later = lax.all_gather(jnp.concatenate([wq, wo], axis=0), "z", axis=0, tiled=False)

    x_split = jnp.transpose(x0.reshape(ROWS, NY, 2, EIGHTH), (1, 2, 0, 3))
    x_tile = lax.all_to_all(x_split, "y", 0, 0, tiled=True)
    x_tile = jnp.transpose(x_tile, (1, 0, 2, 3)).reshape(2, NY * ROWS, EIGHTH)

    def attend(own, layer):
        kv = own[:, HD:]
        lower = shifted(kv, ("x", "core"), 1)
        upper = shifted(kv, ("x", "core"), -1)
        done = attention(idx, own, lower, upper, gains[layer : layer + 1])
        done = lax.all_to_all(done, "z", 0, 0, tiled=True)
        return [done] + [from_ahead(done, "y", NY, j) for j in range(1, NY)]

    heads = qkv_first(idx, shards, mods, w_t, mine, other)
    heads, later, x_tile = lax.optimization_barrier((heads, later, x_tile))
    wq1 = lax.all_gather(later[:, : 3 * HD], ("x", "core"), axis=0, tiled=False)
    wo0 = later[:, 3 * HD : 3 * HD + 2 * ROWS]
    wo0 = jnp.stack([wo0] + [from_ahead(wo0, "x", NX, k) for k in range(1, NX)])
    wo0 = [wo0, swap(wo0)]
    wo1 = lax.all_gather(later[:, 3 * HD + 2 * ROWS :], ("x", "core"), axis=0, tiled=False)

    own = lax.all_to_all(heads, "y", 0, 0, tiled=True)
    x_tile = project(0, idx, attend(own, 0), wo0, mods, x_tile)

    tiles = [x_tile] + [from_ahead(x_tile, "y", NY, j) for j in range(1, NY)]
    heads = qkv_second(idx, tiles, mods, wq1)
    own = lax.all_to_all(heads, "z", 0, 0, tiled=True)
    x_tile = project(1, idx, attend(own, 1), [wo1], mods, x_tile)

    split = x_tile.reshape(2, NY, ROWS, EIGHTH)
    rows = lax.all_to_all(jnp.transpose(split, (1, 0, 2, 3)), "y", 0, 0, tiled=True)
    pieces = []
    for j in range(NY):
        piece = lax.dynamic_index_in_dim(split, lax.rem(y + j, NY), 1, keepdims=False)
        route = []
        for source in range(NX * NC * SEQ):
            target = source - source % NY + (source + j) % NY - SEQ // 2
            if target >= 0:
                route.append((source, target))
        pieces.append(lax.ppermute(piece, ALL, route))
    start_row = jnp.maximum(z * NY + y - SEQ // 2, 0) * ROWS
    fresh = lax.dynamic_slice_in_dim(noise_frame, start_row, ROWS, 0)
    stream, queue = finish(idx, rows, pieces, fresh)
    return (stream[None], queue[None])


def solution(mesh):
    grid = Mesh(mesh.devices.reshape(NX, NC, NZ, NY), ("x", "core", "z", "y"))
    slot, seq = ("x", "core"), ("z", "y")
    placed = (
        P(slot, seq, None),
        P(),
        P(slot, None),
        P(slot),
        P(),
        P(),
        P(None, None, seq, None),
        P(None, seq, None),
        P(None, seq, None),
    )
    return jax.shard_map(
        per_device,
        mesh=grid,
        in_specs=placed,
        out_specs=(P(slot, seq, None), P(slot, seq, None)),
        check_vma=False,
    )
```

time: 367 us -> 315 us (0.86); the launches traced: 360 us -> 314 us
  waiting for transfers between devices: 157 us -> 85.3 us
  blocking collectives: 33.8 us -> 56.5 us
    all_gather x3, waiting for transfers between devices: 52.5 us -> 0.01 us  [the longest x1 0.01 us: per_device(): lax.all_gather(jnp.concatenate([wq, wo], axis=0), 'z', axis=0, tiled=False)]
    ppermute x0 -> x7, starting transfers between devices: none -> 28 us  [the longest x4 24.2 us: per_device(): pieces.append(lax.ppermute(piece, ALL, route))]
    ppermute x25 -> x22, starting transfers between devices: 54.2 us -> 35 us  [from_ahead(): lax.ppermute(block, axis, [(i, (i - distance) % size) for i in range(size)])]
    all_to_all x2 -> x1, waiting for transfers between devices: 23.5 us -> 6.27 us  [per_device(): lax.all_to_all(jnp.transpose(split, (1, 0, 2, 3)), 'y', 0, 0, tiled=True)]
    all_to_all x1 -> x2, blocking collectives: 12.1 us -> 26.4 us  [attend(): done = lax.all_to_all(done, 'z', 0, 0, tiled=True)]
    all_to_all x2, blocking collectives: 21.7 us -> 30.1 us  [the longest x1 17.5 us: per_device(): own = lax.all_to_all(heads, 'z', 0, 0, tiled=True)]
    all_to_all x2 -> x1, starting transfers between devices: 12.3 us -> 3.95 us  [per_device(): lax.all_to_all(jnp.transpose(split, (1, 0, 2, 3)), 'y', 0, 0, tiled=True)]
    slice x6 -> x5, local copies, waits for them, and re-layouts: 3.61 us -> 8.45 us  [the longest x1 3.22 us: per_device(): wq = lax.dynamic_slice_in_dim(w_t[1], slot * EIGHTH, EIGHTH, 1)]
  transfers between devices with their start and end apart: 42 -> 42, of which waited for: 27 -> 21; matrix products, arithmetic and copies ran while one was open for 5% -> 6% of each run, Pallas kernels for 9% -> 11%
where the time goes in v2:
time: 315 us; the launch traced here: 314 us
  waiting for transfers between devices  85.3 us (27%)
  starting transfers between devices  83.2 us (26%)
  blocking collectives  56.5 us (18%)
  Pallas kernels  37.8 us (12%)
  local copies, waits for them, and re-layouts  26.6 us (8%)
  between operations  16 us (5%)
  other arithmetic  8.34 us (3%)
    ppermute x22, waiting for transfers between devices, from_ahead(): lax.ppermute(block, axis, [(i, (i - distance) % size) for i in range(size)])  62.3 us
    ppermute x22, starting transfers between devices, from_ahead(): lax.ppermute(block, axis, [(i, (i - distance) % size) for i in range(size)])  35 us
    all_to_all x2, blocking collectives, attend(): done = lax.all_to_all(done, 'z', 0, 0, tiled=True)  26.4 us
    ppermute x4, starting transfers between devices, per_device(): pieces.append(lax.ppermute(piece, ALL, route))  24.2 us
    all_to_all x1, blocking collectives, per_device(): own = lax.all_to_all(heads, 'z', 0, 0, tiled=True)  17.5 us
    pallas_call x2, Pallas kernels, attention(): pl.pallas_call(functools.partial(attention_kernel, groups), out_shape=jax...  17.4 us
    all_to_all x1, blocking collectives, per_device(): own = lax.all_to_all(heads, 'y', 0, 0, tiled=True)  12.6 us
    ppermute x4, waiting for transfers between devices, shifted(): return lax.ppermute(block, axis, route)  11.6 us
  transfers between devices with their start and end apart: 42, of which 21 were waited for; matrix products, arithmetic and copies ran while one was open for 6% of the time, Pallas kernels for 11%

profile of v2, /device:TPU:4, one launch (start us, length us, event | category | flops | bytes accessed | tf_op | source)
XLA Modules:
  0.0 313.7 jit_solution(7154041018427405650)
XLA Ops:
  7.3 2.0 constant_dynamic-slice_fusion.3
  13.1 3.2 %fusion.4 = (bf16[1,192,3072]{2,1,0:T(8,128)(2,1)}, bf16[1,192,3072]{2,1,0:T(8,128)(2,1)}) fusion(bf16[2,192,3072]{2,1,0:T(8,128)(2,1)} %bitcast.59), kind=kLoop, calls=%fused_computation.26 | loop fusion | bytes 4718592 | tf_op jit(solution)/shard_map/slice | solution.py:349
  17.3 3.3 %collective-permute-done.14 = bf16[2,32,768]{2,1,0:T(8,128)(2,1)} collective-permute-done((bf16[2,32,768]{2,1,0:T(8,128)(2,1)S(1)}, bf16[2,32,768]{2,1,0:T(8,128)(2,1)}, u32[]{:S(2)}, u32[]{:S(2)}) %collective-permute-start.14) | collective-permute-done | bytes 98336 | tf_op jit(solution)/shard_map/ppermute | solution.py:344
  22.7 1.9 dynamic-slice_bitcast_fusion
  24.6 3.7 %collective-permute-start.8 = (bf16[192,1536]{1,0:T(8,128)(2,1)}, bf16[192,1536]{1,0:T(8,128)(2,1)}, u32[]{:S(2)}, u32[]{:S(2)}) collective-permute-start(bf16[192,1536]{1,0:T(8,128)(2,1)} %dynamic-slice_bitcast_fusion), channel_id=1, source_target_pairs={{0,2},{1,3},{2,0},{3,1},{4,6},{5,7},{6,4},{7,5},{8,10},{9,11},{10,... | collective-permute-start | bytes 1769480 | tf_op jit(solution)/shard_map/ppermute | solution.py:288
  34.4 5.9 %collective-permute-start = (bf16[32,3072]{1,0:T(8,128)(2,1)S(1)}, bf16[32,3072]{1,0:T(8,128)(2,1)}, u32[]{:S(2)}, u32[]{:S(2)}) collective-permute-start(bf16[32,3072]{1,0:T(8,128)(2,1)S(1)} %fusion.refs_0_), channel_id=1, source_target_pairs={{0,28},{4,0},{8,4},{12,8},{16,12},{20,16},{24,20},{28,24},{1,29},{... | collective-permute-start | bytes 589832 | tf_op jit(solution)/shard_map/ppermute | solution.py:288
  40.4 6.4 %collective-permute-done.refs_1_ = bf16[32,3072]{1,0:T(8,128)(2,1)} collective-permute-done((bf16[32,3072]{1,0:T(8,128)(2,1)S(1)}, bf16[32,3072]{1,0:T(8,128)(2,1)}, u32[]{:S(2)}, u32[]{:S(2)}) %collective-permute-start) | collective-permute-done | bytes 196640 | tf_op jit(solution)/shard_map/ppermute | solution.py:288
  46.8 3.8 %collective-permute-start.1 = (bf16[32,3072]{1,0:T(8,128)(2,1)}, bf16[32,3072]{1,0:T(8,128)(2,1)}, u32[]{:S(2)}, u32[]{:S(2)}) collective-permute-start(bf16[32,3072]{1,0:T(8,128)(2,1)} %collective-permute-done.refs_1_), channel_id=1, source_target_pairs={{0,28},{4,0},{8,4},{12,8},{16,12},{20,16},{24,20},{28,24},{1,29},{... | collective-permute-start | bytes 589832 | tf_op jit(solution)/shard_map/ppermute | solution.py:288
  50.6 2.1 reshape.42
  52.8 5.0 %collective-permute-done.1.refs_2_ = bf16[32,3072]{1,0:T(8,128)(2,1)} collective-permute-done((bf16[32,3072]{1,0:T(8,128)(2,1)}, bf16[32,3072]{1,0:T(8,128)(2,1)}, u32[]{:S(2)}, u32[]{:S(2)}) %collective-permute-start.1) | collective-permute-done | bytes 196640 | tf_op jit(solution)/shard_map/ppermute | solution.py:288
  57.8 3.7 %collective-permute-start.2 = (bf16[32,3072]{1,0:T(8,128)(2,1)}, bf16[32,3072]{1,0:T(8,128)(2,1)}, u32[]{:S(2)}, u32[]{:S(2)}) collective-permute-start(bf16[32,3072]{1,0:T(8,128)(2,1)} %collective-permute-done.1.refs_2_), channel_id=1, source_target_pairs={{0,28},{4,0},{8,4},{12,8},{16,12},{20,16},{24,20},{28,24},{1,29},{... | collective-permute-start | bytes 589832 | tf_op jit(solution)/shard_map/ppermute | solution.py:288
  63.9 4.3 %all-to-all-start = ((bf16[4,2,32,384]{3,2,1,0:T(8,128)(2,1)}), bf16[4,2,32,384]{3,2,1,0:T(8,128)(2,1)}, u32[]{:S(2)}, u32[]{:S(2)}) async-start(bf16[4,2,32,384]{3,2,1,0:T(8,128)(2,1)} %fusion.2), calls=%async_computation | async-start | bytes 393216 | tf_op jit(solution)/shard_map/all_to_all | solution.py:353
  68.9 3.2 %collective-permute-start.3 = (bf16[32,3072]{1,0:T(8,128)(2,1)}, bf16[32,3072]{1,0:T(8,128)(2,1)}, u32[]{:S(2)}, u32[]{:S(2)}) collective-permute-start(bf16[32,3072]{1,0:T(8,128)(2,1)} %collective-permute-done.2.refs_3_), channel_id=1, source_target_pairs={{0,28},{4,0},{8,4},{12,8},{16,12},{20,16},{24,20},{28,24},{1,29},{... | collective-permute-start | bytes 589832 | tf_op jit(solution)/shard_map/ppermute | solution.py:288
  77.5 6.7 %qkv_first.1 = bf16[4,192,256]{2,1,0:T(8,128)(2,1)S(1)} custom-call(s32[4]{0:T(128)S(1)} %pad_add_fusion.idx, bf16[32,3072]{1,0:T(8,128)(2,1)S(1)} %fusion.refs_0_, bf16[32,3072]{1,0:T(8,128)(2,1)} %collective-permute-done.refs_1_, bf16[32,3072]{1,0:T(8,128)(2,1)} %collective-permute-done.1.refs_2_, bf16[32,3072]{1,0:T(8,128)(2,1)} %collective-permute-done.2.refs_3_, ...), custom_call_target="tpu_custom_call" | custom-call | flops 1200000000 | bytes 7000000 | tf_op jit(solution)/shard_map/qkv_first/pallas_call | solution.py:84
  84.9 2.4 slice.47
  87.4 2.3 fusion.5
  90.7 2.5 collective-permute-start.22
  93.4 8.5 %collective-permute-done.21 = bf16[8,64,384]{2,1,0:T(8,128)(2,1)S(1)} collective-permute-done((bf16[8,64,384]{2,1,0:T(8,128)(2,1)}, bf16[8,64,384]{2,1,0:T(8,128)(2,1)S(1)}, u32[]{:S(2)}, u32[]{:S(2)}) %collective-permute-start.21) | collective-permute-done | bytes 393248 | tf_op jit(solution)/shard_map/ppermute | solution.py:288
  102.0 5.9 %collective-permute-done.22 = bf16[8,64,384]{2,1,0:T(8,128)(2,1)S(1)} collective-permute-done((bf16[8,64,384]{2,1,0:T(8,128)(2,1)}, bf16[8,64,384]{2,1,0:T(8,128)(2,1)S(1)}, u32[]{:S(2)}, u32[]{:S(2)}) %collective-permute-start.22) | collective-permute-done | bytes 393248 | tf_op jit(solution)/shard_map/ppermute | solution.py:288
  107.9 13.1 %collective-permute-done.23 = bf16[8,64,384]{2,1,0:T(8,128)(2,1)S(1)} collective-permute-done((bf16[8,64,384]{2,1,0:T(8,128)(2,1)}, bf16[8,64,384]{2,1,0:T(8,128)(2,1)S(1)}, u32[]{:S(2)}, u32[]{:S(2)}) %collective-permute-start.23) | collective-permute-done | bytes 393248 | tf_op jit(solution)/shard_map/ppermute | solution.py:288
  122.5 12.6 %all_to_all.30.own = bf16[4,192,256]{2,1,0:T(8,128)(2,1)S(1)} all-to-all(bf16[4,192,256]{2,1,0:T(8,128)(2,1)S(1)} %copy-done.3), channel_id=1, replica_groups=mesh['x'=4,'core'=2,'z'=8,'y'=4] {'y'}, dimensions={0} | all-to-all | bytes 786432 | tf_op jit(solution)/shard_map/all_to_all | solution.py:372
  135.1 1.9 collective-permute-start.16
  137.0 3.6 %collective-permute-start.17 = (bf16[4,128,256]{2,1,0:T(8,128)(2,1)S(1)}, bf16[4,128,256]{2,1,0:T(8,128)(2,1)S(1)}, u32[]{:S(2)}, u32[]{:S(2)}) collective-permute-start(bf16[4,128,256]{2,1,0:T(8,128)(2,1)S(1)} %slice.54), channel_id=1, source_target_pairs={{32,0},{64,32},{96,64},{128,96},{160,128},{192,160},{224,192},{33,... | collective-permute-start | bytes 786440 | tf_op jit(solution)/shard_map/ppermute | solution.py:298
  140.7 7.7 %collective-permute-done.16.lower = bf16[4,128,256]{2,1,0:T(8,128)(2,1)S(1)} collective-permute-done((bf16[4,128,256]{2,1,0:T(8,128)(2,1)S(1)}, bf16[4,128,256]{2,1,0:T(8,128)(2,1)S(1)}, u32[]{:S(2)}, u32[]{:S(2)}) %collective-permute-start.16) | collective-permute-done | bytes 262176 | tf_op jit(solution)/shard_map/ppermute | solution.py:298
  148.4 8.8 %attention_4.1 = bf16[8,64,128]{2,1,0:T(8,128)(2,1)S(1)} custom-call(s32[4]{0:T(128)S(1)} %pad_add_fusion.idx, bf16[4,192,256]{2,1,0:T(8,128)(2,1)S(1)} %all_to_all.30.own, bf16[4,128,256]{2,1,0:T(8,128)(2,1)S(1)} %collective-permute-done.16.lower, bf16[4,128,256]{2,1,0:T(8,128)(2,1)S(1)} %collective-permute-done.17.upper, f32[1,128]{1,0:T(1,128)S(1)} %get-tuple-element.27.gain), custom_call_target="tpu_custom_call" | custom-call | flops 3000000000 | bytes 1200000 | tf_op jit(solution)/shard_map/attention_4/pallas_call | solution.py:197
  157.2 14.2 %all_to_all.31.o0 = bf16[8,64,128]{2,1,0:T(8,128)(2,1)S(1)} all-to-all(bf16[8,64,128]{2,1,0:T(8,128)(2,1)S(1)} %attention_4.1), channel_id=1, replica_groups=mesh['x'=4,'core'=2,'z'=8,'y'=4] {'z'}, dimensions={0} | all-to-all | bytes 262144 | tf_op jit(solution)/shard_map/all_to_all | solution.py:361
  171.5 2.0 collective-permute-start.18
  174.8 4.5 %collective-permute-done.18.o1 = bf16[8,64,128]{2,1,0:T(8,128)(2,1)S(1)} collective-permute-done((bf16[8,64,128]{2,1,0:T(8,128)(2,1)S(1)}, bf16[8,64,128]{2,1,0:T(8,128)(2,1)S(1)}, u32[]{:S(2)}, u32[]{:S(2)}) %collective-permute-start.18) | collective-permute-done | bytes 131104 | tf_op jit(solution)/shard_map/ppermute | solution.py:288
  179.3 2.0 collective-permute-done.19.o2
  187.3 5.0 %collective-permute-done.25.x1 = bf16[2,128,384]{2,1,0:T(8,128)(2,1)S(1)} collective-permute-done((bf16[2,128,384]{2,1,0:T(8,128)(2,1)S(1)}, bf16[2,128,384]{2,1,0:T(8,128)(2,1)S(1)}, u32[]{:S(2)}, u32[]{:S(2)}) %collective-permute-start.25) | collective-permute-done | bytes 196640 | tf_op jit(solution)/shard_map/ppermute | solution.py:288
  195.0 2.1 collective-permute-done.27.x3
  200.5 8.7 %qkv_second.1 = bf16[8,192,128]{2,1,0:T(8,128)(2,1)S(1)} custom-call(s32[4]{0:T(128)S(1)} %pad_add_fusion.idx, bf16[2,128,384]{2,1,0:T(8,128)(2,1)S(1)} %project_0.1.x0.refs_2_, bf16[2,128,384]{2,1,0:T(8,128)(2,1)S(1)} %copy-done.6, bf16[2,128,384]{2,1,0:T(8,128)(2,1)S(1)} %copy-done.8, bf16[2,128,384]{2,1,0:T(8,128)(2,1)S(1)} %copy-done.10, ...), custom_call_target="tpu_custom_call" | custom-call | flops 1200000000 | bytes 10500000 | tf_op jit(solution)/shard_map/qkv_second/pallas_call | solution.py:122
  209.2 17.5 %all_to_all.32.own = bf16[8,192,128]{2,1,0:T(8,128)(2,1)S(1)} all-to-all(bf16[8,192,128]{2,1,0:T(8,128)(2,1)S(1)} %qkv_second.1), channel_id=1, replica_groups=mesh['x'=4,'core'=2,'z'=8,'y'=4] {'z'}, dimensions={0} | all-to-all | bytes 786432 | tf_op jit(solution)/shard_map/all_to_all | solution.py:377
  226.8 1.9 collective-permute-start.28
  228.7 3.6 %collective-permute-start.29 = (bf16[8,128,128]{2,1,0:T(8,128)(2,1)S(1)}, bf16[8,128,128]{2,1,0:T(8,128)(2,1)S(1)}, u32[]{:S(2)}, u32[]{:S(2)}) collective-permute-start(bf16[8,128,128]{2,1,0:T(8,128)(2,1)S(1)} %slice.55), channel_id=1, source_target_pairs={{32,0},{64,32},{96,64},{128,96},{160,128},{192,160},{224,192},{33,... | collective-permute-start | bytes 786440 | tf_op jit(solution)/shard_map/ppermute | solution.py:298
  232.4 2.1 collective-permute-done.28.lower
  236.2 8.6 %attention_8.1 = bf16[8,64,128]{2,1,0:T(8,128)(2,1)S(1)} custom-call(s32[4]{0:T(128)S(1)} %pad_add_fusion.idx, bf16[8,192,128]{2,1,0:T(8,128)(2,1)S(1)} %all_to_all.32.own, bf16[8,128,128]{2,1,0:T(8,128)(2,1)S(1)} %collective-permute-done.28.lower, bf16[8,128,128]{2,1,0:T(8,128)(2,1)S(1)} %collective-permute-done.29.upper, f32[1,128]{1,0:T(1,128)S(1)} %get-tuple-element.26.gain), custom_call_target="tpu_custom_call" | custom-call | flops 3000000000 | bytes 1200000 | tf_op jit(solution)/shard_map/attention_8/pallas_call | solution.py:197
  244.9 12.1 %all_to_all.33.o0 = bf16[8,64,128]{2,1,0:T(8,128)(2,1)} all-to-all(bf16[8,64,128]{2,1,0:T(8,128)(2,1)S(1)} %attention_8.1), channel_id=1, replica_groups=mesh['x'=4,'core'=2,'z'=8,'y'=4] {'z'}, dimensions={0} | all-to-all | bytes 262144 | tf_op jit(solution)/shard_map/all_to_all | solution.py:361
  260.1 2.2 collective-permute-done.30.o1
  262.3 2.1 collective-permute-done.31.o2
  265.8 1.9 copy-done.1
  267.7 2.0 project_1.1
  271.0 5.5 %collective-permute-start.33 = (bf16[2,32,384]{2,1,0:T(8,128)(2,1)}, bf16[2,32,384]{2,1,0:T(8,128)(2,1)}, u32[]{:S(2)}, u32[]{:S(2)}) collective-permute-start(bf16[2,32,384]{2,1,0:T(8,128)(2,1)} %get-tuple-element.25), channel_id=1, source_target_pairs={{16,0},{17,1},{18,2},{19,3},{20,4},{21,5},{22,6},{23,7},{24,8},{25... | collective-permute-start | bytes 147464 | tf_op jit(solution)/shard_map/ppermute | solution.py:390
  276.6 5.6 %collective-permute-start.34 = (bf16[2,32,384]{2,1,0:T(8,128)(2,1)}, bf16[2,32,384]{2,1,0:T(8,128)(2,1)}, u32[]{:S(2)}, u32[]{:S(2)}) collective-permute-start(bf16[2,32,384]{2,1,0:T(8,128)(2,1)} %get-tuple-element.24), channel_id=1, source_target_pairs={{16,1},{17,2},{18,3},{19,0},{20,5},{21,6},{22,7},{23,4},{24,9},{25... | collective-permute-start | bytes 147464 | tf_op jit(solution)/shard_map/ppermute | solution.py:390
  282.1 5.1 %collective-permute-start.35 = (bf16[2,32,384]{2,1,0:T(8,128)(2,1)}, bf16[2,32,384]{2,1,0:T(8,128)(2,1)}, u32[]{:S(2)}, u32[]{:S(2)}) collective-permute-start(bf16[2,32,384]{2,1,0:T(8,128)(2,1)} %get-tuple-element.23), channel_id=1, source_target_pairs={{16,2},{17,3},{18,0},{19,1},{20,6},{21,7},{22,4},{23,5},{24,10},{2... | collective-permute-start | bytes 147464 | tf_op jit(solution)/shard_map/ppermute | solution.py:390
  287.3 8.0 %collective-permute-start.36 = (bf16[2,32,384]{2,1,0:T(8,128)(2,1)}, bf16[2,32,384]{2,1,0:T(8,128)(2,1)}, u32[]{:S(2)}, u32[]{:S(2)}) collective-permute-start(bf16[2,32,384]{2,1,0:T(8,128)(2,1)} %get-tuple-element.22), channel_id=1, source_target_pairs={{16,3},{17,0},{18,1},{19,2},{20,7},{21,4},{22,5},{23,6},{24,11},{2... | collective-permute-start | bytes 147464 | tf_op jit(solution)/shard_map/ppermute | solution.py:390
  295.3 4.0 %all-to-all-start.5 = ((bf16[4,2,32,384]{3,2,1,0:T(8,128)(2,1)}), bf16[4,2,32,384]{3,2,1,0:T(8,128)(2,1)S(1)}, u32[]{:S(2)}, u32[]{:S(2)}) async-start(bf16[4,2,32,384]{3,2,1,0:T(8,128)(2,1)} %bitcast.50), calls=%async_computation.5 | async-start | bytes 393216 | tf_op jit(solution)/shard_map/all_to_all | solution.py:381
  299.3 6.3 %all-to-all-done.5.rows = bf16[4,2,32,384]{3,2,1,0:T(8,128)(2,1)S(1)} async-done(((bf16[4,2,32,384]{3,2,1,0:T(8,128)(2,1)}), bf16[4,2,32,384]{3,2,1,0:T(8,128)(2,1)S(1)}, u32[]{:S(2)}, u32[]{:S(2)}) %all-to-all-start.5) | async-done | bytes 196640 | tf_op jit(solution)/shard_map/all_to_all | solution.py:381
  (106 shorter events, 46.2 us)
Async XLA Ops:
  7.2 292.0 %copy-start = (bf16[512,3072]{1,0:T(8,128)(2,1)S(1)}, bf16[512,3072]{1,0:T(8,128)(2,1)}, u32[]{:S(2)}) copy-start(bf16[512,3072]{1,0:T(8,128)(2,1)} %param.10) | copy-start | bytes 9437188
  7.2 77.7 %all-gather.7.cloned.1.call-start = ((), (), s32[]{:S(2)}) async-start(), calls=%async_computation.6 | async-start | bytes 2211840 | tf_op jit(solution)/shard_map/all_gather | solution.py:350
  9.3 8.0 %collective-permute-start.13 = (bf16[2,32,768]{2,1,0:T(8,128)(2,1)}, bf16[2,32,768]{2,1,0:T(8,128)(2,1)}, u32[]{:S(2)}, u32[]{:S(2)}) collective-permute-start(bf16[2,32,768]{2,1,0:T(8,128)(2,1)} %get-tuple-element.19), channel_id=1, source_target_pairs={{0,1},{4,5},{8,9},{12,13},{16,17},{20,21},{24,25},{28,29},{32,33},... | collective-permute-start | bytes 294920 | tf_op jit(solution)/shard_map/ppermute | solution.py:344
  10.6 10.1 %collective-permute-start.14 = (bf16[2,32,768]{2,1,0:T(8,128)(2,1)S(1)}, bf16[2,32,768]{2,1,0:T(8,128)(2,1)}, u32[]{:S(2)}, u32[]{:S(2)}) collective-permute-start(bf16[2,32,768]{2,1,0:T(8,128)(2,1)S(1)} %get-tuple-element.21), channel_id=1, source_target_pairs={{0,2},{4,6},{8,10},{12,14},{16,18},{20,22},{24,26},{28,30},{32,34}... | collective-permute-start | bytes 294920 | tf_op jit(solution)/shard_map/ppermute | solution.py:344
  11.8 8.8 %collective-permute-start.15 = (bf16[2,32,768]{2,1,0:T(8,128)(2,1)S(1)}, bf16[2,32,768]{2,1,0:T(8,128)(2,1)}, u32[]{:S(2)}, u32[]{:S(2)}) collective-permute-start(bf16[2,32,768]{2,1,0:T(8,128)(2,1)S(1)} %get-tuple-element.20), channel_id=1, source_target_pairs={{0,3},{4,7},{8,11},{12,15},{16,19},{20,23},{24,27},{28,31},{32,35}... | collective-permute-start | bytes 294920 | tf_op jit(solution)/shard_map/ppermute | solution.py:344
  16.4 13.3 %copy-start.11 = (s32[1,2]{1,0:T(1,128)S(1)}, s32[1,2]{1,0:T(1,128)}, u32[]{:S(2)}) copy-start(s32[1,2]{1,0:T(1,128)} %param.11) | copy-start | bytes 28
  24.6 37.0 %collective-permute-start.7 = (bf16[192,1536]{1,0:T(8,128)(2,1)}, bf16[192,1536]{1,0:T(8,128)(2,1)}, u32[]{:S(2)}, u32[]{:S(2)}) collective-permute-start(bf16[192,1536]{1,0:T(8,128)(2,1)} %dynamic-slice_bitcast_fusion), channel_id=1, source_target_pairs={{0,3},{1,0},{2,1},{3,2},{4,7},{5,4},{6,5},{7,6},{8,11},{9,8},{10,9... | collective-permute-start | bytes 1769480 | tf_op jit(solution)/shard_map/ppermute | solution.py:288
  24.6 37.0 %collective-permute-start.8 = (bf16[192,1536]{1,0:T(8,128)(2,1)}, bf16[192,1536]{1,0:T(8,128)(2,1)}, u32[]{:S(2)}, u32[]{:S(2)}) collective-permute-start(bf16[192,1536]{1,0:T(8,128)(2,1)} %dynamic-slice_bitcast_fusion), channel_id=1, source_target_pairs={{0,2},{1,3},{2,0},{3,1},{4,6},{5,7},{6,4},{7,5},{8,10},{9,11},{10,... | collective-permute-start | bytes 1769480 | tf_op jit(solution)/shard_map/ppermute | solution.py:288
  28.2 33.8 %collective-permute-start.9 = (bf16[192,1536]{1,0:T(8,128)(2,1)}, bf16[192,1536]{1,0:T(8,128)(2,1)}, u32[]{:S(2)}, u32[]{:S(2)}) collective-permute-start(bf16[192,1536]{1,0:T(8,128)(2,1)} %dynamic-slice_bitcast_fusion), channel_id=1, source_target_pairs={{0,1},{1,2},{2,3},{3,0},{4,5},{5,6},{6,7},{7,4},{8,9},{9,10},{10,1... | collective-permute-start | bytes 1769480 | tf_op jit(solution)/shard_map/ppermute | solution.py:288
  34.4 12.4 %collective-permute-start = (bf16[32,3072]{1,0:T(8,128)(2,1)S(1)}, bf16[32,3072]{1,0:T(8,128)(2,1)}, u32[]{:S(2)}, u32[]{:S(2)}) collective-permute-start(bf16[32,3072]{1,0:T(8,128)(2,1)S(1)} %fusion.refs_0_), channel_id=1, source_target_pairs={{0,28},{4,0},{8,4},{12,8},{16,12},{20,16},{24,20},{28,24},{1,29},{... | collective-permute-start | bytes 589832 | tf_op jit(solution)/shard_map/ppermute | solution.py:288
  40.4 12.3 %collective-permute-start.4 = (bf16[32,3072]{1,0:T(8,128)(2,1)S(1)}, bf16[32,3072]{1,0:T(8,128)(2,1)}, u32[]{:S(2)}, u32[]{:S(2)}) collective-permute-start(bf16[32,3072]{1,0:T(8,128)(2,1)S(1)} %fusion.refs_0_), channel_id=1, source_target_pairs={{0,4},{4,8},{8,12},{12,16},{16,20},{20,24},{24,28},{28,0},{1,5},{5... | collective-permute-start | bytes 589832 | tf_op jit(solution)/shard_map/ppermute | solution.py:288
  46.8 11.0 %collective-permute-start.1 = (bf16[32,3072]{1,0:T(8,128)(2,1)}, bf16[32,3072]{1,0:T(8,128)(2,1)}, u32[]{:S(2)}, u32[]{:S(2)}) collective-permute-start(bf16[32,3072]{1,0:T(8,128)(2,1)} %collective-permute-done.refs_1_), channel_id=1, source_target_pairs={{0,28},{4,0},{8,4},{12,8},{16,12},{20,16},{24,20},{28,24},{1,29},{... | collective-permute-start | bytes 589832 | tf_op jit(solution)/shard_map/ppermute | solution.py:288
  52.7 16.1 %collective-permute-start.5 = (bf16[32,3072]{1,0:T(8,128)(2,1)}, bf16[32,3072]{1,0:T(8,128)(2,1)}, u32[]{:S(2)}, u32[]{:S(2)}) collective-permute-start(bf16[32,3072]{1,0:T(8,128)(2,1)} %collective-permute-done.4.refs_7_), channel_id=1, source_target_pairs={{0,4},{4,8},{8,12},{12,16},{16,20},{20,24},{24,28},{28,0},{1,5},{5... | collective-permute-start | bytes 589832 | tf_op jit(solution)/shard_map/ppermute | solution.py:288
  57.8 11.1 %collective-permute-start.2 = (bf16[32,3072]{1,0:T(8,128)(2,1)}, bf16[32,3072]{1,0:T(8,128)(2,1)}, u32[]{:S(2)}, u32[]{:S(2)}) collective-permute-start(bf16[32,3072]{1,0:T(8,128)(2,1)} %collective-permute-done.1.refs_2_), channel_id=1, source_target_pairs={{0,28},{4,0},{8,4},{12,8},{16,12},{20,16},{24,20},{28,24},{1,29},{... | collective-permute-start | bytes 589832 | tf_op jit(solution)/shard_map/ppermute | solution.py:288
  61.5 15.9 %collective-permute-start.10 = (bf16[192,1536]{1,0:T(8,128)(2,1)}, bf16[192,1536]{1,0:T(8,128)(2,1)}, u32[]{:S(2)}, u32[]{:S(2)}) collective-permute-start(bf16[192,1536]{1,0:T(8,128)(2,1)} %collective-permute-done.7.refs_10_), channel_id=1, source_target_pairs={{0,32},{32,0},{1,33},{33,1},{2,34},{34,2},{3,35},{35,3},{4,36},{36... | collective-permute-start | bytes 1769480 | tf_op jit(solution)/shard_map/ppermute | solution.py:292
  61.5 15.9 %collective-permute-start.11 = (bf16[192,1536]{1,0:T(8,128)(2,1)}, bf16[192,1536]{1,0:T(8,128)(2,1)}, u32[]{:S(2)}, u32[]{:S(2)}) collective-permute-start(bf16[192,1536]{1,0:T(8,128)(2,1)} %collective-permute-done.8.refs_11_), channel_id=1, source_target_pairs={{0,32},{32,0},{1,33},{33,1},{2,34},{34,2},{3,35},{35,3},{4,36},{36... | collective-permute-start | bytes 1769480 | tf_op jit(solution)/shard_map/ppermute | solution.py:292
  62.0 15.4 %collective-permute-start.12 = (bf16[192,1536]{1,0:T(8,128)(2,1)}, bf16[192,1536]{1,0:T(8,128)(2,1)}, u32[]{:S(2)}, u32[]{:S(2)}) collective-permute-start(bf16[192,1536]{1,0:T(8,128)(2,1)} %collective-permute-done.9.refs_12_), channel_id=1, source_target_pairs={{0,32},{32,0},{1,33},{33,1},{2,34},{34,2},{3,35},{35,3},{4,36},{36... | collective-permute-start | bytes 1769480 | tf_op jit(solution)/shard_map/ppermute | solution.py:292
  63.9 10.9 %all-to-all-start = ((bf16[4,2,32,384]{3,2,1,0:T(8,128)(2,1)}), bf16[4,2,32,384]{3,2,1,0:T(8,128)(2,1)}, u32[]{:S(2)}, u32[]{:S(2)}) async-start(bf16[4,2,32,384]{3,2,1,0:T(8,128)(2,1)} %fusion.2), calls=%async_computation | async-start | bytes 393216 | tf_op jit(solution)/shard_map/all_to_all | solution.py:353
  68.1 129.6 %all-gather.9.cloned.1.call-start = ((), (), s32[]{:S(2)}) async-start(), calls=%async_computation.7 | async-start | bytes 10616832 | tf_op jit(solution)/shard_map/all_gather | solution.py:366
  68.8 8.6 %collective-permute-start.6 = (bf16[32,3072]{1,0:T(8,128)(2,1)}, bf16[32,3072]{1,0:T(8,128)(2,1)}, u32[]{:S(2)}, u32[]{:S(2)}) collective-permute-start(bf16[32,3072]{1,0:T(8,128)(2,1)} %collective-permute-done.5.refs_6_), channel_id=1, source_target_pairs={{0,4},{4,8},{8,12},{12,16},{16,20},{20,24},{24,28},{28,0},{1,5},{5... | collective-permute-start | bytes 589832 | tf_op jit(solution)/shard_map/ppermute | solution.py:288
  68.9 8.5 %collective-permute-start.3 = (bf16[32,3072]{1,0:T(8,128)(2,1)}, bf16[32,3072]{1,0:T(8,128)(2,1)}, u32[]{:S(2)}, u32[]{:S(2)}) collective-permute-start(bf16[32,3072]{1,0:T(8,128)(2,1)} %collective-permute-done.2.refs_3_), channel_id=1, source_target_pairs={{0,28},{4,0},{8,4},{12,8},{16,12},{20,16},{24,20},{28,24},{1,29},{... | collective-permute-start | bytes 589832 | tf_op jit(solution)/shard_map/ppermute | solution.py:288
  87.3 172.8 %all-gather.11.cloned.1.call-start = ((), (), s32[]{:S(2)}) async-start(), calls=%async_computation.8 | async-start | bytes 3538944 | tf_op jit(solution)/shard_map/all_gather | solution.py:370
  89.6 12.3 %collective-permute-start.21 = (bf16[8,64,384]{2,1,0:T(8,128)(2,1)}, bf16[8,64,384]{2,1,0:T(8,128)(2,1)S(1)}, u32[]{:S(2)}, u32[]{:S(2)}) collective-permute-start(bf16[8,64,384]{2,1,0:T(8,128)(2,1)} %get-tuple-element.18), channel_id=1, source_target_pairs={{0,192},{64,0},{128,64},{192,128},{1,193},{65,1},{129,65},{193,129... | collective-permute-start | bytes 1179656 | tf_op jit(solution)/shard_map/ppermute | solution.py:288
  90.7 17.1 %collective-permute-start.22 = (bf16[8,64,384]{2,1,0:T(8,128)(2,1)}, bf16[8,64,384]{2,1,0:T(8,128)(2,1)S(1)}, u32[]{:S(2)}, u32[]{:S(2)}) collective-permute-start(bf16[8,64,384]{2,1,0:T(8,128)(2,1)} %get-tuple-element.18), channel_id=1, source_target_pairs={{0,128},{64,192},{128,0},{192,64},{1,129},{65,193},{129,1},{193,65... | collective-permute-start | bytes 1179656 | tf_op jit(solution)/shard_map/ppermute | solution.py:288
  93.2 27.8 %collective-permute-start.23 = (bf16[8,64,384]{2,1,0:T(8,128)(2,1)}, bf16[8,64,384]{2,1,0:T(8,128)(2,1)S(1)}, u32[]{:S(2)}, u32[]{:S(2)}) collective-permute-start(bf16[8,64,384]{2,1,0:T(8,128)(2,1)} %get-tuple-element.18), channel_id=1, source_target_pairs={{0,64},{64,128},{128,192},{192,0},{1,65},{65,129},{129,193},{193,1... | collective-permute-start | bytes 1179656 | tf_op jit(solution)/shard_map/ppermute | solution.py:288
  121.0 1.5 copy-start.3
  121.0 19.7 %copy-start.12 = (bf16[2,1,128]{2,0,1:T(2,128)(2,1)S(1)}, bf16[2,1,128]{2,0,1:T(2,128)(2,1)}, u32[]{:S(2)}) copy-start(bf16[2,1,128]{2,0,1:T(2,128)(2,1)} %param.16) | copy-start | bytes 1540
  122.4 60.6 %collective-permute-start.24 = (bf16[4,8,64,384]{3,2,1,0:T(8,128)(2,1)S(1)}, bf16[4,8,64,384]{3,2,1,0:T(8,128)(2,1)S(1)}, u32[]{:S(2)}, u32[]{:S(2)}) collective-permute-start(bf16[4,8,64,384]{3,2,1,0:T(8,128)(2,1)S(1)} %pad_maximum_fusion.refs_0_), channel_id=1, source_target_pairs={{0,32},{32,0},{1,33},{33,1},{2,34},{34,2},{3,35},{35,3},{4,36},{36... | collective-permute-start | bytes 4718600 | tf_op jit(solution)/shard_map/ppermute | solution.py:292
  135.1 13.3 %collective-permute-start.16 = (bf16[4,128,256]{2,1,0:T(8,128)(2,1)S(1)}, bf16[4,128,256]{2,1,0:T(8,128)(2,1)S(1)}, u32[]{:S(2)}, u32[]{:S(2)}) collective-permute-start(bf16[4,128,256]{2,1,0:T(8,128)(2,1)S(1)} %slice.54), channel_id=1, source_target_pairs={{0,32},{32,64},{64,96},{96,128},{128,160},{160,192},{192,224},{1,3... | collective-permute-start | bytes 786440 | tf_op jit(solution)/shard_map/ppermute | solution.py:298
  137.0 11.4 %collective-permute-start.17 = (bf16[4,128,256]{2,1,0:T(8,128)(2,1)S(1)}, bf16[4,128,256]{2,1,0:T(8,128)(2,1)S(1)}, u32[]{:S(2)}, u32[]{:S(2)}) collective-permute-start(bf16[4,128,256]{2,1,0:T(8,128)(2,1)S(1)} %slice.54), channel_id=1, source_target_pairs={{32,0},{64,32},{96,64},{128,96},{160,128},{192,160},{224,192},{33,... | collective-permute-start | bytes 786440 | tf_op jit(solution)/shard_map/ppermute | solution.py:298
  148.4 34.6 %copy-start.4 = (bf16[2,4,32,384]{3,2,1,0:T(8,128)(2,1)S(1)}, bf16[2,4,32,384]{3,2,1,0:T(8,128)(2,1)}, u32[]{:S(2)}) copy-start(bf16[2,4,32,384]{3,2,1,0:T(8,128)(2,1)} %copy.23) | copy-start | bytes 589828
  171.5 7.8 %collective-permute-start.18 = (bf16[8,64,128]{2,1,0:T(8,128)(2,1)S(1)}, bf16[8,64,128]{2,1,0:T(8,128)(2,1)S(1)}, u32[]{:S(2)}, u32[]{:S(2)}) collective-permute-start(bf16[8,64,128]{2,1,0:T(8,128)(2,1)S(1)} %all_to_all.31.o0), channel_id=1, source_target_pairs={{0,3},{1,0},{2,1},{3,2},{4,7},{5,4},{6,5},{7,6},{8,11},{9,8},{10,9... | collective-permute-start | bytes 393224 | tf_op jit(solution)/shard_map/ppermute | solution.py:288
  173.4 7.9 %collective-permute-start.19 = (bf16[8,64,128]{2,1,0:T(8,128)(2,1)S(1)}, bf16[8,64,128]{2,1,0:T(8,128)(2,1)S(1)}, u32[]{:S(2)}, u32[]{:S(2)}) collective-permute-start(bf16[8,64,128]{2,1,0:T(8,128)(2,1)S(1)} %all_to_all.31.o0), channel_id=1, source_target_pairs={{0,2},{1,3},{2,0},{3,1},{4,6},{5,7},{6,4},{7,5},{8,10},{9,11},{10,... | collective-permute-start | bytes 393224 | tf_op jit(solution)/shard_map/ppermute | solution.py:288
  174.8 8.1 %collective-permute-start.20 = (bf16[8,64,128]{2,1,0:T(8,128)(2,1)S(1)}, bf16[8,64,128]{2,1,0:T(8,128)(2,1)S(1)}, u32[]{:S(2)}, u32[]{:S(2)}) collective-permute-start(bf16[8,64,128]{2,1,0:T(8,128)(2,1)S(1)} %all_to_all.31.o0), channel_id=1, source_target_pairs={{0,1},{1,2},{2,3},{3,0},{4,5},{5,6},{6,7},{7,4},{8,9},{9,10},{10,1... | collective-permute-start | bytes 393224 | tf_op jit(solution)/shard_map/ppermute | solution.py:288
  184.3 7.9 %collective-permute-start.25 = (bf16[2,128,384]{2,1,0:T(8,128)(2,1)S(1)}, bf16[2,128,384]{2,1,0:T(8,128)(2,1)S(1)}, u32[]{:S(2)}, u32[]{:S(2)}) collective-permute-start(bf16[2,128,384]{2,1,0:T(8,128)(2,1)S(1)} %project_0.1.x0.refs_2_), channel_id=1, source_target_pairs={{0,3},{1,0},{2,1},{3,2},{4,7},{5,4},{6,5},{7,6},{8,11},{9,8},{10,9... | collective-permute-start | bytes 589832 | tf_op jit(solution)/shard_map/ppermute | solution.py:288
  185.0 9.4 %collective-permute-start.26 = (bf16[2,128,384]{2,1,0:T(8,128)(2,1)S(1)}, bf16[2,128,384]{2,1,0:T(8,128)(2,1)S(1)}, u32[]{:S(2)}, u32[]{:S(2)}) collective-permute-start(bf16[2,128,384]{2,1,0:T(8,128)(2,1)S(1)} %project_0.1.x0.refs_2_), channel_id=1, source_target_pairs={{0,2},{1,3},{2,0},{3,1},{4,6},{5,7},{6,4},{7,5},{8,10},{9,11},{10,... | collective-permute-start | bytes 589832 | tf_op jit(solution)/shard_map/ppermute | solution.py:288
  186.4 10.7 %collective-permute-start.27 = (bf16[2,128,384]{2,1,0:T(8,128)(2,1)S(1)}, bf16[2,128,384]{2,1,0:T(8,128)(2,1)S(1)}, u32[]{:S(2)}, u32[]{:S(2)}) collective-permute-start(bf16[2,128,384]{2,1,0:T(8,128)(2,1)S(1)} %project_0.1.x0.refs_2_), channel_id=1, source_target_pairs={{0,1},{1,2},{2,3},{3,0},{4,5},{5,6},{6,7},{7,4},{8,9},{9,10},{10,1... | collective-permute-start | bytes 589832 | tf_op jit(solution)/shard_map/ppermute | solution.py:288
  226.8 7.7 %collective-permute-start.28 = (bf16[8,128,128]{2,1,0:T(8,128)(2,1)S(1)}, bf16[8,128,128]{2,1,0:T(8,128)(2,1)S(1)}, u32[]{:S(2)}, u32[]{:S(2)}) collective-permute-start(bf16[8,128,128]{2,1,0:T(8,128)(2,1)S(1)} %slice.55), channel_id=1, source_target_pairs={{0,32},{32,64},{64,96},{96,128},{128,160},{160,192},{192,224},{1,3... | collective-permute-start | bytes 786440 | tf_op jit(solution)/shard_map/ppermute | solution.py:298
  228.7 7.5 %collective-permute-start.29 = (bf16[8,128,128]{2,1,0:T(8,128)(2,1)S(1)}, bf16[8,128,128]{2,1,0:T(8,128)(2,1)S(1)}, u32[]{:S(2)}, u32[]{:S(2)}) collective-permute-start(bf16[8,128,128]{2,1,0:T(8,128)(2,1)S(1)} %slice.55), channel_id=1, source_target_pairs={{32,0},{64,32},{96,64},{128,96},{160,128},{192,160},{224,192},{33,... | collective-permute-start | bytes 786440 | tf_op jit(solution)/shard_map/ppermute | solution.py:298
  257.0 5.3 %collective-permute-start.30 = (bf16[8,64,128]{2,1,0:T(8,128)(2,1)}, bf16[8,64,128]{2,1,0:T(8,128)(2,1)}, u32[]{:S(2)}, u32[]{:S(2)}) collective-permute-start(bf16[8,64,128]{2,1,0:T(8,128)(2,1)} %all_to_all.33.o0), channel_id=1, source_target_pairs={{0,3},{1,0},{2,1},{3,2},{4,7},{5,4},{6,5},{7,6},{8,11},{9,8},{10,9... | collective-permute-start | bytes 393224 | tf_op jit(solution)/shard_map/ppermute | solution.py:288
  257.5 7.0 %collective-permute-start.31 = (bf16[8,64,128]{2,1,0:T(8,128)(2,1)}, bf16[8,64,128]{2,1,0:T(8,128)(2,1)}, u32[]{:S(2)}, u32[]{:S(2)}) collective-permute-start(bf16[8,64,128]{2,1,0:T(8,128)(2,1)} %all_to_all.33.o0), channel_id=1, source_target_pairs={{0,2},{1,3},{2,0},{3,1},{4,6},{5,7},{6,4},{7,5},{8,10},{9,11},{10,... | collective-permute-start | bytes 393224 | tf_op jit(solution)/shard_map/ppermute | solution.py:288
  258.7 7.1 %collective-permute-start.32 = (bf16[8,64,128]{2,1,0:T(8,128)(2,1)}, bf16[8,64,128]{2,1,0:T(8,128)(2,1)}, u32[]{:S(2)}, u32[]{:S(2)}) collective-permute-start(bf16[8,64,128]{2,1,0:T(8,128)(2,1)} %all_to_all.33.o0), channel_id=1, source_target_pairs={{0,1},{1,2},{2,3},{3,0},{4,5},{5,6},{6,7},{7,4},{8,9},{9,10},{10,1... | collective-permute-start | bytes 393224 | tf_op jit(solution)/shard_map/ppermute | solution.py:288
  265.8 1.9 copy-start.1
  271.0 28.2 %collective-permute-start.33 = (bf16[2,32,384]{2,1,0:T(8,128)(2,1)}, bf16[2,32,384]{2,1,0:T(8,128)(2,1)}, u32[]{:S(2)}, u32[]{:S(2)}) collective-permute-start(bf16[2,32,384]{2,1,0:T(8,128)(2,1)} %get-tuple-element.25), channel_id=1, source_target_pairs={{16,0},{17,1},{18,2},{19,3},{20,4},{21,5},{22,6},{23,7},{24,8},{25... | collective-permute-start | bytes 147464 | tf_op jit(solution)/shard_map/ppermute | solution.py:390
  276.6 22.7 %collective-permute-start.34 = (bf16[2,32,384]{2,1,0:T(8,128)(2,1)}, bf16[2,32,384]{2,1,0:T(8,128)(2,1)}, u32[]{:S(2)}, u32[]{:S(2)}) collective-permute-start(bf16[2,32,384]{2,1,0:T(8,128)(2,1)} %get-tuple-element.24), channel_id=1, source_target_pairs={{16,1},{17,2},{18,3},{19,0},{20,5},{21,6},{22,7},{23,4},{24,9},{25... | collective-permute-start | bytes 147464 | tf_op jit(solution)/shard_map/ppermute | solution.py:390
  282.1 17.1 %collective-permute-start.35 = (bf16[2,32,384]{2,1,0:T(8,128)(2,1)}, bf16[2,32,384]{2,1,0:T(8,128)(2,1)}, u32[]{:S(2)}, u32[]{:S(2)}) collective-permute-start(bf16[2,32,384]{2,1,0:T(8,128)(2,1)} %get-tuple-element.23), channel_id=1, source_target_pairs={{16,2},{17,3},{18,0},{19,1},{20,6},{21,7},{22,4},{23,5},{24,10},{2... | collective-permute-start | bytes 147464 | tf_op jit(solution)/shard_map/ppermute | solution.py:390
  287.3 12.0 %collective-permute-start.36 = (bf16[2,32,384]{2,1,0:T(8,128)(2,1)}, bf16[2,32,384]{2,1,0:T(8,128)(2,1)}, u32[]{:S(2)}, u32[]{:S(2)}) collective-permute-start(bf16[2,32,384]{2,1,0:T(8,128)(2,1)} %get-tuple-element.22), channel_id=1, source_target_pairs={{16,3},{17,0},{18,1},{19,2},{20,7},{21,4},{22,5},{23,6},{24,11},{2... | collective-permute-start | bytes 147464 | tf_op jit(solution)/shard_map/ppermute | solution.py:390
  295.3 10.3 %all-to-all-start.5 = ((bf16[4,2,32,384]{3,2,1,0:T(8,128)(2,1)}), bf16[4,2,32,384]{3,2,1,0:T(8,128)(2,1)S(1)}, u32[]{:S(2)}, u32[]{:S(2)}) async-start(bf16[4,2,32,384]{3,2,1,0:T(8,128)(2,1)} %bitcast.50), calls=%async_computation.5 | async-start | bytes 393216 | tf_op jit(solution)/shard_map/all_to_all | solution.py:381
  (7 other events, 5.6 us)
Sparse Core Ops, SparseCore 0:
  22.8 47.8 all-gather.6
  87.4 66.1 all-gather.8
  155.5 26.9 all-gather.10

commit v3 on v2

--- a/solution.py
+++ b/solution.py
@@ -98,41 +98,38 @@
 
     @pl.when(pl.program_id(0) == 0)
     def _():
-        for r in range(NY):
-            rows = slice(r * ROWS, (r + 1) * ROWS)
-            blocks = [x[s, rows, :].astype(F32) for x in (x0, x1, x2, x3) for s in range(2)]
-            norms = normalized(blocks)
-            for j in range(NY):
-                b = lax.rem(y + j, NY)
-                for s in range(2):
-                    cols = pl.ds(pl.multiple_of(b * QUARTER + s * EIGHTH, 128), EIGHTH)
-                    part = norms[2 * j + s] * (1.0 + mods[4:5, cols]) + mods[3:4, cols]
-                    h[b, rows, s * EIGHTH : (s + 1) * EIGHTH] = part.astype(BF)
+        for j, x in enumerate((x0, x1, x2, x3)):
+            (norm,) = normalized([x[...].astype(F32)])
+            at = lax.rem(y + j, NY)
+            for b in range(NY):
+                cols = slice(b * QUARTER, (b + 1) * QUARTER)
+                part = norm[:, cols] * (1.0 + mods[4:5, cols]) + mods[3:4, cols]
+                h[b, at] = part.astype(BF)
 
     total = None
     for b in range(NY):
         w = jnp.concatenate([weight[2 * b, 0], weight[2 * b + 1, 0]], axis=1)
-        term = times(w, h[b])
+        term = times(w, h[b].reshape(NY * ROWS, QUARTER))
         total = term if total is None else total + term
     store_head(out.at[0], total)
 
 
-def qkv_second(idx, tiles, mods, weight):
-    tile = pl.BlockSpec((2, NY * ROWS, EIGHTH), lambda i: (0, 0, 0))
+def qkv_second(idx, shards, mods, weight):
+    shard = pl.BlockSpec((ROWS, D), lambda i: (0, 0))
     return pl.pallas_call(
         qkv_second_kernel,
         grid=(NZ,),
         out_shape=jax.ShapeDtypeStruct((NZ, 3 * HD, NY * ROWS), BF),
         in_specs=[SM]
-        + [tile] * 4
+        + [shard] * 4
         + [pl.BlockSpec((6, D), lambda i: (0, 0))]
         + [pl.BlockSpec((8, 1, 3 * HD, EIGHTH), lambda i: (0, i, 0, 0))],
         out_specs=pl.BlockSpec((1, 3 * HD, NY * ROWS), lambda i: (i, 0, 0)),
-        scratch_shapes=[pltpu.VMEM((NY, NY * ROWS, QUARTER), BF)],
+        scratch_shapes=[pltpu.VMEM((NY, NY, ROWS, QUARTER), BF)],
         compiler_params=params(),
         cost_estimate=pl.CostEstimate(flops=1_200_000_000, bytes_accessed=10_500_000, transcendentals=0),
         name="qkv_second",
-    )(idx, *tiles, mods, weight)
+    )(idx, *shards, mods, weight)
 
 
 def attention_kernel(groups, idx, own, lower, upper, gain, out, acc, den, queries):
@@ -210,78 +207,60 @@
     )(idx, own, lower, upper, gain)
 
 
-def project_kernel(layer, relative, idx, o0, o1, o2, o3, *refs):
-    weights = refs[: 2 if relative else 1]
-    mods, x, out, absolute = refs[len(weights) :]
-    x_pos, core, y = idx[0], idx[1], idx[3]
-    for j, o in enumerate((o0, o1, o2, o3)):
-        b = lax.rem(y + j, NY)
-        for z in range(NZ):
-            for half in range(2):
-                absolute[b, half, z] = o[z, half * ROWS : (half + 1) * ROWS, :]
-    for h in range(2):
-        attn = None
-        for n, weight in enumerate(weights):
-            if relative:
-                side = core if n == 0 else 1 - core
-                rows = [absolute[lax.rem(x_pos + k, NX), side] for k in range(NX)]
-            else:
-                rows = [absolute[s // 2, s % 2] for s in range(8)]
-            rows = jnp.concatenate([r.reshape(NZ * ROWS, NY * ROWS) for r in rows], axis=0)
-            w = weight[:, :, h * ROWS : (h + 1) * ROWS, :].reshape(-1, EIGHTH)
-            term = lax.dot_general(rows, w, (((0,), (0,)), ((), ())), preferred_element_type=F32)
-            attn = term if attn is None else attn + term
-        cols = pl.ds(pl.multiple_of(y * QUARTER + h * EIGHTH, 128), EIGHTH)
-        gate = mods[3 * layer + 2 : 3 * layer + 3, cols]
-        out[h] = (x[h].astype(F32) + gate * attn).astype(BF)
-
-
-def project(layer, idx, parts, weights, mods, x):
-    relative = len(weights) == 2
-    return pl.pallas_call(
-        functools.partial(project_kernel, layer, relative),
-        out_shape=jax.ShapeDtypeStruct((2, NY * ROWS, EIGHTH), BF),
-        in_specs=[SM] + [VM] * (6 + len(weights)),
+def project_kernel(relative, idx, o, *refs):
+    weights, out = refs[:-1], refs[-1]
+    rows = o[...].reshape(NZ * HD, NY * ROWS)
+
+    def put(weight, eighth):
+        w = weight.reshape(NZ * HD, EIGHTH)
+        term = lax.dot_general(rows, w, (((0,), (0,)), ((), ())), preferred_element_type=F32)
+        if isinstance(eighth, int):
+            cols = slice(eighth * EIGHTH, (eighth + 1) * EIGHTH)
+        else:
+            cols = pl.ds(pl.multiple_of(eighth * EIGHTH, 128), EIGHTH)
+        out[:, cols] = term.astype(BF)
+
+    if relative:
+        x_pos, core = idx[0], idx[1]
+        for k in range(NX):
+            at = lax.rem(x_pos + k, NX) * NC
+            put(weights[k][...], at + core)
+            put(weights[NX][k], at + 1 - core)
+    else:
+        for s in range(NX * NC):
+            put(weights[0][s], s)
+
+
+def project(layer, idx, o, weights):
+    relative = len(weights) > 1
+    out = pl.pallas_call(
+        functools.partial(project_kernel, relative),
+        out_shape=jax.ShapeDtypeStruct((NY * ROWS, D), BF),
+        in_specs=[SM] + [VM] * (1 + len(weights)),
         out_specs=VM,
-        scratch_shapes=[pltpu.VMEM((NY, 2, NZ, ROWS, NY * ROWS), BF)],
         compiler_params=params(),
         cost_estimate=pl.CostEstimate(flops=420_000_000, bytes_accessed=4_000_000, transcendentals=0),
         name="project_%d" % layer,
-    )(idx, *parts, *weights, mods, x)
-
-
-def finish_kernel(idx, rows, q0, q1, q2, q3, fresh, out, queue):
-    slot = idx[0] * NC + idx[1]
-    z, y = idx[2], idx[3]
-    for b in range(NY):
-        for h in range(2):
-            out[:, b * QUARTER + h * EIGHTH : b * QUARTER + (h + 1) * EIGHTH] = rows[b, h]
-    tail = jnp.logical_and(slot == NX * NC - 1, z >= NZ // 2)
-
-    @pl.when(tail)
-    def _():
-        queue[...] = fresh[...]
-
-    @pl.when(jnp.logical_not(tail))
-    def _():
-        for j, q in enumerate((q0, q1, q2, q3)):
-            b = lax.rem(y - j + NY, NY)
-            for h in range(2):
-                cols = pl.ds(pl.multiple_of(b * QUARTER + h * EIGHTH, 128), EIGHTH)
-                queue[:, cols] = q[h]
-
-
-def finish(idx, rows, pieces, fresh):
-    shape = jax.ShapeDtypeStruct((ROWS, D), BF)
+    )(idx, o, *weights)
+    return out.reshape(NY, ROWS, D)
+
+
+def residual_kernel(layer, terms, mods, x, out):
+    attn = sum(terms[j].astype(F32) for j in range(NY))
+    gate = mods[3 * layer + 2 : 3 * layer + 3, :]
+    out[...] = (x[...].astype(F32) + gate * attn).astype(BF)
+
+
+def residual(layer, terms, mods, x):
     return pl.pallas_call(
-        finish_kernel,
-        out_shape=(shape, shape),
-        in_specs=[SM] + [VM] * 6,
-        out_specs=(VM, VM),
-        compiler_params=params(),
-        cost_estimate=pl.CostEstimate(flops=0, bytes_accessed=800_000, transcendentals=0),
-        name="finish",
-    )(idx, rows, *pieces, fresh)
+        functools.partial(residual_kernel, layer),
+        out_shape=jax.ShapeDtypeStruct((ROWS, D), BF),
+        in_specs=[VM] * 3,
+        out_specs=VM,
+        compiler_params=params(),
+        cost_estimate=pl.CostEstimate(flops=600_000, bytes_accessed=1_400_000, transcendentals=0),
+        name="residual_%d" % layer,
+    )(terms, mods, x)
 
 
 def from_ahead(block, axis, size, distance):
@@ -302,7 +281,6 @@
     return lax.optimization_barrier((value, *others))[0]
 
 
-ALL = ("x", "core", "z", "y")
 SEQ = NZ * NY
 
 
@@ -331,66 +309,43 @@
     shards = ahead + behind[:0:-1]
     other = [swap(m) for m in mine]
 
-    rows_half = lax.dynamic_slice_in_dim(w_out, core * ROWS, ROWS, 1)
-    wo = None
-    for j in range(NY):
-        columns = lax.dynamic_slice_in_dim(rows_half, lax.rem(y + j, NY) * QUARTER, QUARTER, 2)
-        if j:
-            route = [
-                ((s * NZ + c) * NY + s // NC, (s * NZ + c) * NY + (s // NC + j) % NY)
-                for s in range(NX * NC)
-                for c in range(NZ)
-            ]
-            columns = lax.ppermute(columns, ALL, route)
-        else:
-            columns = jnp.where(y == x_pos, columns, jnp.zeros_like(columns))
-        wo = columns if wo is None else wo + columns
-    wo = jnp.transpose(wo.reshape(2, ROWS, 2, EIGHTH), (0, 2, 1, 3)).reshape(4 * ROWS, EIGHTH)
-    wq = lax.dynamic_slice_in_dim(w_t[1], slot * EIGHTH, EIGHTH, 1)
-    later = lax.all_gather(jnp.concatenate([wq, wo], axis=0), "z", axis=0, tiled=False)
-
-    x_split = jnp.transpose(x0.reshape(ROWS, NY, 2, EIGHTH), (1, 2, 0, 3))
-    x_tile = lax.all_to_all(x_split, "y", 0, 0, tiled=True)
-    x_tile = jnp.transpose(x_tile, (1, 0, 2, 3)).reshape(2, NY * ROWS, EIGHTH)
+    eighth = lambda w: lax.dynamic_slice_in_dim(w, slot * EIGHTH, EIGHTH, 1)
+    pack = jnp.concatenate([eighth(w_t[1]), eighth(w_out[0]), eighth(w_out[1])], axis=0)
+    later = lax.all_gather(after(pack, x0), "z", axis=0, tiled=False)
 
     def attend(own, layer):
         kv = own[:, HD:]
         lower = shifted(kv, ("x", "core"), 1)
         upper = shifted(kv, ("x", "core"), -1)
-        done = attention(idx, own, lower, upper, gains[layer : layer + 1])
-        done = lax.all_to_all(done, "z", 0, 0, tiled=True)
-        return [done] + [from_ahead(done, "y", NY, j) for j in range(1, NY)]
+        return attention(idx, own, lower, upper, gains[layer : layer + 1])
 
     heads = qkv_first(idx, shards, mods, w_t, mine, other)
-    heads, later, x_tile = lax.optimization_barrier((heads, later, x_tile))
+    heads, later = lax.optimization_barrier((heads, later))
     wq1 = lax.all_gather(later[:, : 3 * HD], ("x", "core"), axis=0, tiled=False)
-    wo0 = later[:, 3 * HD : 3 * HD + 2 * ROWS]
-    wo0 = jnp.stack([wo0] + [from_ahead(wo0, "x", NX, k) for k in range(1, NX)])
-    wo0 = [wo0, swap(wo0)]
-    wo1 = lax.all_gather(later[:, 3 * HD + 2 * ROWS :], ("x", "core"), axis=0, tiled=False)
 
     own = lax.all_to_all(heads, "y", 0, 0, tiled=True)
-    x_tile = project(0, idx, attend(own, 0), wo0, mods, x_tile)
-
-    tiles = [x_tile] + [from_ahead(x_tile, "y", NY, j) for j in range(1, NY)]
-    heads = qkv_second(idx, tiles, mods, wq1)
+    own, later = lax.optimization_barrier((own, later))
+    wo0 = later[:, 3 * HD : 4 * HD]
+    wo0 = [wo0] + [from_ahead(wo0, "x", NX, k) for k in range(1, NX)]
+    wo1 = lax.all_gather(later[:, 4 * HD :], ("x", "core"), axis=0, tiled=False)
+    done, *wo0 = lax.optimization_barrier((attend(own, 0), *wo0))
+    wo0 = [*wo0, swap(jnp.stack(wo0))]
+    done = lax.all_to_all(done, "z", 0, 0, tiled=True)
+    terms = lax.all_to_all(project(0, idx, done, wo0), "y", 0, 0, tiled=True)
+    x1 = residual(0, terms, mods, x0)
+
+    shards = [x1] + [from_ahead(x1, "y", NY, j) for j in range(1, NY)]
+    heads = qkv_second(idx, shards, mods, wq1)
     own = lax.all_to_all(heads, "z", 0, 0, tiled=True)
-    x_tile = project(1, idx, attend(own, 1), [wo1], mods, x_tile)
-
-    split = x_tile.reshape(2, NY, ROWS, EIGHTH)
-    rows = lax.all_to_all(jnp.transpose(split, (1, 0, 2, 3)), "y", 0, 0, tiled=True)
-    pieces = []
-    for j in range(NY):
-        piece = lax.dynamic_index_in_dim(split, lax.rem(y + j, NY), 1, keepdims=False)
-        route = []
-        for source in range(NX * NC * SEQ):
-            target = source - source % NY + (source + j) % NY - SEQ // 2
-            if target >= 0:
-                route.append((source, target))
-        pieces.append(lax.ppermute(piece, ALL, route))
+    done = lax.all_to_all(attend(own, 1), "z", 0, 0, tiled=True)
+    terms = lax.all_to_all(project(1, idx, done, [wo1]), "y", 0, 0, tiled=True)
+    stream = residual(1, terms, mods, x1)
+
+    moved = shifted(stream, ("x", "core", "z", "y"), -(SEQ // 2))
     start_row = jnp.maximum(z * NY + y - SEQ // 2, 0) * ROWS
     fresh = lax.dynamic_slice_in_dim(noise_frame, start_row, ROWS, 0)
-    stream, queue = finish(idx, rows, pieces, fresh)
+    tail = jnp.logical_and(slot == NX * NC - 1, z >= NZ // 2)
+    queue = jnp.where(tail, fresh, moved)
     return (stream[None], queue[None])
 
 

time: 315 us -> 277 us (0.88)
  starting transfers between devices: 83.2 us -> 52.1 us
  blocking collectives: 56.5 us -> 71.1 us
  local copies, waits for them, and re-layouts: 26.6 us -> 13.3 us
  waiting for transfers between devices: 85.3 us -> 80.2 us
  other arithmetic: 8.34 us -> 4.35 us
    ppermute x7 -> x0, starting transfers between devices: 28 us -> none  [the longest x4 24.2 us: per_device(): pieces.append(lax.ppermute(piece, ALL, route))]
    all_to_all x2 -> x3, blocking collectives: 26.4 us -> 42.8 us  [the longest x1 15.1 us: per_device(): terms = lax.all_to_all(project(1, idx, done, [wo1]), 'y', 0, 0, tiled=True)]
    ppermute x22 -> x16, waiting for transfers between devices: 62.3 us -> 46.6 us  [from_ahead(): lax.ppermute(block, axis, [(i, (i - distance) % size) for i in range(size)])]
    ppermute x4 -> x5, waiting for transfers between devices: 11.6 us -> 24.3 us  [shifted(): return lax.ppermute(block, axis, route)]
    all_to_all x2 -> x1, starting transfers between devices: 8.21 us -> 3.37 us  [per_device(): done = lax.all_to_all(attend(own, 1), 'z', 0, 0, tiled=True)]
    ppermute x22 -> x16, starting transfers between devices: 35 us -> 30.2 us  [from_ahead(): lax.ppermute(block, axis, [(i, (i - distance) % size) for i in range(size)])]
    ppermute x4 -> x5, starting transfers between devices: 11.1 us -> 15.7 us  [shifted(): return lax.ppermute(block, axis, route)]
    unnamed x26 -> x16, local copies, waits for them, and re-layouts: 7.49 us -> 3.77 us
  transfers between devices with their start and end apart: 42 -> 29, of which waited for: 21 -> 17; matrix products, arithmetic and copies ran while one was open for 6% -> 1% of each run, Pallas kernels for 11% -> 12%
where the time goes in v3:
time: 277 us; the launch traced here: 273 us
  waiting for transfers between devices  80.2 us (29%)
  blocking collectives  71.1 us (26%)
  starting transfers between devices  52.1 us (19%)
  Pallas kernels  35.8 us (13%)
  between operations  16 us (6%)
  local copies, waits for them, and re-layouts  13.3 us (5%)
  other arithmetic  4.35 us (2%)
    ppermute x16, waiting for transfers between devices, from_ahead(): lax.ppermute(block, axis, [(i, (i - distance) % size) for i in range(size)])  46.6 us
    ppermute x16, starting transfers between devices, from_ahead(): lax.ppermute(block, axis, [(i, (i - distance) % size) for i in range(size)])  30.2 us
    ppermute x5, waiting for transfers between devices, shifted(): return lax.ppermute(block, axis, route)  24.3 us
    pallas_call x2, Pallas kernels, attention(): pl.pallas_call(functools.partial(attention_kernel, groups), out_shape=jax...  18.1 us
    all_to_all x1, blocking collectives, per_device(): own = lax.all_to_all(heads, 'z', 0, 0, tiled=True)  17.4 us
    ppermute x5, starting transfers between devices, shifted(): return lax.ppermute(block, axis, route)  15.7 us
    all_to_all x1, blocking collectives, per_device(): terms = lax.all_to_all(project(1, idx, done, [wo1]), 'y', 0, 0, tiled=True)  15.1 us
    all_to_all x1, blocking collectives, per_device(): done = lax.all_to_all(done, 'z', 0, 0, tiled=True)  14.3 us
  transfers between devices with their start and end apart: 29, of which 17 were waited for; matrix products, arithmetic and copies ran while one was open for 1% of the time, Pallas kernels for 12%

profile of v3, /device:TPU:4, one launch (start us, length us, event | category | flops | bytes accessed | tf_op | source)
XLA Modules:
  0.0 273.0 jit_solution(5473547020370886596)
XLA Ops:
  7.2 1.3 fusion.4
  9.8 1.9 fusion.1
  15.3 3.1 %collective-permute-start.7 = (bf16[192,1536]{1,0:T(8,128)(2,1)S(1)}, bf16[192,1536]{1,0:T(8,128)(2,1)S(1)}, u32[]{:S(2)}, u32[]{:S(2)}) collective-permute-start(bf16[192,1536]{1,0:T(8,128)(2,1)S(1)} %dynamic-slice_bitcast_fusion), channel_id=1, source_target_pairs={{0,3},{1,0},{2,1},{3,2},{4,7},{5,4},{6,5},{7,6},{8,11},{9,8},{10,9... | collective-permute-start | bytes 1769480 | tf_op jit(solution)/shard_map/ppermute | solution.py:267
  20.0 5.9 %collective-permute-start = (bf16[32,3072]{1,0:T(8,128)(2,1)S(1)}, bf16[32,3072]{1,0:T(8,128)(2,1)S(1)}, u32[]{:S(2)}, u32[]{:S(2)}) collective-permute-start(bf16[32,3072]{1,0:T(8,128)(2,1)S(1)} %fusion.refs_0_.x), channel_id=1, source_target_pairs={{0,28},{4,0},{8,4},{12,8},{16,12},{20,16},{24,20},{28,24},{1,29},{... | collective-permute-start | bytes 589832 | tf_op jit(solution)/shard_map/ppermute | solution.py:267
  25.8 3.3 %collective-permute-done.refs_1_ = bf16[32,3072]{1,0:T(8,128)(2,1)S(1)} collective-permute-done((bf16[32,3072]{1,0:T(8,128)(2,1)S(1)}, bf16[32,3072]{1,0:T(8,128)(2,1)S(1)}, u32[]{:S(2)}, u32[]{:S(2)}) %collective-permute-start) | collective-permute-done | bytes 196640 | tf_op jit(solution)/shard_map/ppermute | solution.py:267
  29.2 3.7 %collective-permute-start.1 = (bf16[32,3072]{1,0:T(8,128)(2,1)S(1)}, bf16[32,3072]{1,0:T(8,128)(2,1)S(1)}, u32[]{:S(2)}, u32[]{:S(2)}) collective-permute-start(bf16[32,3072]{1,0:T(8,128)(2,1)S(1)} %collective-permute-done.refs_1_), channel_id=1, source_target_pairs={{0,28},{4,0},{8,4},{12,8},{16,12},{20,16},{24,20},{28,24},{1,29},{... | collective-permute-start | bytes 589832 | tf_op jit(solution)/shard_map/ppermute | solution.py:267
  32.9 6.6 %collective-permute-done.1.refs_2_ = bf16[32,3072]{1,0:T(8,128)(2,1)S(1)} collective-permute-done((bf16[32,3072]{1,0:T(8,128)(2,1)S(1)}, bf16[32,3072]{1,0:T(8,128)(2,1)S(1)}, u32[]{:S(2)}, u32[]{:S(2)}) %collective-permute-start.1) | collective-permute-done | bytes 196640 | tf_op jit(solution)/shard_map/ppermute | solution.py:267
  39.5 3.7 %collective-permute-start.2 = (bf16[32,3072]{1,0:T(8,128)(2,1)S(1)}, bf16[32,3072]{1,0:T(8,128)(2,1)}, u32[]{:S(2)}, u32[]{:S(2)}) collective-permute-start(bf16[32,3072]{1,0:T(8,128)(2,1)S(1)} %collective-permute-done.1.refs_2_), channel_id=1, source_target_pairs={{0,28},{4,0},{8,4},{12,8},{16,12},{20,16},{24,20},{28,24},{1,29},{... | collective-permute-start | bytes 589832 | tf_op jit(solution)/shard_map/ppermute | solution.py:267
  44.1 3.2 %collective-permute-done.9.refs_12_ = bf16[192,1536]{1,0:T(8,128)(2,1)S(1)} collective-permute-done((bf16[192,1536]{1,0:T(8,128)(2,1)S(1)}, bf16[192,1536]{1,0:T(8,128)(2,1)S(1)}, u32[]{:S(2)}, u32[]{:S(2)}) %collective-permute-start.9) | collective-permute-done | bytes 589856 | tf_op jit(solution)/shard_map/ppermute | solution.py:267
  48.0 2.0 collective-permute-start.6
  50.2 4.1 %collective-permute-start.3 = (bf16[32,3072]{1,0:T(8,128)(2,1)}, bf16[32,3072]{1,0:T(8,128)(2,1)}, u32[]{:S(2)}, u32[]{:S(2)}) collective-permute-start(bf16[32,3072]{1,0:T(8,128)(2,1)} %collective-permute-done.2.refs_3_), channel_id=1, source_target_pairs={{0,28},{4,0},{8,4},{12,8},{16,12},{20,16},{24,20},{28,24},{1,29},{... | collective-permute-start | bytes 589832 | tf_op jit(solution)/shard_map/ppermute | solution.py:267
  55.3 7.9 %collective-permute-done.6.refs_5_ = bf16[32,3072]{1,0:T(8,128)(2,1)} collective-permute-done((bf16[32,3072]{1,0:T(8,128)(2,1)S(1)}, bf16[32,3072]{1,0:T(8,128)(2,1)}, u32[]{:S(2)}, u32[]{:S(2)}) %collective-permute-start.6) | collective-permute-done | bytes 196640 | tf_op jit(solution)/shard_map/ppermute | solution.py:267
  65.1 5.7 %qkv_first.1 = bf16[4,192,256]{2,1,0:T(8,128)(2,1)S(1)} custom-call(s32[4]{0:T(128)S(1)} %pad_add_fusion.idx, bf16[32,3072]{1,0:T(8,128)(2,1)S(1)} %fusion.refs_0_.x, bf16[32,3072]{1,0:T(8,128)(2,1)S(1)} %collective-permute-done.refs_1_, bf16[32,3072]{1,0:T(8,128)(2,1)S(1)} %copy-done.2, bf16[32,3072]{1,0:T(8,128)(2,1)} %collective-permute-done.2.refs_3_, ...), custom_call_target="tpu_custom_call" | custom-call | flops 1200000000 | bytes 7000000 | tf_op jit(solution)/shard_map/qkv_first/pallas_call | solution.py:84
  70.8 2.4 slice.55
  73.3 10.9 %all_to_all.30.own = bf16[4,192,256]{2,1,0:T(8,128)(2,1)S(1)} all-to-all(bf16[4,192,256]{2,1,0:T(8,128)(2,1)S(1)} %qkv_first.1), channel_id=1, replica_groups=mesh['x'=4,'core'=2,'z'=8,'y'=4] {'y'}, dimensions={0} | all-to-all | bytes 786432 | tf_op jit(solution)/shard_map/all_to_all | solution.py:326
  84.3 2.0 fusion.2
  86.3 1.9 collective-permute-start.13
  88.3 3.6 %collective-permute-start.14 = (bf16[4,128,256]{2,1,0:T(8,128)(2,1)S(1)}, bf16[4,128,256]{2,1,0:T(8,128)(2,1)S(1)}, u32[]{:S(2)}, u32[]{:S(2)}) collective-permute-start(bf16[4,128,256]{2,1,0:T(8,128)(2,1)S(1)} %slice.51), channel_id=1, source_target_pairs={{32,0},{64,32},{96,64},{128,96},{160,128},{192,160},{224,192},{33,... | collective-permute-start | bytes 786440 | tf_op jit(solution)/shard_map/ppermute | solution.py:277
  92.3 2.9 %collective-permute-start.16 = (bf16[8,64,384]{2,1,0:T(8,128)(2,1)S(1)}, bf16[8,64,384]{2,1,0:T(8,128)(2,1)S(1)}, u32[]{:S(2)}, u32[]{:S(2)}) collective-permute-start(bf16[8,64,384]{2,1,0:T(8,128)(2,1)S(1)} %get-tuple-element.18.refs_0_), channel_id=1, source_target_pairs={{0,128},{64,192},{128,0},{192,64},{1,129},{65,193},{129,1},{193,65... | collective-permute-start | bytes 1179656 | tf_op jit(solution)/shard_map/ppermute | solution.py:267
  95.3 6.0 %collective-permute-done.13.lower = bf16[4,128,256]{2,1,0:T(8,128)(2,1)S(1)} collective-permute-done((bf16[4,128,256]{2,1,0:T(8,128)(2,1)S(1)}, bf16[4,128,256]{2,1,0:T(8,128)(2,1)S(1)}, u32[]{:S(2)}, u32[]{:S(2)}) %collective-permute-start.13) | collective-permute-done | bytes 262176 | tf_op jit(solution)/shard_map/ppermute | solution.py:277
  101.3 2.9 %collective-permute-done.14.upper = bf16[4,128,256]{2,1,0:T(8,128)(2,1)S(1)} collective-permute-done((bf16[4,128,256]{2,1,0:T(8,128)(2,1)S(1)}, bf16[4,128,256]{2,1,0:T(8,128)(2,1)S(1)}, u32[]{:S(2)}, u32[]{:S(2)}) %collective-permute-start.14) | collective-permute-done | bytes 262176 | tf_op jit(solution)/shard_map/ppermute | solution.py:277
  104.2 8.8 %attention_4.1 = bf16[8,64,128]{2,1,0:T(8,128)(2,1)S(1)} custom-call(s32[4]{0:T(128)S(1)} %pad_add_fusion.idx, bf16[4,192,256]{2,1,0:T(8,128)(2,1)S(1)} %all_to_all.30.own, bf16[4,128,256]{2,1,0:T(8,128)(2,1)S(1)} %collective-permute-done.13.lower, bf16[4,128,256]{2,1,0:T(8,128)(2,1)S(1)} %collective-permute-done.14.upper, f32[1,128]{1,0:T(1,128)S(1)} %get-tuple-element.29.gain), custom_call_target="tpu_custom_call" | custom-call | flops 3000000000 | bytes 1200000 | tf_op jit(solution)/shard_map/attention_4/pallas_call | solution.py:194
  113.0 9.7 %collective-permute-done.15.refs_1_ = bf16[8,64,384]{2,1,0:T(8,128)(2,1)S(1)} collective-permute-done((bf16[8,64,384]{2,1,0:T(8,128)(2,1)S(1)}, bf16[8,64,384]{2,1,0:T(8,128)(2,1)S(1)}, u32[]{:S(2)}, u32[]{:S(2)}) %collective-permute-start.15) | collective-permute-done | bytes 393248 | tf_op jit(solution)/shard_map/ppermute | solution.py:267
  122.7 7.4 %collective-permute-done.17.refs_3_ = bf16[8,64,384]{2,1,0:T(8,128)(2,1)S(1)} collective-permute-done((bf16[8,64,384]{2,1,0:T(8,128)(2,1)S(1)}, bf16[8,64,384]{2,1,0:T(8,128)(2,1)S(1)}, u32[]{:S(2)}, u32[]{:S(2)}) %collective-permute-start.17) | collective-permute-done | bytes 393248 | tf_op jit(solution)/shard_map/ppermute | solution.py:267
  130.3 2.2 collective-permute-start.18
  132.5 14.3 %all_to_all.31.o = bf16[8,64,128]{2,1,0:T(8,128)(2,1)S(1)} all-to-all(bf16[8,64,128]{2,1,0:T(8,128)(2,1)S(1)} %attention_4.1), channel_id=1, replica_groups=mesh['x'=4,'core'=2,'z'=8,'y'=4] {'z'}, dimensions={0} | all-to-all | bytes 262144 | tf_op jit(solution)/shard_map/all_to_all | solution.py:333
  146.8 1.3 project_0.1
  148.0 13.4 %all_to_all.32.terms = bf16[4,32,3072]{2,1,0:T(8,128)(2,1)S(1)} all-to-all(bf16[4,32,3072]{2,1,0:T(8,128)(2,1)S(1)} %bitcast.42), channel_id=1, replica_groups=mesh['x'=4,'core'=2,'z'=8,'y'=4] {'y'}, dimensions={0} | all-to-all | bytes 1572864 | tf_op jit(solution)/shard_map/all_to_all | solution.py:334
  161.6 1.2 collective-permute-start.19
  162.8 1.6 collective-permute-start.20
  164.4 3.4 %collective-permute-done.19.x1 = bf16[32,3072]{1,0:T(8,128)(2,1)S(1)} collective-permute-done((bf16[32,3072]{1,0:T(8,128)(2,1)S(1)}, bf16[32,3072]{1,0:T(8,128)(2,1)S(1)}, u32[]{:S(2)}, u32[]{:S(2)}) %collective-permute-start.19) | collective-permute-done | bytes 196640 | tf_op jit(solution)/shard_map/ppermute | solution.py:267
  167.9 2.5 collective-permute-done.20.x2
  170.3 2.0 collective-permute-done.21.x3
  172.4 8.5 %qkv_second.1 = bf16[8,192,128]{2,1,0:T(8,128)(2,1)S(1)} custom-call(s32[4]{0:T(128)S(1)} %pad_add_fusion.idx, bf16[32,3072]{1,0:T(8,128)(2,1)S(1)} %residual_0.1.x0.x, bf16[32,3072]{1,0:T(8,128)(2,1)S(1)} %collective-permute-done.19.x1, bf16[32,3072]{1,0:T(8,128)(2,1)S(1)} %collective-permute-done.20.x2, bf16[32,3072]{1,0:T(8,128)(2,1)S(1)} %collective-permute-done.21.x3, ...), custom_call_target="tpu_custom_call" | custom-call | flops 1200000000 | bytes 10500000 | tf_op jit(solution)/shard_map/qkv_second/pallas_call | solution.py:119
  180.9 17.4 %all_to_all.33.own = bf16[8,192,128]{2,1,0:T(8,128)(2,1)S(1)} all-to-all(bf16[8,192,128]{2,1,0:T(8,128)(2,1)S(1)} %qkv_second.1), channel_id=1, replica_groups=mesh['x'=4,'core'=2,'z'=8,'y'=4] {'z'}, dimensions={0} | all-to-all | bytes 786432 | tf_op jit(solution)/shard_map/all_to_all | solution.py:339
  198.3 2.1 collective-permute-start.22
  200.4 6.0 %collective-permute-start.23 = (bf16[8,128,128]{2,1,0:T(8,128)(2,1)S(1)}, bf16[8,128,128]{2,1,0:T(8,128)(2,1)S(1)}, u32[]{:S(2)}, u32[]{:S(2)}) collective-permute-start(bf16[8,128,128]{2,1,0:T(8,128)(2,1)S(1)} %slice.62), channel_id=1, source_target_pairs={{32,0},{64,32},{96,64},{128,96},{160,128},{192,160},{224,192},{33,... | collective-permute-start | bytes 786440 | tf_op jit(solution)/shard_map/ppermute | solution.py:277
  206.5 2.1 collective-permute-done.22.lower
  208.6 2.1 collective-permute-done.23.upper
  210.7 9.3 %attention_8.1 = bf16[8,64,128]{2,1,0:T(8,128)(2,1)} custom-call(s32[4]{0:T(128)S(1)} %pad_add_fusion.idx, bf16[8,192,128]{2,1,0:T(8,128)(2,1)S(1)} %all_to_all.33.own, bf16[8,128,128]{2,1,0:T(8,128)(2,1)S(1)} %collective-permute-done.22.lower, bf16[8,128,128]{2,1,0:T(8,128)(2,1)S(1)} %collective-permute-done.23.upper, f32[1,128]{1,0:T(1,128)S(1)} %get-tuple-element.28.gain), custom_call_target="tpu_custom_call" | custom-call | flops 3000000000 | bytes 1200000 | tf_op jit(solution)/shard_map/attention_8/pallas_call | solution.py:194
  220.0 3.4 %all-to-all-start.4 = ((bf16[8,64,128]{2,1,0:T(8,128)(2,1)}), bf16[8,64,128]{2,1,0:T(8,128)(2,1)S(1)}, u32[]{:S(2)}, u32[]{:S(2)}) async-start(bf16[8,64,128]{2,1,0:T(8,128)(2,1)} %attention_8.1), calls=%async_computation.4 | async-start | bytes 262144 | tf_op jit(solution)/shard_map/all_to_all | solution.py:340
  223.4 9.1 %all-to-all-done.4.o = bf16[8,64,128]{2,1,0:T(8,128)(2,1)S(1)} async-done(((bf16[8,64,128]{2,1,0:T(8,128)(2,1)}), bf16[8,64,128]{2,1,0:T(8,128)(2,1)S(1)}, u32[]{:S(2)}, u32[]{:S(2)}) %all-to-all-start.4) | async-done | bytes 131104 | tf_op jit(solution)/shard_map/all_to_all | solution.py:340
  232.5 1.9 copy-done
  234.4 1.3 project_1.1
  235.7 15.1 %all_to_all.34.terms = bf16[4,32,3072]{2,1,0:T(8,128)(2,1)S(1)} all-to-all(bf16[4,32,3072]{2,1,0:T(8,128)(2,1)S(1)} %bitcast.43), channel_id=1, replica_groups=mesh['x'=4,'core'=2,'z'=8,'y'=4] {'y'}, dimensions={0} | all-to-all | bytes 1572864 | tf_op jit(solution)/shard_map/all_to_all | solution.py:341
  251.6 1.9 collective-permute-start.24
  253.6 11.3 %collective-permute-done.24 = bf16[32,3072]{1,0:T(8,128)(2,1)S(1)} collective-permute-done((bf16[32,3072]{1,0:T(8,128)(2,1)}, bf16[32,3072]{1,0:T(8,128)(2,1)S(1)}, u32[]{:S(2)}, u32[]{:S(2)}) %collective-permute-start.24) | collective-permute-done | bytes 196640 | tf_op jit(solution)/shard_map/ppermute | solution.py:277
  264.8 1.7 select_bitcast_fusion
  (63 shorter events, 11.0 us)
Async XLA Ops:
  7.2 63.7 %all-gather.7.cloned.1.call-start = ((), (), s32[]{:S(2)}) async-start(), calls=%async_computation.6 | async-start | bytes 2211840 | tf_op jit(solution)/shard_map/all_gather | solution.py:314
  9.8 1.9 copy-start.5
  11.7 1.8 copy-start.6
  15.2 157.2 %all-gather.9.cloned.1.call-start = ((), (), s32[]{:S(2)}) async-start(), calls=%async_computation.7 | async-start | bytes 10616832 | tf_op jit(solution)/shard_map/all_gather | solution.py:324
  15.3 28.3 %collective-permute-start.7 = (bf16[192,1536]{1,0:T(8,128)(2,1)S(1)}, bf16[192,1536]{1,0:T(8,128)(2,1)S(1)}, u32[]{:S(2)}, u32[]{:S(2)}) collective-permute-start(bf16[192,1536]{1,0:T(8,128)(2,1)S(1)} %dynamic-slice_bitcast_fusion), channel_id=1, source_target_pairs={{0,3},{1,0},{2,1},{3,2},{4,7},{5,4},{6,5},{7,6},{8,11},{9,8},{10,9... | collective-permute-start | bytes 1769480 | tf_op jit(solution)/shard_map/ppermute | solution.py:267
  18.4 25.2 %collective-permute-start.8 = (bf16[192,1536]{1,0:T(8,128)(2,1)S(1)}, bf16[192,1536]{1,0:T(8,128)(2,1)S(1)}, u32[]{:S(2)}, u32[]{:S(2)}) collective-permute-start(bf16[192,1536]{1,0:T(8,128)(2,1)S(1)} %dynamic-slice_bitcast_fusion), channel_id=1, source_target_pairs={{0,2},{1,3},{2,0},{3,1},{4,6},{5,7},{6,4},{7,5},{8,10},{9,11},{10,... | collective-permute-start | bytes 1769480 | tf_op jit(solution)/shard_map/ppermute | solution.py:267
  19.0 28.3 %collective-permute-start.9 = (bf16[192,1536]{1,0:T(8,128)(2,1)S(1)}, bf16[192,1536]{1,0:T(8,128)(2,1)S(1)}, u32[]{:S(2)}, u32[]{:S(2)}) collective-permute-start(bf16[192,1536]{1,0:T(8,128)(2,1)S(1)} %dynamic-slice_bitcast_fusion), channel_id=1, source_target_pairs={{0,1},{1,2},{2,3},{3,0},{4,5},{5,6},{6,7},{7,4},{8,9},{9,10},{10,1... | collective-permute-start | bytes 1769480 | tf_op jit(solution)/shard_map/ppermute | solution.py:267
  20.0 9.2 %collective-permute-start = (bf16[32,3072]{1,0:T(8,128)(2,1)S(1)}, bf16[32,3072]{1,0:T(8,128)(2,1)S(1)}, u32[]{:S(2)}, u32[]{:S(2)}) collective-permute-start(bf16[32,3072]{1,0:T(8,128)(2,1)S(1)} %fusion.refs_0_.x), channel_id=1, source_target_pairs={{0,28},{4,0},{8,4},{12,8},{16,12},{20,16},{24,20},{28,24},{1,29},{... | collective-permute-start | bytes 589832 | tf_op jit(solution)/shard_map/ppermute | solution.py:267
  25.8 7.0 %collective-permute-start.4 = (bf16[32,3072]{1,0:T(8,128)(2,1)S(1)}, bf16[32,3072]{1,0:T(8,128)(2,1)S(1)}, u32[]{:S(2)}, u32[]{:S(2)}) collective-permute-start(bf16[32,3072]{1,0:T(8,128)(2,1)S(1)} %fusion.refs_0_.x), channel_id=1, source_target_pairs={{0,4},{4,8},{8,12},{12,16},{16,20},{20,24},{24,28},{28,0},{1,5},{5... | collective-permute-start | bytes 589832 | tf_op jit(solution)/shard_map/ppermute | solution.py:267
  29.2 10.3 %collective-permute-start.1 = (bf16[32,3072]{1,0:T(8,128)(2,1)S(1)}, bf16[32,3072]{1,0:T(8,128)(2,1)S(1)}, u32[]{:S(2)}, u32[]{:S(2)}) collective-permute-start(bf16[32,3072]{1,0:T(8,128)(2,1)S(1)} %collective-permute-done.refs_1_), channel_id=1, source_target_pairs={{0,28},{4,0},{8,4},{12,8},{16,12},{20,16},{24,20},{28,24},{1,29},{... | collective-permute-start | bytes 589832 | tf_op jit(solution)/shard_map/ppermute | solution.py:267
  32.9 15.1 %collective-permute-start.5 = (bf16[32,3072]{1,0:T(8,128)(2,1)S(1)}, bf16[32,3072]{1,0:T(8,128)(2,1)S(1)}, u32[]{:S(2)}, u32[]{:S(2)}) collective-permute-start(bf16[32,3072]{1,0:T(8,128)(2,1)S(1)} %collective-permute-done.4.refs_7_), channel_id=1, source_target_pairs={{0,4},{4,8},{8,12},{12,16},{16,20},{20,24},{24,28},{28,0},{1,5},{5... | collective-permute-start | bytes 589832 | tf_op jit(solution)/shard_map/ppermute | solution.py:267
  39.5 23.8 %copy-start.1 = (bf16[32,3072]{1,0:T(8,128)(2,1)}, bf16[32,3072]{1,0:T(8,128)(2,1)S(1)}, u32[]{:S(2)}) copy-start(bf16[32,3072]{1,0:T(8,128)(2,1)S(1)} %collective-permute-done.1.refs_2_) | copy-start | bytes 589828
  39.5 10.7 %collective-permute-start.2 = (bf16[32,3072]{1,0:T(8,128)(2,1)S(1)}, bf16[32,3072]{1,0:T(8,128)(2,1)}, u32[]{:S(2)}, u32[]{:S(2)}) collective-permute-start(bf16[32,3072]{1,0:T(8,128)(2,1)S(1)} %collective-permute-done.1.refs_2_), channel_id=1, source_target_pairs={{0,28},{4,0},{8,4},{12,8},{16,12},{20,16},{24,20},{28,24},{1,29},{... | collective-permute-start | bytes 589832 | tf_op jit(solution)/shard_map/ppermute | solution.py:267
  43.6 19.6 %collective-permute-start.10 = (bf16[192,1536]{1,0:T(8,128)(2,1)S(1)}, bf16[192,1536]{1,0:T(8,128)(2,1)S(1)}, u32[]{:S(2)}, u32[]{:S(2)}) collective-permute-start(bf16[192,1536]{1,0:T(8,128)(2,1)S(1)} %collective-permute-done.7.refs_10_), channel_id=1, source_target_pairs={{0,32},{32,0},{1,33},{33,1},{2,34},{34,2},{3,35},{35,3},{4,36},{36... | collective-permute-start | bytes 1769480 | tf_op jit(solution)/shard_map/ppermute | solution.py:271
  43.6 19.6 %collective-permute-start.11 = (bf16[192,1536]{1,0:T(8,128)(2,1)S(1)}, bf16[192,1536]{1,0:T(8,128)(2,1)}, u32[]{:S(2)}, u32[]{:S(2)}) collective-permute-start(bf16[192,1536]{1,0:T(8,128)(2,1)S(1)} %collective-permute-done.8.refs_11_), channel_id=1, source_target_pairs={{0,32},{32,0},{1,33},{33,1},{2,34},{34,2},{3,35},{35,3},{4,36},{36... | collective-permute-start | bytes 1769480 | tf_op jit(solution)/shard_map/ppermute | solution.py:271
  47.3 15.9 %collective-permute-start.12 = (bf16[192,1536]{1,0:T(8,128)(2,1)S(1)}, bf16[192,1536]{1,0:T(8,128)(2,1)}, u32[]{:S(2)}, u32[]{:S(2)}) collective-permute-start(bf16[192,1536]{1,0:T(8,128)(2,1)S(1)} %collective-permute-done.9.refs_12_), channel_id=1, source_target_pairs={{0,32},{32,0},{1,33},{33,1},{2,34},{34,2},{3,35},{35,3},{4,36},{36... | collective-permute-start | bytes 1769480 | tf_op jit(solution)/shard_map/ppermute | solution.py:271
  48.0 15.3 %copy-start.3 = (bf16[32,3072]{1,0:T(8,128)(2,1)}, bf16[32,3072]{1,0:T(8,128)(2,1)S(1)}, u32[]{:S(2)}) copy-start(bf16[32,3072]{1,0:T(8,128)(2,1)S(1)} %collective-permute-done.5.refs_6_) | copy-start | bytes 589828
  48.0 15.2 %collective-permute-start.6 = (bf16[32,3072]{1,0:T(8,128)(2,1)S(1)}, bf16[32,3072]{1,0:T(8,128)(2,1)}, u32[]{:S(2)}, u32[]{:S(2)}) collective-permute-start(bf16[32,3072]{1,0:T(8,128)(2,1)S(1)} %collective-permute-done.5.refs_6_), channel_id=1, source_target_pairs={{0,4},{4,8},{8,12},{12,16},{16,20},{20,24},{24,28},{28,0},{1,5},{5... | collective-permute-start | bytes 589832 | tf_op jit(solution)/shard_map/ppermute | solution.py:267
  50.2 13.0 %collective-permute-start.3 = (bf16[32,3072]{1,0:T(8,128)(2,1)}, bf16[32,3072]{1,0:T(8,128)(2,1)}, u32[]{:S(2)}, u32[]{:S(2)}) collective-permute-start(bf16[32,3072]{1,0:T(8,128)(2,1)} %collective-permute-done.2.refs_3_), channel_id=1, source_target_pairs={{0,28},{4,0},{8,4},{12,8},{16,12},{20,16},{24,20},{28,24},{1,29},{... | collective-permute-start | bytes 589832 | tf_op jit(solution)/shard_map/ppermute | solution.py:267
  63.3 0.9 copy-start.2
  64.2 0.9 copy-start.4
  73.3 18.7 %copy-start.7 = (bf16[2,1,128]{2,0,1:T(2,128)(2,1)S(1)}, bf16[2,1,128]{2,0,1:T(2,128)(2,1)}, u32[]{:S(2)}) copy-start(bf16[2,1,128]{2,0,1:T(2,128)(2,1)} %param.16) | copy-start | bytes 1540
  73.3 150.1 %all-gather.11.cloned.1.call-start = ((), (), s32[]{:S(2)}) async-start(), calls=%async_computation.8 | async-start | bytes 3538944 | tf_op jit(solution)/shard_map/all_gather | solution.py:330
  86.3 15.0 %collective-permute-start.13 = (bf16[4,128,256]{2,1,0:T(8,128)(2,1)S(1)}, bf16[4,128,256]{2,1,0:T(8,128)(2,1)S(1)}, u32[]{:S(2)}, u32[]{:S(2)}) collective-permute-start(bf16[4,128,256]{2,1,0:T(8,128)(2,1)S(1)} %slice.51), channel_id=1, source_target_pairs={{0,32},{32,64},{64,96},{96,128},{128,160},{160,192},{192,224},{1,3... | collective-permute-start | bytes 786440 | tf_op jit(solution)/shard_map/ppermute | solution.py:277
  88.3 15.9 %collective-permute-start.14 = (bf16[4,128,256]{2,1,0:T(8,128)(2,1)S(1)}, bf16[4,128,256]{2,1,0:T(8,128)(2,1)S(1)}, u32[]{:S(2)}, u32[]{:S(2)}) collective-permute-start(bf16[4,128,256]{2,1,0:T(8,128)(2,1)S(1)} %slice.51), channel_id=1, source_target_pairs={{32,0},{64,32},{96,64},{128,96},{160,128},{192,160},{224,192},{33,... | collective-permute-start | bytes 786440 | tf_op jit(solution)/shard_map/ppermute | solution.py:277
  91.9 30.7 %collective-permute-start.15 = (bf16[8,64,384]{2,1,0:T(8,128)(2,1)S(1)}, bf16[8,64,384]{2,1,0:T(8,128)(2,1)S(1)}, u32[]{:S(2)}, u32[]{:S(2)}) collective-permute-start(bf16[8,64,384]{2,1,0:T(8,128)(2,1)S(1)} %get-tuple-element.18.refs_0_), channel_id=1, source_target_pairs={{0,192},{64,0},{128,64},{192,128},{1,193},{65,1},{129,65},{193,129... | collective-permute-start | bytes 1179656 | tf_op jit(solution)/shard_map/ppermute | solution.py:267
  92.3 30.3 %collective-permute-start.16 = (bf16[8,64,384]{2,1,0:T(8,128)(2,1)S(1)}, bf16[8,64,384]{2,1,0:T(8,128)(2,1)S(1)}, u32[]{:S(2)}, u32[]{:S(2)}) collective-permute-start(bf16[8,64,384]{2,1,0:T(8,128)(2,1)S(1)} %get-tuple-element.18.refs_0_), channel_id=1, source_target_pairs={{0,128},{64,192},{128,0},{192,64},{1,129},{65,193},{129,1},{193,65... | collective-permute-start | bytes 1179656 | tf_op jit(solution)/shard_map/ppermute | solution.py:267
  95.3 34.7 %collective-permute-start.17 = (bf16[8,64,384]{2,1,0:T(8,128)(2,1)S(1)}, bf16[8,64,384]{2,1,0:T(8,128)(2,1)S(1)}, u32[]{:S(2)}, u32[]{:S(2)}) collective-permute-start(bf16[8,64,384]{2,1,0:T(8,128)(2,1)S(1)} %get-tuple-element.18.refs_0_), channel_id=1, source_target_pairs={{0,64},{64,128},{128,192},{192,0},{1,65},{65,129},{129,193},{193,1... | collective-permute-start | bytes 1179656 | tf_op jit(solution)/shard_map/ppermute | solution.py:267
  130.3 16.5 %collective-permute-start.18 = (bf16[4,8,64,384]{3,2,1,0:T(8,128)(2,1)S(1)}, bf16[4,8,64,384]{3,2,1,0:T(8,128)(2,1)S(1)}, u32[]{:S(2)}, u32[]{:S(2)}) collective-permute-start(bf16[4,8,64,384]{3,2,1,0:T(8,128)(2,1)S(1)} %pad_maximum_fusion), channel_id=1, source_target_pairs={{0,32},{32,0},{1,33},{33,1},{2,34},{34,2},{3,35},{35,3},{4,36},{36... | collective-permute-start | bytes 4718600 | tf_op jit(solution)/shard_map/ppermute | solution.py:271
  161.6 6.3 %collective-permute-start.19 = (bf16[32,3072]{1,0:T(8,128)(2,1)S(1)}, bf16[32,3072]{1,0:T(8,128)(2,1)S(1)}, u32[]{:S(2)}, u32[]{:S(2)}) collective-permute-start(bf16[32,3072]{1,0:T(8,128)(2,1)S(1)} %residual_0.1.x0.x), channel_id=1, source_target_pairs={{0,3},{1,0},{2,1},{3,2},{4,7},{5,4},{6,5},{7,6},{8,11},{9,8},{10,9... | collective-permute-start | bytes 589832 | tf_op jit(solution)/shard_map/ppermute | solution.py:267
  162.8 7.5 %collective-permute-start.20 = (bf16[32,3072]{1,0:T(8,128)(2,1)S(1)}, bf16[32,3072]{1,0:T(8,128)(2,1)S(1)}, u32[]{:S(2)}, u32[]{:S(2)}) collective-permute-start(bf16[32,3072]{1,0:T(8,128)(2,1)S(1)} %residual_0.1.x0.x), channel_id=1, source_target_pairs={{0,2},{1,3},{2,0},{3,1},{4,6},{5,7},{6,4},{7,5},{8,10},{9,11},{10,... | collective-permute-start | bytes 589832 | tf_op jit(solution)/shard_map/ppermute | solution.py:267
  164.4 7.9 %collective-permute-start.21 = (bf16[32,3072]{1,0:T(8,128)(2,1)S(1)}, bf16[32,3072]{1,0:T(8,128)(2,1)S(1)}, u32[]{:S(2)}, u32[]{:S(2)}) collective-permute-start(bf16[32,3072]{1,0:T(8,128)(2,1)S(1)} %residual_0.1.x0.x), channel_id=1, source_target_pairs={{0,1},{1,2},{2,3},{3,0},{4,5},{5,6},{6,7},{7,4},{8,9},{9,10},{10,1... | collective-permute-start | bytes 589832 | tf_op jit(solution)/shard_map/ppermute | solution.py:267
  198.3 10.3 %collective-permute-start.22 = (bf16[8,128,128]{2,1,0:T(8,128)(2,1)S(1)}, bf16[8,128,128]{2,1,0:T(8,128)(2,1)S(1)}, u32[]{:S(2)}, u32[]{:S(2)}) collective-permute-start(bf16[8,128,128]{2,1,0:T(8,128)(2,1)S(1)} %slice.62), channel_id=1, source_target_pairs={{0,32},{32,64},{64,96},{96,128},{128,160},{160,192},{192,224},{1,3... | collective-permute-start | bytes 786440 | tf_op jit(solution)/shard_map/ppermute | solution.py:277
  200.4 10.2 %collective-permute-start.23 = (bf16[8,128,128]{2,1,0:T(8,128)(2,1)S(1)}, bf16[8,128,128]{2,1,0:T(8,128)(2,1)S(1)}, u32[]{:S(2)}, u32[]{:S(2)}) collective-permute-start(bf16[8,128,128]{2,1,0:T(8,128)(2,1)S(1)} %slice.62), channel_id=1, source_target_pairs={{32,0},{64,32},{96,64},{128,96},{160,128},{192,160},{224,192},{33,... | collective-permute-start | bytes 786440 | tf_op jit(solution)/shard_map/ppermute | solution.py:277
  220.0 12.5 %all-to-all-start.4 = ((bf16[8,64,128]{2,1,0:T(8,128)(2,1)}), bf16[8,64,128]{2,1,0:T(8,128)(2,1)S(1)}, u32[]{:S(2)}, u32[]{:S(2)}) async-start(bf16[8,64,128]{2,1,0:T(8,128)(2,1)} %attention_8.1), calls=%async_computation.4 | async-start | bytes 262144 | tf_op jit(solution)/shard_map/all_to_all | solution.py:340
  232.5 1.9 copy-start
  251.6 13.2 %collective-permute-start.24 = (bf16[32,3072]{1,0:T(8,128)(2,1)}, bf16[32,3072]{1,0:T(8,128)(2,1)S(1)}, u32[]{:S(2)}, u32[]{:S(2)}) collective-permute-start(bf16[32,3072]{1,0:T(8,128)(2,1)} %residual_1.1), channel_id=1, source_target_pairs={{16,0},{17,1},{18,2},{19,3},{20,4},{21,5},{22,6},{23,7},{24,8},{25... | collective-permute-start | bytes 589832 | tf_op jit(solution)/shard_map/ppermute | solution.py:277
Sparse Core Ops, SparseCore 0:
  15.3 48.2 all-gather.6
  73.4 73.4 all-gather.8
  148.7 30.3 all-gather.10

commit v4 on v3

--- a/solution.py
+++ b/solution.py
@@ -16,6 +16,7 @@
 ROWS = 32
 QUARTER = D // NY
 EIGHTH = QUARTER // 2
+PACK = (8 * ROWS, 3 * HD, 4 * HD, HD)
 VMEM_LIMIT = 48 * 1024 * 1024
 
 VM = pl.BlockSpec(memory_space=pltpu.VMEM)
@@ -50,27 +51,33 @@
     return lax.dot_general(weight, h, (((1,), (1,)), ((), ())), preferred_element_type=F32)
 
 
-def qkv_first_kernel(idx, *refs):
-    shards = refs[0:8]
-    mods, own = refs[8:10]
-    mine, other = refs[10:13], refs[13:16]
-    out, h = refs[16:18]
-    core, z, y = idx[1], idx[2], idx[3]
-    for k in range(NZ):
-        value = shards[k][...].astype(F32)
-        at = lax.rem(z + k, NZ)
-        (norm,) = normalized([value])
-        for b in range(NY):
-            cols = slice(b * QUARTER, (b + 1) * QUARTER)
-            part = norm[:, cols] * (1.0 + mods[1:2, cols]) + mods[0:1, cols]
-            h[b, at] = part.astype(BF)
+def qkv_first_kernel(idx, later, mods, w_t, *refs):
+    mine, other = refs[0:3], refs[3:6]
+    out, wq, wo0, wo1, h, x, own, sems = refs[6:]
+    core, y = idx[1], idx[3]
+    copies = []
+    row = 0
+    for n, (rows, target) in enumerate(zip(PACK, (x, wq, wo0, wo1))):
+        copies.append(pltpu.make_async_copy(later.at[:, row : row + rows, :], target, sems.at[n]))
+        row += rows
+    copies.insert(1, pltpu.make_async_copy(w_t.at[0], own, sems.at[4]))
+    for copy in copies:
+        copy.start()
+    copies[0].wait()
+    for z in range(NZ):
+        blocks = [x[z, e * ROWS : (e + 1) * ROWS, :].astype(F32) for e in range(8)]
+        for e, norm in enumerate(normalized(blocks)):
+            cols = slice(e * EIGHTH, (e + 1) * EIGHTH)
+            part = norm * (1.0 + mods[1:2, cols]) + mods[0:1, cols]
+            h[e // 2, z, :, (e % 2) * EIGHTH : (e % 2 + 1) * EIGHTH] = part.astype(BF)
 
     def tokens(b):
         return h[b].reshape(NZ * ROWS, QUARTER)
 
+    copies[1].wait()
     for j in range(NY):
         if j == 0:
-            total = sum(times(own[0, :, b * QUARTER : (b + 1) * QUARTER], tokens(b)) for b in range(NY))
+            total = sum(times(own[:, b * QUARTER : (b + 1) * QUARTER], tokens(b)) for b in range(NY))
         else:
             total = None
             for weight, side in ((mine[j - 1], core), (other[j - 1], 1 - core)):
@@ -78,19 +85,28 @@
                     term = times(weight[:, t * QUARTER : (t + 1) * QUARTER], tokens(2 * side + t))
                     total = term if total is None else total + term
         store_head(out.at[lax.rem(y + j, NY)], total)
-
-
-def qkv_first(idx, shards, mods, w_t, mine, other):
+    for copy in copies[2:]:
+        copy.wait()
+
+
+def qkv_first(idx, later, mods, w_t, mine, other):
+    anywhere = pl.BlockSpec(memory_space=pl.ANY)
     return pl.pallas_call(
         qkv_first_kernel,
-        out_shape=jax.ShapeDtypeStruct((NY, 3 * HD, NZ * ROWS), BF),
-        in_specs=[SM] + [VM] * 16,
-        out_specs=VM,
-        scratch_shapes=[pltpu.VMEM((NY, NZ, ROWS, QUARTER), BF)],
-        compiler_params=params(),
-        cost_estimate=pl.CostEstimate(flops=1_200_000_000, bytes_accessed=7_000_000, transcendentals=0),
+        out_shape=[jax.ShapeDtypeStruct((NY, 3 * HD, NZ * ROWS), BF)]
+        + [jax.ShapeDtypeStruct((NZ, rows, EIGHTH), BF) for rows in PACK[1:]],
+        in_specs=[SM, anywhere, VM, anywhere] + [VM] * 6,
+        out_specs=[VM] + [anywhere] * 3,
+        scratch_shapes=[
+            pltpu.VMEM((NY, NZ, ROWS, QUARTER), BF),
+            pltpu.VMEM((NZ, PACK[0], EIGHTH), BF),
+            pltpu.VMEM((3 * HD, D), BF),
+            pltpu.SemaphoreType.DMA((5,)),
+        ],
+        compiler_params=params(),
+        cost_estimate=pl.CostEstimate(flops=1_200_000_000, bytes_accessed=14_000_000, transcendentals=0),
         name="qkv_first",
-    )(idx, *shards, mods, w_t, *mine, *other)
+    )(idx, later, mods, w_t, *mine, *other)
 
 
 def qkv_second_kernel(idx, x0, x1, x2, x3, mods, weight, out, h):
@@ -149,14 +165,14 @@
     acc[...] = jnp.zeros_like(acc)
     den[...] = jnp.zeros_like(den)
 
-    def source(ref, first):
+    def source(ref):
         def body(m, carry):
             q = queries[m]
             total = acc[m]
             norm = den[m]
             for n in range(4):
-                keys = wide(ref, n, first, first + HD)
-                values = wide(ref, n, first + HD, first + 2 * HD)
+                keys = wide(ref, n, HD, 2 * HD)
+                values = wide(ref, n, 2 * HD, 3 * HD)
                 score = lax.dot_general(keys, q, (((0,), (0,)), ((), ())), preferred_element_type=F32)
                 e = jnp.exp(score)
                 norm = norm + jnp.sum(e, axis=0, keepdims=True)
@@ -167,15 +183,15 @@
 
         lax.fori_loop(0, 4, body, 0)
 
-    source(own, HD)
+    source(own)
 
     @pl.when(slot > 0)
     def _():
-        source(lower, 0)
+        source(lower)
 
     @pl.when(slot < NX * NC - 1)
     def _():
-        source(upper, 0)
+        source(upper)
 
     if per == 1:
         done = [acc[n] / den[n] for n in range(4)]
@@ -207,12 +223,11 @@
     )(idx, own, lower, upper, gain)
 
 
-def project_kernel(relative, idx, o, *refs):
+def project_kernel(halves, idx, o, *refs):
     weights, out = refs[:-1], refs[-1]
     rows = o[...].reshape(NZ * HD, NY * ROWS)
 
-    def put(weight, eighth):
-        w = weight.reshape(NZ * HD, EIGHTH)
+    def put(w, eighth):
         term = lax.dot_general(rows, w, (((0,), (0,)), ((), ())), preferred_element_type=F32)
         if isinstance(eighth, int):
             cols = slice(eighth * EIGHTH, (eighth + 1) * EIGHTH)
@@ -220,21 +235,19 @@
             cols = pl.ds(pl.multiple_of(eighth * EIGHTH, 128), EIGHTH)
         out[:, cols] = term.astype(BF)
 
-    if relative:
-        x_pos, core = idx[0], idx[1]
-        for k in range(NX):
-            at = lax.rem(x_pos + k, NX) * NC
-            put(weights[k][...], at + core)
-            put(weights[NX][k], at + 1 - core)
+    if halves:
+        for weight, side in zip(weights, (idx[1], 1 - idx[1])):
+            for e in range(4):
+                w = weight[:, e * HD : (e + 1) * HD, :].reshape(NZ * HD, EIGHTH)
+                put(w, 4 * side + e)
     else:
         for s in range(NX * NC):
-            put(weights[0][s], s)
+            put(weights[0][s].reshape(NZ * HD, EIGHTH), s)
 
 
 def project(layer, idx, o, weights):
-    relative = len(weights) > 1
     out = pl.pallas_call(
-        functools.partial(project_kernel, relative),
+        functools.partial(project_kernel, len(weights) == 2),
         out_shape=jax.ShapeDtypeStruct((NY * ROWS, D), BF),
         in_specs=[SM] + [VM] * (1 + len(weights)),
         out_specs=VM,
@@ -275,10 +288,6 @@
     devices = range(lax.axis_size(axis))
     route = [(i - distance, i) for i in devices if i - distance in devices]
     return lax.ppermute(block, axis, route)
-
-
-def after(value, *others):
-    return lax.optimization_barrier((value, *others))[0]
 
 
 SEQ = NZ * NY
@@ -301,37 +310,30 @@
 
     half = lax.dynamic_slice_in_dim(w_t[0], core * (D // 2), D // 2, 1)
     mine = [from_ahead(half, "y", NY, j) for j in range(1, NY)]
-    ahead, behind = [x0], [x0]
-    for _ in range(NZ // 2):
-        ahead.append(from_ahead(ahead[-1], "z", NZ, 1))
-    for _ in range(NZ // 2 - 1):
-        behind.append(from_ahead(behind[-1], "z", NZ, -1))
-    shards = ahead + behind[:0:-1]
     other = [swap(m) for m in mine]
 
-    eighth = lambda w: lax.dynamic_slice_in_dim(w, slot * EIGHTH, EIGHTH, 1)
-    pack = jnp.concatenate([eighth(w_t[1]), eighth(w_out[0]), eighth(w_out[1])], axis=0)
-    later = lax.all_gather(after(pack, x0), "z", axis=0, tiled=False)
+    def split(w, parts):
+        return jnp.transpose(w.reshape(-1, parts, EIGHTH), (1, 0, 2)).reshape(-1, EIGHTH)
+
+    def eighth(w):
+        return lax.dynamic_slice_in_dim(w, slot * EIGHTH, EIGHTH, 1)
+
+    wo_half = lax.dynamic_slice_in_dim(w_out[0], core * (D // 2), D // 2, 1)
+    pack = jnp.concatenate([split(x0, 8), eighth(w_t[1]), split(wo_half, 4), eighth(w_out[1])], axis=0)
+    later = lax.all_gather(pack, "z", axis=0, tiled=False)
 
     def attend(own, layer):
-        kv = own[:, HD:]
-        lower = shifted(kv, ("x", "core"), 1)
-        upper = shifted(kv, ("x", "core"), -1)
+        lower = shifted(own, ("x", "core"), 1)
+        upper = shifted(own, ("x", "core"), -1)
         return attention(idx, own, lower, upper, gains[layer : layer + 1])
 
-    heads = qkv_first(idx, shards, mods, w_t, mine, other)
-    heads, later = lax.optimization_barrier((heads, later))
-    wq1 = lax.all_gather(later[:, : 3 * HD], ("x", "core"), axis=0, tiled=False)
-
+    heads, wq1, wo0, wo1 = qkv_first(idx, later, mods, w_t, mine, other)
+    wq1 = lax.all_gather(wq1, ("x", "core"), axis=0, tiled=False)
     own = lax.all_to_all(heads, "y", 0, 0, tiled=True)
-    own, later = lax.optimization_barrier((own, later))
-    wo0 = later[:, 3 * HD : 4 * HD]
-    wo0 = [wo0] + [from_ahead(wo0, "x", NX, k) for k in range(1, NX)]
-    wo1 = lax.all_gather(later[:, 4 * HD :], ("x", "core"), axis=0, tiled=False)
-    done, *wo0 = lax.optimization_barrier((attend(own, 0), *wo0))
-    wo0 = [*wo0, swap(jnp.stack(wo0))]
-    done = lax.all_to_all(done, "z", 0, 0, tiled=True)
-    terms = lax.all_to_all(project(0, idx, done, wo0), "y", 0, 0, tiled=True)
+    own, wo0, wo1 = lax.optimization_barrier((own, wo0, wo1))
+    wo1 = lax.all_gather(wo1, ("x", "core"), axis=0, tiled=False)
+    done = lax.all_to_all(attend(own, 0), "z", 0, 0, tiled=True)
+    terms = lax.all_to_all(project(0, idx, done, [wo0, swap(wo0)]), "y", 0, 0, tiled=True)
     x1 = residual(0, terms, mods, x0)
 
     shards = [x1] + [from_ahead(x1, "y", NY, j) for j in range(1, NY)]

time: 277 us -> 365 us (1.32)
  Pallas kernels: 35.8 us -> 129 us
  waiting for transfers between devices: 80.2 us -> 113 us
  starting transfers between devices: 52.1 us -> 31.6 us
  blocking collectives: 71.1 us -> 57.3 us
  local copies, waits for them, and re-layouts: 13.3 us -> 5.74 us
    pallas_call x3, Pallas kernels: 8.22 us -> 101 us  [the longest x1 97.5 us: qkv_first(): pl.pallas_call(qkv_first_kernel, out_shape=[jax.ShapeDtypeStruct((NY, 3 *...]
    all_gather x3, waiting for transfers between devices: 0.04 us -> 28.6 us  [the longest x1 28.5 us: per_device(): later = lax.all_gather(pack, 'z', axis=0, tiled=False)]
    ppermute x16 -> x6, starting transfers between devices: 30.2 us -> 8.58 us  [from_ahead(): lax.ppermute(block, axis, [(i, (i - distance) % size) for i in range(size)])]
    all_to_all x2 -> x1, blocking collectives: 27.7 us -> 13.8 us  [per_device(): done = lax.all_to_all(attend(own, 0), 'z', 0, 0, tiled=True)]
    all_to_all x0 -> x1, waiting for transfers between devices: none -> 13.2 us  [per_device(): lax.all_to_all(project(0, idx, done, [wo0, swap(wo0)]), 'y', 0, 0, tiled=...]
    ppermute x16 -> x6, waiting for transfers between devices: 46.6 us -> 35.4 us  [from_ahead(): lax.ppermute(block, axis, [(i, (i - distance) % size) for i in range(size)])]
    slice x6 -> x2, local copies, waits for them, and re-layouts: 7.27 us -> 1.91 us  [the longest x1 1.85 us: per_device(): half = lax.dynamic_slice_in_dim(w_t[0], core * (D // 2), D // 2, 1)]
  transfers between devices with their start and end apart: 29 -> 20, of which waited for: 17 -> 13; matrix products, arithmetic and copies ran while one was open for 1% -> 0% of each run, Pallas kernels for 12% -> 8%
where the time goes in v4:
time: 365 us; the launch traced here: 358 us
  Pallas kernels  129 us (35%)
  waiting for transfers between devices  113 us (31%)
  blocking collectives  57.3 us (16%)
  starting transfers between devices  31.6 us (9%)
  between operations  16 us (4%)
  local copies, waits for them, and re-layouts  5.74 us (2%)
  other arithmetic  4.94 us (1%)
    pallas_call x1, Pallas kernels, qkv_first(): pl.pallas_call(qkv_first_kernel, out_shape=[jax.ShapeDtypeStruct((NY, 3 *...  97.5 us
    ppermute x6, waiting for transfers between devices, from_ahead(): lax.ppermute(block, axis, [(i, (i - distance) % size) for i in range(size)])  35.4 us
    all_gather x1, waiting for transfers between devices, per_device(): later = lax.all_gather(pack, 'z', axis=0, tiled=False)  28.5 us
    ppermute x5, waiting for transfers between devices, shifted(): return lax.ppermute(block, axis, route)  26.8 us
    pallas_call x2, Pallas kernels, attention(): pl.pallas_call(functools.partial(attention_kernel, groups), out_shape=jax...  18.1 us
    all_to_all x1, blocking collectives, per_device(): own = lax.all_to_all(heads, 'z', 0, 0, tiled=True)  17.5 us
    ppermute x5, starting transfers between devices, shifted(): return lax.ppermute(block, axis, route)  15.2 us
    all_to_all x1, blocking collectives, per_device(): done = lax.all_to_all(attend(own, 0), 'z', 0, 0, tiled=True)  13.8 us
  transfers between devices with their start and end apart: 20, of which 13 were waited for; matrix products, arithmetic and copies ran while one was open for 0% of the time, Pallas kernels for 8%

profile of v4, /device:TPU:4, one launch (start us, length us, event | category | flops | bytes accessed | tf_op | source)
XLA Modules:
  0.0 357.5 jit_solution(3194492556965442628)
XLA Ops:
  7.2 1.9 fusion.3
  9.2 0.5 copy-done.5
  9.8 0.6 fusion.5
  11.5 0.5 broadcast.5
  12.0 1.4 fusion.2
  13.7 0.9 pad_maximum_fusion
  14.7 3.1 collective-permute-start
  17.8 0.6 collective-permute-start.1
  18.5 1.0 collective-permute-start.2
  19.4 23.6 %collective-permute-done.refs_0_ = bf16[192,1536]{1,0:T(8,128)(2,1)S(1)} collective-permute-done((bf16[192,1536]{1,0:T(8,128)(2,1)S(1)}, bf16[192,1536]{1,0:T(8,128)(2,1)S(1)}, u32[]{:S(2)}, u32[]{:S(2)}) %collective-permute-start) | collective-permute-done | bytes 589856 | tf_op jit(solution)/shard_map/ppermute | solution.py:280
  43.1 0.5 collective-permute-start.4
  43.6 3.2 collective-permute-done.2.refs_2_
  47.5 0.8 dynamic-slice_convert_fusion
  48.5 0.4 collective-permute-done.5.refs_5_
  48.9 28.5 %all-gather.7.cloned.1.call-done = bf16[6144,384]{1,0:T(8,128)(2,1)} async-done(((bf16[768,384]{1,0:T(8,128)(2,1)}), bf16[6144,384]{1,0:T(8,128)(2,1)}) %all-gather.7.cloned.1.call-update) | async-done | bytes 4718608 | tf_op jit(solution)/shard_map/all_gather | solution.py:323
  77.4 97.5 %qkv_first.1 = (bf16[4,192,256]{2,1,0:T(8,128)(2,1)S(1)}, bf16[8,192,384]{2,1,0:T(8,128)(2,1)}, bf16[8,256,384]{2,1,0:T(8,128)(2,1)}, bf16[8,64,384]{2,1,0:T(8,128)(2,1)}) custom-call(s32[4]{0:T(128)S(1)} %pad_add_fusion.idx, bf16[8,768,384]{2,1,0:T(8,128)(2,1)} %bitcast.50, f32[6,3072]{1,0:T(8,128)S(1)} %reshape.48.mods, bf16[2,192,3072]{2,1,0:T(8,128)(2,1)} %bitcast.49, ...), custom_call_target="tpu_custom_call" | custom-call | flops 1200000000 | bytes 14000000 | tf_op jit(solution)/shard_map/qkv_first/pallas_call | solution.py:94
  175.1 12.3 %all_to_all.30.own = bf16[4,192,256]{2,1,0:T(8,128)(2,1)S(1)} all-to-all(bf16[4,192,256]{2,1,0:T(8,128)(2,1)S(1)} %get-tuple-element.9), channel_id=1, replica_groups=mesh['x'=4,'core'=2,'z'=8,'y'=4] {'y'}, dimensions={0} | all-to-all | bytes 786432 | tf_op jit(solution)/shard_map/all_to_all | solution.py:332
  187.5 2.4 collective-permute-start.6
  189.9 3.2 collective-permute-start.7
  193.1 11.9 %collective-permute-done.6.lower = bf16[4,192,256]{2,1,0:T(8,128)(2,1)S(1)} collective-permute-done((bf16[4,192,256]{2,1,0:T(8,128)(2,1)S(1)}, bf16[4,192,256]{2,1,0:T(8,128)(2,1)S(1)}, u32[]{:S(2)}, u32[]{:S(2)}) %collective-permute-start.6) | collective-permute-done | bytes 393248 | tf_op jit(solution)/shard_map/ppermute | solution.py:290
  205.0 1.8 collective-permute-done.7.upper
  206.7 8.8 %attention_4.1 = bf16[8,64,128]{2,1,0:T(8,128)(2,1)S(1)} custom-call(s32[4]{0:T(128)S(1)} %pad_add_fusion.idx, bf16[4,192,256]{2,1,0:T(8,128)(2,1)S(1)} %all_to_all.30.own, bf16[4,192,256]{2,1,0:T(8,128)(2,1)S(1)} %collective-permute-done.6.lower, bf16[4,192,256]{2,1,0:T(8,128)(2,1)S(1)} %collective-permute-done.7.upper, f32[1,128]{1,0:T(1,128)S(1)} %get-tuple-element.23.gain), custom_call_target="tpu_custom_call" | custom-call | flops 3000000000 | bytes 1200000 | tf_op jit(solution)/shard_map/attention_4/pallas_call | solution.py:210
  215.5 13.8 %all_to_all.31.o = bf16[8,64,128]{2,1,0:T(8,128)(2,1)S(1)} all-to-all(bf16[8,64,128]{2,1,0:T(8,128)(2,1)S(1)} %attention_4.1), channel_id=1, replica_groups=mesh['x'=4,'core'=2,'z'=8,'y'=4] {'z'}, dimensions={0} | all-to-all | bytes 262144 | tf_op jit(solution)/shard_map/all_to_all | solution.py:335
  229.4 2.2 project_0.1
  231.6 3.6 %all-to-all-start.2 = ((bf16[4,32,3072]{2,1,0:T(8,128)(2,1)}), bf16[4,32,3072]{2,1,0:T(8,128)(2,1)S(1)}, u32[]{:S(2)}, u32[]{:S(2)}) async-start(bf16[4,32,3072]{2,1,0:T(8,128)(2,1)} %bitcast.19), calls=%async_computation.2 | async-start | bytes 1572864 | tf_op jit(solution)/shard_map/all_to_all | solution.py:336
  235.3 13.2 %all-to-all-done.2.terms = bf16[4,32,3072]{2,1,0:T(8,128)(2,1)S(1)} async-done(((bf16[4,32,3072]{2,1,0:T(8,128)(2,1)}), bf16[4,32,3072]{2,1,0:T(8,128)(2,1)S(1)}, u32[]{:S(2)}, u32[]{:S(2)}) %all-to-all-start.2) | async-done | bytes 786464 | tf_op jit(solution)/shard_map/all_to_all | solution.py:336
  248.5 0.1 residual_0.1.x0.x
  248.7 0.6 collective-permute-start.10
  249.3 1.5 collective-permute-start.11
  250.8 1.8 collective-permute-start.9
  252.5 5.5 %collective-permute-done.10.x2 = bf16[32,3072]{1,0:T(8,128)(2,1)S(1)} collective-permute-done((bf16[32,3072]{1,0:T(8,128)(2,1)S(1)}, bf16[32,3072]{1,0:T(8,128)(2,1)S(1)}, u32[]{:S(2)}, u32[]{:S(2)}) %collective-permute-start.10) | collective-permute-done | bytes 196640 | tf_op jit(solution)/shard_map/ppermute | solution.py:280
  258.0 3.0 collective-permute-done.11.x3
  261.1 8.5 %qkv_second.1 = bf16[8,192,128]{2,1,0:T(8,128)(2,1)S(1)} custom-call(s32[4]{0:T(128)S(1)} %pad_add_fusion.idx, bf16[32,3072]{1,0:T(8,128)(2,1)S(1)} %residual_0.1.x0.x, bf16[32,3072]{1,0:T(8,128)(2,1)S(1)} %collective-permute-done.9.x1, bf16[32,3072]{1,0:T(8,128)(2,1)S(1)} %collective-permute-done.10.x2, bf16[32,3072]{1,0:T(8,128)(2,1)S(1)} %collective-permute-done.11.x3, ...), custom_call_target="tpu_custom_call" | custom-call | flops 1200000000 | bytes 10500000 | tf_op jit(solution)/shard_map/qkv_second/pallas_call | solution.py:135
  269.6 17.5 %all_to_all.32.own = bf16[8,192,128]{2,1,0:T(8,128)(2,1)S(1)} all-to-all(bf16[8,192,128]{2,1,0:T(8,128)(2,1)S(1)} %qkv_second.1), channel_id=1, replica_groups=mesh['x'=4,'core'=2,'z'=8,'y'=4] {'z'}, dimensions={0} | all-to-all | bytes 786432 | tf_op jit(solution)/shard_map/all_to_all | solution.py:341
  287.1 1.9 collective-permute-start.12
  289.0 3.6 %collective-permute-start.13 = (bf16[8,192,128]{2,1,0:T(8,128)(2,1)S(1)}, bf16[8,192,128]{2,1,0:T(8,128)(2,1)S(1)}, u32[]{:S(2)}, u32[]{:S(2)}) collective-permute-start(bf16[8,192,128]{2,1,0:T(8,128)(2,1)S(1)} %all_to_all.32.own), channel_id=1, source_target_pairs={{32,0},{64,32},{96,64},{128,96},{160,128},{192,160},{224,192},{33,... | collective-permute-start | bytes 1179656 | tf_op jit(solution)/shard_map/ppermute | solution.py:290
  292.7 3.5 collective-permute-done.12.lower
  296.2 1.8 collective-permute-done.13.upper
  297.9 9.3 %attention_8.1 = bf16[8,64,128]{2,1,0:T(8,128)(2,1)} custom-call(s32[4]{0:T(128)S(1)} %pad_add_fusion.idx, bf16[8,192,128]{2,1,0:T(8,128)(2,1)S(1)} %all_to_all.32.own, bf16[8,192,128]{2,1,0:T(8,128)(2,1)S(1)} %collective-permute-done.12.lower, bf16[8,192,128]{2,1,0:T(8,128)(2,1)S(1)} %collective-permute-done.13.upper, f32[1,128]{1,0:T(1,128)S(1)} %get-tuple-element.22.gain), custom_call_target="tpu_custom_call" | custom-call | flops 3000000000 | bytes 1200000 | tf_op jit(solution)/shard_map/attention_8/pallas_call | solution.py:210
  307.2 3.4 all-to-all-start.4
  310.6 9.0 %all-to-all-done.4.o = bf16[8,64,128]{2,1,0:T(8,128)(2,1)S(1)} async-done(((bf16[8,64,128]{2,1,0:T(8,128)(2,1)}), bf16[8,64,128]{2,1,0:T(8,128)(2,1)S(1)}, u32[]{:S(2)}, u32[]{:S(2)}) %all-to-all-start.4) | async-done | bytes 131104 | tf_op jit(solution)/shard_map/all_to_all | solution.py:342
  319.6 1.9 copy-done
  321.5 1.3 project_1.1
  322.8 13.8 %all_to_all.33.terms = bf16[4,32,3072]{2,1,0:T(8,128)(2,1)S(1)} all-to-all(bf16[4,32,3072]{2,1,0:T(8,128)(2,1)S(1)} %bitcast.45), channel_id=1, replica_groups=mesh['x'=4,'core'=2,'z'=8,'y'=4] {'y'}, dimensions={0} | all-to-all | bytes 1572864 | tf_op jit(solution)/shard_map/all_to_all | solution.py:343
  336.6 0.8 residual_1.1
  337.4 4.1 %collective-permute-start.14 = (bf16[32,3072]{1,0:T(8,128)(2,1)}, bf16[32,3072]{1,0:T(8,128)(2,1)S(1)}, u32[]{:S(2)}, u32[]{:S(2)}) collective-permute-start(bf16[32,3072]{1,0:T(8,128)(2,1)} %residual_1.1), channel_id=1, source_target_pairs={{16,0},{17,1},{18,2},{19,3},{20,4},{21,5},{22,6},{23,7},{24,8},{25... | collective-permute-start | bytes 589832 | tf_op jit(solution)/shard_map/ppermute | solution.py:290
  341.5 7.8 %collective-permute-done.14 = bf16[32,3072]{1,0:T(8,128)(2,1)S(1)} collective-permute-done((bf16[32,3072]{1,0:T(8,128)(2,1)}, bf16[32,3072]{1,0:T(8,128)(2,1)S(1)}, u32[]{:S(2)}, u32[]{:S(2)}) %collective-permute-start.14) | collective-permute-done | bytes 196640 | tf_op jit(solution)/shard_map/ppermute | solution.py:290
  349.4 1.7 select_bitcast_fusion
  (44 shorter events, 1.0 us)
Async XLA Ops:
  7.2 70.3 %all-gather.7.cloned.1.call-start = ((), (), s32[]{:S(2)}) async-start(), calls=%async_computation.6 | async-start | bytes 5308416 | tf_op jit(solution)/shard_map/all_gather | solution.py:323
  7.2 1.9 copy-start.2
  9.1 0.7 copy-start.5
  9.1 4.4 %copy-start.3 = (bf16[1,32,3072]{2,1,0:T(8,128)(2,1)S(1)}, bf16[1,32,3072]{2,1,0:T(8,128)(2,1)}, u32[]{:S(2)}) copy-start(bf16[1,32,3072]{2,1,0:T(8,128)(2,1)} %param.9) | copy-start | bytes 589828
  14.6 246.5 %all-gather.9.cloned.1.call-start = ((), (), s32[]{:S(2)}) async-start(), calls=%async_computation.7 | async-start | bytes 10616832 | tf_op jit(solution)/shard_map/all_gather | solution.py:331
  14.7 28.3 %collective-permute-start = (bf16[192,1536]{1,0:T(8,128)(2,1)S(1)}, bf16[192,1536]{1,0:T(8,128)(2,1)S(1)}, u32[]{:S(2)}, u32[]{:S(2)}) collective-permute-start(bf16[192,1536]{1,0:T(8,128)(2,1)S(1)} %dynamic-slice_bitcast_fusion), channel_id=1, source_target_pairs={{0,3},{1,0},{2,1},{3,2},{4,7},{5,4},{6,5},{7,6},{8,11},{9,8},{10,9... | collective-permute-start | bytes 1769480 | tf_op jit(solution)/shard_map/ppermute | solution.py:280
  17.8 25.2 %collective-permute-start.1 = (bf16[192,1536]{1,0:T(8,128)(2,1)S(1)}, bf16[192,1536]{1,0:T(8,128)(2,1)S(1)}, u32[]{:S(2)}, u32[]{:S(2)}) collective-permute-start(bf16[192,1536]{1,0:T(8,128)(2,1)S(1)} %dynamic-slice_bitcast_fusion), channel_id=1, source_target_pairs={{0,2},{1,3},{2,0},{3,1},{4,6},{5,7},{6,4},{7,5},{8,10},{9,11},{10,... | collective-permute-start | bytes 1769480 | tf_op jit(solution)/shard_map/ppermute | solution.py:280
  18.5 28.3 %collective-permute-start.2 = (bf16[192,1536]{1,0:T(8,128)(2,1)S(1)}, bf16[192,1536]{1,0:T(8,128)(2,1)S(1)}, u32[]{:S(2)}, u32[]{:S(2)}) collective-permute-start(bf16[192,1536]{1,0:T(8,128)(2,1)S(1)} %dynamic-slice_bitcast_fusion), channel_id=1, source_target_pairs={{0,1},{1,2},{2,3},{3,0},{4,5},{5,6},{6,7},{7,4},{8,9},{9,10},{10,1... | collective-permute-start | bytes 1769480 | tf_op jit(solution)/shard_map/ppermute | solution.py:280
  43.1 5.5 %collective-permute-start.3 = (bf16[192,1536]{1,0:T(8,128)(2,1)S(1)}, bf16[192,1536]{1,0:T(8,128)(2,1)S(1)}, u32[]{:S(2)}, u32[]{:S(2)}) collective-permute-start(bf16[192,1536]{1,0:T(8,128)(2,1)S(1)} %collective-permute-done.refs_0_), channel_id=1, source_target_pairs={{0,32},{32,0},{1,33},{33,1},{2,34},{34,2},{3,35},{35,3},{4,36},{36... | collective-permute-start | bytes 1769480 | tf_op jit(solution)/shard_map/ppermute | solution.py:284
  43.1 5.5 %collective-permute-start.4 = (bf16[192,1536]{1,0:T(8,128)(2,1)S(1)}, bf16[192,1536]{1,0:T(8,128)(2,1)S(1)}, u32[]{:S(2)}, u32[]{:S(2)}) collective-permute-start(bf16[192,1536]{1,0:T(8,128)(2,1)S(1)} %collective-permute-done.1.refs_1_), channel_id=1, source_target_pairs={{0,32},{32,0},{1,33},{33,1},{2,34},{34,2},{3,35},{35,3},{4,36},{36... | collective-permute-start | bytes 1769480 | tf_op jit(solution)/shard_map/ppermute | solution.py:284
  46.8 2.1 collective-permute-start.5
  175.0 12.4 %copy-start.1 = (bf16[8,256,384]{2,1,0:T(8,128)(2,1)S(1)}, bf16[8,256,384]{2,1,0:T(8,128)(2,1)}, u32[]{:S(2)}) copy-start(bf16[8,256,384]{2,1,0:T(8,128)(2,1)} %get-tuple-element.13.refs_0_) | copy-start | bytes 4718596
  175.0 18.1 %copy-start.6 = (bf16[2,1,128]{2,0,1:T(2,128)(2,1)S(1)}, bf16[2,1,128]{2,0,1:T(2,128)(2,1)}, u32[]{:S(2)}) copy-start(bf16[2,1,128]{2,0,1:T(2,128)(2,1)} %param.16) | copy-start | bytes 1540
  175.0 135.6 %all-gather.11.cloned.1.call-start = ((), (), s32[]{:S(2)}) async-start(), calls=%async_computation.8 | async-start | bytes 3538944 | tf_op jit(solution)/shard_map/all_gather | solution.py:334
  187.4 42.0 %collective-permute-start.8 = (bf16[8,256,384]{2,1,0:T(8,128)(2,1)S(1)}, bf16[8,256,384]{2,1,0:T(8,128)(2,1)S(1)}, u32[]{:S(2)}, u32[]{:S(2)}) collective-permute-start(bf16[8,256,384]{2,1,0:T(8,128)(2,1)S(1)} %copy-done.1), channel_id=1, source_target_pairs={{0,32},{32,0},{1,33},{33,1},{2,34},{34,2},{3,35},{35,3},{4,36},{36... | collective-permute-start | bytes 4718600 | tf_op jit(solution)/shard_map/ppermute | solution.py:284
  187.5 17.5 %collective-permute-start.6 = (bf16[4,192,256]{2,1,0:T(8,128)(2,1)S(1)}, bf16[4,192,256]{2,1,0:T(8,128)(2,1)S(1)}, u32[]{:S(2)}, u32[]{:S(2)}) collective-permute-start(bf16[4,192,256]{2,1,0:T(8,128)(2,1)S(1)} %all_to_all.30.own), channel_id=1, source_target_pairs={{0,32},{32,64},{64,96},{96,128},{128,160},{160,192},{192,224},{1,3... | collective-permute-start | bytes 1179656 | tf_op jit(solution)/shard_map/ppermute | solution.py:290
  189.9 16.8 %collective-permute-start.7 = (bf16[4,192,256]{2,1,0:T(8,128)(2,1)S(1)}, bf16[4,192,256]{2,1,0:T(8,128)(2,1)S(1)}, u32[]{:S(2)}, u32[]{:S(2)}) collective-permute-start(bf16[4,192,256]{2,1,0:T(8,128)(2,1)S(1)} %all_to_all.30.own), channel_id=1, source_target_pairs={{32,0},{64,32},{96,64},{128,96},{160,128},{192,160},{224,192},{33,... | collective-permute-start | bytes 1179656 | tf_op jit(solution)/shard_map/ppermute | solution.py:290
  231.6 3.6 %copy-start.4 = (bf16[1,32,3072]{2,1,0:T(8,128)(2,1)S(1)}, bf16[1,32,3072]{2,1,0:T(8,128)(2,1)}, u32[]{:S(2)}) copy-start(bf16[1,32,3072]{2,1,0:T(8,128)(2,1)} %param.9) | copy-start | bytes 589828
  231.6 16.9 %all-to-all-start.2 = ((bf16[4,32,3072]{2,1,0:T(8,128)(2,1)}), bf16[4,32,3072]{2,1,0:T(8,128)(2,1)S(1)}, u32[]{:S(2)}, u32[]{:S(2)}) async-start(bf16[4,32,3072]{2,1,0:T(8,128)(2,1)} %bitcast.19), calls=%async_computation.2 | async-start | bytes 1572864 | tf_op jit(solution)/shard_map/all_to_all | solution.py:336
  248.7 9.4 %collective-permute-start.10 = (bf16[32,3072]{1,0:T(8,128)(2,1)S(1)}, bf16[32,3072]{1,0:T(8,128)(2,1)S(1)}, u32[]{:S(2)}, u32[]{:S(2)}) collective-permute-start(bf16[32,3072]{1,0:T(8,128)(2,1)S(1)} %residual_0.1.x0.x), channel_id=1, source_target_pairs={{0,2},{1,3},{2,0},{3,1},{4,6},{5,7},{6,4},{7,5},{8,10},{9,11},{10,... | collective-permute-start | bytes 589832 | tf_op jit(solution)/shard_map/ppermute | solution.py:280
  249.3 11.8 %collective-permute-start.11 = (bf16[32,3072]{1,0:T(8,128)(2,1)S(1)}, bf16[32,3072]{1,0:T(8,128)(2,1)S(1)}, u32[]{:S(2)}, u32[]{:S(2)}) collective-permute-start(bf16[32,3072]{1,0:T(8,128)(2,1)S(1)} %residual_0.1.x0.x), channel_id=1, source_target_pairs={{0,1},{1,2},{2,3},{3,0},{4,5},{5,6},{6,7},{7,4},{8,9},{9,10},{10,1... | collective-permute-start | bytes 589832 | tf_op jit(solution)/shard_map/ppermute | solution.py:280
  250.8 10.3 %collective-permute-start.9 = (bf16[32,3072]{1,0:T(8,128)(2,1)S(1)}, bf16[32,3072]{1,0:T(8,128)(2,1)S(1)}, u32[]{:S(2)}, u32[]{:S(2)}) collective-permute-start(bf16[32,3072]{1,0:T(8,128)(2,1)S(1)} %residual_0.1.x0.x), channel_id=1, source_target_pairs={{0,3},{1,0},{2,1},{3,2},{4,7},{5,4},{6,5},{7,6},{8,11},{9,8},{10,9... | collective-permute-start | bytes 589832 | tf_op jit(solution)/shard_map/ppermute | solution.py:280
  287.1 9.1 %collective-permute-start.12 = (bf16[8,192,128]{2,1,0:T(8,128)(2,1)S(1)}, bf16[8,192,128]{2,1,0:T(8,128)(2,1)S(1)}, u32[]{:S(2)}, u32[]{:S(2)}) collective-permute-start(bf16[8,192,128]{2,1,0:T(8,128)(2,1)S(1)} %all_to_all.32.own), channel_id=1, source_target_pairs={{0,32},{32,64},{64,96},{96,128},{128,160},{160,192},{192,224},{1,3... | collective-permute-start | bytes 1179656 | tf_op jit(solution)/shard_map/ppermute | solution.py:290
  289.0 8.9 %collective-permute-start.13 = (bf16[8,192,128]{2,1,0:T(8,128)(2,1)S(1)}, bf16[8,192,128]{2,1,0:T(8,128)(2,1)S(1)}, u32[]{:S(2)}, u32[]{:S(2)}) collective-permute-start(bf16[8,192,128]{2,1,0:T(8,128)(2,1)S(1)} %all_to_all.32.own), channel_id=1, source_target_pairs={{32,0},{64,32},{96,64},{128,96},{160,128},{192,160},{224,192},{33,... | collective-permute-start | bytes 1179656 | tf_op jit(solution)/shard_map/ppermute | solution.py:290
  307.2 12.4 %all-to-all-start.4 = ((bf16[8,64,128]{2,1,0:T(8,128)(2,1)}), bf16[8,64,128]{2,1,0:T(8,128)(2,1)S(1)}, u32[]{:S(2)}, u32[]{:S(2)}) async-start(bf16[8,64,128]{2,1,0:T(8,128)(2,1)} %attention_8.1), calls=%async_computation.4 | async-start | bytes 262144 | tf_op jit(solution)/shard_map/all_to_all | solution.py:342
  319.6 1.9 copy-start
  337.4 12.0 %collective-permute-start.14 = (bf16[32,3072]{1,0:T(8,128)(2,1)}, bf16[32,3072]{1,0:T(8,128)(2,1)S(1)}, u32[]{:S(2)}, u32[]{:S(2)}) collective-permute-start(bf16[32,3072]{1,0:T(8,128)(2,1)} %residual_1.1), channel_id=1, source_target_pairs={{16,0},{17,1},{18,2},{19,3},{20,4},{21,5},{22,6},{23,7},{24,8},{25... | collective-permute-start | bytes 589832 | tf_op jit(solution)/shard_map/ppermute | solution.py:290
Sparse Core Ops, SparseCore 0:
  14.8 62.6 all-gather.6
  175.1 58.4 all-gather.8
  235.5 30.3 all-gather.10

commit v5 on v4

--- a/solution.py
+++ b/solution.py
@@ -16,7 +16,7 @@
 ROWS = 32
 QUARTER = D // NY
 EIGHTH = QUARTER // 2
-PACK = (8 * ROWS, 3 * HD, 4 * HD, HD)
+PACK = (8 * ROWS, 3 * HD, HD)
 VMEM_LIMIT = 48 * 1024 * 1024
 
 VM = pl.BlockSpec(memory_space=pltpu.VMEM)
@@ -53,14 +53,14 @@
 
 def qkv_first_kernel(idx, later, mods, w_t, *refs):
     mine, other = refs[0:3], refs[3:6]
-    out, wq, wo0, wo1, h, x, own, sems = refs[6:]
+    out, wq, wo1, h, x, own, sems = refs[6:]
     core, y = idx[1], idx[3]
     copies = []
     row = 0
-    for n, (rows, target) in enumerate(zip(PACK, (x, wq, wo0, wo1))):
+    for n, (rows, target) in enumerate(zip(PACK, (x, wq, wo1))):
         copies.append(pltpu.make_async_copy(later.at[:, row : row + rows, :], target, sems.at[n]))
         row += rows
-    copies.insert(1, pltpu.make_async_copy(w_t.at[0], own, sems.at[4]))
+    copies.insert(1, pltpu.make_async_copy(w_t.at[0], own, sems.at[3]))
     for copy in copies:
         copy.start()
     copies[0].wait()
@@ -96,12 +96,12 @@
         out_shape=[jax.ShapeDtypeStruct((NY, 3 * HD, NZ * ROWS), BF)]
         + [jax.ShapeDtypeStruct((NZ, rows, EIGHTH), BF) for rows in PACK[1:]],
         in_specs=[SM, anywhere, VM, anywhere] + [VM] * 6,
-        out_specs=[VM] + [anywhere] * 3,
+        out_specs=[VM] * 3,
         scratch_shapes=[
             pltpu.VMEM((NY, NZ, ROWS, QUARTER), BF),
             pltpu.VMEM((NZ, PACK[0], EIGHTH), BF),
             pltpu.VMEM((3 * HD, D), BF),
-            pltpu.SemaphoreType.DMA((5,)),
+            pltpu.SemaphoreType.DMA((4,)),
         ],
         compiler_params=params(),
         cost_estimate=pl.CostEstimate(flops=1_200_000_000, bytes_accessed=14_000_000, transcendentals=0),
@@ -109,43 +109,49 @@
     )(idx, later, mods, w_t, *mine, *other)
 
 
-def qkv_second_kernel(idx, x0, x1, x2, x3, mods, weight, out, h):
-    y = idx[3]
-
-    @pl.when(pl.program_id(0) == 0)
+def qkv_second_kernel(idx, x0, x1, x2, x3, mods, *refs):
+    weights, (out, h) = refs[:10], refs[10:]
+    x_pos, core, y = idx[0], idx[1], idx[3]
+    step = pl.program_id(0)
+
+    @pl.when(step == 0)
     def _():
         for j, x in enumerate((x0, x1, x2, x3)):
             (norm,) = normalized([x[...].astype(F32)])
             at = lax.rem(y + j, NY)
-            for b in range(NY):
-                cols = slice(b * QUARTER, (b + 1) * QUARTER)
+            for e in range(8):
+                cols = slice(e * EIGHTH, (e + 1) * EIGHTH)
                 part = norm[:, cols] * (1.0 + mods[4:5, cols]) + mods[3:4, cols]
-                h[b, at] = part.astype(BF)
+                h[e, at] = part.astype(BF)
 
     total = None
-    for b in range(NY):
-        w = jnp.concatenate([weight[2 * b, 0], weight[2 * b + 1, 0]], axis=1)
-        term = times(w, h[b].reshape(NY * ROWS, QUARTER))
-        total = term if total is None else total + term
+    for n in range(2):
+        side = core if n == 0 else 1 - core
+        group = [w[0] for w in weights[5 * n : 5 * n + 5]]
+        group[3:] = [jnp.where(step < NZ // 2, group[3], group[4])]
+        for k, weight in zip((0, 1, 3, 2), group):
+            tokens = h[lax.rem(x_pos + k, NX) * NC + side].reshape(NY * ROWS, EIGHTH)
+            term = times(weight, tokens)
+            total = term if total is None else total + term
     store_head(out.at[0], total)
 
 
-def qkv_second(idx, shards, mods, weight):
+def qkv_second(idx, shards, mods, weights):
+    half = NZ // 2
     shard = pl.BlockSpec((ROWS, D), lambda i: (0, 0))
+    head = lambda at: pl.BlockSpec((1, 3 * HD, EIGHTH), lambda i: (at(i), 0, 0))
+    heads = [head(lambda i: i)] * 3 + [head(lambda i: jnp.minimum(i, half - 1)), head(lambda i: jnp.maximum(i - half, 0))]
     return pl.pallas_call(
         qkv_second_kernel,
         grid=(NZ,),
         out_shape=jax.ShapeDtypeStruct((NZ, 3 * HD, NY * ROWS), BF),
-        in_specs=[SM]
-        + [shard] * 4
-        + [pl.BlockSpec((6, D), lambda i: (0, 0))]
-        + [pl.BlockSpec((8, 1, 3 * HD, EIGHTH), lambda i: (0, i, 0, 0))],
+        in_specs=[SM] + [shard] * 4 + [pl.BlockSpec((6, D), lambda i: (0, 0))] + heads * 2,
         out_specs=pl.BlockSpec((1, 3 * HD, NY * ROWS), lambda i: (i, 0, 0)),
-        scratch_shapes=[pltpu.VMEM((NY, NY, ROWS, QUARTER), BF)],
+        scratch_shapes=[pltpu.VMEM((8, NY, ROWS, EIGHTH), BF)],
         compiler_params=params(),
         cost_estimate=pl.CostEstimate(flops=1_200_000_000, bytes_accessed=10_500_000, transcendentals=0),
         name="qkv_second",
-    )(idx, *shards, mods, weight)
+    )(idx, *shards, mods, *weights)
 
 
 def attention_kernel(groups, idx, own, lower, upper, gain, out, acc, den, queries):
@@ -218,7 +224,7 @@
             pltpu.VMEM((4, HD, 256), BF),
         ],
         compiler_params=params(),
-        cost_estimate=pl.CostEstimate(flops=3_000_000_000, bytes_accessed=1_200_000, transcendentals=3_000_000),
+        cost_estimate=pl.CostEstimate(flops=0, bytes_accessed=1_200_000, transcendentals=0),
         name="attention_%d" % groups,
     )(idx, own, lower, upper, gain)
 
@@ -238,7 +244,7 @@
     if halves:
         for weight, side in zip(weights, (idx[1], 1 - idx[1])):
             for e in range(4):
-                w = weight[:, e * HD : (e + 1) * HD, :].reshape(NZ * HD, EIGHTH)
+                w = weight[:, :, e * EIGHTH : (e + 1) * EIGHTH].reshape(NZ * HD, EIGHTH)
                 put(w, 4 * side + e)
     else:
         for s in range(NX * NC):
@@ -312,27 +318,30 @@
     mine = [from_ahead(half, "y", NY, j) for j in range(1, NY)]
     other = [swap(m) for m in mine]
 
-    def split(w, parts):
-        return jnp.transpose(w.reshape(-1, parts, EIGHTH), (1, 0, 2)).reshape(-1, EIGHTH)
-
     def eighth(w):
         return lax.dynamic_slice_in_dim(w, slot * EIGHTH, EIGHTH, 1)
 
+    tokens = jnp.transpose(x0.reshape(ROWS, 8, EIGHTH), (1, 0, 2)).reshape(8 * ROWS, EIGHTH)
+    pack = jnp.concatenate([tokens, eighth(w_t[1]), eighth(w_out[1])], axis=0)
+    later = lax.all_gather(pack, "z", axis=0, tiled=False)
     wo_half = lax.dynamic_slice_in_dim(w_out[0], core * (D // 2), D // 2, 1)
-    pack = jnp.concatenate([split(x0, 8), eighth(w_t[1]), split(wo_half, 4), eighth(w_out[1])], axis=0)
-    later = lax.all_gather(pack, "z", axis=0, tiled=False)
+    wo0 = lax.all_gather(wo_half, "z", axis=0, tiled=False)
 
     def attend(own, layer):
         lower = shifted(own, ("x", "core"), 1)
         upper = shifted(own, ("x", "core"), -1)
         return attention(idx, own, lower, upper, gains[layer : layer + 1])
 
-    heads, wq1, wo0, wo1 = qkv_first(idx, later, mods, w_t, mine, other)
-    wq1 = lax.all_gather(wq1, ("x", "core"), axis=0, tiled=False)
+    heads, wq1, wo1 = qkv_first(idx, later, mods, w_t, mine, other)
+    ahead, behind = from_ahead(wq1, "x", NX, 1), from_ahead(wq1, "x", NX, 3)
     own = lax.all_to_all(heads, "y", 0, 0, tiled=True)
-    own, wo0, wo1 = lax.optimization_barrier((own, wo0, wo1))
+    own, wo1 = lax.optimization_barrier((own, wo1))
     wo1 = lax.all_gather(wo1, ("x", "core"), axis=0, tiled=False)
-    done = lax.all_to_all(attend(own, 0), "z", 0, 0, tiled=True)
+    done, wo0, ahead, behind = lax.optimization_barrier((attend(own, 0), wo0, ahead, behind))
+    far = [from_ahead(ahead[: NZ // 2], "x", NX, 1), from_ahead(behind[NZ // 2 :], "x", NX, 3)]
+    done = lax.all_to_all(done, "z", 0, 0, tiled=True)
+    done, *wq1 = lax.optimization_barrier((done, wq1, ahead, behind, *far))
+    wq1 = wq1 + [swap(w) for w in wq1]
     terms = lax.all_to_all(project(0, idx, done, [wo0, swap(wo0)]), "y", 0, 0, tiled=True)
     x1 = residual(0, terms, mods, x0)
 

time: 365 us -> 285 us (0.78); the launches traced: 358 us -> 284 us
  Pallas kernels: 129 us -> 37.4 us
  blocking collectives: 57.3 us -> 75 us
  waiting for transfers between devices: 113 us -> 106 us
  local copies, waits for them, and re-layouts: 5.74 us -> 12.3 us
    pallas_call x1, Pallas kernels: 97.5 us -> 7.01 us  [qkv_first(): pl.pallas_call(qkv_first_kernel, out_shape=[jax.ShapeDtypeStruct((NY, 3 *...]
    all_gather x1, waiting for transfers between devices: 28.5 us -> 11.7 us  [per_device(): later = lax.all_gather(pack, 'z', axis=0, tiled=False)]
    ppermute x5, waiting for transfers between devices: 26.8 us -> 41.9 us  [shifted(): return lax.ppermute(block, axis, route)]
    all_to_all x1 -> x2, blocking collectives: 13.8 us -> 25.7 us  [the longest x1 13.7 us: per_device(): done = lax.all_to_all(done, 'z', 0, 0, tiled=True)]
    all_to_all x1 -> x0, waiting for transfers between devices: 8.97 us -> none  [per_device(): done = lax.all_to_all(attend(own, 1), 'z', 0, 0, tiled=True)]
    ppermute x6 -> x10, waiting for transfers between devices: 35.4 us -> 40.3 us  [from_ahead(): lax.ppermute(block, axis, [(i, (i - distance) % size) for i in range(size)])]
    unnamed x15 -> x25, local copies, waits for them, and re-layouts: 2.46 us -> 7.17 us
    all_to_all x1, blocking collectives: 17.5 us -> 21.3 us  [per_device(): own = lax.all_to_all(heads, 'z', 0, 0, tiled=True)]
  transfers between devices with their start and end apart: 20 -> 28, of which waited for: 13 -> 12; matrix products, arithmetic and copies ran while one was open for 0% -> 1% of each run, Pallas kernels for 8% -> 12%
where the time goes in v5:
time: 285 us; the launch traced here: 284 us
  waiting for transfers between devices  106 us (37%)
  blocking collectives  75 us (26%)
  Pallas kernels  37.4 us (13%)
  starting transfers between devices  31.2 us (11%)
  between operations  16 us (6%)
  local copies, waits for them, and re-layouts  12.3 us (4%)
  other arithmetic  5.62 us (2%)
    ppermute x5, waiting for transfers between devices, shifted(): return lax.ppermute(block, axis, route)  41.9 us
    ppermute x10, waiting for transfers between devices, from_ahead(): lax.ppermute(block, axis, [(i, (i - distance) % size) for i in range(size)])  40.3 us
    all_to_all x1, blocking collectives, per_device(): own = lax.all_to_all(heads, 'z', 0, 0, tiled=True)  21.3 us
    pallas_call x2, Pallas kernels, attention(): pl.pallas_call(functools.partial(attention_kernel, groups), out_shape=jax...  17.4 us
    all_to_all x1, blocking collectives, per_device(): terms = lax.all_to_all(project(1, idx, done, [wo1]), 'y', 0, 0, tiled=True)  16 us
    all_to_all x1, blocking collectives, per_device(): done = lax.all_to_all(done, 'z', 0, 0, tiled=True)  13.7 us
    ppermute x5, starting transfers between devices, shifted(): return lax.ppermute(block, axis, route)  13 us
    all_to_all x1, waiting for transfers between devices, per_device(): lax.all_to_all(project(0, idx, done, [wo0, swap(wo0)]), 'y', 0, 0, tiled=...  12.2 us
  transfers between devices with their start and end apart: 28, of which 12 were waited for; matrix products, arithmetic and copies ran while one was open for 1% of the time, Pallas kernels for 12%

profile of v5, /device:TPU:4, one launch (start us, length us, event | category | flops | bytes accessed | tf_op | source)
XLA Modules:
  0.0 283.8 jit_solution(5997832024351132697)
XLA Ops:
  7.2 1.9 fusion.3
  12.2 1.5 fusion.2
  13.8 0.8 pad_maximum_fusion
  15.5 3.1 %collective-permute-start = (bf16[192,1536]{1,0:T(8,128)(2,1)S(1)}, bf16[192,1536]{1,0:T(8,128)(2,1)S(1)}, u32[]{:S(2)}, u32[]{:S(2)}) collective-permute-start(bf16[192,1536]{1,0:T(8,128)(2,1)S(1)} %dynamic-slice_bitcast_fusion), channel_id=1, source_target_pairs={{0,3},{1,0},{2,1},{3,2},{4,7},{5,4},{6,5},{7,6},{8,11},{9,8},{10,9... | collective-permute-start | bytes 1769480 | tf_op jit(solution)/shard_map/ppermute | solution.py:286
  19.2 1.0 collective-permute-start.2
  20.2 23.6 %collective-permute-done.refs_0_ = bf16[192,1536]{1,0:T(8,128)(2,1)S(1)} collective-permute-done((bf16[192,1536]{1,0:T(8,128)(2,1)S(1)}, bf16[192,1536]{1,0:T(8,128)(2,1)S(1)}, u32[]{:S(2)}, u32[]{:S(2)}) %collective-permute-start) | collective-permute-done | bytes 589856 | tf_op jit(solution)/shard_map/ppermute | solution.py:286
  44.4 3.2 %collective-permute-done.2.refs_2_ = bf16[192,1536]{1,0:T(8,128)(2,1)S(1)} collective-permute-done((bf16[192,1536]{1,0:T(8,128)(2,1)S(1)}, bf16[192,1536]{1,0:T(8,128)(2,1)S(1)}, u32[]{:S(2)}, u32[]{:S(2)}) %collective-permute-start.2) | collective-permute-done | bytes 589856 | tf_op jit(solution)/shard_map/ppermute | solution.py:286
  48.3 0.8 dynamic-slice_convert_fusion
  49.3 0.8 copy-done.3
  50.1 0.8 copy-done.5
  51.0 11.7 %all-gather.8.cloned.1.call-done = bf16[4096,384]{1,0:T(8,128)(2,1)} async-done(((bf16[512,384]{1,0:T(8,128)(2,1)}), bf16[4096,384]{1,0:T(8,128)(2,1)}) %all-gather.8.cloned.1.call-update) | async-done | bytes 3145744 | tf_op jit(solution)/shard_map/all_gather | solution.py:326
  62.7 1.1 copy-done.4
  63.8 1.1 copy-done.6
  64.8 7.0 %qkv_first.1 = (bf16[4,192,256]{2,1,0:T(8,128)(2,1)S(1)}, bf16[8,192,384]{2,1,0:T(8,128)(2,1)S(1)}, bf16[8,64,384]{2,1,0:T(8,128)(2,1)}) custom-call(s32[4]{0:T(128)S(1)} %pad_add_fusion.idx, bf16[8,512,384]{2,1,0:T(8,128)(2,1)} %bitcast.46, f32[6,3072]{1,0:T(8,128)S(1)} %reshape.40.mods, bf16[2,192,3072]{2,1,0:T(8,128)(2,1)} %bitcast.45, ...), custom_call_target="tpu_custom_call" | custom-call | flops 1200000000 | bytes 14000000 | tf_op jit(solution)/shard_map/qkv_first/pallas_call | solution.py:94
  71.9 11.9 %all_to_all.30.own = bf16[4,192,256]{2,1,0:T(8,128)(2,1)S(1)} all-to-all(bf16[4,192,256]{2,1,0:T(8,128)(2,1)S(1)} %get-tuple-element.17), channel_id=1, replica_groups=mesh['x'=4,'core'=2,'z'=8,'y'=4] {'y'}, dimensions={0} | all-to-all | bytes 786432 | tf_op jit(solution)/shard_map/all_to_all | solution.py:337
  84.5 1.5 collective-permute-start.9
  85.9 1.9 collective-permute-start.6
  87.8 3.6 %collective-permute-start.7 = (bf16[4,192,256]{2,1,0:T(8,128)(2,1)S(1)}, bf16[4,192,256]{2,1,0:T(8,128)(2,1)S(1)}, u32[]{:S(2)}, u32[]{:S(2)}) collective-permute-start(bf16[4,192,256]{2,1,0:T(8,128)(2,1)S(1)} %all_to_all.30.own), channel_id=1, source_target_pairs={{32,0},{64,32},{96,64},{128,96},{160,128},{192,160},{224,192},{33,... | collective-permute-start | bytes 1179656 | tf_op jit(solution)/shard_map/ppermute | solution.py:296
  91.5 23.1 %collective-permute-done.6.lower = bf16[4,192,256]{2,1,0:T(8,128)(2,1)S(1)} collective-permute-done((bf16[4,192,256]{2,1,0:T(8,128)(2,1)S(1)}, bf16[4,192,256]{2,1,0:T(8,128)(2,1)S(1)}, u32[]{:S(2)}, u32[]{:S(2)}) %collective-permute-start.6) | collective-permute-done | bytes 393248 | tf_op jit(solution)/shard_map/ppermute | solution.py:296
  114.7 8.8 %attention_4.1 = bf16[8,64,128]{2,1,0:T(8,128)(2,1)S(1)} custom-call(s32[4]{0:T(128)S(1)} %pad_add_fusion.idx, bf16[4,192,256]{2,1,0:T(8,128)(2,1)S(1)} %all_to_all.30.own, bf16[4,192,256]{2,1,0:T(8,128)(2,1)S(1)} %collective-permute-done.6.lower, bf16[4,192,256]{2,1,0:T(8,128)(2,1)S(1)} %collective-permute-done.7.upper, f32[1,128]{1,0:T(1,128)S(1)} %get-tuple-element.39.gain), custom_call_target="tpu_custom_call" | custom-call | bytes 1200000 | tf_op jit(solution)/shard_map/attention_4/pallas_call | solution.py:216
  123.7 1.7 collective-permute-start.10
  125.5 1.1 slice.45
  127.2 13.7 %all_to_all.31.o = bf16[8,64,128]{2,1,0:T(8,128)(2,1)S(1)} all-to-all(bf16[8,64,128]{2,1,0:T(8,128)(2,1)S(1)} %attention_4.1), channel_id=1, replica_groups=mesh['x'=4,'core'=2,'z'=8,'y'=4] {'z'}, dimensions={0} | all-to-all | bytes 262144 | tf_op jit(solution)/shard_map/all_to_all | solution.py:342
  140.9 3.4 %collective-permute-done.10.refs_3_ = bf16[4,192,384]{2,1,0:T(8,128)(2,1)} collective-permute-done((bf16[4,192,384]{2,1,0:T(8,128)(2,1)S(1)}, bf16[4,192,384]{2,1,0:T(8,128)(2,1)}, u32[]{:S(2)}, u32[]{:S(2)}) %collective-permute-start.10) | collective-permute-done | bytes 589856 | tf_op jit(solution)/shard_map/ppermute | solution.py:286
  145.3 2.2 project_0.1
  147.5 4.4 %all-to-all-start.2 = ((bf16[4,32,3072]{2,1,0:T(8,128)(2,1)}), bf16[4,32,3072]{2,1,0:T(8,128)(2,1)S(1)}, u32[]{:S(2)}, u32[]{:S(2)}) async-start(bf16[4,32,3072]{2,1,0:T(8,128)(2,1)} %bitcast.17), calls=%async_computation.2 | async-start | bytes 1572864 | tf_op jit(solution)/shard_map/all_to_all | solution.py:345
  152.6 12.2 %all-to-all-done.2.terms = bf16[4,32,3072]{2,1,0:T(8,128)(2,1)S(1)} async-done(((bf16[4,32,3072]{2,1,0:T(8,128)(2,1)}), bf16[4,32,3072]{2,1,0:T(8,128)(2,1)S(1)}, u32[]{:S(2)}, u32[]{:S(2)}) %all-to-all-start.2) | async-done | bytes 786464 | tf_op jit(solution)/shard_map/all_to_all | solution.py:345
  164.9 0.9 copy-done.2
  166.0 1.2 collective-permute-start.13
  167.2 1.5 collective-permute-start.14
  168.7 5.2 %collective-permute-done.13.x1 = bf16[32,3072]{1,0:T(8,128)(2,1)S(1)} collective-permute-done((bf16[32,3072]{1,0:T(8,128)(2,1)S(1)}, bf16[32,3072]{1,0:T(8,128)(2,1)S(1)}, u32[]{:S(2)}, u32[]{:S(2)}) %collective-permute-start.13) | collective-permute-done | bytes 196640 | tf_op jit(solution)/shard_map/ppermute | solution.py:286
  173.9 2.7 collective-permute-done.14.x2
  176.6 2.3 collective-permute-done.15.x3
  178.9 8.5 %qkv_second.1 = bf16[8,192,128]{2,1,0:T(8,128)(2,1)S(1)} custom-call(s32[4]{0:T(128)S(1)} %pad_add_fusion.idx, bf16[32,3072]{1,0:T(8,128)(2,1)S(1)} %residual_0.1.x0.x, bf16[32,3072]{1,0:T(8,128)(2,1)S(1)} %collective-permute-done.13.x1, bf16[32,3072]{1,0:T(8,128)(2,1)S(1)} %collective-permute-done.14.x2, bf16[32,3072]{1,0:T(8,128)(2,1)S(1)} %collective-permute-done.15.x3, ...), custom_call_target="tpu_custom_call" | custom-call | flops 1200000000 | bytes 10500000 | tf_op jit(solution)/shard_map/qkv_second/pallas_call | solution.py:144
  187.4 21.3 %all_to_all.32.own = bf16[8,192,128]{2,1,0:T(8,128)(2,1)S(1)} all-to-all(bf16[8,192,128]{2,1,0:T(8,128)(2,1)S(1)} %qkv_second.1), channel_id=1, replica_groups=mesh['x'=4,'core'=2,'z'=8,'y'=4] {'z'}, dimensions={0} | all-to-all | bytes 786432 | tf_op jit(solution)/shard_map/all_to_all | solution.py:350
  208.8 1.9 collective-permute-start.21
  210.7 3.6 %collective-permute-start.22 = (bf16[8,192,128]{2,1,0:T(8,128)(2,1)S(1)}, bf16[8,192,128]{2,1,0:T(8,128)(2,1)S(1)}, u32[]{:S(2)}, u32[]{:S(2)}) collective-permute-start(bf16[8,192,128]{2,1,0:T(8,128)(2,1)S(1)} %all_to_all.32.own), channel_id=1, source_target_pairs={{32,0},{64,32},{96,64},{128,96},{160,128},{192,160},{224,192},{33,... | collective-permute-start | bytes 1179656 | tf_op jit(solution)/shard_map/ppermute | solution.py:296
  214.3 3.5 %collective-permute-done.21.lower = bf16[8,192,128]{2,1,0:T(8,128)(2,1)S(1)} collective-permute-done((bf16[8,192,128]{2,1,0:T(8,128)(2,1)S(1)}, bf16[8,192,128]{2,1,0:T(8,128)(2,1)S(1)}, u32[]{:S(2)}, u32[]{:S(2)}) %collective-permute-start.21) | collective-permute-done | bytes 393248 | tf_op jit(solution)/shard_map/ppermute | solution.py:296
  217.8 1.8 collective-permute-done.22.upper
  219.6 8.6 %attention_8.1 = bf16[8,64,128]{2,1,0:T(8,128)(2,1)S(1)} custom-call(s32[4]{0:T(128)S(1)} %pad_add_fusion.idx, bf16[8,192,128]{2,1,0:T(8,128)(2,1)S(1)} %all_to_all.32.own, bf16[8,192,128]{2,1,0:T(8,128)(2,1)S(1)} %collective-permute-done.21.lower, bf16[8,192,128]{2,1,0:T(8,128)(2,1)S(1)} %collective-permute-done.22.upper, f32[1,128]{1,0:T(1,128)S(1)} %get-tuple-element.38.gain), custom_call_target="tpu_custom_call" | custom-call | bytes 1200000 | tf_op jit(solution)/shard_map/attention_8/pallas_call | solution.py:216
  228.2 12.0 %all_to_all.33.o = bf16[8,64,128]{2,1,0:T(8,128)(2,1)S(1)} all-to-all(bf16[8,64,128]{2,1,0:T(8,128)(2,1)S(1)} %attention_8.1), channel_id=1, replica_groups=mesh['x'=4,'core'=2,'z'=8,'y'=4] {'z'}, dimensions={0} | all-to-all | bytes 262144 | tf_op jit(solution)/shard_map/all_to_all | solution.py:351
  240.3 1.9 copy-done
  242.1 1.3 project_1.1
  243.4 16.0 %all_to_all.34.terms = bf16[4,32,3072]{2,1,0:T(8,128)(2,1)S(1)} all-to-all(bf16[4,32,3072]{2,1,0:T(8,128)(2,1)S(1)} %bitcast.42), channel_id=1, replica_groups=mesh['x'=4,'core'=2,'z'=8,'y'=4] {'y'}, dimensions={0} | all-to-all | bytes 1572864 | tf_op jit(solution)/shard_map/all_to_all | solution.py:352
  259.5 0.8 residual_1.1
  260.3 1.9 collective-permute-start.23
  262.2 13.4 %collective-permute-done.23 = bf16[32,3072]{1,0:T(8,128)(2,1)S(1)} collective-permute-done((bf16[32,3072]{1,0:T(8,128)(2,1)}, bf16[32,3072]{1,0:T(8,128)(2,1)S(1)}, u32[]{:S(2)}, u32[]{:S(2)}) %collective-permute-start.23) | collective-permute-done | bytes 196640 | tf_op jit(solution)/shard_map/ppermute | solution.py:296
  275.7 1.7 select_bitcast_fusion
  (71 shorter events, 7.6 us)
Async XLA Ops:
  7.2 55.5 %all-gather.8.cloned.1.call-start = ((), (), s32[]{:S(2)}) async-start(), calls=%async_computation.7 | async-start | bytes 3538944 | tf_op jit(solution)/shard_map/all_gather | solution.py:326
  7.2 1.9 copy-start.7
  9.1 0.7 copy-start.10
  9.1 4.6 %copy-start.8 = (bf16[1,32,3072]{2,1,0:T(8,128)(2,1)S(1)}, bf16[1,32,3072]{2,1,0:T(8,128)(2,1)}, u32[]{:S(2)}) copy-start(bf16[1,32,3072]{2,1,0:T(8,128)(2,1)} %param.9) | copy-start | bytes 589828
  14.6 108.9 %all-gather.6.cloned.1.call-start = ((), (), s32[]{:S(2)}) async-start(), calls=%async_computation.6 | async-start | bytes 1769472 | tf_op jit(solution)/shard_map/all_gather | solution.py:328
  15.4 224.8 %all-gather.10.cloned.1.call-start = ((), (), s32[]{:S(2)}) async-start(), calls=%async_computation.8 | async-start | bytes 3538944 | tf_op jit(solution)/shard_map/all_gather | solution.py:339
  15.5 28.3 %collective-permute-start = (bf16[192,1536]{1,0:T(8,128)(2,1)S(1)}, bf16[192,1536]{1,0:T(8,128)(2,1)S(1)}, u32[]{:S(2)}, u32[]{:S(2)}) collective-permute-start(bf16[192,1536]{1,0:T(8,128)(2,1)S(1)} %dynamic-slice_bitcast_fusion), channel_id=1, source_target_pairs={{0,3},{1,0},{2,1},{3,2},{4,7},{5,4},{6,5},{7,6},{8,11},{9,8},{10,9... | collective-permute-start | bytes 1769480 | tf_op jit(solution)/shard_map/ppermute | solution.py:286
  18.6 25.2 %collective-permute-start.1 = (bf16[192,1536]{1,0:T(8,128)(2,1)S(1)}, bf16[192,1536]{1,0:T(8,128)(2,1)S(1)}, u32[]{:S(2)}, u32[]{:S(2)}) collective-permute-start(bf16[192,1536]{1,0:T(8,128)(2,1)S(1)} %dynamic-slice_bitcast_fusion), channel_id=1, source_target_pairs={{0,2},{1,3},{2,0},{3,1},{4,6},{5,7},{6,4},{7,5},{8,10},{9,11},{10,... | collective-permute-start | bytes 1769480 | tf_op jit(solution)/shard_map/ppermute | solution.py:286
  19.2 28.3 %collective-permute-start.2 = (bf16[192,1536]{1,0:T(8,128)(2,1)S(1)}, bf16[192,1536]{1,0:T(8,128)(2,1)S(1)}, u32[]{:S(2)}, u32[]{:S(2)}) collective-permute-start(bf16[192,1536]{1,0:T(8,128)(2,1)S(1)} %dynamic-slice_bitcast_fusion), channel_id=1, source_target_pairs={{0,1},{1,2},{2,3},{3,0},{4,5},{5,6},{6,7},{7,4},{8,9},{9,10},{10,1... | collective-permute-start | bytes 1769480 | tf_op jit(solution)/shard_map/ppermute | solution.py:286
  43.8 5.5 %collective-permute-start.3 = (bf16[192,1536]{1,0:T(8,128)(2,1)S(1)}, bf16[192,1536]{1,0:T(8,128)(2,1)S(1)}, u32[]{:S(2)}, u32[]{:S(2)}) collective-permute-start(bf16[192,1536]{1,0:T(8,128)(2,1)S(1)} %collective-permute-done.refs_0_), channel_id=1, source_target_pairs={{0,32},{32,0},{1,33},{33,1},{2,34},{34,2},{3,35},{35,3},{4,36},{36... | collective-permute-start | bytes 1769480 | tf_op jit(solution)/shard_map/ppermute | solution.py:290
  43.8 6.3 %collective-permute-start.4 = (bf16[192,1536]{1,0:T(8,128)(2,1)S(1)}, bf16[192,1536]{1,0:T(8,128)(2,1)S(1)}, u32[]{:S(2)}, u32[]{:S(2)}) collective-permute-start(bf16[192,1536]{1,0:T(8,128)(2,1)S(1)} %collective-permute-done.1.refs_1_), channel_id=1, source_target_pairs={{0,32},{32,0},{1,33},{33,1},{2,34},{34,2},{3,35},{35,3},{4,36},{36... | collective-permute-start | bytes 1769480 | tf_op jit(solution)/shard_map/ppermute | solution.py:290
  47.5 3.4 %collective-permute-start.5 = (bf16[192,1536]{1,0:T(8,128)(2,1)S(1)}, bf16[192,1536]{1,0:T(8,128)(2,1)}, u32[]{:S(2)}, u32[]{:S(2)}) collective-permute-start(bf16[192,1536]{1,0:T(8,128)(2,1)S(1)} %collective-permute-done.2.refs_2_), channel_id=1, source_target_pairs={{0,32},{32,0},{1,33},{33,1},{2,34},{34,2},{3,35},{35,3},{4,36},{36... | collective-permute-start | bytes 1769480 | tf_op jit(solution)/shard_map/ppermute | solution.py:290
  49.3 0.8 copy-start.3
  50.1 0.8 copy-start.5
  62.7 1.1 copy-start.4
  63.8 1.1 copy-start.6
  71.9 19.6 %copy-start.11 = (bf16[2,1,128]{2,0,1:T(2,128)(2,1)S(1)}, bf16[2,1,128]{2,0,1:T(2,128)(2,1)}, u32[]{:S(2)}) copy-start(bf16[2,1,128]{2,0,1:T(2,128)(2,1)} %param.16) | copy-start | bytes 1540
  83.8 39.7 %collective-permute-start.8 = (bf16[8,192,384]{2,1,0:T(8,128)(2,1)S(1)}, bf16[8,192,384]{2,1,0:T(8,128)(2,1)S(1)}, u32[]{:S(2)}, u32[]{:S(2)}) collective-permute-start(bf16[8,192,384]{2,1,0:T(8,128)(2,1)S(1)} %get-tuple-element.26.refs_0_), channel_id=1, source_target_pairs={{0,192},{64,0},{128,64},{192,128},{1,193},{65,1},{129,65},{193,129... | collective-permute-start | bytes 3538952 | tf_op jit(solution)/shard_map/ppermute | solution.py:286
  84.5 39.1 %collective-permute-start.9 = (bf16[8,192,384]{2,1,0:T(8,128)(2,1)S(1)}, bf16[8,192,384]{2,1,0:T(8,128)(2,1)}, u32[]{:S(2)}, u32[]{:S(2)}) collective-permute-start(bf16[8,192,384]{2,1,0:T(8,128)(2,1)S(1)} %get-tuple-element.26.refs_0_), channel_id=1, source_target_pairs={{0,64},{64,128},{128,192},{192,0},{1,65},{65,129},{129,193},{193,1... | collective-permute-start | bytes 3538952 | tf_op jit(solution)/shard_map/ppermute | solution.py:286
  85.9 28.7 %collective-permute-start.6 = (bf16[4,192,256]{2,1,0:T(8,128)(2,1)S(1)}, bf16[4,192,256]{2,1,0:T(8,128)(2,1)S(1)}, u32[]{:S(2)}, u32[]{:S(2)}) collective-permute-start(bf16[4,192,256]{2,1,0:T(8,128)(2,1)S(1)} %all_to_all.30.own), channel_id=1, source_target_pairs={{0,32},{32,64},{64,96},{96,128},{128,160},{160,192},{192,224},{1,3... | collective-permute-start | bytes 1179656 | tf_op jit(solution)/shard_map/ppermute | solution.py:296
  87.8 26.8 %collective-permute-start.7 = (bf16[4,192,256]{2,1,0:T(8,128)(2,1)S(1)}, bf16[4,192,256]{2,1,0:T(8,128)(2,1)S(1)}, u32[]{:S(2)}, u32[]{:S(2)}) collective-permute-start(bf16[4,192,256]{2,1,0:T(8,128)(2,1)S(1)} %all_to_all.30.own), channel_id=1, source_target_pairs={{32,0},{64,32},{96,64},{128,96},{160,128},{192,160},{224,192},{33,... | collective-permute-start | bytes 1179656 | tf_op jit(solution)/shard_map/ppermute | solution.py:296
  123.5 21.8 %copy-start.1 = (bf16[8,64,1536]{2,1,0:T(8,128)(2,1)S(1)}, bf16[8,64,1536]{2,1,0:T(8,128)(2,1)}, u32[]{:S(2)}) copy-start(bf16[8,64,1536]{2,1,0:T(8,128)(2,1)} %all-gather.6.cloned.1.call-done.refs_0_) | copy-start | bytes 4718596
  123.6 21.8 %collective-permute-start.12 = (bf16[8,64,1536]{2,1,0:T(8,128)(2,1)}, bf16[8,64,1536]{2,1,0:T(8,128)(2,1)S(1)}, u32[]{:S(2)}, u32[]{:S(2)}) collective-permute-start(bf16[8,64,1536]{2,1,0:T(8,128)(2,1)} %all-gather.6.cloned.1.call-done.refs_0_), channel_id=1, source_target_pairs={{0,32},{32,0},{1,33},{33,1},{2,34},{34,2},{3,35},{35,3},{4,36},{36... | collective-permute-start | bytes 4718600 | tf_op jit(solution)/shard_map/ppermute | solution.py:290
  123.7 20.6 %collective-permute-start.10 = (bf16[4,192,384]{2,1,0:T(8,128)(2,1)S(1)}, bf16[4,192,384]{2,1,0:T(8,128)(2,1)}, u32[]{:S(2)}, u32[]{:S(2)}) collective-permute-start(bf16[4,192,384]{2,1,0:T(8,128)(2,1)S(1)} %slice.44), channel_id=1, source_target_pairs={{0,192},{64,0},{128,64},{192,128},{1,193},{65,1},{129,65},{193,129... | collective-permute-start | bytes 1769480 | tf_op jit(solution)/shard_map/ppermute | solution.py:286
  126.6 17.7 %collective-permute-start.11 = (bf16[4,192,384]{2,1,0:T(8,128)(2,1)S(1)}, bf16[4,192,384]{2,1,0:T(8,128)(2,1)}, u32[]{:S(2)}, u32[]{:S(2)}) collective-permute-start(bf16[4,192,384]{2,1,0:T(8,128)(2,1)S(1)} %slice.45), channel_id=1, source_target_pairs={{0,64},{64,128},{128,192},{192,0},{1,65},{65,129},{129,193},{193,1... | collective-permute-start | bytes 1769480 | tf_op jit(solution)/shard_map/ppermute | solution.py:286
  144.3 24.4 %collective-permute-start.16 = (bf16[8,192,384]{2,1,0:T(8,128)(2,1)S(1)}, bf16[8,192,384]{2,1,0:T(8,128)(2,1)}, u32[]{:S(2)}, u32[]{:S(2)}) collective-permute-start(bf16[8,192,384]{2,1,0:T(8,128)(2,1)S(1)} %get-tuple-element.26.refs_0_), channel_id=1, source_target_pairs={{0,32},{32,0},{1,33},{33,1},{2,34},{34,2},{3,35},{35,3},{4,36},{36... | collective-permute-start | bytes 3538952 | tf_op jit(solution)/shard_map/ppermute | solution.py:290
  144.3 24.4 %collective-permute-start.17 = (bf16[8,192,384]{2,1,0:T(8,128)(2,1)S(1)}, bf16[8,192,384]{2,1,0:T(8,128)(2,1)}, u32[]{:S(2)}, u32[]{:S(2)}) collective-permute-start(bf16[8,192,384]{2,1,0:T(8,128)(2,1)S(1)} %collective-permute-done.8.refs_1_), channel_id=1, source_target_pairs={{0,32},{32,0},{1,33},{33,1},{2,34},{34,2},{3,35},{35,3},{4,36},{36... | collective-permute-start | bytes 3538952 | tf_op jit(solution)/shard_map/ppermute | solution.py:290
  144.8 23.9 %collective-permute-start.18 = (bf16[8,192,384]{2,1,0:T(8,128)(2,1)}, bf16[8,192,384]{2,1,0:T(8,128)(2,1)}, u32[]{:S(2)}, u32[]{:S(2)}) collective-permute-start(bf16[8,192,384]{2,1,0:T(8,128)(2,1)} %collective-permute-done.9.refs_2_), channel_id=1, source_target_pairs={{0,32},{32,0},{1,33},{33,1},{2,34},{34,2},{3,35},{35,3},{4,36},{36... | collective-permute-start | bytes 3538952 | tf_op jit(solution)/shard_map/ppermute | solution.py:290
  144.8 21.1 %collective-permute-start.19 = (bf16[4,192,384]{2,1,0:T(8,128)(2,1)}, bf16[4,192,384]{2,1,0:T(8,128)(2,1)}, u32[]{:S(2)}, u32[]{:S(2)}) collective-permute-start(bf16[4,192,384]{2,1,0:T(8,128)(2,1)} %collective-permute-done.10.refs_3_), channel_id=1, source_target_pairs={{0,32},{32,0},{1,33},{33,1},{2,34},{34,2},{3,35},{35,3},{4,36},{36... | collective-permute-start | bytes 1769480 | tf_op jit(solution)/shard_map/ppermute | solution.py:290
  145.3 21.9 %collective-permute-start.20 = (bf16[4,192,384]{2,1,0:T(8,128)(2,1)}, bf16[4,192,384]{2,1,0:T(8,128)(2,1)}, u32[]{:S(2)}, u32[]{:S(2)}) collective-permute-start(bf16[4,192,384]{2,1,0:T(8,128)(2,1)} %collective-permute-done.11.refs_4_), channel_id=1, source_target_pairs={{0,32},{32,0},{1,33},{33,1},{2,34},{34,2},{3,35},{35,3},{4,36},{36... | collective-permute-start | bytes 1769480 | tf_op jit(solution)/shard_map/ppermute | solution.py:290
  147.5 4.4 %copy-start.9 = (bf16[1,32,3072]{2,1,0:T(8,128)(2,1)S(1)}, bf16[1,32,3072]{2,1,0:T(8,128)(2,1)}, u32[]{:S(2)}) copy-start(bf16[1,32,3072]{2,1,0:T(8,128)(2,1)} %param.9) | copy-start | bytes 589828
  147.5 17.4 %all-to-all-start.2 = ((bf16[4,32,3072]{2,1,0:T(8,128)(2,1)}), bf16[4,32,3072]{2,1,0:T(8,128)(2,1)S(1)}, u32[]{:S(2)}, u32[]{:S(2)}) async-start(bf16[4,32,3072]{2,1,0:T(8,128)(2,1)} %bitcast.17), calls=%async_computation.2 | async-start | bytes 1572864 | tf_op jit(solution)/shard_map/all_to_all | solution.py:345
  164.9 0.9 copy-start.2
  166.0 7.9 %collective-permute-start.13 = (bf16[32,3072]{1,0:T(8,128)(2,1)S(1)}, bf16[32,3072]{1,0:T(8,128)(2,1)S(1)}, u32[]{:S(2)}, u32[]{:S(2)}) collective-permute-start(bf16[32,3072]{1,0:T(8,128)(2,1)S(1)} %residual_0.1.x0.x), channel_id=1, source_target_pairs={{0,3},{1,0},{2,1},{3,2},{4,7},{5,4},{6,5},{7,6},{8,11},{9,8},{10,9... | collective-permute-start | bytes 589832 | tf_op jit(solution)/shard_map/ppermute | solution.py:286
  167.2 9.3 %collective-permute-start.14 = (bf16[32,3072]{1,0:T(8,128)(2,1)S(1)}, bf16[32,3072]{1,0:T(8,128)(2,1)S(1)}, u32[]{:S(2)}, u32[]{:S(2)}) collective-permute-start(bf16[32,3072]{1,0:T(8,128)(2,1)S(1)} %residual_0.1.x0.x), channel_id=1, source_target_pairs={{0,2},{1,3},{2,0},{3,1},{4,6},{5,7},{6,4},{7,5},{8,10},{9,11},{10,... | collective-permute-start | bytes 589832 | tf_op jit(solution)/shard_map/ppermute | solution.py:286
  168.7 10.2 %collective-permute-start.15 = (bf16[32,3072]{1,0:T(8,128)(2,1)S(1)}, bf16[32,3072]{1,0:T(8,128)(2,1)S(1)}, u32[]{:S(2)}, u32[]{:S(2)}) collective-permute-start(bf16[32,3072]{1,0:T(8,128)(2,1)S(1)} %residual_0.1.x0.x), channel_id=1, source_target_pairs={{0,1},{1,2},{2,3},{3,0},{4,5},{5,6},{6,7},{7,4},{8,9},{9,10},{10,1... | collective-permute-start | bytes 589832 | tf_op jit(solution)/shard_map/ppermute | solution.py:286
  208.8 9.1 %collective-permute-start.21 = (bf16[8,192,128]{2,1,0:T(8,128)(2,1)S(1)}, bf16[8,192,128]{2,1,0:T(8,128)(2,1)S(1)}, u32[]{:S(2)}, u32[]{:S(2)}) collective-permute-start(bf16[8,192,128]{2,1,0:T(8,128)(2,1)S(1)} %all_to_all.32.own), channel_id=1, source_target_pairs={{0,32},{32,64},{64,96},{96,128},{128,160},{160,192},{192,224},{1,3... | collective-permute-start | bytes 1179656 | tf_op jit(solution)/shard_map/ppermute | solution.py:296
  210.7 8.9 %collective-permute-start.22 = (bf16[8,192,128]{2,1,0:T(8,128)(2,1)S(1)}, bf16[8,192,128]{2,1,0:T(8,128)(2,1)S(1)}, u32[]{:S(2)}, u32[]{:S(2)}) collective-permute-start(bf16[8,192,128]{2,1,0:T(8,128)(2,1)S(1)} %all_to_all.32.own), channel_id=1, source_target_pairs={{32,0},{64,32},{96,64},{128,96},{160,128},{192,160},{224,192},{33,... | collective-permute-start | bytes 1179656 | tf_op jit(solution)/shard_map/ppermute | solution.py:296
  240.3 1.9 copy-start
  260.3 15.4 %collective-permute-start.23 = (bf16[32,3072]{1,0:T(8,128)(2,1)}, bf16[32,3072]{1,0:T(8,128)(2,1)S(1)}, u32[]{:S(2)}, u32[]{:S(2)}) collective-permute-start(bf16[32,3072]{1,0:T(8,128)(2,1)} %residual_1.1), channel_id=1, source_target_pairs={{16,0},{17,1},{18,2},{19,3},{20,4},{21,5},{22,6},{23,7},{24,8},{25... | collective-permute-start | bytes 589832 | tf_op jit(solution)/shard_map/ppermute | solution.py:296
Sparse Core Ops, SparseCore 0:
  14.8 47.9 all-gather.7
  65.1 38.6 all-gather.5
  105.6 32.0 all-gather.9

commit v6 on v5

v6 whole, which is shorter than its diff:
```python
import functools

import jax
import jax.numpy as jnp
from jax import lax
from jax.experimental import pallas as pl
from jax.experimental.pallas import tpu as pltpu
from jax.sharding import Mesh, PartitionSpec as P

BF = jnp.bfloat16
F32 = jnp.float32
EPS = 1e-6
NX, NC, NZ, NY = 4, 2, 8, 4
D = 3072
NF = 16
HD = 64
ROWS = 32
SEQ = NZ * NY
QUARTER = D // NY
EIGHTH = QUARTER // 2
PACK = (8 * ROWS, 3 * HD)

VM = pl.BlockSpec(memory_space=pltpu.VMEM)
SM = pl.BlockSpec(memory_space=pltpu.SMEM)
HB = pl.BlockSpec(memory_space=pltpu.HBM)
ANY = pl.BlockSpec(memory_space=pl.ANY)


def params(mebibytes):
    return pltpu.CompilerParams(vmem_limit_bytes=mebibytes * 1024 * 1024)


def position():
    return [lax.axis_index(name) for name in ("x", "core", "z", "y")]


def in_hbm(array):
    return pltpu.with_memory_space_constraint(array, pltpu.HBM)


def normalized(blocks):
    mean = sum(jnp.sum(b, axis=-1, keepdims=True) for b in blocks) / D
    centers = [b - mean for b in blocks]
    spread = sum(jnp.sum(c * c, axis=-1, keepdims=True) for c in centers) / D
    inv = lax.rsqrt(spread + EPS)
    return [c * inv for c in centers]


def head_rows(value):
    center = value - jnp.mean(value, axis=0, keepdims=True)
    spread = jnp.mean(center * center, axis=0, keepdims=True)
    return center * lax.rsqrt(spread + EPS)


def store_head(out, result):
    out[0:HD, :] = head_rows(result[0:HD]).astype(BF)
    out[HD : 2 * HD, :] = head_rows(result[HD : 2 * HD]).astype(BF)
    out[2 * HD :, :] = result[2 * HD :].astype(BF)


def times(weight, h):
    return lax.dot_general(weight, h, (((1,), (1,)), ((), ())), preferred_element_type=F32)


def prepare_kernel(frame_pos, latent, pos, w_t, w_out, x0, pack, half, wo, x, table, sems):
    x_pos, core, z, _ = position()

    def columns(start, width):
        return pl.ds(pl.multiple_of(start, 128), width)

    eighth = columns((x_pos * NC + core) * EIGHTH, EIGHTH)
    copies = [
        (latent.at[0], x),
        (pos, table),
        (w_t.at[1, :, eighth], pack.at[PACK[0] :, :]),
        (w_t.at[0, :, columns(core * (D // 2), D // 2)], half),
    ]
    for e in range(4):
        part = columns((4 * core + e) * EIGHTH, EIGHTH)
        copies.append((w_out.at[0, :, part], wo.at[e * HD : (e + 1) * HD, :]))
    copies.append((w_out.at[1, :, eighth], wo.at[4 * HD :, :]))
    copies = [pltpu.make_async_copy(*pair, sems.at[n]) for n, pair in enumerate(copies)]
    for copy in copies:
        copy.start()
    frame = jnp.where(z >= NZ // 2, frame_pos[0, 1], frame_pos[0, 0])
    for copy in copies[:2]:
        copy.wait()
    chosen = lax.broadcasted_iota(jnp.int32, table.shape, 0) == frame
    row = jnp.sum(jnp.where(chosen, table[...].astype(F32), 0.0), axis=0, keepdims=True)
    value = (x[...].astype(F32) + row).astype(BF)
    x0[...] = value
    for e in range(8):
        pack[e * ROWS : (e + 1) * ROWS, :] = value[:, e * EIGHTH : (e + 1) * EIGHTH]
    for copy in copies[2:]:
        copy.wait()


def prepare(frame_pos, latent, pos, w_t, w_out):
    shapes = ((ROWS, D), (sum(PACK), EIGHTH), (3 * HD, D // 2), (5 * HD, EIGHTH))
    return pl.pallas_call(
        prepare_kernel,
        out_shape=[jax.ShapeDtypeStruct(shape, BF) for shape in shapes],
        in_specs=[SM] + [HB] * 4,
        out_specs=[VM] * 4,
        scratch_shapes=[
            pltpu.VMEM((ROWS, D), BF),
            pltpu.VMEM((NF, D), BF),
            pltpu.SemaphoreType.DMA((9,)),
        ],
        compiler_params=params(8),
        cost_estimate=pl.CostEstimate(flops=300_000, bytes_accessed=2_500_000, transcendentals=0),
        name="prepare",
    )(frame_pos, *map(in_hbm, (latent, pos, w_t, w_out)))


def qkv_first_kernel(later, mods, w_t, *refs):
    mine, other = refs[0:3], refs[3:6]
    out, wq_low, wq_high, h, x, own, held, sems = refs[6:]
    _, core, _, y = position()
    first = pl.ds(PACK[0], PACK[1])
    copies = [
        pltpu.make_async_copy(later.at[:, : PACK[0], :], x, sems.at[0]),
        pltpu.make_async_copy(w_t.at[0], own, sems.at[1]),
        pltpu.make_async_copy(later.at[:, first, :], held, sems.at[2]),
        pltpu.make_async_copy(held.at[: NZ // 2], wq_low, sems.at[3]),
        pltpu.make_async_copy(held.at[NZ // 2 :], wq_high, sems.at[4]),
    ]
    for copy in copies[:3]:
        copy.start()
    copies[0].wait()
    for z in range(NZ):
        blocks = [x[z, e * ROWS : (e + 1) * ROWS, :].astype(F32) for e in range(8)]
        for e, norm in enumerate(normalized(blocks)):
            cols = slice(e * EIGHTH, (e + 1) * EIGHTH)
            part = norm * (1.0 + mods[1:2, cols]) + mods[0:1, cols]
            h[e // 2, z, :, (e % 2) * EIGHTH : (e % 2 + 1) * EIGHTH] = part.astype(BF)

    def tokens(b):
        return h[b].reshape(NZ * ROWS, QUARTER)

    copies[2].wait()
    for copy in copies[3:]:
        copy.start()
    copies[1].wait()
    for j in range(NY):
        if j == 0:
            total = sum(times(own[:, b * QUARTER : (b + 1) * QUARTER], tokens(b)) for b in range(NY))
        else:
            total = None
            for weight, side in ((mine[j - 1], core), (other[j - 1], 1 - core)):
                for t in range(2):
                    term = times(weight[:, t * QUARTER : (t + 1) * QUARTER], tokens(2 * side + t))
                    total = term if total is None else total + term
        store_head(out.at[lax.rem(y + j, NY)], total)
    for copy in copies[3:]:
        copy.wait()


def qkv_first(later, mods, w_t, mine, other):
    return pl.pallas_call(
        qkv_first_kernel,
        out_shape=[jax.ShapeDtypeStruct((NY, 3 * HD, NZ * ROWS), BF)]
        + [jax.ShapeDtypeStruct((NZ // 2, 3 * HD, EIGHTH), BF)] * 2,
        in_specs=[HB, VM, HB] + [VM] * 6,
        out_specs=[VM, HB, HB],
        scratch_shapes=[
            pltpu.VMEM((NY, NZ, ROWS, QUARTER), BF),
            pltpu.VMEM((NZ, PACK[0], EIGHTH), BF),
            pltpu.VMEM((3 * HD, D), BF),
            pltpu.VMEM((NZ, PACK[1], EIGHTH), BF),
            pltpu.SemaphoreType.DMA((5,)),
        ],
        compiler_params=params(24),
        cost_estimate=pl.CostEstimate(flops=1_200_000_000, bytes_accessed=14_000_000, transcendentals=0),
        name="qkv_first",
    )(in_hbm(later), mods, in_hbm(w_t), *mine, *other)


def qkv_second_kernel(x0, x1, x2, x3, mods, gathered, *refs):
    weights, (out, h) = refs[:8], refs[8:]
    x_pos, core, _, y = position()

    @pl.when(pl.program_id(0) == 0)
    def _():
        for j, x in enumerate((x0, x1, x2, x3)):
            (norm,) = normalized([x[...].astype(F32)])
            at = lax.rem(y + j, NY)
            for e in range(8):
                cols = slice(e * EIGHTH, (e + 1) * EIGHTH)
                part = norm[:, cols] * (1.0 + mods[4:5, cols]) + mods[3:4, cols]
                h[e, at] = part.astype(BF)

    def tokens(e):
        return h[e].reshape(NY * ROWS, EIGHTH)

    @pl.when(pl.program_id(0) < NZ // 2)
    def _():
        store_head(out.at[0], sum(times(gathered[e, 0], tokens(e)) for e in range(8)))

    @pl.when(pl.program_id(0) >= NZ // 2)
    def _():
        total = None
        for n, weight in enumerate(weights):
            side = core if n < NX else 1 - core
            term = times(weight[0], tokens(lax.rem(x_pos + n % NX, NX) * NC + side))
            total = term if total is None else total + term
        store_head(out.at[0], total)


def qkv_second(shards, mods, gathered, weights):
    half = NZ // 2
    shard = pl.BlockSpec((ROWS, D), lambda i: (0, 0))
    low = pl.BlockSpec((8, 1, 3 * HD, EIGHTH), lambda i: (0, jnp.minimum(i, half - 1), 0, 0))
    high = pl.BlockSpec((1, 3 * HD, EIGHTH), lambda i: (jnp.maximum(i - half, 0), 0, 0))
    return pl.pallas_call(
        qkv_second_kernel,
        grid=(NZ,),
        out_shape=jax.ShapeDtypeStruct((NZ, 3 * HD, NY * ROWS), BF),
        in_specs=[shard] * 4 + [pl.BlockSpec((6, D), lambda i: (0, 0)), low] + [high] * 8,
        out_specs=pl.BlockSpec((1, 3 * HD, NY * ROWS), lambda i: (i, 0, 0)),
        scratch_shapes=[pltpu.VMEM((8, NY, ROWS, EIGHTH), BF)],
        compiler_params=params(24),
        cost_estimate=pl.CostEstimate(flops=1_200_000_000, bytes_accessed=10_500_000, transcendentals=0),
        name="qkv_second",
    )(*shards, mods, in_hbm(gathered), *weights)


def over_keys(per, ref, queries, acc, den, begin):
    def wide(n, lo, hi):
        if per == 1:
            return ref[n, lo:hi, :]
        return jnp.concatenate([ref[n * per + i, lo:hi, :] for i in range(per)], axis=1)

    def body(m, carry):
        q = queries[m]
        total, norm = (None, None) if begin else (acc[m], den[m])
        for n in range(4):
            keys, values = wide(n, HD, 2 * HD), wide(n, 2 * HD, 3 * HD)
            score = lax.dot_general(keys, q, (((0,), (0,)), ((), ())), preferred_element_type=F32)
            e = jnp.exp(score)
            sums = jnp.sum(e, axis=0, keepdims=True)
            term = jnp.dot(values, e.astype(BF), preferred_element_type=F32)
            total = term if total is None else total + term
            norm = sums if norm is None else norm + sums
        acc[m] = total
        den[m] = norm
        return carry

    lax.fori_loop(0, 4, body, 0)


def own_kernel(per, own, gain, queries, acc, den):
    column = jnp.transpose(jnp.broadcast_to(gain[...], (8, 2 * HD)))[:, 0:1]
    g = column[0:HD] * column[HD:] * 0.125
    for n in range(4):
        parts = [own[n * per + i, 0:HD, :] for i in range(per)]
        q = parts[0] if per == 1 else jnp.concatenate(parts, axis=1)
        queries[n] = (q.astype(F32) * g).astype(BF)
    over_keys(per, own, queries, acc, den, True)


def neighbours_kernel(per, lower, upper, queries, acc_in, den_in, out, acc, den):
    x_pos, core, _, _ = position()
    slot = x_pos * NC + core
    acc[...] = acc_in[...]
    den[...] = den_in[...]

    @pl.when(slot > 0)
    def _():
        over_keys(per, lower, queries, acc, den, False)

    @pl.when(slot < NX * NC - 1)
    def _():
        over_keys(per, upper, queries, acc, den, False)

    if per == 1:
        done = [acc[n] / den[n] for n in range(4)]
        for z in range(NZ):
            cols = slice(z * ROWS, (z + 1) * ROWS)
            out[z] = jnp.concatenate([d[:, cols] for d in done], axis=1).astype(BF)
    else:
        for n in range(4):
            done = (acc[n] / den[n]).astype(BF)
            for i in range(per):
                out[n * per + i] = done[:, i * 256 // per : (i + 1) * 256 // per]


def attention(own, lower, upper, gain):
    per = own.shape[0] // 4
    sums = [jax.ShapeDtypeStruct((4, HD, 256), F32), jax.ShapeDtypeStruct((4, 1, 256), F32)]
    queries, acc, den = pl.pallas_call(
        functools.partial(own_kernel, per),
        out_shape=[jax.ShapeDtypeStruct((4, HD, 256), BF)] + sums,
        in_specs=[VM] * 2,
        out_specs=[VM] * 3,
        compiler_params=params(8),
        cost_estimate=pl.CostEstimate(flops=3_000_000_000, bytes_accessed=800_000, transcendentals=0),
        name="own_%d" % per,
    )(own, gain)
    return pl.pallas_call(
        functools.partial(neighbours_kernel, per),
        out_shape=jax.ShapeDtypeStruct((NZ, HD, NY * ROWS), BF),
        in_specs=[VM] * 5,
        out_specs=VM,
        scratch_shapes=[pltpu.VMEM(s.shape, F32) for s in sums],
        compiler_params=params(8),
        cost_estimate=pl.CostEstimate(flops=6_000_000_000, bytes_accessed=1_200_000, transcendentals=0),
        name="neighbours_%d" % per,
    )(lower, upper, queries, acc, den)


def project_kernel(halves, o, *refs):
    (*sources, out, weights, sems) = refs
    _, core, _, _ = position()
    if halves:
        eighths = [(w.at[:, e * HD : (e + 1) * HD, :], 4 * side + e) for w, side in zip(sources, (core, 1 - core)) for e in range(4)]
    else:
        eighths = [(sources[0].at[s], s) for s in range(NX * NC)]
    copies = [pltpu.make_async_copy(w, weights.at[n], sems.at[n]) for n, (w, _) in enumerate(eighths)]
    for copy in copies:
        copy.start()
    rows = o[...].reshape(NZ * HD, NY * ROWS)
    for n in range(0, 8, 2):
        copies[n].wait()
        copies[n + 1].wait()
        w = jnp.concatenate([weights[n + t].reshape(NZ * HD, EIGHTH) for t in range(2)], axis=1)
        term = lax.dot_general(rows, w, (((0,), (0,)), ((), ())), preferred_element_type=F32)
        start = eighths[n][1] * EIGHTH
        out[:, pl.ds(pl.multiple_of(start, 128), QUARTER)] = term.astype(BF)


def project(o, weights):
    halves = len(weights) == 2
    out = pl.pallas_call(
        functools.partial(project_kernel, halves),
        out_shape=jax.ShapeDtypeStruct((NY * ROWS, D), BF),
        in_specs=[VM, HB, ANY][: 1 + len(weights)],
        out_specs=VM,
        scratch_shapes=[pltpu.VMEM((8, NZ, HD, EIGHTH), BF), pltpu.SemaphoreType.DMA((8,))],
        compiler_params=params(12),
        cost_estimate=pl.CostEstimate(flops=420_000_000, bytes_accessed=4_000_000, transcendentals=0),
        name="project_%d" % len(weights),
    )(o, in_hbm(weights[0]), *weights[1:])
    return out.reshape(NY, ROWS, D)


def added(layer, terms, mods, x):
    attn = sum(terms[j].astype(F32) for j in range(NY))
    gate = mods[3 * layer + 2 : 3 * layer + 3, :]
    return (x[...].astype(F32) + gate * attn).astype(BF)


def residual_kernel(terms, mods, x, out):
    out[...] = added(0, terms, mods, x)


def residual(terms, mods, x):
    return pl.pallas_call(
        residual_kernel,
        out_shape=jax.ShapeDtypeStruct((ROWS, D), BF),
        in_specs=[VM] * 3,
        out_specs=VM,
        compiler_params=params(8),
        cost_estimate=pl.CostEstimate(flops=600_000, bytes_accessed=1_400_000, transcendentals=0),
        name="residual",
    )(terms, mods, x)


def last_kernel(terms, mods, x, noise, out, leaving, sem):
    x_pos, core, z, y = position()
    value = added(1, terms, mods, x)
    out[...] = value
    head = jnp.logical_and(x_pos * NC + core == 0, z < NZ // 2)

    @pl.when(head)
    def _():
        at = pl.multiple_of(jnp.minimum(z * NY + y, SEQ // 2 - 1) * ROWS, ROWS)
        copy = pltpu.make_async_copy(noise.at[pl.ds(at, ROWS), :], leaving, sem)
        copy.start()
        copy.wait()

    @pl.when(jnp.logical_not(head))
    def _():
        leaving[...] = value


def last(terms, mods, x, noise):
    shape = jax.ShapeDtypeStruct((ROWS, D), BF)
    return pl.pallas_call(
        last_kernel,
        out_shape=[shape, shape],
        in_specs=[VM] * 3 + [HB],
        out_specs=[VM] * 2,
        scratch_shapes=[pltpu.SemaphoreType.DMA],
        compiler_params=params(8),
        cost_estimate=pl.CostEstimate(flops=600_000, bytes_accessed=1_600_000, transcendentals=0),
        name="last",
    )(terms, mods, x, in_hbm(noise))


def from_ahead(block, axis, size, distance):
    return lax.ppermute(block, axis, [(i, (i - distance) % size) for i in range(size)])


def swap(block):
    return lax.ppermute(block, "core", [(0, 1), (1, 0)])


def shifted(block, axis, distance):
    devices = range(lax.axis_size(axis))
    route = [(i - distance, i) for i in devices if i - distance in devices]
    return lax.ppermute(block, axis, route)


def per_device(
    latent, noise_frame, frame_pos, t_index, pos_table, mod_table, w_qkv, qk_gain, w_out
):
    mods = lax.dynamic_slice_in_dim(mod_table, t_index[0], 1, 0)[0].astype(F32).reshape(6, D)
    gains = qk_gain[:, 0].astype(F32)
    w_t = jnp.transpose(w_qkv[:, :, 0, :], (0, 2, 1))
    x0, pack, half, wo = prepare(frame_pos, latent, pos_table, w_t, w_out)

    later = lax.all_gather(pack, "z", axis=0, tiled=False)
    wo = lax.all_gather(wo, "z", axis=0, tiled=False)

    mine = [from_ahead(half, "y", NY, j) for j in range(1, NY)]
    other = [swap(m) for m in mine]

    def neighbours(own):
        return shifted(own, ("x", "core"), 1), shifted(own, ("x", "core"), -1)

    heads, low, high = qkv_first(later, mods, w_t, mine, other)
    low = lax.all_gather(low, ("x", "core"), axis=0, tiled=False)
    high_1, high_3 = from_ahead(high, "x", NX, 1), from_ahead(high, "x", NX, 3)
    own = lax.all_to_all(heads, "y", 0, 0, tiled=True)
    own, high_1, high_3 = lax.optimization_barrier((own, high_1, high_3))
    done = attention(own, *neighbours(own), gains[0:1])
    done, wo, high, high_1, high_3 = lax.optimization_barrier((done, wo, high, high_1, high_3))
    wo_s, high_2 = swap(wo), from_ahead(high_1, "x", NX, 1)
    wo1 = lax.all_gather(wo[:, 4 * HD :], ("x", "core"), axis=0, tiled=False)
    done = lax.all_to_all(done, "z", 0, 0, tiled=True)
    done, wo_s, high_2 = lax.optimization_barrier((done, wo_s, high_2))
    weights = [high, high_1, high_2, high_3]
    weights += [swap(w) for w in weights]
    terms = lax.all_to_all(project(done, [wo, wo_s]), "y", 0, 0, tiled=True)
    x1 = residual(terms, mods, x0)

    shards = [x1] + [from_ahead(x1, "y", NY, j) for j in range(1, NY)]
    heads = qkv_second(shards, mods, low, weights)
    own = lax.all_to_all(heads, "z", 0, 0, tiled=True)
    done = lax.all_to_all(attention(own, *neighbours(own), gains[1:2]), "z", 0, 0, tiled=True)
    terms = lax.all_to_all(project(done, [wo1]), "y", 0, 0, tiled=True)
    stream, leaving = last(terms, mods, x1, noise_frame)

    ranks = NX * NC * SEQ
    route = [(i, (i - SEQ // 2) % ranks) for i in range(ranks)]
    queue = lax.ppermute(leaving, ("x", "core", "z", "y"), route)
    return (stream[None], queue[None])


def solution(mesh):
    grid = Mesh(mesh.devices.reshape(NX, NC, NZ, NY), ("x", "core", "z", "y"))
    slot, seq = ("x", "core"), ("z", "y")
    placed = (
        P(slot, seq, None),
        P(),
        P(slot, None),
        P(slot),
        P(),
        P(),
        P(None, None, seq, None),
        P(None, seq, None),
        P(None, seq, None),
    )
    return jax.shard_map(
        per_device,
        mesh=grid,
        in_specs=placed,
        out_specs=(P(slot, seq, None), P(slot, seq, None)),
        check_vma=False,
    )
```

time: 285 us -> 247 us (0.87)
  blocking collectives: 75 us -> 47 us
  waiting for transfers between devices: 106 us -> 100 us
  local copies, waits for them, and re-layouts: 12.3 us -> 6.41 us
  other arithmetic: 5.62 us -> 0.8 us
  Pallas kernels: 37.4 us -> 41.7 us
  starting transfers between devices: 31.2 us -> 34.9 us
    ppermute x5 -> x4, waiting for transfers between devices: 41.9 us -> 5.94 us  [shifted(): return lax.ppermute(block, axis, route)]
    all_to_all x3 -> x1, blocking collectives: 40 us -> 16.6 us  [per_device(): terms = lax.all_to_all(project(done, [wo1]), 'y', 0, 0, tiled=True)]
    ppermute x0 -> x1, waiting for transfers between devices: none -> 13.8 us  [per_device(): queue = lax.ppermute(leaving, ('x', 'core', 'z', 'y'), route)]
    all_to_all x1 -> x3, waiting for transfers between devices: 12.2 us -> 25.8 us  [the longest x1 9.5 us: per_device(): terms = lax.all_to_all(project(done, [wo, wo_s]), 'y', 0, 0, tiled=True)]
    all_to_all x1 -> x3, starting transfers between devices: 4.41 us -> 11.2 us  [the longest x1 4.28 us: per_device(): own = lax.all_to_all(heads, 'y', 0, 0, tiled=True)]
    all_to_all x1, blocking collectives: 21.3 us -> 17.1 us  [per_device(): own = lax.all_to_all(heads, 'z', 0, 0, tiled=True)]
    pallas_call x6 -> x9, Pallas kernels: 21.9 us -> 25.8 us  [the longest x2 11.4 us: attention(): pl.pallas_call(functools.partial(neighbours_kernel, per), out_shape=jax.S...]
    unnamed x25 -> x15, local copies, waits for them, and re-layouts: 7.17 us -> 4.55 us
  transfers between devices with their start and end apart: 28 -> 29, of which waited for: 12 -> 17; matrix products, arithmetic and copies ran while one was open for 1% -> 1% of each run, Pallas kernels for 12% -> 14%
where the time goes in v6:
time: 247 us; the launch traced here: 246 us
  waiting for transfers between devices  100 us (40%)
  blocking collectives  47 us (19%)
  Pallas kernels  41.7 us (17%)
  starting transfers between devices  34.9 us (14%)
  between operations  14.7 us (6%)
  local copies, waits for them, and re-layouts  6.41 us (3%)
    ppermute x9, waiting for transfers between devices, from_ahead(): lax.ppermute(block, axis, [(i, (i - distance) % size) for i in range(size)])  40.4 us
    all_to_all x1, blocking collectives, per_device(): own = lax.all_to_all(heads, 'z', 0, 0, tiled=True)  17.1 us
    all_to_all x1, blocking collectives, per_device(): terms = lax.all_to_all(project(done, [wo1]), 'y', 0, 0, tiled=True)  16.6 us
    ppermute x1, waiting for transfers between devices, per_device(): queue = lax.ppermute(leaving, ('x', 'core', 'z', 'y'), route)  13.8 us
    all_to_all x1, blocking collectives, per_device(): done = lax.all_to_all(done, 'z', 0, 0, tiled=True)  13.3 us
    pallas_call x2, Pallas kernels, attention(): pl.pallas_call(functools.partial(neighbours_kernel, per), out_shape=jax.S...  11.4 us
    ppermute x4, starting transfers between devices, shifted(): return lax.ppermute(block, axis, route)  11.1 us
    all_gather x1, waiting for transfers between devices, per_device(): later = lax.all_gather(pack, 'z', axis=0, tiled=False)  11 us
  transfers between devices with their start and end apart: 29, of which 17 were waited for; matrix products, arithmetic and copies ran while one was open for 1% of the time, Pallas kernels for 14%

profile of v6, /device:TPU:4, one launch (start us, length us, event | category | flops | bytes accessed | tf_op | source)
XLA Modules:
  0.0 245.7 jit_solution(6653316186382790007)
XLA Ops:
  7.9 3.0 %prepare.1 = (bf16[32,3072]{1,0:T(8,128)(2,1)S(1)}, bf16[448,384]{1,0:T(8,128)(2,1)}, bf16[192,1536]{1,0:T(8,128)(2,1)}, bf16[320,384]{1,0:T(8,128)(2,1)}) custom-call(s32[1,2]{1,0:T(1,128)S(1)} %copy-done.5, bf16[1,32,3072]{2,1,0:T(8,128)(2,1)} %latent.1, bf16[16,3072]{1,0:T(8,128)(2,1)} %pos.1, bf16[2,192,3072]{2,1,0:T(8,128)(2,1)} %bitcast.20, ...), custom_call_target="tpu_custom_call" | custom-call | flops 300000 | bytes 2500000 | tf_op jit(solution)/shard_map/prepare/pallas_call | solution.py:100
  11.6 0.7 all-gather.11.cloned.1.call-update
  12.3 3.1 %collective-permute-start = (bf16[192,1536]{1,0:T(8,128)(2,1)}, bf16[192,1536]{1,0:T(8,128)(2,1)S(1)}, u32[]{:S(2)}, u32[]{:S(2)}) collective-permute-start(bf16[192,1536]{1,0:T(8,128)(2,1)} %get-tuple-element.29), channel_id=1, source_target_pairs={{0,3},{1,0},{2,1},{3,2},{4,7},{5,4},{6,5},{7,6},{8,11},{9,8},{10,9... | collective-permute-start | bytes 1769480 | tf_op jit(solution)/shard_map/ppermute | solution.py:402
  16.1 1.0 collective-permute-start.2
  17.0 23.9 %collective-permute-done.refs_0_ = bf16[192,1536]{1,0:T(8,128)(2,1)S(1)} collective-permute-done((bf16[192,1536]{1,0:T(8,128)(2,1)}, bf16[192,1536]{1,0:T(8,128)(2,1)S(1)}, u32[]{:S(2)}, u32[]{:S(2)}) %collective-permute-start) | collective-permute-done | bytes 589856 | tf_op jit(solution)/shard_map/ppermute | solution.py:402
  41.5 3.1 %collective-permute-done.2.refs_2_ = bf16[192,1536]{1,0:T(8,128)(2,1)S(1)} collective-permute-done((bf16[192,1536]{1,0:T(8,128)(2,1)}, bf16[192,1536]{1,0:T(8,128)(2,1)S(1)}, u32[]{:S(2)}, u32[]{:S(2)}) %collective-permute-start.2) | collective-permute-done | bytes 589856 | tf_op jit(solution)/shard_map/ppermute | solution.py:402
  45.3 0.8 dynamic-slice_convert_fusion
  46.7 11.0 %all-gather.9.cloned.1.call-done = bf16[3584,384]{1,0:T(8,128)(2,1)} async-done(((bf16[448,384]{1,0:T(8,128)(2,1)}), bf16[3584,384]{1,0:T(8,128)(2,1)}) %all-gather.9.cloned.1.call-update) | async-done | bytes 2752528 | tf_op jit(solution)/shard_map/all_gather | solution.py:423
  57.7 7.3 %qkv_first.1 = (bf16[4,192,256]{2,1,0:T(8,128)(2,1)}, bf16[4,192,384]{2,1,0:T(8,128)(2,1)S(1)}, bf16[4,192,384]{2,1,0:T(8,128)(2,1)S(1)}) custom-call(bf16[8,448,384]{2,1,0:T(8,128)(2,1)} %bitcast.27, f32[6,3072]{1,0:T(8,128)S(1)} %reshape.19.mods, bf16[2,192,3072]{2,1,0:T(8,128)(2,1)} %bitcast.21, bf16[192,1536]{1,0:T(8,128)(2,1)S(1)} %collective-permute-done.refs_0_, ...), custom_call_target="tpu_custom_call" | custom-call | flops 1200000000 | bytes 14000000 | tf_op jit(solution)/shard_map/qkv_first/pallas_call | solution.py:160
  65.0 0.8 copy-done
  65.8 0.8 copy-done.1
  67.3 1.5 collective-permute-start.7
  68.8 4.3 %all-to-all-start = ((bf16[4,192,256]{2,1,0:T(8,128)(2,1)}), bf16[4,192,256]{2,1,0:T(8,128)(2,1)S(1)}, u32[]{:S(2)}, u32[]{:S(2)}) async-start(bf16[4,192,256]{2,1,0:T(8,128)(2,1)} %get-tuple-element.30), calls=%async_computation | async-start | bytes 786432 | tf_op jit(solution)/shard_map/all_to_all | solution.py:435
  73.1 7.4 %all-to-all-done.own = bf16[4,192,256]{2,1,0:T(8,128)(2,1)S(1)} async-done(((bf16[4,192,256]{2,1,0:T(8,128)(2,1)}), bf16[4,192,256]{2,1,0:T(8,128)(2,1)S(1)}, u32[]{:S(2)}, u32[]{:S(2)}) %all-to-all-start) | async-done | bytes 393248 | tf_op jit(solution)/shard_map/all_to_all | solution.py:435
  80.4 1.9 collective-permute-start.8
  82.3 3.6 %collective-permute-start.9 = (bf16[4,192,256]{2,1,0:T(8,128)(2,1)S(1)}, bf16[4,192,256]{2,1,0:T(8,128)(2,1)S(1)}, u32[]{:S(2)}, u32[]{:S(2)}) collective-permute-start(bf16[4,192,256]{2,1,0:T(8,128)(2,1)S(1)} %all-to-all-done.own), channel_id=1, source_target_pairs={{32,0},{64,32},{96,64},{128,96},{160,128},{192,160},{224,192},{33,... | collective-permute-start | bytes 1179656 | tf_op jit(solution)/shard_map/ppermute | solution.py:412
  86.0 2.3 own_1.1
  88.3 1.2 collective-permute-done.8.lower
  89.5 1.8 collective-permute-done.9.upper
  91.3 5.5 %neighbours_1.1 = bf16[8,64,128]{2,1,0:T(8,128)(2,1)S(1)} custom-call(bf16[4,192,256]{2,1,0:T(8,128)(2,1)S(1)} %collective-permute-done.8.lower, bf16[4,192,256]{2,1,0:T(8,128)(2,1)S(1)} %collective-permute-done.9.upper, bf16[4,64,256]{2,1,0:T(8,128)(2,1)S(1)} %get-tuple-element.33.queries, f32[4,64,256]{2,1,0:T(8,128)S(1)} %get-tuple-element.34.acc_in, ...), custom_call_target="tpu_custom_call" | custom-call | flops 6000000000 | bytes 1200000 | tf_op jit(solution)/shard_map/neighbours_1/pallas_call | solution.py:300
  96.8 2.0 all-gather.11.cloned.1.call-done
  98.8 1.8 slice.19
  100.6 1.2 collective-permute-start.10
  101.8 13.3 %all_to_all.30.o = bf16[8,64,128]{2,1,0:T(8,128)(2,1)S(1)} all-to-all(bf16[8,64,128]{2,1,0:T(8,128)(2,1)S(1)} %neighbours_1.1), channel_id=1, replica_groups=mesh['x'=4,'core'=2,'z'=8,'y'=4] {'z'}, dimensions={0} | all-to-all | bytes 262144 | tf_op jit(solution)/shard_map/all_to_all | solution.py:441
  115.1 5.5 %collective-permute-done.11.refs_2_ = bf16[4,192,384]{2,1,0:T(8,128)(2,1)S(1)} collective-permute-done((bf16[4,192,384]{2,1,0:T(8,128)(2,1)S(1)}, bf16[4,192,384]{2,1,0:T(8,128)(2,1)S(1)}, u32[]{:S(2)}, u32[]{:S(2)}) %collective-permute-start.11) | collective-permute-done | bytes 589856 | tf_op jit(solution)/shard_map/ppermute | solution.py:402
  120.6 3.4 %project_2.1 = bf16[128,3072]{1,0:T(8,128)(2,1)} custom-call(bf16[8,64,128]{2,1,0:T(8,128)(2,1)S(1)} %all_to_all.30.o, bf16[8,320,384]{2,1,0:T(8,128)(2,1)} %bitcast.26, bf16[8,320,384]{2,1,0:T(8,128)(2,1)S(1)} %collective-permute-done.10.refs_1_), custom_call_target="tpu_custom_call" | custom-call | flops 420000000 | bytes 4000000 | tf_op jit(solution)/shard_map/project_2/pallas_call | solution.py:334
  123.9 3.5 %all-to-all-start.2 = ((bf16[4,32,3072]{2,1,0:T(8,128)(2,1)}), bf16[4,32,3072]{2,1,0:T(8,128)(2,1)S(1)}, u32[]{:S(2)}, u32[]{:S(2)}) async-start(bf16[4,32,3072]{2,1,0:T(8,128)(2,1)} %bitcast.6), calls=%async_computation.2 | async-start | bytes 1572864 | tf_op jit(solution)/shard_map/all_to_all | solution.py:445
  128.6 9.5 %all-to-all-done.2.terms = bf16[4,32,3072]{2,1,0:T(8,128)(2,1)S(1)} async-done(((bf16[4,32,3072]{2,1,0:T(8,128)(2,1)}), bf16[4,32,3072]{2,1,0:T(8,128)(2,1)S(1)}, u32[]{:S(2)}, u32[]{:S(2)}) %all-to-all-start.2) | async-done | bytes 786464 | tf_op jit(solution)/shard_map/all_to_all | solution.py:445
  138.1 0.9 copy-done.4
  139.2 1.3 collective-permute-start.12
  140.5 1.4 collective-permute-start.13
  141.9 3.0 %collective-permute-done.12.x1 = bf16[32,3072]{1,0:T(8,128)(2,1)S(1)} collective-permute-done((bf16[32,3072]{1,0:T(8,128)(2,1)S(1)}, bf16[32,3072]{1,0:T(8,128)(2,1)S(1)}, u32[]{:S(2)}, u32[]{:S(2)}) %collective-permute-start.12) | collective-permute-done | bytes 196640 | tf_op jit(solution)/shard_map/ppermute | solution.py:402
  144.9 2.8 %collective-permute-done.13.x2 = bf16[32,3072]{1,0:T(8,128)(2,1)S(1)} collective-permute-done((bf16[32,3072]{1,0:T(8,128)(2,1)S(1)}, bf16[32,3072]{1,0:T(8,128)(2,1)S(1)}, u32[]{:S(2)}, u32[]{:S(2)}) %collective-permute-start.13) | collective-permute-done | bytes 196640 | tf_op jit(solution)/shard_map/ppermute | solution.py:402
  147.7 2.0 collective-permute-done.14.x3
  149.7 8.6 %qkv_second.1 = bf16[8,192,128]{2,1,0:T(8,128)(2,1)S(1)} custom-call(bf16[32,3072]{1,0:T(8,128)(2,1)S(1)} %residual.1.x0.x, bf16[32,3072]{1,0:T(8,128)(2,1)S(1)} %collective-permute-done.12.x1, bf16[32,3072]{1,0:T(8,128)(2,1)S(1)} %collective-permute-done.13.x2, bf16[32,3072]{1,0:T(8,128)(2,1)S(1)} %collective-permute-done.14.x3, ...), custom_call_target="tpu_custom_call" | custom-call | flops 1200000000 | bytes 10500000 | tf_op jit(solution)/shard_map/qkv_second/pallas_call | solution.py:215
  158.3 17.1 %all_to_all.31.own = bf16[8,192,128]{2,1,0:T(8,128)(2,1)S(1)} all-to-all(bf16[8,192,128]{2,1,0:T(8,128)(2,1)S(1)} %qkv_second.1), channel_id=1, replica_groups=mesh['x'=4,'core'=2,'z'=8,'y'=4] {'z'}, dimensions={0} | all-to-all | bytes 786432 | tf_op jit(solution)/shard_map/all_to_all | solution.py:450
  175.5 1.9 collective-permute-start.19
  177.4 3.6 %collective-permute-start.20 = (bf16[8,192,128]{2,1,0:T(8,128)(2,1)S(1)}, bf16[8,192,128]{2,1,0:T(8,128)(2,1)S(1)}, u32[]{:S(2)}, u32[]{:S(2)}) collective-permute-start(bf16[8,192,128]{2,1,0:T(8,128)(2,1)S(1)} %all_to_all.31.own), channel_id=1, source_target_pairs={{32,0},{64,32},{96,64},{128,96},{160,128},{192,160},{224,192},{33,... | collective-permute-start | bytes 1179656 | tf_op jit(solution)/shard_map/ppermute | solution.py:412
  181.1 2.3 own_2.1
  183.4 1.2 collective-permute-done.19.lower
  184.6 1.8 collective-permute-done.20.upper
  186.3 6.0 %neighbours_2.1 = bf16[8,64,128]{2,1,0:T(8,128)(2,1)} custom-call(bf16[8,192,128]{2,1,0:T(8,128)(2,1)S(1)} %collective-permute-done.19.lower, bf16[8,192,128]{2,1,0:T(8,128)(2,1)S(1)} %collective-permute-done.20.upper, bf16[4,64,256]{2,1,0:T(8,128)(2,1)S(1)} %get-tuple-element.49.queries, f32[4,64,256]{2,1,0:T(8,128)S(1)} %get-tuple-element.50.acc_in, ...), custom_call_target="tpu_custom_call" | custom-call | flops 6000000000 | bytes 1200000 | tf_op jit(solution)/shard_map/neighbours_2/pallas_call | solution.py:300
  192.3 3.4 %all-to-all-start.4 = ((bf16[8,64,128]{2,1,0:T(8,128)(2,1)}), bf16[8,64,128]{2,1,0:T(8,128)(2,1)S(1)}, u32[]{:S(2)}, u32[]{:S(2)}) async-start(bf16[8,64,128]{2,1,0:T(8,128)(2,1)} %neighbours_2.1), calls=%async_computation.4 | async-start | bytes 262144 | tf_op jit(solution)/shard_map/all_to_all | solution.py:451
  195.7 9.0 %all-to-all-done.4.o = bf16[8,64,128]{2,1,0:T(8,128)(2,1)S(1)} async-done(((bf16[8,64,128]{2,1,0:T(8,128)(2,1)}), bf16[8,64,128]{2,1,0:T(8,128)(2,1)S(1)}, u32[]{:S(2)}, u32[]{:S(2)}) %all-to-all-start.4) | async-done | bytes 131104 | tf_op jit(solution)/shard_map/all_to_all | solution.py:451
  204.7 2.4 project_1.1
  207.1 16.6 %all_to_all.32.terms = bf16[4,32,3072]{2,1,0:T(8,128)(2,1)S(1)} all-to-all(bf16[4,32,3072]{2,1,0:T(8,128)(2,1)S(1)} %bitcast.19), channel_id=1, replica_groups=mesh['x'=4,'core'=2,'z'=8,'y'=4] {'y'}, dimensions={0} | all-to-all | bytes 1572864 | tf_op jit(solution)/shard_map/all_to_all | solution.py:452
  223.7 0.8 last.1
  224.6 13.8 %collective-permute-done.21 = bf16[32,3072]{1,0:T(8,128)(2,1)S(1)} collective-permute-done((bf16[32,3072]{1,0:T(8,128)(2,1)S(1)}, bf16[32,3072]{1,0:T(8,128)(2,1)S(1)}, u32[]{:S(2)}, u32[]{:S(2)}) %collective-permute-start.21) | collective-permute-done | bytes 196640 | tf_op jit(solution)/shard_map/ppermute | solution.py:457
  (49 shorter events, 6.0 us)
Async XLA Ops:
  7.2 50.6 %all-gather.9.cloned.1.call-start = ((), (), s32[]{:S(2)}) async-start(), calls=%async_computation.6 | async-start | bytes 3096576 | tf_op jit(solution)/shard_map/all_gather | solution.py:423
  7.2 0.7 copy-start.5
  10.8 0.7 copy-start.3
  11.5 87.3 %all-gather.11.cloned.1.call-start = ((), (), s32[]{:S(2)}) async-start(), calls=%async_computation.7 | async-start | bytes 2211840 | tf_op jit(solution)/shard_map/all_gather | solution.py:424
  12.3 137.4 %all-gather.13.cloned.1.call-start = ((), (), s32[]{:S(2)}) async-start(), calls=%async_computation.8 | async-start | bytes 5308416 | tf_op jit(solution)/shard_map/all_gather | solution.py:433
  12.3 28.6 %collective-permute-start = (bf16[192,1536]{1,0:T(8,128)(2,1)}, bf16[192,1536]{1,0:T(8,128)(2,1)S(1)}, u32[]{:S(2)}, u32[]{:S(2)}) collective-permute-start(bf16[192,1536]{1,0:T(8,128)(2,1)} %get-tuple-element.29), channel_id=1, source_target_pairs={{0,3},{1,0},{2,1},{3,2},{4,7},{5,4},{6,5},{7,6},{8,11},{9,8},{10,9... | collective-permute-start | bytes 1769480 | tf_op jit(solution)/shard_map/ppermute | solution.py:402
  15.4 25.5 %collective-permute-start.1 = (bf16[192,1536]{1,0:T(8,128)(2,1)}, bf16[192,1536]{1,0:T(8,128)(2,1)S(1)}, u32[]{:S(2)}, u32[]{:S(2)}) collective-permute-start(bf16[192,1536]{1,0:T(8,128)(2,1)} %get-tuple-element.29), channel_id=1, source_target_pairs={{0,2},{1,3},{2,0},{3,1},{4,6},{5,7},{6,4},{7,5},{8,10},{9,11},{10,... | collective-permute-start | bytes 1769480 | tf_op jit(solution)/shard_map/ppermute | solution.py:402
  16.1 28.5 %collective-permute-start.2 = (bf16[192,1536]{1,0:T(8,128)(2,1)}, bf16[192,1536]{1,0:T(8,128)(2,1)S(1)}, u32[]{:S(2)}, u32[]{:S(2)}) collective-permute-start(bf16[192,1536]{1,0:T(8,128)(2,1)} %get-tuple-element.29), channel_id=1, source_target_pairs={{0,1},{1,2},{2,3},{3,0},{4,5},{5,6},{6,7},{7,4},{8,9},{9,10},{10,1... | collective-permute-start | bytes 1769480 | tf_op jit(solution)/shard_map/ppermute | solution.py:402
  41.0 5.3 %collective-permute-start.3 = (bf16[192,1536]{1,0:T(8,128)(2,1)S(1)}, bf16[192,1536]{1,0:T(8,128)(2,1)S(1)}, u32[]{:S(2)}, u32[]{:S(2)}) collective-permute-start(bf16[192,1536]{1,0:T(8,128)(2,1)S(1)} %collective-permute-done.refs_0_), channel_id=1, source_target_pairs={{0,32},{32,0},{1,33},{33,1},{2,34},{34,2},{3,35},{35,3},{4,36},{36... | collective-permute-start | bytes 1769480 | tf_op jit(solution)/shard_map/ppermute | solution.py:406
  41.0 5.3 %collective-permute-start.4 = (bf16[192,1536]{1,0:T(8,128)(2,1)S(1)}, bf16[192,1536]{1,0:T(8,128)(2,1)S(1)}, u32[]{:S(2)}, u32[]{:S(2)}) collective-permute-start(bf16[192,1536]{1,0:T(8,128)(2,1)S(1)} %collective-permute-done.1.refs_1_), channel_id=1, source_target_pairs={{0,32},{32,0},{1,33},{33,1},{2,34},{34,2},{3,35},{35,3},{4,36},{36... | collective-permute-start | bytes 1769480 | tf_op jit(solution)/shard_map/ppermute | solution.py:406
  44.6 2.1 collective-permute-start.5
  57.7 15.3 %copy-start.6 = (bf16[2,1,128]{2,0,1:T(2,128)(2,1)S(1)}, bf16[2,1,128]{2,0,1:T(2,128)(2,1)}, u32[]{:S(2)}) copy-start(bf16[2,1,128]{2,0,1:T(2,128)(2,1)} %param.16) | copy-start | bytes 1540
  65.0 0.8 copy-start
  65.8 0.8 copy-start.1
  66.7 13.8 %collective-permute-start.6 = (bf16[4,192,384]{2,1,0:T(8,128)(2,1)}, bf16[4,192,384]{2,1,0:T(8,128)(2,1)S(1)}, u32[]{:S(2)}, u32[]{:S(2)}) collective-permute-start(bf16[4,192,384]{2,1,0:T(8,128)(2,1)} %copy-done.1), channel_id=1, source_target_pairs={{0,192},{64,0},{128,64},{192,128},{1,193},{65,1},{129,65},{193,129... | collective-permute-start | bytes 1769480 | tf_op jit(solution)/shard_map/ppermute | solution.py:402
  67.3 13.1 %collective-permute-start.7 = (bf16[4,192,384]{2,1,0:T(8,128)(2,1)}, bf16[4,192,384]{2,1,0:T(8,128)(2,1)S(1)}, u32[]{:S(2)}, u32[]{:S(2)}) collective-permute-start(bf16[4,192,384]{2,1,0:T(8,128)(2,1)} %copy-done.1), channel_id=1, source_target_pairs={{0,64},{64,128},{128,192},{192,0},{1,65},{65,129},{129,193},{193,1... | collective-permute-start | bytes 1769480 | tf_op jit(solution)/shard_map/ppermute | solution.py:402
  68.8 11.7 %all-to-all-start = ((bf16[4,192,256]{2,1,0:T(8,128)(2,1)}), bf16[4,192,256]{2,1,0:T(8,128)(2,1)S(1)}, u32[]{:S(2)}, u32[]{:S(2)}) async-start(bf16[4,192,256]{2,1,0:T(8,128)(2,1)} %get-tuple-element.30), calls=%async_computation | async-start | bytes 786432 | tf_op jit(solution)/shard_map/all_to_all | solution.py:435
  73.0 122.6 %all-gather.15.cloned.1.call-start = ((), (), s32[]{:S(2)}) async-start(), calls=%async_computation.9 | async-start | bytes 3538944 | tf_op jit(solution)/shard_map/all_gather | solution.py:440
  80.4 9.1 %collective-permute-start.8 = (bf16[4,192,256]{2,1,0:T(8,128)(2,1)S(1)}, bf16[4,192,256]{2,1,0:T(8,128)(2,1)S(1)}, u32[]{:S(2)}, u32[]{:S(2)}) collective-permute-start(bf16[4,192,256]{2,1,0:T(8,128)(2,1)S(1)} %all-to-all-done.own), channel_id=1, source_target_pairs={{0,32},{32,64},{64,96},{96,128},{128,160},{160,192},{192,224},{1,3... | collective-permute-start | bytes 1179656 | tf_op jit(solution)/shard_map/ppermute | solution.py:412
  82.3 8.9 %collective-permute-start.9 = (bf16[4,192,256]{2,1,0:T(8,128)(2,1)S(1)}, bf16[4,192,256]{2,1,0:T(8,128)(2,1)S(1)}, u32[]{:S(2)}, u32[]{:S(2)}) collective-permute-start(bf16[4,192,256]{2,1,0:T(8,128)(2,1)S(1)} %all-to-all-done.own), channel_id=1, source_target_pairs={{32,0},{64,32},{96,64},{128,96},{160,128},{192,160},{224,192},{33,... | collective-permute-start | bytes 1179656 | tf_op jit(solution)/shard_map/ppermute | solution.py:412
  100.6 19.9 %collective-permute-start.10 = (bf16[8,320,384]{2,1,0:T(8,128)(2,1)}, bf16[8,320,384]{2,1,0:T(8,128)(2,1)S(1)}, u32[]{:S(2)}, u32[]{:S(2)}) collective-permute-start(bf16[8,320,384]{2,1,0:T(8,128)(2,1)} %bitcast.25), channel_id=1, source_target_pairs={{0,32},{32,0},{1,33},{33,1},{2,34},{34,2},{3,35},{35,3},{4,36},{36... | collective-permute-start | bytes 5898248 | tf_op jit(solution)/shard_map/ppermute | solution.py:406
  101.8 18.8 %collective-permute-start.11 = (bf16[4,192,384]{2,1,0:T(8,128)(2,1)S(1)}, bf16[4,192,384]{2,1,0:T(8,128)(2,1)S(1)}, u32[]{:S(2)}, u32[]{:S(2)}) collective-permute-start(bf16[4,192,384]{2,1,0:T(8,128)(2,1)S(1)} %collective-permute-done.6.refs_1_), channel_id=1, source_target_pairs={{0,192},{64,0},{128,64},{192,128},{1,193},{65,1},{129,65},{193,129... | collective-permute-start | bytes 1769480 | tf_op jit(solution)/shard_map/ppermute | solution.py:402
  115.1 12.4 %copy-start.2 = (bf16[4,192,384]{2,1,0:T(8,128)(2,1)S(1)}, bf16[4,192,384]{2,1,0:T(8,128)(2,1)}, u32[]{:S(2)}) copy-start(bf16[4,192,384]{2,1,0:T(8,128)(2,1)} %copy-done.1) | copy-start | bytes 1769476
  123.9 14.1 %all-to-all-start.2 = ((bf16[4,32,3072]{2,1,0:T(8,128)(2,1)}), bf16[4,32,3072]{2,1,0:T(8,128)(2,1)S(1)}, u32[]{:S(2)}, u32[]{:S(2)}) async-start(bf16[4,32,3072]{2,1,0:T(8,128)(2,1)} %bitcast.6), calls=%async_computation.2 | async-start | bytes 1572864 | tf_op jit(solution)/shard_map/all_to_all | solution.py:445
  127.5 13.0 %collective-permute-start.15 = (bf16[4,192,384]{2,1,0:T(8,128)(2,1)S(1)}, bf16[4,192,384]{2,1,0:T(8,128)(2,1)}, u32[]{:S(2)}, u32[]{:S(2)}) collective-permute-start(bf16[4,192,384]{2,1,0:T(8,128)(2,1)S(1)} %copy-done.2), channel_id=1, source_target_pairs={{0,32},{32,0},{1,33},{33,1},{2,34},{34,2},{3,35},{35,3},{4,36},{36... | collective-permute-start | bytes 1769480 | tf_op jit(solution)/shard_map/ppermute | solution.py:406
  127.6 14.3 %collective-permute-start.16 = (bf16[4,192,384]{2,1,0:T(8,128)(2,1)S(1)}, bf16[4,192,384]{2,1,0:T(8,128)(2,1)}, u32[]{:S(2)}, u32[]{:S(2)}) collective-permute-start(bf16[4,192,384]{2,1,0:T(8,128)(2,1)S(1)} %collective-permute-done.6.refs_1_), channel_id=1, source_target_pairs={{0,32},{32,0},{1,33},{33,1},{2,34},{34,2},{3,35},{35,3},{4,36},{36... | collective-permute-start | bytes 1769480 | tf_op jit(solution)/shard_map/ppermute | solution.py:406
  128.1 13.8 %collective-permute-start.18 = (bf16[4,192,384]{2,1,0:T(8,128)(2,1)S(1)}, bf16[4,192,384]{2,1,0:T(8,128)(2,1)}, u32[]{:S(2)}, u32[]{:S(2)}) collective-permute-start(bf16[4,192,384]{2,1,0:T(8,128)(2,1)S(1)} %collective-permute-done.7.refs_3_), channel_id=1, source_target_pairs={{0,32},{32,0},{1,33},{33,1},{2,34},{34,2},{3,35},{35,3},{4,36},{36... | collective-permute-start | bytes 1769480 | tf_op jit(solution)/shard_map/ppermute | solution.py:406
  128.2 13.7 %collective-permute-start.17 = (bf16[4,192,384]{2,1,0:T(8,128)(2,1)S(1)}, bf16[4,192,384]{2,1,0:T(8,128)(2,1)}, u32[]{:S(2)}, u32[]{:S(2)}) collective-permute-start(bf16[4,192,384]{2,1,0:T(8,128)(2,1)S(1)} %collective-permute-done.11.refs_2_), channel_id=1, source_target_pairs={{0,32},{32,0},{1,33},{33,1},{2,34},{34,2},{3,35},{35,3},{4,36},{36... | collective-permute-start | bytes 1769480 | tf_op jit(solution)/shard_map/ppermute | solution.py:406
  138.1 0.9 copy-start.4
  139.2 5.7 %collective-permute-start.12 = (bf16[32,3072]{1,0:T(8,128)(2,1)S(1)}, bf16[32,3072]{1,0:T(8,128)(2,1)S(1)}, u32[]{:S(2)}, u32[]{:S(2)}) collective-permute-start(bf16[32,3072]{1,0:T(8,128)(2,1)S(1)} %residual.1.x0.x), channel_id=1, source_target_pairs={{0,3},{1,0},{2,1},{3,2},{4,7},{5,4},{6,5},{7,6},{8,11},{9,8},{10,9... | collective-permute-start | bytes 589832 | tf_op jit(solution)/shard_map/ppermute | solution.py:402
  140.5 7.3 %collective-permute-start.13 = (bf16[32,3072]{1,0:T(8,128)(2,1)S(1)}, bf16[32,3072]{1,0:T(8,128)(2,1)S(1)}, u32[]{:S(2)}, u32[]{:S(2)}) collective-permute-start(bf16[32,3072]{1,0:T(8,128)(2,1)S(1)} %residual.1.x0.x), channel_id=1, source_target_pairs={{0,2},{1,3},{2,0},{3,1},{4,6},{5,7},{6,4},{7,5},{8,10},{9,11},{10,... | collective-permute-start | bytes 589832 | tf_op jit(solution)/shard_map/ppermute | solution.py:402
  141.9 7.9 %collective-permute-start.14 = (bf16[32,3072]{1,0:T(8,128)(2,1)S(1)}, bf16[32,3072]{1,0:T(8,128)(2,1)S(1)}, u32[]{:S(2)}, u32[]{:S(2)}) collective-permute-start(bf16[32,3072]{1,0:T(8,128)(2,1)S(1)} %residual.1.x0.x), channel_id=1, source_target_pairs={{0,1},{1,2},{2,3},{3,0},{4,5},{5,6},{6,7},{7,4},{8,9},{9,10},{10,1... | collective-permute-start | bytes 589832 | tf_op jit(solution)/shard_map/ppermute | solution.py:402
  175.5 9.1 %collective-permute-start.19 = (bf16[8,192,128]{2,1,0:T(8,128)(2,1)S(1)}, bf16[8,192,128]{2,1,0:T(8,128)(2,1)S(1)}, u32[]{:S(2)}, u32[]{:S(2)}) collective-permute-start(bf16[8,192,128]{2,1,0:T(8,128)(2,1)S(1)} %all_to_all.31.own), channel_id=1, source_target_pairs={{0,32},{32,64},{64,96},{96,128},{128,160},{160,192},{192,224},{1,3... | collective-permute-start | bytes 1179656 | tf_op jit(solution)/shard_map/ppermute | solution.py:412
  177.4 8.9 %collective-permute-start.20 = (bf16[8,192,128]{2,1,0:T(8,128)(2,1)S(1)}, bf16[8,192,128]{2,1,0:T(8,128)(2,1)S(1)}, u32[]{:S(2)}, u32[]{:S(2)}) collective-permute-start(bf16[8,192,128]{2,1,0:T(8,128)(2,1)S(1)} %all_to_all.31.own), channel_id=1, source_target_pairs={{32,0},{64,32},{96,64},{128,96},{160,128},{192,160},{224,192},{33,... | collective-permute-start | bytes 1179656 | tf_op jit(solution)/shard_map/ppermute | solution.py:412
  192.3 12.4 %all-to-all-start.4 = ((bf16[8,64,128]{2,1,0:T(8,128)(2,1)}), bf16[8,64,128]{2,1,0:T(8,128)(2,1)S(1)}, u32[]{:S(2)}, u32[]{:S(2)}) async-start(bf16[8,64,128]{2,1,0:T(8,128)(2,1)} %neighbours_2.1), calls=%async_computation.4 | async-start | bytes 262144 | tf_op jit(solution)/shard_map/all_to_all | solution.py:451
  224.5 13.9 %collective-permute-start.21 = (bf16[32,3072]{1,0:T(8,128)(2,1)S(1)}, bf16[32,3072]{1,0:T(8,128)(2,1)S(1)}, u32[]{:S(2)}, u32[]{:S(2)}) collective-permute-start(bf16[32,3072]{1,0:T(8,128)(2,1)S(1)} %get-tuple-element.53), channel_id=1, source_target_pairs={{0,240},{1,241},{2,242},{3,243},{4,244},{5,245},{6,246},{7,247},{8... | collective-permute-start | bytes 589832 | tf_op jit(solution)/shard_map/ppermute | solution.py:457
Sparse Core Ops, SparseCore 0:
  11.7 46.0 all-gather.8
  59.5 39.2 all-gather.10
  100.6 36.9 all-gather.12
  139.3 28.0 all-gather.14

commit v7 on v6

--- a/solution.py
+++ b/solution.py
@@ -19,6 +19,7 @@
 QUARTER = D // NY
 EIGHTH = QUARTER // 2
 PACK = (8 * ROWS, 3 * HD)
+LOW = 5
 
 VM = pl.BlockSpec(memory_space=pltpu.VMEM)
 SM = pl.BlockSpec(memory_space=pltpu.SMEM)
@@ -115,17 +116,21 @@
 
 def qkv_first_kernel(later, mods, w_t, *refs):
     mine, other = refs[0:3], refs[3:6]
-    out, wq_low, wq_high, h, x, own, held, sems = refs[6:]
+    out, wq_low, wq_high, h, x, weights, held, sems = refs[6:]
     _, core, _, y = position()
     first = pl.ds(PACK[0], PACK[1])
-    copies = [
-        pltpu.make_async_copy(later.at[:, : PACK[0], :], x, sems.at[0]),
-        pltpu.make_async_copy(w_t.at[0], own, sems.at[1]),
-        pltpu.make_async_copy(later.at[:, first, :], held, sems.at[2]),
-        pltpu.make_async_copy(held.at[: NZ // 2], wq_low, sems.at[3]),
-        pltpu.make_async_copy(held.at[NZ // 2 :], wq_high, sems.at[4]),
+    pairs = [
+        (later.at[:, : PACK[0], :], x),
+        (later.at[:, first, :], held),
+        (w_t.at[0], weights.at[: 3 * HD, :]),
     ]
-    for copy in copies[:3]:
+    for group, side in ((mine, core), (other, 1 - core)):
+        cols = pl.ds(pl.multiple_of(side * (D // 2), 128), D // 2)
+        for n, weight in enumerate(group):
+            pairs.append((weight, weights.at[(n + 1) * 3 * HD : (n + 2) * 3 * HD, cols]))
+    pairs += [(held.at[:LOW], wq_low), (held.at[LOW:], wq_high)]
+    copies = [pltpu.make_async_copy(*pair, sems.at[n]) for n, pair in enumerate(pairs)]
+    for copy in copies[:9]:
         copy.start()
     copies[0].wait()
     for z in range(NZ):
@@ -133,42 +138,32 @@
         for e, norm in enumerate(normalized(blocks)):
             cols = slice(e * EIGHTH, (e + 1) * EIGHTH)
             part = norm * (1.0 + mods[1:2, cols]) + mods[0:1, cols]
-            h[e // 2, z, :, (e % 2) * EIGHTH : (e % 2 + 1) * EIGHTH] = part.astype(BF)
-
-    def tokens(b):
-        return h[b].reshape(NZ * ROWS, QUARTER)
-
-    copies[2].wait()
-    for copy in copies[3:]:
+            h[z * ROWS : (z + 1) * ROWS, cols] = part.astype(BF)
+    copies[1].wait()
+    for copy in copies[9:]:
         copy.start()
-    copies[1].wait()
+    for copy in copies[2:9]:
+        copy.wait()
+    result = times(weights[...], h[...])
     for j in range(NY):
-        if j == 0:
-            total = sum(times(own[:, b * QUARTER : (b + 1) * QUARTER], tokens(b)) for b in range(NY))
-        else:
-            total = None
-            for weight, side in ((mine[j - 1], core), (other[j - 1], 1 - core)):
-                for t in range(2):
-                    term = times(weight[:, t * QUARTER : (t + 1) * QUARTER], tokens(2 * side + t))
-                    total = term if total is None else total + term
-        store_head(out.at[lax.rem(y + j, NY)], total)
-    for copy in copies[3:]:
+        store_head(out.at[lax.rem(y + j, NY)], result[j * 3 * HD : (j + 1) * 3 * HD])
+    for copy in copies[9:]:
         copy.wait()
 
 
 def qkv_first(later, mods, w_t, mine, other):
+    parts = [pltpu.HBM((n, 3 * HD, EIGHTH), BF) for n in (LOW, NZ - LOW)]
     return pl.pallas_call(
         qkv_first_kernel,
-        out_shape=[jax.ShapeDtypeStruct((NY, 3 * HD, NZ * ROWS), BF)]
-        + [jax.ShapeDtypeStruct((NZ // 2, 3 * HD, EIGHTH), BF)] * 2,
-        in_specs=[HB, VM, HB] + [VM] * 6,
+        out_shape=[jax.ShapeDtypeStruct((NY, 3 * HD, NZ * ROWS), BF), *parts],
+        in_specs=[HB, VM, HB] + [ANY] * 6,
         out_specs=[VM, HB, HB],
         scratch_shapes=[
-            pltpu.VMEM((NY, NZ, ROWS, QUARTER), BF),
+            pltpu.VMEM((NZ * ROWS, D), BF),
             pltpu.VMEM((NZ, PACK[0], EIGHTH), BF),
-            pltpu.VMEM((3 * HD, D), BF),
+            pltpu.VMEM((NY * 3 * HD, D), BF),
             pltpu.VMEM((NZ, PACK[1], EIGHTH), BF),
-            pltpu.SemaphoreType.DMA((5,)),
+            pltpu.SemaphoreType.DMA((11,)),
         ],
         compiler_params=params(24),
         cost_estimate=pl.CostEstimate(flops=1_200_000_000, bytes_accessed=14_000_000, transcendentals=0),
@@ -177,48 +172,43 @@
 
 
 def qkv_second_kernel(x0, x1, x2, x3, mods, gathered, *refs):
-    weights, (out, h) = refs[:8], refs[8:]
+    high, (out, h, weights, sems) = refs[:8], refs[8:]
     x_pos, core, _, y = position()
-
-    @pl.when(pl.program_id(0) == 0)
-    def _():
-        for j, x in enumerate((x0, x1, x2, x3)):
-            (norm,) = normalized([x[...].astype(F32)])
-            at = lax.rem(y + j, NY)
-            for e in range(8):
-                cols = slice(e * EIGHTH, (e + 1) * EIGHTH)
-                part = norm[:, cols] * (1.0 + mods[4:5, cols]) + mods[3:4, cols]
-                h[e, at] = part.astype(BF)
-
-    def tokens(e):
-        return h[e].reshape(NY * ROWS, EIGHTH)
-
-    @pl.when(pl.program_id(0) < NZ // 2)
-    def _():
-        store_head(out.at[0], sum(times(gathered[e, 0], tokens(e)) for e in range(8)))
-
-    @pl.when(pl.program_id(0) >= NZ // 2)
-    def _():
-        total = None
-        for n, weight in enumerate(weights):
-            side = core if n < NX else 1 - core
-            term = times(weight[0], tokens(lax.rem(x_pos + n % NX, NX) * NC + side))
-            total = term if total is None else total + term
-        store_head(out.at[0], total)
+    copies = []
+    for e in range(8):
+        target = weights.at[:LOW, :, e * EIGHTH : (e + 1) * EIGHTH]
+        copies.append(pltpu.make_async_copy(gathered.at[e], target, sems.at[e]))
+    for n, weight in enumerate(high):
+        side = core if n < NX else 1 - core
+        start = (lax.rem(x_pos + n % NX, NX) * NC + side) * EIGHTH
+        target = weights.at[LOW:, :, pl.ds(pl.multiple_of(start, 128), EIGHTH)]
+        copies.append(pltpu.make_async_copy(weight, target, sems.at[8 + n]))
+    for copy in copies:
+        copy.start()
+    for j, x in enumerate((x0, x1, x2, x3)):
+        (norm,) = normalized([x[...].astype(F32)])
+        part = norm * (1.0 + mods[4:5, :]) + mods[3:4, :]
+        h[lax.rem(y + j, NY)] = part.astype(BF)
+    tokens = h[...].reshape(NY * ROWS, D)
+    for part, (begin, end) in enumerate(((0, LOW), (LOW, NZ))):
+        for copy in copies[8 * part : 8 * part + 8]:
+            copy.wait()
+        result = times(weights[begin:end].reshape((end - begin) * 3 * HD, D), tokens)
+        for j in range(end - begin):
+            store_head(out.at[begin + j], result[j * 3 * HD : (j + 1) * 3 * HD])
 
 
 def qkv_second(shards, mods, gathered, weights):
-    half = NZ // 2
-    shard = pl.BlockSpec((ROWS, D), lambda i: (0, 0))
-    low = pl.BlockSpec((8, 1, 3 * HD, EIGHTH), lambda i: (0, jnp.minimum(i, half - 1), 0, 0))
-    high = pl.BlockSpec((1, 3 * HD, EIGHTH), lambda i: (jnp.maximum(i - half, 0), 0, 0))
     return pl.pallas_call(
         qkv_second_kernel,
-        grid=(NZ,),
         out_shape=jax.ShapeDtypeStruct((NZ, 3 * HD, NY * ROWS), BF),
-        in_specs=[shard] * 4 + [pl.BlockSpec((6, D), lambda i: (0, 0)), low] + [high] * 8,
-        out_specs=pl.BlockSpec((1, 3 * HD, NY * ROWS), lambda i: (i, 0, 0)),
-        scratch_shapes=[pltpu.VMEM((8, NY, ROWS, EIGHTH), BF)],
+        in_specs=[VM] * 5 + [HB] + [ANY] * 8,
+        out_specs=VM,
+        scratch_shapes=[
+            pltpu.VMEM((NY, ROWS, D), BF),
+            pltpu.VMEM((NZ, 3 * HD, D), BF),
+            pltpu.SemaphoreType.DMA((16,)),
+        ],
         compiler_params=params(24),
         cost_estimate=pl.CostEstimate(flops=1_200_000_000, bytes_accessed=10_500_000, transcendentals=0),
         name="qkv_second",
@@ -285,37 +275,37 @@
                 out[n * per + i] = done[:, i * 256 // per : (i + 1) * 256 // per]
 
 
-def attention(own, lower, upper, gain):
+SUMS = (jax.ShapeDtypeStruct((4, HD, 256), F32), jax.ShapeDtypeStruct((4, 1, 256), F32))
+
+
+def own_keys(own, gain):
     per = own.shape[0] // 4
-    sums = [jax.ShapeDtypeStruct((4, HD, 256), F32), jax.ShapeDtypeStruct((4, 1, 256), F32)]
-    queries, acc, den = pl.pallas_call(
+    return pl.pallas_call(
         functools.partial(own_kernel, per),
-        out_shape=[jax.ShapeDtypeStruct((4, HD, 256), BF)] + sums,
+        out_shape=[jax.ShapeDtypeStruct((4, HD, 256), BF), *SUMS],
         in_specs=[VM] * 2,
         out_specs=[VM] * 3,
         compiler_params=params(8),
         cost_estimate=pl.CostEstimate(flops=3_000_000_000, bytes_accessed=800_000, transcendentals=0),
         name="own_%d" % per,
     )(own, gain)
+
+
+def neighbour_keys(lower, upper, queries, acc, den):
+    per = lower.shape[0] // 4
     return pl.pallas_call(
         functools.partial(neighbours_kernel, per),
         out_shape=jax.ShapeDtypeStruct((NZ, HD, NY * ROWS), BF),
         in_specs=[VM] * 5,
         out_specs=VM,
-        scratch_shapes=[pltpu.VMEM(s.shape, F32) for s in sums],
+        scratch_shapes=[pltpu.VMEM(s.shape, F32) for s in SUMS],
         compiler_params=params(8),
         cost_estimate=pl.CostEstimate(flops=6_000_000_000, bytes_accessed=1_200_000, transcendentals=0),
         name="neighbours_%d" % per,
     )(lower, upper, queries, acc, den)
 
 
-def project_kernel(halves, o, *refs):
-    (*sources, out, weights, sems) = refs
-    _, core, _, _ = position()
-    if halves:
-        eighths = [(w.at[:, e * HD : (e + 1) * HD, :], 4 * side + e) for w, side in zip(sources, (core, 1 - core)) for e in range(4)]
-    else:
-        eighths = [(sources[0].at[s], s) for s in range(NX * NC)]
+def project_terms(o, eighths, weights, sems, put):
     copies = [pltpu.make_async_copy(w, weights.at[n], sems.at[n]) for n, (w, _) in enumerate(eighths)]
     for copy in copies:
         copy.start()
@@ -325,33 +315,77 @@
         copies[n + 1].wait()
         w = jnp.concatenate([weights[n + t].reshape(NZ * HD, EIGHTH) for t in range(2)], axis=1)
         term = lax.dot_general(rows, w, (((0,), (0,)), ((), ())), preferred_element_type=F32)
-        start = eighths[n][1] * EIGHTH
-        out[:, pl.ds(pl.multiple_of(start, 128), QUARTER)] = term.astype(BF)
-
-
-def project(o, weights):
-    halves = len(weights) == 2
-    out = pl.pallas_call(
-        functools.partial(project_kernel, halves),
-        out_shape=jax.ShapeDtypeStruct((NY * ROWS, D), BF),
-        in_specs=[VM, HB, ANY][: 1 + len(weights)],
-        out_specs=VM,
-        scratch_shapes=[pltpu.VMEM((8, NZ, HD, EIGHTH), BF), pltpu.SemaphoreType.DMA((8,))],
+        put(pl.ds(pl.multiple_of(eighths[n][1] * EIGHTH, 128), QUARTER), term.astype(BF))
+
+
+def project_first_kernel(o, mine, other, out, wo1, weights, held, sems):
+    _, core, _, _ = position()
+    inner = pltpu.make_async_copy(mine.at[:, 4 * HD :, :], held, sems.at[8])
+    outer = pltpu.make_async_copy(held, wo1, sems.at[9])
+    inner.start()
+    eighths = [
+        (w.at[:, e * HD : (e + 1) * HD, :], 4 * side + e)
+        for w, side in ((mine, core), (other, 1 - core))
+        for e in range(4)
+    ]
+
+    def put(cols, term):
+        out[:, cols] = term
+
+    project_terms(o, eighths, weights, sems, put)
+    inner.wait()
+    outer.start()
+    outer.wait()
+
+
+def project_first(o, mine, other):
+    share = (NZ, HD, EIGHTH)
+    out, wo1 = pl.pallas_call(
+        project_first_kernel,
+        out_shape=[jax.ShapeDtypeStruct((NY * ROWS, D), BF), pltpu.HBM(share, BF)],
+        in_specs=[VM, HB, ANY],
+        out_specs=[VM, HB],
+        scratch_shapes=[pltpu.VMEM((8, *share), BF), pltpu.VMEM(share, BF), pltpu.SemaphoreType.DMA((10,))],
         compiler_params=params(12),
         cost_estimate=pl.CostEstimate(flops=420_000_000, bytes_accessed=4_000_000, transcendentals=0),
-        name="project_%d" % len(weights),
-    )(o, in_hbm(weights[0]), *weights[1:])
-    return out.reshape(NY, ROWS, D)
+        name="project_first",
+    )(o, in_hbm(mine), other)
+    return out.reshape(NY, ROWS, D), wo1
+
+
+def project_second_kernel(o, gathered, out0, out1, out2, out3, weights, held, sems):
+    _, _, _, y = position()
+
+    def put(cols, term):
+        held[:, :, cols] = term.reshape(NY, ROWS, QUARTER)
+
+    project_terms(o, [(gathered.at[s], s) for s in range(NX * NC)], weights, sems, put)
+    for j, out in enumerate((out0, out1, out2, out3)):
+        out[...] = held[lax.rem(y + j, NY)]
+
+
+def project_second(o, gathered):
+    share = (NZ, HD, EIGHTH)
+    return pl.pallas_call(
+        project_second_kernel,
+        out_shape=[jax.ShapeDtypeStruct((ROWS, D), BF)] * NY,
+        in_specs=[VM, HB],
+        out_specs=[VM] * NY,
+        scratch_shapes=[pltpu.VMEM((8, *share), BF), pltpu.VMEM((NY, ROWS, D), BF), pltpu.SemaphoreType.DMA((8,))],
+        compiler_params=params(12),
+        cost_estimate=pl.CostEstimate(flops=420_000_000, bytes_accessed=4_000_000, transcendentals=0),
+        name="project_second",
+    )(o, in_hbm(gathered))
 
 
 def added(layer, terms, mods, x):
-    attn = sum(terms[j].astype(F32) for j in range(NY))
+    attn = sum(term.astype(F32) for term in terms)
     gate = mods[3 * layer + 2 : 3 * layer + 3, :]
     return (x[...].astype(F32) + gate * attn).astype(BF)
 
 
 def residual_kernel(terms, mods, x, out):
-    out[...] = added(0, terms, mods, x)
+    out[...] = added(0, [terms[j] for j in range(NY)], mods, x)
 
 
 def residual(terms, mods, x):
@@ -366,9 +400,9 @@
     )(terms, mods, x)
 
 
-def last_kernel(terms, mods, x, noise, out, leaving, sem):
+def last_kernel(t0, t1, t2, t3, mods, x, noise, out, leaving, sem):
     x_pos, core, z, y = position()
-    value = added(1, terms, mods, x)
+    value = added(1, [t[...] for t in (t0, t1, t2, t3)], mods, x)
     out[...] = value
     head = jnp.logical_and(x_pos * NC + core == 0, z < NZ // 2)
 
@@ -389,13 +423,13 @@
     return pl.pallas_call(
         last_kernel,
         out_shape=[shape, shape],
-        in_specs=[VM] * 3 + [HB],
+        in_specs=[VM] * 6 + [HB],
         out_specs=[VM] * 2,
         scratch_shapes=[pltpu.SemaphoreType.DMA],
         compiler_params=params(8),
         cost_estimate=pl.CostEstimate(flops=600_000, bytes_accessed=1_600_000, transcendentals=0),
         name="last",
-    )(terms, mods, x, in_hbm(noise))
+    )(*terms, mods, x, in_hbm(noise))
 
 
 def from_ahead(block, axis, size, distance):
@@ -434,22 +468,30 @@
     high_1, high_3 = from_ahead(high, "x", NX, 1), from_ahead(high, "x", NX, 3)
     own = lax.all_to_all(heads, "y", 0, 0, tiled=True)
     own, high_1, high_3 = lax.optimization_barrier((own, high_1, high_3))
-    done = attention(own, *neighbours(own), gains[0:1])
-    done, wo, high, high_1, high_3 = lax.optimization_barrier((done, wo, high, high_1, high_3))
-    wo_s, high_2 = swap(wo), from_ahead(high_1, "x", NX, 1)
-    wo1 = lax.all_gather(wo[:, 4 * HD :], ("x", "core"), axis=0, tiled=False)
+    lower, upper = neighbours(own)
+    queries, acc, den = own_keys(own, gains[0:1])
+    lower, upper, acc, high_1 = lax.optimization_barrier((lower, upper, acc, high_1))
+    high_2 = from_ahead(high_1, "x", NX, 1)
+    done = neighbour_keys(lower, upper, queries, acc, den)
+    done, wo, high, high_1, high_2, high_3 = lax.optimization_barrier((done, wo, high, high_1, high_2, high_3))
+    wo_s = swap(wo)
     done = lax.all_to_all(done, "z", 0, 0, tiled=True)
-    done, wo_s, high_2 = lax.optimization_barrier((done, wo_s, high_2))
+    done, wo_s, high, high_1, high_2, high_3 = lax.optimization_barrier((done, wo_s, high, high_1, high_2, high_3))
     weights = [high, high_1, high_2, high_3]
     weights += [swap(w) for w in weights]
-    terms = lax.all_to_all(project(done, [wo, wo_s]), "y", 0, 0, tiled=True)
+    terms, wo1 = project_first(done, wo, wo_s)
+    wo1 = lax.all_gather(wo1, ("x", "core"), axis=0, tiled=False)
+    terms = lax.all_to_all(terms, "y", 0, 0, tiled=True)
     x1 = residual(terms, mods, x0)
 
     shards = [x1] + [from_ahead(x1, "y", NY, j) for j in range(1, NY)]
     heads = qkv_second(shards, mods, low, weights)
     own = lax.all_to_all(heads, "z", 0, 0, tiled=True)
-    done = lax.all_to_all(attention(own, *neighbours(own), gains[1:2]), "z", 0, 0, tiled=True)
-    terms = lax.all_to_all(project(done, [wo1]), "y", 0, 0, tiled=True)
+    lower, upper = neighbours(own)
+    done = neighbour_keys(lower, upper, *own_keys(own, gains[1:2]))
+    done = lax.all_to_all(done, "z", 0, 0, tiled=True)
+    terms = project_second(done, wo1)
+    terms = [terms[0]] + [from_ahead(terms[j], "y", NY, NY - j) for j in range(1, NY)]
     stream, leaving = last(terms, mods, x1, noise_frame)
 
     ranks = NX * NC * SEQ

time: 247 us -> 237 us (0.960)
  blocking collectives: 47 us -> 30.8 us
  starting transfers between devices: 34.9 us -> 42.8 us
  waiting for transfers between devices: 100 us -> 106 us
  local copies, waits for them, and re-layouts: 6.41 us -> 1.41 us
    all_to_all x1 -> x0, blocking collectives: 16.6 us -> none  [per_device(): terms = lax.all_to_all(project(done, [wo1]), 'y', 0, 0, tiled=True)]
    ppermute x9 -> x12, starting transfers between devices: 9.51 us -> 17 us  [from_ahead(): lax.ppermute(block, axis, [(i, (i - distance) % size) for i in range(size)])]
    all_gather x1, waiting for transfers between devices: 2.03 us -> 5.34 us  [per_device(): wo = lax.all_gather(wo, 'z', axis=0, tiled=False)]
    unnamed x15 -> x7, local copies, waits for them, and re-layouts: 4.55 us -> 1.33 us
    ppermute x9 -> x12, waiting for transfers between devices: 40.4 us -> 42.8 us  [from_ahead(): lax.ppermute(block, axis, [(i, (i - distance) % size) for i in range(size)])]
  transfers between devices with their start and end apart: 29 -> 32, of which waited for: 17 -> 19; matrix products, arithmetic and copies ran while one was open for 1% -> 0% of each run, Pallas kernels for 14% -> 14%
where the time goes in v7:
time: 237 us; the launch traced here: 236 us
  waiting for transfers between devices  106 us (45%)
  starting transfers between devices  42.8 us (18%)
  Pallas kernels  39.3 us (17%)
  blocking collectives  30.8 us (13%)
  between operations  14.7 us (6%)
    ppermute x12, waiting for transfers between devices, from_ahead(): lax.ppermute(block, axis, [(i, (i - distance) % size) for i in range(size)])  42.8 us
    all_to_all x1, blocking collectives, per_device(): own = lax.all_to_all(heads, 'z', 0, 0, tiled=True)  17.6 us
    ppermute x12, starting transfers between devices, from_ahead(): lax.ppermute(block, axis, [(i, (i - distance) % size) for i in range(size)])  17 us
    all_to_all x1, blocking collectives, per_device(): done = lax.all_to_all(done, 'z', 0, 0, tiled=True)  13.2 us
    ppermute x1, waiting for transfers between devices, per_device(): queue = lax.ppermute(leaving, ('x', 'core', 'z', 'y'), route)  12.7 us
    pallas_call x2, Pallas kernels, neighbour_keys(): pl.pallas_call(functools.partial(neighbours_kernel, per), out_shape=jax.S...  11.5 us
    ppermute x4, starting transfers between devices, shifted(): return lax.ppermute(block, axis, route)  11.1 us
    all_gather x1, waiting for transfers between devices, per_device(): later = lax.all_gather(pack, 'z', axis=0, tiled=False)  11 us
  transfers between devices with their start and end apart: 32, of which 19 were waited for; matrix products, arithmetic and copies ran while one was open for 0% of the time, Pallas kernels for 14%

profile of v7, /device:TPU:4, one launch (start us, length us, event | category | flops | bytes accessed | tf_op | source)
XLA Modules:
  0.0 235.6 jit_solution(8197923205680525820)
XLA Ops:
  7.9 2.9 %prepare.1 = (bf16[32,3072]{1,0:T(8,128)(2,1)S(1)}, bf16[448,384]{1,0:T(8,128)(2,1)}, bf16[192,1536]{1,0:T(8,128)(2,1)}, bf16[320,384]{1,0:T(8,128)(2,1)}) custom-call(s32[1,2]{1,0:T(1,128)S(1)} %copy-done.1, bf16[1,32,3072]{2,1,0:T(8,128)(2,1)} %latent.1, bf16[16,3072]{1,0:T(8,128)(2,1)} %pos.1, bf16[2,192,3072]{2,1,0:T(8,128)(2,1)} %bitcast.18, ...), custom_call_target="tpu_custom_call" | custom-call | flops 300000 | bytes 2500000 | tf_op jit(solution)/shard_map/prepare/pallas_call | solution.py:101
  10.9 0.7 all-gather.11.cloned.1.call-update
  11.6 3.1 %collective-permute-start = (bf16[192,1536]{1,0:T(8,128)(2,1)}, bf16[192,1536]{1,0:T(8,128)(2,1)S(1)}, u32[]{:S(2)}, u32[]{:S(2)}) collective-permute-start(bf16[192,1536]{1,0:T(8,128)(2,1)} %get-tuple-element.43), channel_id=1, source_target_pairs={{0,3},{1,0},{2,1},{3,2},{4,7},{5,4},{6,5},{7,6},{8,11},{9,8},{10,9... | collective-permute-start | bytes 1769480 | tf_op jit(solution)/shard_map/ppermute | solution.py:436
  15.3 1.0 collective-permute-start.2
  16.3 23.9 %collective-permute-done.refs_0_ = bf16[192,1536]{1,0:T(8,128)(2,1)S(1)} collective-permute-done((bf16[192,1536]{1,0:T(8,128)(2,1)}, bf16[192,1536]{1,0:T(8,128)(2,1)S(1)}, u32[]{:S(2)}, u32[]{:S(2)}) %collective-permute-start) | collective-permute-done | bytes 589856 | tf_op jit(solution)/shard_map/ppermute | solution.py:436
  40.8 3.1 %collective-permute-done.2.refs_2_ = bf16[192,1536]{1,0:T(8,128)(2,1)S(1)} collective-permute-done((bf16[192,1536]{1,0:T(8,128)(2,1)}, bf16[192,1536]{1,0:T(8,128)(2,1)S(1)}, u32[]{:S(2)}, u32[]{:S(2)}) %collective-permute-start.2) | collective-permute-done | bytes 589856 | tf_op jit(solution)/shard_map/ppermute | solution.py:436
  44.6 0.8 dynamic-slice_convert_fusion
  46.0 11.0 %all-gather.9.cloned.1.call-done = bf16[3584,384]{1,0:T(8,128)(2,1)} async-done(((bf16[448,384]{1,0:T(8,128)(2,1)}), bf16[3584,384]{1,0:T(8,128)(2,1)}) %all-gather.9.cloned.1.call-update) | async-done | bytes 2752528 | tf_op jit(solution)/shard_map/all_gather | solution.py:457
  57.0 5.3 %qkv_first.1 = (bf16[4,192,256]{2,1,0:T(8,128)(2,1)}, bf16[5,192,384]{2,1,0:T(8,128)(2,1)}, bf16[3,192,384]{2,1,0:T(8,128)(2,1)}) custom-call(bf16[8,448,384]{2,1,0:T(8,128)(2,1)} %bitcast.22, f32[6,3072]{1,0:T(8,128)S(1)} %reshape.15.mods, bf16[2,192,3072]{2,1,0:T(8,128)(2,1)} %bitcast.19, bf16[192,1536]{1,0:T(8,128)(2,1)S(1)} %collective-permute-done.refs_0_, ...), custom_call_target="tpu_custom_call" | custom-call | flops 1200000000 | bytes 14000000 | tf_op jit(solution)/shard_map/qkv_first/pallas_call | solution.py:156
  62.9 1.5 collective-permute-start.7
  64.4 4.3 %all-to-all-start = ((bf16[4,192,256]{2,1,0:T(8,128)(2,1)}), bf16[4,192,256]{2,1,0:T(8,128)(2,1)S(1)}, u32[]{:S(2)}, u32[]{:S(2)}) async-start(bf16[4,192,256]{2,1,0:T(8,128)(2,1)} %get-tuple-element.44), calls=%async_computation | async-start | bytes 786432 | tf_op jit(solution)/shard_map/all_to_all | solution.py:469
  68.7 7.4 %all-to-all-done.own = bf16[4,192,256]{2,1,0:T(8,128)(2,1)S(1)} async-done(((bf16[4,192,256]{2,1,0:T(8,128)(2,1)}), bf16[4,192,256]{2,1,0:T(8,128)(2,1)S(1)}, u32[]{:S(2)}, u32[]{:S(2)}) %all-to-all-start) | async-done | bytes 393248 | tf_op jit(solution)/shard_map/all_to_all | solution.py:469
  76.1 1.9 collective-permute-start.8
  78.0 3.6 %collective-permute-start.9 = (bf16[4,192,256]{2,1,0:T(8,128)(2,1)S(1)}, bf16[4,192,256]{2,1,0:T(8,128)(2,1)S(1)}, u32[]{:S(2)}, u32[]{:S(2)}) collective-permute-start(bf16[4,192,256]{2,1,0:T(8,128)(2,1)S(1)} %all-to-all-done.own), channel_id=1, source_target_pairs={{32,0},{64,32},{96,64},{128,96},{160,128},{192,160},{224,192},{33,... | collective-permute-start | bytes 1179656 | tf_op jit(solution)/shard_map/ppermute | solution.py:446
  81.7 2.3 own_1.1
  83.9 1.2 collective-permute-done.8.lower
  85.2 1.8 collective-permute-done.9.upper
  87.5 5.5 %neighbours_1.1 = bf16[8,64,128]{2,1,0:T(8,128)(2,1)S(1)} custom-call(bf16[4,192,256]{2,1,0:T(8,128)(2,1)S(1)} %collective-permute-done.8.lower, bf16[4,192,256]{2,1,0:T(8,128)(2,1)S(1)} %collective-permute-done.9.upper, bf16[4,64,256]{2,1,0:T(8,128)(2,1)S(1)} %get-tuple-element.51.queries, f32[4,64,256]{2,1,0:T(8,128)S(1)} %get-tuple-element.52.acc_in, ...), custom_call_target="tpu_custom_call" | custom-call | flops 6000000000 | bytes 1200000 | tf_op jit(solution)/shard_map/neighbours_1/pallas_call | solution.py:296
  93.0 5.3 %all-gather.11.cloned.1.call-done = bf16[2560,384]{1,0:T(8,128)(2,1)} async-done(((bf16[320,384]{1,0:T(8,128)(2,1)}), bf16[2560,384]{1,0:T(8,128)(2,1)}) %all-gather.11.cloned.1.call-update) | async-done | bytes 1966096 | tf_op jit(solution)/shard_map/all_gather | solution.py:458
  98.5 1.6 collective-permute-start.11
  100.1 13.2 %all_to_all.25.o = bf16[8,64,128]{2,1,0:T(8,128)(2,1)S(1)} all-to-all(bf16[8,64,128]{2,1,0:T(8,128)(2,1)S(1)} %neighbours_1.1), channel_id=1, replica_groups=mesh['x'=4,'core'=2,'z'=8,'y'=4] {'z'}, dimensions={0} | all-to-all | bytes 262144 | tf_op jit(solution)/shard_map/all_to_all | solution.py:478
  113.4 4.3 %project_first.1 = (bf16[128,3072]{1,0:T(8,128)(2,1)}, bf16[8,64,384]{2,1,0:T(8,128)(2,1)}) custom-call(bf16[8,64,128]{2,1,0:T(8,128)(2,1)S(1)} %all_to_all.25.o, bf16[8,320,384]{2,1,0:T(8,128)(2,1)} %bitcast.24, bf16[8,320,384]{2,1,0:T(8,128)(2,1)S(1)} %collective-permute-done.11.other), custom_call_target="tpu_custom_call" | custom-call | flops 420000000 | bytes 4000000 | tf_op jit(solution)/shard_map/project_first/pallas_call | solution.py:343
  117.7 3.5 %all-to-all-start.2 = ((bf16[4,32,3072]{2,1,0:T(8,128)(2,1)}), bf16[4,32,3072]{2,1,0:T(8,128)(2,1)S(1)}, u32[]{:S(2)}, u32[]{:S(2)}) async-start(bf16[4,32,3072]{2,1,0:T(8,128)(2,1)} %bitcast.6), calls=%async_computation.2 | async-start | bytes 1572864 | tf_op jit(solution)/shard_map/all_to_all | solution.py:484
  122.3 10.1 %all-to-all-done.2.terms = bf16[4,32,3072]{2,1,0:T(8,128)(2,1)S(1)} async-done(((bf16[4,32,3072]{2,1,0:T(8,128)(2,1)}), bf16[4,32,3072]{2,1,0:T(8,128)(2,1)S(1)}, u32[]{:S(2)}, u32[]{:S(2)}) %all-to-all-start.2) | async-done | bytes 786464 | tf_op jit(solution)/shard_map/all_to_all | solution.py:484
  132.6 1.2 collective-permute-start.12
  133.8 1.5 collective-permute-start.13
  135.4 3.5 %collective-permute-done.12.x1 = bf16[32,3072]{1,0:T(8,128)(2,1)S(1)} collective-permute-done((bf16[32,3072]{1,0:T(8,128)(2,1)S(1)}, bf16[32,3072]{1,0:T(8,128)(2,1)S(1)}, u32[]{:S(2)}, u32[]{:S(2)}) %collective-permute-start.12) | collective-permute-done | bytes 196640 | tf_op jit(solution)/shard_map/ppermute | solution.py:436
  138.9 2.5 %collective-permute-done.13.x2 = bf16[32,3072]{1,0:T(8,128)(2,1)S(1)} collective-permute-done((bf16[32,3072]{1,0:T(8,128)(2,1)S(1)}, bf16[32,3072]{1,0:T(8,128)(2,1)S(1)}, u32[]{:S(2)}, u32[]{:S(2)}) %collective-permute-start.13) | collective-permute-done | bytes 196640 | tf_op jit(solution)/shard_map/ppermute | solution.py:436
  141.4 2.0 collective-permute-done.14.x3
  143.4 7.4 %qkv_second.1 = bf16[8,192,128]{2,1,0:T(8,128)(2,1)S(1)} custom-call(bf16[32,3072]{1,0:T(8,128)(2,1)S(1)} %residual.1.x0.x, bf16[32,3072]{1,0:T(8,128)(2,1)S(1)} %collective-permute-done.12.x1, bf16[32,3072]{1,0:T(8,128)(2,1)S(1)} %collective-permute-done.13.x2, bf16[32,3072]{1,0:T(8,128)(2,1)S(1)} %collective-permute-done.14.x3, ...), custom_call_target="tpu_custom_call" | custom-call | flops 1200000000 | bytes 10500000 | tf_op jit(solution)/shard_map/qkv_second/pallas_call | solution.py:202
  150.8 17.6 %all_to_all.26.own = bf16[8,192,128]{2,1,0:T(8,128)(2,1)S(1)} all-to-all(bf16[8,192,128]{2,1,0:T(8,128)(2,1)S(1)} %qkv_second.1), channel_id=1, replica_groups=mesh['x'=4,'core'=2,'z'=8,'y'=4] {'z'}, dimensions={0} | all-to-all | bytes 786432 | tf_op jit(solution)/shard_map/all_to_all | solution.py:489
  168.4 1.9 collective-permute-start.19
  170.3 3.6 %collective-permute-start.20 = (bf16[8,192,128]{2,1,0:T(8,128)(2,1)S(1)}, bf16[8,192,128]{2,1,0:T(8,128)(2,1)S(1)}, u32[]{:S(2)}, u32[]{:S(2)}) collective-permute-start(bf16[8,192,128]{2,1,0:T(8,128)(2,1)S(1)} %all_to_all.26.own), channel_id=1, source_target_pairs={{32,0},{64,32},{96,64},{128,96},{160,128},{192,160},{224,192},{33,... | collective-permute-start | bytes 1179656 | tf_op jit(solution)/shard_map/ppermute | solution.py:446
  174.0 2.3 own_2.1
  176.3 1.2 collective-permute-done.19.lower
  177.5 1.8 collective-permute-done.20.upper
  179.2 6.0 %neighbours_2.1 = bf16[8,64,128]{2,1,0:T(8,128)(2,1)} custom-call(bf16[8,192,128]{2,1,0:T(8,128)(2,1)S(1)} %collective-permute-done.19.lower, bf16[8,192,128]{2,1,0:T(8,128)(2,1)S(1)} %collective-permute-done.20.upper, bf16[4,64,256]{2,1,0:T(8,128)(2,1)S(1)} %get-tuple-element.72.queries, f32[4,64,256]{2,1,0:T(8,128)S(1)} %get-tuple-element.73.acc_in, ...), custom_call_target="tpu_custom_call" | custom-call | flops 6000000000 | bytes 1200000 | tf_op jit(solution)/shard_map/neighbours_2/pallas_call | solution.py:296
  185.2 3.4 %all-to-all-start.4 = ((bf16[8,64,128]{2,1,0:T(8,128)(2,1)}), bf16[8,64,128]{2,1,0:T(8,128)(2,1)S(1)}, u32[]{:S(2)}, u32[]{:S(2)}) async-start(bf16[8,64,128]{2,1,0:T(8,128)(2,1)} %neighbours_2.1), calls=%async_computation.4 | async-start | bytes 262144 | tf_op jit(solution)/shard_map/all_to_all | solution.py:492
  188.6 9.2 %all-to-all-done.4.o = bf16[8,64,128]{2,1,0:T(8,128)(2,1)S(1)} async-done(((bf16[8,64,128]{2,1,0:T(8,128)(2,1)}), bf16[8,64,128]{2,1,0:T(8,128)(2,1)S(1)}, u32[]{:S(2)}, u32[]{:S(2)}) %all-to-all-start.4) | async-done | bytes 131104 | tf_op jit(solution)/shard_map/all_to_all | solution.py:492
  197.8 2.4 %project_second.1 = (bf16[32,3072]{1,0:T(8,128)(2,1)S(1)}, bf16[32,3072]{1,0:T(8,128)(2,1)S(1)}, bf16[32,3072]{1,0:T(8,128)(2,1)S(1)}, bf16[32,3072]{1,0:T(8,128)(2,1)S(1)}) custom-call(bf16[8,64,128]{2,1,0:T(8,128)(2,1)S(1)} %all-to-all-done.4.o, bf16[8,8,64,384]{3,2,1,0:T(8,128)(2,1)} %bitcast.21), custom_call_target="tpu_custom_call" | custom-call | flops 420000000 | bytes 4000000 | tf_op jit(solution)/shard_map/project_second/pallas_call | solution.py:369
  200.3 2.6 %collective-permute-start.21 = (bf16[32,3072]{1,0:T(8,128)(2,1)S(1)}, bf16[32,3072]{1,0:T(8,128)(2,1)S(1)}, u32[]{:S(2)}, u32[]{:S(2)}) collective-permute-start(bf16[32,3072]{1,0:T(8,128)(2,1)S(1)} %get-tuple-element.77), channel_id=1, source_target_pairs={{0,1},{1,2},{2,3},{3,0},{4,5},{5,6},{6,7},{7,4},{8,9},{9,10},{10,1... | collective-permute-start | bytes 589832 | tf_op jit(solution)/shard_map/ppermute | solution.py:436
  202.8 2.7 %collective-permute-start.22 = (bf16[32,3072]{1,0:T(8,128)(2,1)S(1)}, bf16[32,3072]{1,0:T(8,128)(2,1)S(1)}, u32[]{:S(2)}, u32[]{:S(2)}) collective-permute-start(bf16[32,3072]{1,0:T(8,128)(2,1)S(1)} %get-tuple-element.78), channel_id=1, source_target_pairs={{0,2},{1,3},{2,0},{3,1},{4,6},{5,7},{6,4},{7,5},{8,10},{9,11},{10,... | collective-permute-start | bytes 589832 | tf_op jit(solution)/shard_map/ppermute | solution.py:436
  205.6 1.5 collective-permute-start.23
  207.1 2.2 collective-permute-done.21.t1
  209.4 5.3 %collective-permute-done.22.t2 = bf16[32,3072]{1,0:T(8,128)(2,1)S(1)} collective-permute-done((bf16[32,3072]{1,0:T(8,128)(2,1)S(1)}, bf16[32,3072]{1,0:T(8,128)(2,1)S(1)}, u32[]{:S(2)}, u32[]{:S(2)}) %collective-permute-start.22) | collective-permute-done | bytes 196640 | tf_op jit(solution)/shard_map/ppermute | solution.py:436
  214.7 0.8 last.1
  215.6 12.7 %collective-permute-done.24 = bf16[32,3072]{1,0:T(8,128)(2,1)S(1)} collective-permute-done((bf16[32,3072]{1,0:T(8,128)(2,1)S(1)}, bf16[32,3072]{1,0:T(8,128)(2,1)S(1)}, u32[]{:S(2)}, u32[]{:S(2)}) %collective-permute-start.24) | collective-permute-done | bytes 196640 | tf_op jit(solution)/shard_map/ppermute | solution.py:499
  228.4 0.7 copy.16
  (45 shorter events, 5.4 us)
Async XLA Ops:
  7.2 49.8 %all-gather.9.cloned.1.call-start = ((), (), s32[]{:S(2)}) async-start(), calls=%async_computation.5 | async-start | bytes 3096576 | tf_op jit(solution)/shard_map/all_gather | solution.py:457
  7.2 0.7 copy-start.1
  10.8 87.5 %all-gather.11.cloned.1.call-start = ((), (), s32[]{:S(2)}) async-start(), calls=%async_computation.6 | async-start | bytes 2211840 | tf_op jit(solution)/shard_map/all_gather | solution.py:458
  11.6 131.8 %all-gather.13.cloned.1.call-start = ((), (), s32[]{:S(2)}) async-start(), calls=%async_computation.7 | async-start | bytes 6635520 | tf_op jit(solution)/shard_map/all_gather | solution.py:467
  11.6 28.6 %collective-permute-start = (bf16[192,1536]{1,0:T(8,128)(2,1)}, bf16[192,1536]{1,0:T(8,128)(2,1)S(1)}, u32[]{:S(2)}, u32[]{:S(2)}) collective-permute-start(bf16[192,1536]{1,0:T(8,128)(2,1)} %get-tuple-element.43), channel_id=1, source_target_pairs={{0,3},{1,0},{2,1},{3,2},{4,7},{5,4},{6,5},{7,6},{8,11},{9,8},{10,9... | collective-permute-start | bytes 1769480 | tf_op jit(solution)/shard_map/ppermute | solution.py:436
  14.7 25.5 %collective-permute-start.1 = (bf16[192,1536]{1,0:T(8,128)(2,1)}, bf16[192,1536]{1,0:T(8,128)(2,1)S(1)}, u32[]{:S(2)}, u32[]{:S(2)}) collective-permute-start(bf16[192,1536]{1,0:T(8,128)(2,1)} %get-tuple-element.43), channel_id=1, source_target_pairs={{0,2},{1,3},{2,0},{3,1},{4,6},{5,7},{6,4},{7,5},{8,10},{9,11},{10,... | collective-permute-start | bytes 1769480 | tf_op jit(solution)/shard_map/ppermute | solution.py:436
  15.3 28.5 %collective-permute-start.2 = (bf16[192,1536]{1,0:T(8,128)(2,1)}, bf16[192,1536]{1,0:T(8,128)(2,1)S(1)}, u32[]{:S(2)}, u32[]{:S(2)}) collective-permute-start(bf16[192,1536]{1,0:T(8,128)(2,1)} %get-tuple-element.43), channel_id=1, source_target_pairs={{0,1},{1,2},{2,3},{3,0},{4,5},{5,6},{6,7},{7,4},{8,9},{9,10},{10,1... | collective-permute-start | bytes 1769480 | tf_op jit(solution)/shard_map/ppermute | solution.py:436
  40.2 5.3 %collective-permute-start.3 = (bf16[192,1536]{1,0:T(8,128)(2,1)S(1)}, bf16[192,1536]{1,0:T(8,128)(2,1)S(1)}, u32[]{:S(2)}, u32[]{:S(2)}) collective-permute-start(bf16[192,1536]{1,0:T(8,128)(2,1)S(1)} %collective-permute-done.refs_0_), channel_id=1, source_target_pairs={{0,32},{32,0},{1,33},{33,1},{2,34},{34,2},{3,35},{35,3},{4,36},{36... | collective-permute-start | bytes 1769480 | tf_op jit(solution)/shard_map/ppermute | solution.py:440
  40.3 5.3 %collective-permute-start.4 = (bf16[192,1536]{1,0:T(8,128)(2,1)S(1)}, bf16[192,1536]{1,0:T(8,128)(2,1)S(1)}, u32[]{:S(2)}, u32[]{:S(2)}) collective-permute-start(bf16[192,1536]{1,0:T(8,128)(2,1)S(1)} %collective-permute-done.1.refs_1_), channel_id=1, source_target_pairs={{0,32},{32,0},{1,33},{33,1},{2,34},{34,2},{3,35},{35,3},{4,36},{36... | collective-permute-start | bytes 1769480 | tf_op jit(solution)/shard_map/ppermute | solution.py:440
  43.8 2.1 collective-permute-start.5
  57.0 11.7 %copy-start.2 = (bf16[2,1,128]{2,0,1:T(2,128)(2,1)S(1)}, bf16[2,1,128]{2,0,1:T(2,128)(2,1)}, u32[]{:S(2)}) copy-start(bf16[2,1,128]{2,0,1:T(2,128)(2,1)} %param.16) | copy-start | bytes 1540
  62.3 13.8 %collective-permute-start.6 = (bf16[3,192,384]{2,1,0:T(8,128)(2,1)}, bf16[3,192,384]{2,1,0:T(8,128)(2,1)S(1)}, u32[]{:S(2)}, u32[]{:S(2)}) collective-permute-start(bf16[3,192,384]{2,1,0:T(8,128)(2,1)} %get-tuple-element.68.refs_0_), channel_id=1, source_target_pairs={{0,192},{64,0},{128,64},{192,128},{1,193},{65,1},{129,65},{193,129... | collective-permute-start | bytes 1327112 | tf_op jit(solution)/shard_map/ppermute | solution.py:436
  62.9 13.1 %collective-permute-start.7 = (bf16[3,192,384]{2,1,0:T(8,128)(2,1)}, bf16[3,192,384]{2,1,0:T(8,128)(2,1)S(1)}, u32[]{:S(2)}, u32[]{:S(2)}) collective-permute-start(bf16[3,192,384]{2,1,0:T(8,128)(2,1)} %get-tuple-element.68.refs_0_), channel_id=1, source_target_pairs={{0,64},{64,128},{128,192},{192,0},{1,65},{65,129},{129,193},{193,1... | collective-permute-start | bytes 1327112 | tf_op jit(solution)/shard_map/ppermute | solution.py:436
  64.4 11.7 %all-to-all-start = ((bf16[4,192,256]{2,1,0:T(8,128)(2,1)}), bf16[4,192,256]{2,1,0:T(8,128)(2,1)S(1)}, u32[]{:S(2)}, u32[]{:S(2)}) async-start(bf16[4,192,256]{2,1,0:T(8,128)(2,1)} %get-tuple-element.44), calls=%async_computation | async-start | bytes 786432 | tf_op jit(solution)/shard_map/all_to_all | solution.py:469
  68.7 119.9 %all-gather.15.cloned.1.call-start = ((), (), s32[]{:S(2)}) async-start(), calls=%async_computation.8 | async-start | bytes 3538944 | tf_op jit(solution)/shard_map/all_gather | solution.py:483
  76.1 9.1 %collective-permute-start.8 = (bf16[4,192,256]{2,1,0:T(8,128)(2,1)S(1)}, bf16[4,192,256]{2,1,0:T(8,128)(2,1)S(1)}, u32[]{:S(2)}, u32[]{:S(2)}) collective-permute-start(bf16[4,192,256]{2,1,0:T(8,128)(2,1)S(1)} %all-to-all-done.own), channel_id=1, source_target_pairs={{0,32},{32,64},{64,96},{96,128},{128,160},{160,192},{192,224},{1,3... | collective-permute-start | bytes 1179656 | tf_op jit(solution)/shard_map/ppermute | solution.py:446
  78.0 8.9 %collective-permute-start.9 = (bf16[4,192,256]{2,1,0:T(8,128)(2,1)S(1)}, bf16[4,192,256]{2,1,0:T(8,128)(2,1)S(1)}, u32[]{:S(2)}, u32[]{:S(2)}) collective-permute-start(bf16[4,192,256]{2,1,0:T(8,128)(2,1)S(1)} %all-to-all-done.own), channel_id=1, source_target_pairs={{32,0},{64,32},{96,64},{128,96},{160,128},{192,160},{224,192},{33,... | collective-permute-start | bytes 1179656 | tf_op jit(solution)/shard_map/ppermute | solution.py:446
  86.9 11.6 %collective-permute-start.10 = (bf16[3,192,384]{2,1,0:T(8,128)(2,1)S(1)}, bf16[3,192,384]{2,1,0:T(8,128)(2,1)S(1)}, u32[]{:S(2)}, u32[]{:S(2)}) collective-permute-start(bf16[3,192,384]{2,1,0:T(8,128)(2,1)S(1)} %collective-permute-done.6.refs_1_), channel_id=1, source_target_pairs={{0,192},{64,0},{128,64},{192,128},{1,193},{65,1},{129,65},{193,129... | collective-permute-start | bytes 1327112 | tf_op jit(solution)/shard_map/ppermute | solution.py:436
  98.5 14.8 %collective-permute-start.11 = (bf16[8,320,384]{2,1,0:T(8,128)(2,1)}, bf16[8,320,384]{2,1,0:T(8,128)(2,1)S(1)}, u32[]{:S(2)}, u32[]{:S(2)}) collective-permute-start(bf16[8,320,384]{2,1,0:T(8,128)(2,1)} %bitcast.23), channel_id=1, source_target_pairs={{0,32},{32,0},{1,33},{33,1},{2,34},{34,2},{3,35},{35,3},{4,36},{36... | collective-permute-start | bytes 5898248 | tf_op jit(solution)/shard_map/ppermute | solution.py:440
  113.4 7.8 %copy-start = (bf16[3,192,384]{2,1,0:T(8,128)(2,1)S(1)}, bf16[3,192,384]{2,1,0:T(8,128)(2,1)}, u32[]{:S(2)}) copy-start(bf16[3,192,384]{2,1,0:T(8,128)(2,1)} %get-tuple-element.68.refs_0_) | copy-start | bytes 1327108
  117.7 14.8 %all-to-all-start.2 = ((bf16[4,32,3072]{2,1,0:T(8,128)(2,1)}), bf16[4,32,3072]{2,1,0:T(8,128)(2,1)S(1)}, u32[]{:S(2)}, u32[]{:S(2)}) async-start(bf16[4,32,3072]{2,1,0:T(8,128)(2,1)} %bitcast.6), calls=%async_computation.2 | async-start | bytes 1572864 | tf_op jit(solution)/shard_map/all_to_all | solution.py:484
  121.2 12.6 %collective-permute-start.15 = (bf16[3,192,384]{2,1,0:T(8,128)(2,1)S(1)}, bf16[3,192,384]{2,1,0:T(8,128)(2,1)S(1)}, u32[]{:S(2)}, u32[]{:S(2)}) collective-permute-start(bf16[3,192,384]{2,1,0:T(8,128)(2,1)S(1)} %copy-done), channel_id=1, source_target_pairs={{0,32},{32,0},{1,33},{33,1},{2,34},{34,2},{3,35},{35,3},{4,36},{36... | collective-permute-start | bytes 1327112 | tf_op jit(solution)/shard_map/ppermute | solution.py:440
  121.3 14.1 %collective-permute-start.16 = (bf16[3,192,384]{2,1,0:T(8,128)(2,1)S(1)}, bf16[3,192,384]{2,1,0:T(8,128)(2,1)}, u32[]{:S(2)}, u32[]{:S(2)}) collective-permute-start(bf16[3,192,384]{2,1,0:T(8,128)(2,1)S(1)} %collective-permute-done.6.refs_1_), channel_id=1, source_target_pairs={{0,32},{32,0},{1,33},{33,1},{2,34},{34,2},{3,35},{35,3},{4,36},{36... | collective-permute-start | bytes 1327112 | tf_op jit(solution)/shard_map/ppermute | solution.py:440
  121.8 13.6 %collective-permute-start.17 = (bf16[3,192,384]{2,1,0:T(8,128)(2,1)S(1)}, bf16[3,192,384]{2,1,0:T(8,128)(2,1)}, u32[]{:S(2)}, u32[]{:S(2)}) collective-permute-start(bf16[3,192,384]{2,1,0:T(8,128)(2,1)S(1)} %collective-permute-done.10.refs_2_), channel_id=1, source_target_pairs={{0,32},{32,0},{1,33},{33,1},{2,34},{34,2},{3,35},{35,3},{4,36},{36... | collective-permute-start | bytes 1327112 | tf_op jit(solution)/shard_map/ppermute | solution.py:440
  121.9 13.5 %collective-permute-start.18 = (bf16[3,192,384]{2,1,0:T(8,128)(2,1)S(1)}, bf16[3,192,384]{2,1,0:T(8,128)(2,1)}, u32[]{:S(2)}, u32[]{:S(2)}) collective-permute-start(bf16[3,192,384]{2,1,0:T(8,128)(2,1)S(1)} %collective-permute-done.7.refs_3_), channel_id=1, source_target_pairs={{0,32},{32,0},{1,33},{33,1},{2,34},{34,2},{3,35},{35,3},{4,36},{36... | collective-permute-start | bytes 1327112 | tf_op jit(solution)/shard_map/ppermute | solution.py:440
  132.6 6.3 %collective-permute-start.12 = (bf16[32,3072]{1,0:T(8,128)(2,1)S(1)}, bf16[32,3072]{1,0:T(8,128)(2,1)S(1)}, u32[]{:S(2)}, u32[]{:S(2)}) collective-permute-start(bf16[32,3072]{1,0:T(8,128)(2,1)S(1)} %residual.1.x0.x), channel_id=1, source_target_pairs={{0,3},{1,0},{2,1},{3,2},{4,7},{5,4},{6,5},{7,6},{8,11},{9,8},{10,9... | collective-permute-start | bytes 589832 | tf_op jit(solution)/shard_map/ppermute | solution.py:436
  133.8 7.6 %collective-permute-start.13 = (bf16[32,3072]{1,0:T(8,128)(2,1)S(1)}, bf16[32,3072]{1,0:T(8,128)(2,1)S(1)}, u32[]{:S(2)}, u32[]{:S(2)}) collective-permute-start(bf16[32,3072]{1,0:T(8,128)(2,1)S(1)} %residual.1.x0.x), channel_id=1, source_target_pairs={{0,2},{1,3},{2,0},{3,1},{4,6},{5,7},{6,4},{7,5},{8,10},{9,11},{10,... | collective-permute-start | bytes 589832 | tf_op jit(solution)/shard_map/ppermute | solution.py:436
  135.3 8.1 %collective-permute-start.14 = (bf16[32,3072]{1,0:T(8,128)(2,1)S(1)}, bf16[32,3072]{1,0:T(8,128)(2,1)S(1)}, u32[]{:S(2)}, u32[]{:S(2)}) collective-permute-start(bf16[32,3072]{1,0:T(8,128)(2,1)S(1)} %residual.1.x0.x), channel_id=1, source_target_pairs={{0,1},{1,2},{2,3},{3,0},{4,5},{5,6},{6,7},{7,4},{8,9},{9,10},{10,1... | collective-permute-start | bytes 589832 | tf_op jit(solution)/shard_map/ppermute | solution.py:436
  168.4 9.1 %collective-permute-start.19 = (bf16[8,192,128]{2,1,0:T(8,128)(2,1)S(1)}, bf16[8,192,128]{2,1,0:T(8,128)(2,1)S(1)}, u32[]{:S(2)}, u32[]{:S(2)}) collective-permute-start(bf16[8,192,128]{2,1,0:T(8,128)(2,1)S(1)} %all_to_all.26.own), channel_id=1, source_target_pairs={{0,32},{32,64},{64,96},{96,128},{128,160},{160,192},{192,224},{1,3... | collective-permute-start | bytes 1179656 | tf_op jit(solution)/shard_map/ppermute | solution.py:446
  170.3 8.9 %collective-permute-start.20 = (bf16[8,192,128]{2,1,0:T(8,128)(2,1)S(1)}, bf16[8,192,128]{2,1,0:T(8,128)(2,1)S(1)}, u32[]{:S(2)}, u32[]{:S(2)}) collective-permute-start(bf16[8,192,128]{2,1,0:T(8,128)(2,1)S(1)} %all_to_all.26.own), channel_id=1, source_target_pairs={{32,0},{64,32},{96,64},{128,96},{160,128},{192,160},{224,192},{33,... | collective-permute-start | bytes 1179656 | tf_op jit(solution)/shard_map/ppermute | solution.py:446
  185.2 12.6 %all-to-all-start.4 = ((bf16[8,64,128]{2,1,0:T(8,128)(2,1)}), bf16[8,64,128]{2,1,0:T(8,128)(2,1)S(1)}, u32[]{:S(2)}, u32[]{:S(2)}) async-start(bf16[8,64,128]{2,1,0:T(8,128)(2,1)} %neighbours_2.1), calls=%async_computation.4 | async-start | bytes 262144 | tf_op jit(solution)/shard_map/all_to_all | solution.py:492
  200.3 9.1 %collective-permute-start.21 = (bf16[32,3072]{1,0:T(8,128)(2,1)S(1)}, bf16[32,3072]{1,0:T(8,128)(2,1)S(1)}, u32[]{:S(2)}, u32[]{:S(2)}) collective-permute-start(bf16[32,3072]{1,0:T(8,128)(2,1)S(1)} %get-tuple-element.77), channel_id=1, source_target_pairs={{0,1},{1,2},{2,3},{3,0},{4,5},{5,6},{6,7},{7,4},{8,9},{9,10},{10,1... | collective-permute-start | bytes 589832 | tf_op jit(solution)/shard_map/ppermute | solution.py:436
  202.8 11.8 %collective-permute-start.22 = (bf16[32,3072]{1,0:T(8,128)(2,1)S(1)}, bf16[32,3072]{1,0:T(8,128)(2,1)S(1)}, u32[]{:S(2)}, u32[]{:S(2)}) collective-permute-start(bf16[32,3072]{1,0:T(8,128)(2,1)S(1)} %get-tuple-element.78), channel_id=1, source_target_pairs={{0,2},{1,3},{2,0},{3,1},{4,6},{5,7},{6,4},{7,5},{8,10},{9,11},{10,... | collective-permute-start | bytes 589832 | tf_op jit(solution)/shard_map/ppermute | solution.py:436
  205.6 9.1 %collective-permute-start.23 = (bf16[32,3072]{1,0:T(8,128)(2,1)S(1)}, bf16[32,3072]{1,0:T(8,128)(2,1)S(1)}, u32[]{:S(2)}, u32[]{:S(2)}) collective-permute-start(bf16[32,3072]{1,0:T(8,128)(2,1)S(1)} %get-tuple-element.79), channel_id=1, source_target_pairs={{0,3},{1,0},{2,1},{3,2},{4,7},{5,4},{6,5},{7,6},{8,11},{9,8},{10,9... | collective-permute-start | bytes 589832 | tf_op jit(solution)/shard_map/ppermute | solution.py:436
  215.5 12.8 %collective-permute-start.24 = (bf16[32,3072]{1,0:T(8,128)(2,1)S(1)}, bf16[32,3072]{1,0:T(8,128)(2,1)S(1)}, u32[]{:S(2)}, u32[]{:S(2)}) collective-permute-start(bf16[32,3072]{1,0:T(8,128)(2,1)S(1)} %get-tuple-element.81), channel_id=1, source_target_pairs={{0,240},{1,241},{2,242},{3,243},{4,244},{5,245},{6,246},{7,247},{8... | collective-permute-start | bytes 589832 | tf_op jit(solution)/shard_map/ppermute | solution.py:499
Sparse Core Ops, SparseCore 0:
  10.9 46.0 all-gather.8
  58.8 39.4 all-gather.10
  100.2 38.8 all-gather.12
  140.8 30.3 all-gather.14

commit v8 on v7

--- a/solution.py
+++ b/solution.py
@@ -63,24 +63,18 @@
     return lax.dot_general(weight, h, (((1,), (1,)), ((), ())), preferred_element_type=F32)
 
 
-def prepare_kernel(frame_pos, latent, pos, w_t, w_out, x0, pack, half, wo, x, table, sems):
+def columns(start, width):
+    return pl.ds(pl.multiple_of(start, 128), width)
+
+
+def prepare_kernel(frame_pos, latent, pos, w_t, x0, pack, x, table, sems):
     x_pos, core, z, _ = position()
-
-    def columns(start, width):
-        return pl.ds(pl.multiple_of(start, 128), width)
-
-    eighth = columns((x_pos * NC + core) * EIGHTH, EIGHTH)
-    copies = [
+    pairs = [
         (latent.at[0], x),
         (pos, table),
-        (w_t.at[1, :, eighth], pack.at[PACK[0] :, :]),
-        (w_t.at[0, :, columns(core * (D // 2), D // 2)], half),
+        (w_t.at[1, :, columns((x_pos * NC + core) * EIGHTH, EIGHTH)], pack.at[PACK[0] :, :]),
     ]
-    for e in range(4):
-        part = columns((4 * core + e) * EIGHTH, EIGHTH)
-        copies.append((w_out.at[0, :, part], wo.at[e * HD : (e + 1) * HD, :]))
-    copies.append((w_out.at[1, :, eighth], wo.at[4 * HD :, :]))
-    copies = [pltpu.make_async_copy(*pair, sems.at[n]) for n, pair in enumerate(copies)]
+    copies = [pltpu.make_async_copy(*pair, sems.at[n]) for n, pair in enumerate(pairs)]
     for copy in copies:
         copy.start()
     frame = jnp.where(z >= NZ // 2, frame_pos[0, 1], frame_pos[0, 0])
@@ -92,26 +86,50 @@
     x0[...] = value
     for e in range(8):
         pack[e * ROWS : (e + 1) * ROWS, :] = value[:, e * EIGHTH : (e + 1) * EIGHTH]
-    for copy in copies[2:]:
-        copy.wait()
-
-
-def prepare(frame_pos, latent, pos, w_t, w_out):
-    shapes = ((ROWS, D), (sum(PACK), EIGHTH), (3 * HD, D // 2), (5 * HD, EIGHTH))
+    copies[2].wait()
+
+
+def prepare(frame_pos, latent, pos, w_t):
     return pl.pallas_call(
         prepare_kernel,
-        out_shape=[jax.ShapeDtypeStruct(shape, BF) for shape in shapes],
-        in_specs=[SM] + [HB] * 4,
-        out_specs=[VM] * 4,
+        out_shape=[jax.ShapeDtypeStruct(shape, BF) for shape in ((ROWS, D), (sum(PACK), EIGHTH))],
+        in_specs=[SM] + [HB] * 3,
+        out_specs=[VM] * 2,
         scratch_shapes=[
             pltpu.VMEM((ROWS, D), BF),
             pltpu.VMEM((NF, D), BF),
-            pltpu.SemaphoreType.DMA((9,)),
+            pltpu.SemaphoreType.DMA((3,)),
         ],
         compiler_params=params(8),
-        cost_estimate=pl.CostEstimate(flops=300_000, bytes_accessed=2_500_000, transcendentals=0),
+        cost_estimate=pl.CostEstimate(flops=300_000, bytes_accessed=800_000, transcendentals=0),
         name="prepare",
-    )(frame_pos, *map(in_hbm, (latent, pos, w_t, w_out)))
+    )(frame_pos, *map(in_hbm, (latent, pos, w_t)))
+
+
+def shares_kernel(w_t, w_out, half, wo, sems):
+    x_pos, core, _, _ = position()
+    pairs = [(w_t.at[0, :, columns(core * (D // 2), D // 2)], half)]
+    for e in range(4):
+        pairs.append((w_out.at[0, :, columns((4 * core + e) * EIGHTH, EIGHTH)], wo.at[e * HD : (e + 1) * HD, :]))
+    pairs.append((w_out.at[1, :, columns((x_pos * NC + core) * EIGHTH, EIGHTH)], wo.at[4 * HD :, :]))
+    copies = [pltpu.make_async_copy(*pair, sems.at[n]) for n, pair in enumerate(pairs)]
+    for copy in copies:
+        copy.start()
+    for copy in copies:
+        copy.wait()
+
+
+def shares(w_t, w_out):
+    return pl.pallas_call(
+        shares_kernel,
+        out_shape=[jax.ShapeDtypeStruct(shape, BF) for shape in ((3 * HD, D // 2), (5 * HD, EIGHTH))],
+        in_specs=[HB] * 2,
+        out_specs=[VM] * 2,
+        scratch_shapes=[pltpu.SemaphoreType.DMA((6,))],
+        compiler_params=params(8),
+        cost_estimate=pl.CostEstimate(flops=0, bytes_accessed=1_700_000, transcendentals=0),
+        name="shares",
+    )(in_hbm(w_t), in_hbm(w_out))
 
 
 def qkv_first_kernel(later, mods, w_t, *refs):
@@ -193,7 +211,7 @@
     for part, (begin, end) in enumerate(((0, LOW), (LOW, NZ))):
         for copy in copies[8 * part : 8 * part + 8]:
             copy.wait()
-        result = times(weights[begin:end].reshape((end - begin) * 3 * HD, D), tokens)
+        result = jnp.transpose(times(tokens, weights[begin:end].reshape((end - begin) * 3 * HD, D)))
         for j in range(end - begin):
             store_head(out.at[begin + j], result[j * 3 * HD : (j + 1) * 3 * HD])
 
@@ -452,7 +470,8 @@
     mods = lax.dynamic_slice_in_dim(mod_table, t_index[0], 1, 0)[0].astype(F32).reshape(6, D)
     gains = qk_gain[:, 0].astype(F32)
     w_t = jnp.transpose(w_qkv[:, :, 0, :], (0, 2, 1))
-    x0, pack, half, wo = prepare(frame_pos, latent, pos_table, w_t, w_out)
+    x0, pack = prepare(frame_pos, latent, pos_table, w_t)
+    half, wo = shares(w_t, w_out)
 
     later = lax.all_gather(pack, "z", axis=0, tiled=False)
     wo = lax.all_gather(wo, "z", axis=0, tiled=False)

time: 237 us -> 236 us (level)
  transfers between devices with their start and end apart: 32 -> 32, of which waited for: 19 -> 19; matrix products, arithmetic and copies ran while one was open for 0% -> 0% of each run, Pallas kernels for 14% -> 15%
where the time goes in v8:
time: 236 us; the launch traced here: 234 us
  waiting for transfers between devices  104 us (44%)
  starting transfers between devices  42.8 us (18%)
  Pallas kernels  40 us (17%)
  blocking collectives  30.8 us (13%)
  between operations  14.7 us (6%)
    ppermute x12, waiting for transfers between devices, from_ahead(): lax.ppermute(block, axis, [(i, (i - distance) % size) for i in range(size)])  42.9 us
    all_to_all x1, blocking collectives, per_device(): own = lax.all_to_all(heads, 'z', 0, 0, tiled=True)  17.6 us
    ppermute x12, starting transfers between devices, from_ahead(): lax.ppermute(block, axis, [(i, (i - distance) % size) for i in range(size)])  17 us
    all_to_all x1, blocking collectives, per_device(): done = lax.all_to_all(done, 'z', 0, 0, tiled=True)  13.2 us
    ppermute x1, waiting for transfers between devices, per_device(): queue = lax.ppermute(leaving, ('x', 'core', 'z', 'y'), route)  12.8 us
    pallas_call x2, Pallas kernels, neighbour_keys(): pl.pallas_call(functools.partial(neighbours_kernel, per), out_shape=jax.S...  11.5 us
    ppermute x4, starting transfers between devices, shifted(): return lax.ppermute(block, axis, route)  11.1 us
    all_to_all x1, waiting for transfers between devices, per_device(): terms = lax.all_to_all(terms, 'y', 0, 0, tiled=True)  10.1 us
  transfers between devices with their start and end apart: 32, of which 19 were waited for; matrix products, arithmetic and copies ran while one was open for 0% of the time, Pallas kernels for 15%

profile of v8, /device:TPU:4, one launch (start us, length us, event | category | flops | bytes accessed | tf_op | source)
XLA Modules:
  0.0 234.3 jit_solution(12467261336701766822)
XLA Ops:
  7.9 2.4 %prepare.1 = (bf16[32,3072]{1,0:T(8,128)(2,1)S(1)}, bf16[448,384]{1,0:T(8,128)(2,1)}) custom-call(s32[1,2]{1,0:T(1,128)S(1)} %copy-done.1, bf16[1,32,3072]{2,1,0:T(8,128)(2,1)} %latent.1, bf16[16,3072]{1,0:T(8,128)(2,1)} %pos.1, bf16[2,192,3072]{2,1,0:T(8,128)(2,1)} %bitcast.18), custom_call_target="tpu_custom_call" | custom-call | flops 300000 | bytes 800000 | tf_op jit(solution)/shard_map/prepare/pallas_call | solution.py:93
  10.3 2.0 shares.1
  12.4 3.1 %collective-permute-start = (bf16[192,1536]{1,0:T(8,128)(2,1)}, bf16[192,1536]{1,0:T(8,128)(2,1)S(1)}, u32[]{:S(2)}, u32[]{:S(2)}) collective-permute-start(bf16[192,1536]{1,0:T(8,128)(2,1)} %get-tuple-element.43), channel_id=1, source_target_pairs={{0,3},{1,0},{2,1},{3,2},{4,7},{5,4},{6,5},{7,6},{8,11},{9,8},{10,9... | collective-permute-start | bytes 1769480 | tf_op jit(solution)/shard_map/ppermute | solution.py:454
  16.2 1.0 collective-permute-start.2
  17.1 23.9 %collective-permute-done.refs_0_ = bf16[192,1536]{1,0:T(8,128)(2,1)S(1)} collective-permute-done((bf16[192,1536]{1,0:T(8,128)(2,1)}, bf16[192,1536]{1,0:T(8,128)(2,1)S(1)}, u32[]{:S(2)}, u32[]{:S(2)}) %collective-permute-start) | collective-permute-done | bytes 589856 | tf_op jit(solution)/shard_map/ppermute | solution.py:454
  41.6 3.1 %collective-permute-done.2.refs_2_ = bf16[192,1536]{1,0:T(8,128)(2,1)S(1)} collective-permute-done((bf16[192,1536]{1,0:T(8,128)(2,1)}, bf16[192,1536]{1,0:T(8,128)(2,1)S(1)}, u32[]{:S(2)}, u32[]{:S(2)}) %collective-permute-start.2) | collective-permute-done | bytes 589856 | tf_op jit(solution)/shard_map/ppermute | solution.py:454
  45.4 0.8 dynamic-slice_convert_fusion
  46.8 9.6 %all-gather.9.cloned.1.call-done = bf16[3584,384]{1,0:T(8,128)(2,1)} async-done(((bf16[448,384]{1,0:T(8,128)(2,1)}), bf16[3584,384]{1,0:T(8,128)(2,1)}) %all-gather.9.cloned.1.call-update) | async-done | bytes 2752528 | tf_op jit(solution)/shard_map/all_gather | solution.py:476
  56.5 5.3 %qkv_first.1 = (bf16[4,192,256]{2,1,0:T(8,128)(2,1)}, bf16[5,192,384]{2,1,0:T(8,128)(2,1)}, bf16[3,192,384]{2,1,0:T(8,128)(2,1)}) custom-call(bf16[8,448,384]{2,1,0:T(8,128)(2,1)} %bitcast.23, f32[6,3072]{1,0:T(8,128)S(1)} %reshape.15.mods, bf16[2,192,3072]{2,1,0:T(8,128)(2,1)} %bitcast.20, bf16[192,1536]{1,0:T(8,128)(2,1)S(1)} %collective-permute-done.refs_0_, ...), custom_call_target="tpu_custom_call" | custom-call | flops 1200000000 | bytes 14000000 | tf_op jit(solution)/shard_map/qkv_first/pallas_call | solution.py:174
  62.4 1.5 collective-permute-start.7
  63.8 4.3 %all-to-all-start = ((bf16[4,192,256]{2,1,0:T(8,128)(2,1)}), bf16[4,192,256]{2,1,0:T(8,128)(2,1)S(1)}, u32[]{:S(2)}, u32[]{:S(2)}) async-start(bf16[4,192,256]{2,1,0:T(8,128)(2,1)} %get-tuple-element.44), calls=%async_computation | async-start | bytes 786432 | tf_op jit(solution)/shard_map/all_to_all | solution.py:488
  68.1 7.4 %all-to-all-done.own = bf16[4,192,256]{2,1,0:T(8,128)(2,1)S(1)} async-done(((bf16[4,192,256]{2,1,0:T(8,128)(2,1)}), bf16[4,192,256]{2,1,0:T(8,128)(2,1)S(1)}, u32[]{:S(2)}, u32[]{:S(2)}) %all-to-all-start) | async-done | bytes 393248 | tf_op jit(solution)/shard_map/all_to_all | solution.py:488
  75.5 1.9 collective-permute-start.8
  77.4 3.6 %collective-permute-start.9 = (bf16[4,192,256]{2,1,0:T(8,128)(2,1)S(1)}, bf16[4,192,256]{2,1,0:T(8,128)(2,1)S(1)}, u32[]{:S(2)}, u32[]{:S(2)}) collective-permute-start(bf16[4,192,256]{2,1,0:T(8,128)(2,1)S(1)} %all-to-all-done.own), channel_id=1, source_target_pairs={{32,0},{64,32},{96,64},{128,96},{160,128},{192,160},{224,192},{33,... | collective-permute-start | bytes 1179656 | tf_op jit(solution)/shard_map/ppermute | solution.py:464
  81.1 2.3 own_1.1
  83.4 1.2 collective-permute-done.8.lower
  84.6 1.8 collective-permute-done.9.upper
  86.9 5.5 %neighbours_1.1 = bf16[8,64,128]{2,1,0:T(8,128)(2,1)S(1)} custom-call(bf16[4,192,256]{2,1,0:T(8,128)(2,1)S(1)} %collective-permute-done.8.lower, bf16[4,192,256]{2,1,0:T(8,128)(2,1)S(1)} %collective-permute-done.9.upper, bf16[4,64,256]{2,1,0:T(8,128)(2,1)S(1)} %get-tuple-element.51.queries, f32[4,64,256]{2,1,0:T(8,128)S(1)} %get-tuple-element.52.acc_in, ...), custom_call_target="tpu_custom_call" | custom-call | flops 6000000000 | bytes 1200000 | tf_op jit(solution)/shard_map/neighbours_1/pallas_call | solution.py:314
  92.4 5.3 %all-gather.11.cloned.1.call-done = bf16[2560,384]{1,0:T(8,128)(2,1)} async-done(((bf16[320,384]{1,0:T(8,128)(2,1)}), bf16[2560,384]{1,0:T(8,128)(2,1)}) %all-gather.11.cloned.1.call-update) | async-done | bytes 1966096 | tf_op jit(solution)/shard_map/all_gather | solution.py:477
  98.0 1.6 collective-permute-start.11
  99.6 13.2 %all_to_all.25.o = bf16[8,64,128]{2,1,0:T(8,128)(2,1)S(1)} all-to-all(bf16[8,64,128]{2,1,0:T(8,128)(2,1)S(1)} %neighbours_1.1), channel_id=1, replica_groups=mesh['x'=4,'core'=2,'z'=8,'y'=4] {'z'}, dimensions={0} | all-to-all | bytes 262144 | tf_op jit(solution)/shard_map/all_to_all | solution.py:497
  112.8 4.3 %project_first.1 = (bf16[128,3072]{1,0:T(8,128)(2,1)}, bf16[8,64,384]{2,1,0:T(8,128)(2,1)}) custom-call(bf16[8,64,128]{2,1,0:T(8,128)(2,1)S(1)} %all_to_all.25.o, bf16[8,320,384]{2,1,0:T(8,128)(2,1)} %bitcast.25, bf16[8,320,384]{2,1,0:T(8,128)(2,1)S(1)} %collective-permute-done.11.other), custom_call_target="tpu_custom_call" | custom-call | flops 420000000 | bytes 4000000 | tf_op jit(solution)/shard_map/project_first/pallas_call | solution.py:361
  117.1 3.5 %all-to-all-start.2 = ((bf16[4,32,3072]{2,1,0:T(8,128)(2,1)}), bf16[4,32,3072]{2,1,0:T(8,128)(2,1)S(1)}, u32[]{:S(2)}, u32[]{:S(2)}) async-start(bf16[4,32,3072]{2,1,0:T(8,128)(2,1)} %bitcast.7), calls=%async_computation.2 | async-start | bytes 1572864 | tf_op jit(solution)/shard_map/all_to_all | solution.py:503
  121.7 10.1 %all-to-all-done.2.terms = bf16[4,32,3072]{2,1,0:T(8,128)(2,1)S(1)} async-done(((bf16[4,32,3072]{2,1,0:T(8,128)(2,1)}), bf16[4,32,3072]{2,1,0:T(8,128)(2,1)S(1)}, u32[]{:S(2)}, u32[]{:S(2)}) %all-to-all-start.2) | async-done | bytes 786464 | tf_op jit(solution)/shard_map/all_to_all | solution.py:503
  132.0 1.2 collective-permute-start.12
  133.3 1.5 collective-permute-start.13
  134.8 3.6 %collective-permute-done.12.x1 = bf16[32,3072]{1,0:T(8,128)(2,1)S(1)} collective-permute-done((bf16[32,3072]{1,0:T(8,128)(2,1)S(1)}, bf16[32,3072]{1,0:T(8,128)(2,1)S(1)}, u32[]{:S(2)}, u32[]{:S(2)}) %collective-permute-start.12) | collective-permute-done | bytes 196640 | tf_op jit(solution)/shard_map/ppermute | solution.py:454
  138.4 2.5 %collective-permute-done.13.x2 = bf16[32,3072]{1,0:T(8,128)(2,1)S(1)} collective-permute-done((bf16[32,3072]{1,0:T(8,128)(2,1)S(1)}, bf16[32,3072]{1,0:T(8,128)(2,1)S(1)}, u32[]{:S(2)}, u32[]{:S(2)}) %collective-permute-start.13) | collective-permute-done | bytes 196640 | tf_op jit(solution)/shard_map/ppermute | solution.py:454
  140.9 2.0 collective-permute-done.14.x3
  142.9 6.6 %qkv_second.1 = bf16[8,192,128]{2,1,0:T(8,128)(2,1)S(1)} custom-call(bf16[32,3072]{1,0:T(8,128)(2,1)S(1)} %residual.1.x0.x, bf16[32,3072]{1,0:T(8,128)(2,1)S(1)} %collective-permute-done.12.x1, bf16[32,3072]{1,0:T(8,128)(2,1)S(1)} %collective-permute-done.13.x2, bf16[32,3072]{1,0:T(8,128)(2,1)S(1)} %collective-permute-done.14.x3, ...), custom_call_target="tpu_custom_call" | custom-call | flops 1200000000 | bytes 10500000 | tf_op jit(solution)/shard_map/qkv_second/pallas_call | solution.py:220
  149.5 17.6 %all_to_all.26.own = bf16[8,192,128]{2,1,0:T(8,128)(2,1)S(1)} all-to-all(bf16[8,192,128]{2,1,0:T(8,128)(2,1)S(1)} %qkv_second.1), channel_id=1, replica_groups=mesh['x'=4,'core'=2,'z'=8,'y'=4] {'z'}, dimensions={0} | all-to-all | bytes 786432 | tf_op jit(solution)/shard_map/all_to_all | solution.py:508
  167.1 1.9 collective-permute-start.19
  169.0 3.6 %collective-permute-start.20 = (bf16[8,192,128]{2,1,0:T(8,128)(2,1)S(1)}, bf16[8,192,128]{2,1,0:T(8,128)(2,1)S(1)}, u32[]{:S(2)}, u32[]{:S(2)}) collective-permute-start(bf16[8,192,128]{2,1,0:T(8,128)(2,1)S(1)} %all_to_all.26.own), channel_id=1, source_target_pairs={{32,0},{64,32},{96,64},{128,96},{160,128},{192,160},{224,192},{33,... | collective-permute-start | bytes 1179656 | tf_op jit(solution)/shard_map/ppermute | solution.py:464
  172.6 2.3 own_2.1
  174.9 1.2 collective-permute-done.19.lower
  176.1 1.8 collective-permute-done.20.upper
  177.9 6.0 %neighbours_2.1 = bf16[8,64,128]{2,1,0:T(8,128)(2,1)} custom-call(bf16[8,192,128]{2,1,0:T(8,128)(2,1)S(1)} %collective-permute-done.19.lower, bf16[8,192,128]{2,1,0:T(8,128)(2,1)S(1)} %collective-permute-done.20.upper, bf16[4,64,256]{2,1,0:T(8,128)(2,1)S(1)} %get-tuple-element.72.queries, f32[4,64,256]{2,1,0:T(8,128)S(1)} %get-tuple-element.73.acc_in, ...), custom_call_target="tpu_custom_call" | custom-call | flops 6000000000 | bytes 1200000 | tf_op jit(solution)/shard_map/neighbours_2/pallas_call | solution.py:314
  183.9 3.4 %all-to-all-start.4 = ((bf16[8,64,128]{2,1,0:T(8,128)(2,1)}), bf16[8,64,128]{2,1,0:T(8,128)(2,1)S(1)}, u32[]{:S(2)}, u32[]{:S(2)}) async-start(bf16[8,64,128]{2,1,0:T(8,128)(2,1)} %neighbours_2.1), calls=%async_computation.4 | async-start | bytes 262144 | tf_op jit(solution)/shard_map/all_to_all | solution.py:511
  187.3 9.2 %all-to-all-done.4.o = bf16[8,64,128]{2,1,0:T(8,128)(2,1)S(1)} async-done(((bf16[8,64,128]{2,1,0:T(8,128)(2,1)}), bf16[8,64,128]{2,1,0:T(8,128)(2,1)S(1)}, u32[]{:S(2)}, u32[]{:S(2)}) %all-to-all-start.4) | async-done | bytes 131104 | tf_op jit(solution)/shard_map/all_to_all | solution.py:511
  196.5 2.4 %project_second.1 = (bf16[32,3072]{1,0:T(8,128)(2,1)S(1)}, bf16[32,3072]{1,0:T(8,128)(2,1)S(1)}, bf16[32,3072]{1,0:T(8,128)(2,1)S(1)}, bf16[32,3072]{1,0:T(8,128)(2,1)S(1)}) custom-call(bf16[8,64,128]{2,1,0:T(8,128)(2,1)S(1)} %all-to-all-done.4.o, bf16[8,8,64,384]{3,2,1,0:T(8,128)(2,1)} %bitcast.22), custom_call_target="tpu_custom_call" | custom-call | flops 420000000 | bytes 4000000 | tf_op jit(solution)/shard_map/project_second/pallas_call | solution.py:387
  198.9 2.6 %collective-permute-start.21 = (bf16[32,3072]{1,0:T(8,128)(2,1)S(1)}, bf16[32,3072]{1,0:T(8,128)(2,1)S(1)}, u32[]{:S(2)}, u32[]{:S(2)}) collective-permute-start(bf16[32,3072]{1,0:T(8,128)(2,1)S(1)} %get-tuple-element.77), channel_id=1, source_target_pairs={{0,1},{1,2},{2,3},{3,0},{4,5},{5,6},{6,7},{7,4},{8,9},{9,10},{10,1... | collective-permute-start | bytes 589832 | tf_op jit(solution)/shard_map/ppermute | solution.py:454
  201.5 2.8 %collective-permute-start.22 = (bf16[32,3072]{1,0:T(8,128)(2,1)S(1)}, bf16[32,3072]{1,0:T(8,128)(2,1)S(1)}, u32[]{:S(2)}, u32[]{:S(2)}) collective-permute-start(bf16[32,3072]{1,0:T(8,128)(2,1)S(1)} %get-tuple-element.78), channel_id=1, source_target_pairs={{0,2},{1,3},{2,0},{3,1},{4,6},{5,7},{6,4},{7,5},{8,10},{9,11},{10,... | collective-permute-start | bytes 589832 | tf_op jit(solution)/shard_map/ppermute | solution.py:454
  204.3 1.5 collective-permute-start.23
  205.8 2.2 collective-permute-done.21.t1
  208.0 5.3 %collective-permute-done.22.t2 = bf16[32,3072]{1,0:T(8,128)(2,1)S(1)} collective-permute-done((bf16[32,3072]{1,0:T(8,128)(2,1)S(1)}, bf16[32,3072]{1,0:T(8,128)(2,1)S(1)}, u32[]{:S(2)}, u32[]{:S(2)}) %collective-permute-start.22) | collective-permute-done | bytes 196640 | tf_op jit(solution)/shard_map/ppermute | solution.py:454
  213.3 0.8 last.1
  214.3 12.8 %collective-permute-done.24 = bf16[32,3072]{1,0:T(8,128)(2,1)S(1)} collective-permute-done((bf16[32,3072]{1,0:T(8,128)(2,1)S(1)}, bf16[32,3072]{1,0:T(8,128)(2,1)S(1)}, u32[]{:S(2)}, u32[]{:S(2)}) %collective-permute-start.24) | collective-permute-done | bytes 196640 | tf_op jit(solution)/shard_map/ppermute | solution.py:518
  227.1 0.7 copy.16
  (46 shorter events, 5.4 us)
Async XLA Ops:
  7.2 49.3 %all-gather.9.cloned.1.call-start = ((), (), s32[]{:S(2)}) async-start(), calls=%async_computation.5 | async-start | bytes 3096576 | tf_op jit(solution)/shard_map/all_gather | solution.py:476
  7.2 0.7 copy-start.1
  10.3 87.5 %all-gather.11.cloned.1.call-start = ((), (), s32[]{:S(2)}) async-start(), calls=%async_computation.6 | async-start | bytes 2211840 | tf_op jit(solution)/shard_map/all_gather | solution.py:477
  12.4 130.5 %all-gather.13.cloned.1.call-start = ((), (), s32[]{:S(2)}) async-start(), calls=%async_computation.7 | async-start | bytes 6635520 | tf_op jit(solution)/shard_map/all_gather | solution.py:486
  12.4 28.6 %collective-permute-start = (bf16[192,1536]{1,0:T(8,128)(2,1)}, bf16[192,1536]{1,0:T(8,128)(2,1)S(1)}, u32[]{:S(2)}, u32[]{:S(2)}) collective-permute-start(bf16[192,1536]{1,0:T(8,128)(2,1)} %get-tuple-element.43), channel_id=1, source_target_pairs={{0,3},{1,0},{2,1},{3,2},{4,7},{5,4},{6,5},{7,6},{8,11},{9,8},{10,9... | collective-permute-start | bytes 1769480 | tf_op jit(solution)/shard_map/ppermute | solution.py:454
  15.5 25.5 %collective-permute-start.1 = (bf16[192,1536]{1,0:T(8,128)(2,1)}, bf16[192,1536]{1,0:T(8,128)(2,1)S(1)}, u32[]{:S(2)}, u32[]{:S(2)}) collective-permute-start(bf16[192,1536]{1,0:T(8,128)(2,1)} %get-tuple-element.43), channel_id=1, source_target_pairs={{0,2},{1,3},{2,0},{3,1},{4,6},{5,7},{6,4},{7,5},{8,10},{9,11},{10,... | collective-permute-start | bytes 1769480 | tf_op jit(solution)/shard_map/ppermute | solution.py:454
  16.2 28.5 %collective-permute-start.2 = (bf16[192,1536]{1,0:T(8,128)(2,1)}, bf16[192,1536]{1,0:T(8,128)(2,1)S(1)}, u32[]{:S(2)}, u32[]{:S(2)}) collective-permute-start(bf16[192,1536]{1,0:T(8,128)(2,1)} %get-tuple-element.43), channel_id=1, source_target_pairs={{0,1},{1,2},{2,3},{3,0},{4,5},{5,6},{6,7},{7,4},{8,9},{9,10},{10,1... | collective-permute-start | bytes 1769480 | tf_op jit(solution)/shard_map/ppermute | solution.py:454
  41.1 5.3 %collective-permute-start.3 = (bf16[192,1536]{1,0:T(8,128)(2,1)S(1)}, bf16[192,1536]{1,0:T(8,128)(2,1)S(1)}, u32[]{:S(2)}, u32[]{:S(2)}) collective-permute-start(bf16[192,1536]{1,0:T(8,128)(2,1)S(1)} %collective-permute-done.refs_0_), channel_id=1, source_target_pairs={{0,32},{32,0},{1,33},{33,1},{2,34},{34,2},{3,35},{35,3},{4,36},{36... | collective-permute-start | bytes 1769480 | tf_op jit(solution)/shard_map/ppermute | solution.py:458
  41.1 5.3 %collective-permute-start.4 = (bf16[192,1536]{1,0:T(8,128)(2,1)S(1)}, bf16[192,1536]{1,0:T(8,128)(2,1)S(1)}, u32[]{:S(2)}, u32[]{:S(2)}) collective-permute-start(bf16[192,1536]{1,0:T(8,128)(2,1)S(1)} %collective-permute-done.1.refs_1_), channel_id=1, source_target_pairs={{0,32},{32,0},{1,33},{33,1},{2,34},{34,2},{3,35},{35,3},{4,36},{36... | collective-permute-start | bytes 1769480 | tf_op jit(solution)/shard_map/ppermute | solution.py:458
  44.7 2.1 collective-permute-start.5
  56.4 11.7 %copy-start.2 = (bf16[2,1,128]{2,0,1:T(2,128)(2,1)S(1)}, bf16[2,1,128]{2,0,1:T(2,128)(2,1)}, u32[]{:S(2)}) copy-start(bf16[2,1,128]{2,0,1:T(2,128)(2,1)} %param.16) | copy-start | bytes 1540
  61.7 13.8 %collective-permute-start.6 = (bf16[3,192,384]{2,1,0:T(8,128)(2,1)}, bf16[3,192,384]{2,1,0:T(8,128)(2,1)S(1)}, u32[]{:S(2)}, u32[]{:S(2)}) collective-permute-start(bf16[3,192,384]{2,1,0:T(8,128)(2,1)} %get-tuple-element.68.refs_0_), channel_id=1, source_target_pairs={{0,192},{64,0},{128,64},{192,128},{1,193},{65,1},{129,65},{193,129... | collective-permute-start | bytes 1327112 | tf_op jit(solution)/shard_map/ppermute | solution.py:454
  62.4 13.1 %collective-permute-start.7 = (bf16[3,192,384]{2,1,0:T(8,128)(2,1)}, bf16[3,192,384]{2,1,0:T(8,128)(2,1)S(1)}, u32[]{:S(2)}, u32[]{:S(2)}) collective-permute-start(bf16[3,192,384]{2,1,0:T(8,128)(2,1)} %get-tuple-element.68.refs_0_), channel_id=1, source_target_pairs={{0,64},{64,128},{128,192},{192,0},{1,65},{65,129},{129,193},{193,1... | collective-permute-start | bytes 1327112 | tf_op jit(solution)/shard_map/ppermute | solution.py:454
  63.8 11.7 %all-to-all-start = ((bf16[4,192,256]{2,1,0:T(8,128)(2,1)}), bf16[4,192,256]{2,1,0:T(8,128)(2,1)S(1)}, u32[]{:S(2)}, u32[]{:S(2)}) async-start(bf16[4,192,256]{2,1,0:T(8,128)(2,1)} %get-tuple-element.44), calls=%async_computation | async-start | bytes 786432 | tf_op jit(solution)/shard_map/all_to_all | solution.py:488
  68.1 119.1 %all-gather.15.cloned.1.call-start = ((), (), s32[]{:S(2)}) async-start(), calls=%async_computation.8 | async-start | bytes 3538944 | tf_op jit(solution)/shard_map/all_gather | solution.py:502
  75.5 9.1 %collective-permute-start.8 = (bf16[4,192,256]{2,1,0:T(8,128)(2,1)S(1)}, bf16[4,192,256]{2,1,0:T(8,128)(2,1)S(1)}, u32[]{:S(2)}, u32[]{:S(2)}) collective-permute-start(bf16[4,192,256]{2,1,0:T(8,128)(2,1)S(1)} %all-to-all-done.own), channel_id=1, source_target_pairs={{0,32},{32,64},{64,96},{96,128},{128,160},{160,192},{192,224},{1,3... | collective-permute-start | bytes 1179656 | tf_op jit(solution)/shard_map/ppermute | solution.py:464
  77.4 8.9 %collective-permute-start.9 = (bf16[4,192,256]{2,1,0:T(8,128)(2,1)S(1)}, bf16[4,192,256]{2,1,0:T(8,128)(2,1)S(1)}, u32[]{:S(2)}, u32[]{:S(2)}) collective-permute-start(bf16[4,192,256]{2,1,0:T(8,128)(2,1)S(1)} %all-to-all-done.own), channel_id=1, source_target_pairs={{32,0},{64,32},{96,64},{128,96},{160,128},{192,160},{224,192},{33,... | collective-permute-start | bytes 1179656 | tf_op jit(solution)/shard_map/ppermute | solution.py:464
  86.4 11.6 %collective-permute-start.10 = (bf16[3,192,384]{2,1,0:T(8,128)(2,1)S(1)}, bf16[3,192,384]{2,1,0:T(8,128)(2,1)S(1)}, u32[]{:S(2)}, u32[]{:S(2)}) collective-permute-start(bf16[3,192,384]{2,1,0:T(8,128)(2,1)S(1)} %collective-permute-done.6.refs_1_), channel_id=1, source_target_pairs={{0,192},{64,0},{128,64},{192,128},{1,193},{65,1},{129,65},{193,129... | collective-permute-start | bytes 1327112 | tf_op jit(solution)/shard_map/ppermute | solution.py:454
  98.0 14.8 %collective-permute-start.11 = (bf16[8,320,384]{2,1,0:T(8,128)(2,1)}, bf16[8,320,384]{2,1,0:T(8,128)(2,1)S(1)}, u32[]{:S(2)}, u32[]{:S(2)}) collective-permute-start(bf16[8,320,384]{2,1,0:T(8,128)(2,1)} %bitcast.24), channel_id=1, source_target_pairs={{0,32},{32,0},{1,33},{33,1},{2,34},{34,2},{3,35},{35,3},{4,36},{36... | collective-permute-start | bytes 5898248 | tf_op jit(solution)/shard_map/ppermute | solution.py:458
  112.8 7.8 %copy-start = (bf16[3,192,384]{2,1,0:T(8,128)(2,1)S(1)}, bf16[3,192,384]{2,1,0:T(8,128)(2,1)}, u32[]{:S(2)}) copy-start(bf16[3,192,384]{2,1,0:T(8,128)(2,1)} %get-tuple-element.68.refs_0_) | copy-start | bytes 1327108
  117.1 14.8 %all-to-all-start.2 = ((bf16[4,32,3072]{2,1,0:T(8,128)(2,1)}), bf16[4,32,3072]{2,1,0:T(8,128)(2,1)S(1)}, u32[]{:S(2)}, u32[]{:S(2)}) async-start(bf16[4,32,3072]{2,1,0:T(8,128)(2,1)} %bitcast.7), calls=%async_computation.2 | async-start | bytes 1572864 | tf_op jit(solution)/shard_map/all_to_all | solution.py:503
  120.6 12.6 %collective-permute-start.15 = (bf16[3,192,384]{2,1,0:T(8,128)(2,1)S(1)}, bf16[3,192,384]{2,1,0:T(8,128)(2,1)S(1)}, u32[]{:S(2)}, u32[]{:S(2)}) collective-permute-start(bf16[3,192,384]{2,1,0:T(8,128)(2,1)S(1)} %copy-done), channel_id=1, source_target_pairs={{0,32},{32,0},{1,33},{33,1},{2,34},{34,2},{3,35},{35,3},{4,36},{36... | collective-permute-start | bytes 1327112 | tf_op jit(solution)/shard_map/ppermute | solution.py:458
  120.7 14.1 %collective-permute-start.16 = (bf16[3,192,384]{2,1,0:T(8,128)(2,1)S(1)}, bf16[3,192,384]{2,1,0:T(8,128)(2,1)}, u32[]{:S(2)}, u32[]{:S(2)}) collective-permute-start(bf16[3,192,384]{2,1,0:T(8,128)(2,1)S(1)} %collective-permute-done.6.refs_1_), channel_id=1, source_target_pairs={{0,32},{32,0},{1,33},{33,1},{2,34},{34,2},{3,35},{35,3},{4,36},{36... | collective-permute-start | bytes 1327112 | tf_op jit(solution)/shard_map/ppermute | solution.py:458
  121.2 13.6 %collective-permute-start.17 = (bf16[3,192,384]{2,1,0:T(8,128)(2,1)S(1)}, bf16[3,192,384]{2,1,0:T(8,128)(2,1)}, u32[]{:S(2)}, u32[]{:S(2)}) collective-permute-start(bf16[3,192,384]{2,1,0:T(8,128)(2,1)S(1)} %collective-permute-done.10.refs_2_), channel_id=1, source_target_pairs={{0,32},{32,0},{1,33},{33,1},{2,34},{34,2},{3,35},{35,3},{4,36},{36... | collective-permute-start | bytes 1327112 | tf_op jit(solution)/shard_map/ppermute | solution.py:458
  121.3 13.5 %collective-permute-start.18 = (bf16[3,192,384]{2,1,0:T(8,128)(2,1)S(1)}, bf16[3,192,384]{2,1,0:T(8,128)(2,1)}, u32[]{:S(2)}, u32[]{:S(2)}) collective-permute-start(bf16[3,192,384]{2,1,0:T(8,128)(2,1)S(1)} %collective-permute-done.7.refs_3_), channel_id=1, source_target_pairs={{0,32},{32,0},{1,33},{33,1},{2,34},{34,2},{3,35},{35,3},{4,36},{36... | collective-permute-start | bytes 1327112 | tf_op jit(solution)/shard_map/ppermute | solution.py:458
  132.0 6.3 %collective-permute-start.12 = (bf16[32,3072]{1,0:T(8,128)(2,1)S(1)}, bf16[32,3072]{1,0:T(8,128)(2,1)S(1)}, u32[]{:S(2)}, u32[]{:S(2)}) collective-permute-start(bf16[32,3072]{1,0:T(8,128)(2,1)S(1)} %residual.1.x0.x), channel_id=1, source_target_pairs={{0,3},{1,0},{2,1},{3,2},{4,7},{5,4},{6,5},{7,6},{8,11},{9,8},{10,9... | collective-permute-start | bytes 589832 | tf_op jit(solution)/shard_map/ppermute | solution.py:454
  133.3 7.6 %collective-permute-start.13 = (bf16[32,3072]{1,0:T(8,128)(2,1)S(1)}, bf16[32,3072]{1,0:T(8,128)(2,1)S(1)}, u32[]{:S(2)}, u32[]{:S(2)}) collective-permute-start(bf16[32,3072]{1,0:T(8,128)(2,1)S(1)} %residual.1.x0.x), channel_id=1, source_target_pairs={{0,2},{1,3},{2,0},{3,1},{4,6},{5,7},{6,4},{7,5},{8,10},{9,11},{10,... | collective-permute-start | bytes 589832 | tf_op jit(solution)/shard_map/ppermute | solution.py:454
  134.8 8.1 %collective-permute-start.14 = (bf16[32,3072]{1,0:T(8,128)(2,1)S(1)}, bf16[32,3072]{1,0:T(8,128)(2,1)S(1)}, u32[]{:S(2)}, u32[]{:S(2)}) collective-permute-start(bf16[32,3072]{1,0:T(8,128)(2,1)S(1)} %residual.1.x0.x), channel_id=1, source_target_pairs={{0,1},{1,2},{2,3},{3,0},{4,5},{5,6},{6,7},{7,4},{8,9},{9,10},{10,1... | collective-permute-start | bytes 589832 | tf_op jit(solution)/shard_map/ppermute | solution.py:454
  167.1 9.1 %collective-permute-start.19 = (bf16[8,192,128]{2,1,0:T(8,128)(2,1)S(1)}, bf16[8,192,128]{2,1,0:T(8,128)(2,1)S(1)}, u32[]{:S(2)}, u32[]{:S(2)}) collective-permute-start(bf16[8,192,128]{2,1,0:T(8,128)(2,1)S(1)} %all_to_all.26.own), channel_id=1, source_target_pairs={{0,32},{32,64},{64,96},{96,128},{128,160},{160,192},{192,224},{1,3... | collective-permute-start | bytes 1179656 | tf_op jit(solution)/shard_map/ppermute | solution.py:464
  169.0 8.9 %collective-permute-start.20 = (bf16[8,192,128]{2,1,0:T(8,128)(2,1)S(1)}, bf16[8,192,128]{2,1,0:T(8,128)(2,1)S(1)}, u32[]{:S(2)}, u32[]{:S(2)}) collective-permute-start(bf16[8,192,128]{2,1,0:T(8,128)(2,1)S(1)} %all_to_all.26.own), channel_id=1, source_target_pairs={{32,0},{64,32},{96,64},{128,96},{160,128},{192,160},{224,192},{33,... | collective-permute-start | bytes 1179656 | tf_op jit(solution)/shard_map/ppermute | solution.py:464
  183.9 12.6 %all-to-all-start.4 = ((bf16[8,64,128]{2,1,0:T(8,128)(2,1)}), bf16[8,64,128]{2,1,0:T(8,128)(2,1)S(1)}, u32[]{:S(2)}, u32[]{:S(2)}) async-start(bf16[8,64,128]{2,1,0:T(8,128)(2,1)} %neighbours_2.1), calls=%async_computation.4 | async-start | bytes 262144 | tf_op jit(solution)/shard_map/all_to_all | solution.py:511
  198.9 9.1 %collective-permute-start.21 = (bf16[32,3072]{1,0:T(8,128)(2,1)S(1)}, bf16[32,3072]{1,0:T(8,128)(2,1)S(1)}, u32[]{:S(2)}, u32[]{:S(2)}) collective-permute-start(bf16[32,3072]{1,0:T(8,128)(2,1)S(1)} %get-tuple-element.77), channel_id=1, source_target_pairs={{0,1},{1,2},{2,3},{3,0},{4,5},{5,6},{6,7},{7,4},{8,9},{9,10},{10,1... | collective-permute-start | bytes 589832 | tf_op jit(solution)/shard_map/ppermute | solution.py:454
  201.5 11.8 %collective-permute-start.22 = (bf16[32,3072]{1,0:T(8,128)(2,1)S(1)}, bf16[32,3072]{1,0:T(8,128)(2,1)S(1)}, u32[]{:S(2)}, u32[]{:S(2)}) collective-permute-start(bf16[32,3072]{1,0:T(8,128)(2,1)S(1)} %get-tuple-element.78), channel_id=1, source_target_pairs={{0,2},{1,3},{2,0},{3,1},{4,6},{5,7},{6,4},{7,5},{8,10},{9,11},{10,... | collective-permute-start | bytes 589832 | tf_op jit(solution)/shard_map/ppermute | solution.py:454
  204.3 9.1 %collective-permute-start.23 = (bf16[32,3072]{1,0:T(8,128)(2,1)S(1)}, bf16[32,3072]{1,0:T(8,128)(2,1)S(1)}, u32[]{:S(2)}, u32[]{:S(2)}) collective-permute-start(bf16[32,3072]{1,0:T(8,128)(2,1)S(1)} %get-tuple-element.79), channel_id=1, source_target_pairs={{0,3},{1,0},{2,1},{3,2},{4,7},{5,4},{6,5},{7,6},{8,11},{9,8},{10,9... | collective-permute-start | bytes 589832 | tf_op jit(solution)/shard_map/ppermute | solution.py:454
  214.2 12.9 %collective-permute-start.24 = (bf16[32,3072]{1,0:T(8,128)(2,1)S(1)}, bf16[32,3072]{1,0:T(8,128)(2,1)S(1)}, u32[]{:S(2)}, u32[]{:S(2)}) collective-permute-start(bf16[32,3072]{1,0:T(8,128)(2,1)S(1)} %get-tuple-element.81), channel_id=1, source_target_pairs={{0,240},{1,241},{2,242},{3,243},{4,244},{5,245},{6,246},{7,247},{8... | collective-permute-start | bytes 589832 | tf_op jit(solution)/shard_map/ppermute | solution.py:518
Sparse Core Ops, SparseCore 0:
  10.4 46.0 all-gather.8
  58.2 39.4 all-gather.10
  99.6 38.8 all-gather.12
  140.2 30.3 all-gather.14

commit v9 on v8

--- a/solution.py
+++ b/solution.py
@@ -233,21 +233,23 @@
     )(*shards, mods, in_hbm(gathered), *weights)
 
 
-def over_keys(per, ref, queries, acc, den, begin):
+def over_keys(per, ref, queries, acc, den, keys, begin):
     def wide(n, lo, hi):
         if per == 1:
             return ref[n, lo:hi, :]
         return jnp.concatenate([ref[n * per + i, lo:hi, :] for i in range(per)], axis=1)
 
+    for n in range(4):
+        keys[n] = jnp.transpose(wide(n, HD, 2 * HD))
+
     def body(m, carry):
         q = queries[m]
         total, norm = (None, None) if begin else (acc[m], den[m])
         for n in range(4):
-            keys, values = wide(n, HD, 2 * HD), wide(n, 2 * HD, 3 * HD)
-            score = lax.dot_general(keys, q, (((0,), (0,)), ((), ())), preferred_element_type=F32)
+            score = jnp.dot(keys[n], q, preferred_element_type=F32)
             e = jnp.exp(score)
             sums = jnp.sum(e, axis=0, keepdims=True)
-            term = jnp.dot(values, e.astype(BF), preferred_element_type=F32)
+            term = jnp.dot(wide(n, 2 * HD, 3 * HD), e.astype(BF), preferred_element_type=F32)
             total = term if total is None else total + term
             norm = sums if norm is None else norm + sums
         acc[m] = total
@@ -257,29 +259,34 @@
     lax.fori_loop(0, 4, body, 0)
 
 
-def own_kernel(per, own, gain, queries, acc, den):
+def own_kernel(per, own, gain, queries, acc, den, keys):
     column = jnp.transpose(jnp.broadcast_to(gain[...], (8, 2 * HD)))[:, 0:1]
     g = column[0:HD] * column[HD:] * 0.125
     for n in range(4):
         parts = [own[n * per + i, 0:HD, :] for i in range(per)]
         q = parts[0] if per == 1 else jnp.concatenate(parts, axis=1)
         queries[n] = (q.astype(F32) * g).astype(BF)
-    over_keys(per, own, queries, acc, den, True)
-
-
-def neighbours_kernel(per, lower, upper, queries, acc_in, den_in, out, acc, den):
+    over_keys(per, own, queries, acc, den, keys, True)
+
+
+def below_kernel(per, lower, queries, acc_in, den_in, acc, den, keys):
     x_pos, core, _, _ = position()
-    slot = x_pos * NC + core
     acc[...] = acc_in[...]
     den[...] = den_in[...]
 
-    @pl.when(slot > 0)
+    @pl.when(x_pos * NC + core > 0)
     def _():
-        over_keys(per, lower, queries, acc, den, False)
-
-    @pl.when(slot < NX * NC - 1)
+        over_keys(per, lower, queries, acc, den, keys, False)
+
+
+def above_kernel(per, upper, queries, acc_in, den_in, out, acc, den, keys):
+    x_pos, core, _, _ = position()
+    acc[...] = acc_in[...]
+    den[...] = den_in[...]
+
+    @pl.when(x_pos * NC + core < NX * NC - 1)
     def _():
-        over_keys(per, upper, queries, acc, den, False)
+        over_keys(per, upper, queries, acc, den, keys, False)
 
     if per == 1:
         done = [acc[n] / den[n] for n in range(4)]
@@ -303,36 +310,51 @@
         out_shape=[jax.ShapeDtypeStruct((4, HD, 256), BF), *SUMS],
         in_specs=[VM] * 2,
         out_specs=[VM] * 3,
+        scratch_shapes=[pltpu.VMEM((4, 256, HD), BF)],
         compiler_params=params(8),
         cost_estimate=pl.CostEstimate(flops=3_000_000_000, bytes_accessed=800_000, transcendentals=0),
         name="own_%d" % per,
     )(own, gain)
 
 
-def neighbour_keys(lower, upper, queries, acc, den):
+def below_keys(lower, queries, acc, den):
     per = lower.shape[0] // 4
     return pl.pallas_call(
-        functools.partial(neighbours_kernel, per),
+        functools.partial(below_kernel, per),
+        out_shape=list(SUMS),
+        in_specs=[VM] * 4,
+        out_specs=[VM] * 2,
+        scratch_shapes=[pltpu.VMEM((4, 256, HD), BF)],
+        compiler_params=params(8),
+        cost_estimate=pl.CostEstimate(flops=3_000_000_000, bytes_accessed=1_000_000, transcendentals=0),
+        name="below_%d" % per,
+    )(lower, queries, acc, den)
+
+
+def above_keys(upper, queries, acc, den):
+    per = upper.shape[0] // 4
+    return pl.pallas_call(
+        functools.partial(above_kernel, per),
         out_shape=jax.ShapeDtypeStruct((NZ, HD, NY * ROWS), BF),
-        in_specs=[VM] * 5,
+        in_specs=[VM] * 4,
         out_specs=VM,
-        scratch_shapes=[pltpu.VMEM(s.shape, F32) for s in SUMS],
-        compiler_params=params(8),
-        cost_estimate=pl.CostEstimate(flops=6_000_000_000, bytes_accessed=1_200_000, transcendentals=0),
-        name="neighbours_%d" % per,
-    )(lower, upper, queries, acc, den)
+        scratch_shapes=[pltpu.VMEM(s.shape, F32) for s in SUMS] + [pltpu.VMEM((4, 256, HD), BF)],
+        compiler_params=params(8),
+        cost_estimate=pl.CostEstimate(flops=3_000_000_000, bytes_accessed=1_000_000, transcendentals=0),
+        name="above_%d" % per,
+    )(upper, queries, acc, den)
 
 
 def project_terms(o, eighths, weights, sems, put):
     copies = [pltpu.make_async_copy(w, weights.at[n], sems.at[n]) for n, (w, _) in enumerate(eighths)]
     for copy in copies:
         copy.start()
-    rows = o[...].reshape(NZ * HD, NY * ROWS)
+    rows = jnp.transpose(o[...].reshape(NZ * HD, NY * ROWS))
     for n in range(0, 8, 2):
         copies[n].wait()
         copies[n + 1].wait()
         w = jnp.concatenate([weights[n + t].reshape(NZ * HD, EIGHTH) for t in range(2)], axis=1)
-        term = lax.dot_general(rows, w, (((0,), (0,)), ((), ())), preferred_element_type=F32)
+        term = jnp.dot(rows, w, preferred_element_type=F32)
         put(pl.ds(pl.multiple_of(eighths[n][1] * EIGHTH, 128), QUARTER), term.astype(BF))
 
 
@@ -489,9 +511,11 @@
     own, high_1, high_3 = lax.optimization_barrier((own, high_1, high_3))
     lower, upper = neighbours(own)
     queries, acc, den = own_keys(own, gains[0:1])
-    lower, upper, acc, high_1 = lax.optimization_barrier((lower, upper, acc, high_1))
+    lower, acc, high_1 = lax.optimization_barrier((lower, acc, high_1))
+    acc, den = below_keys(lower, queries, acc, den)
+    upper, high_1 = lax.optimization_barrier((upper, high_1))
     high_2 = from_ahead(high_1, "x", NX, 1)
-    done = neighbour_keys(lower, upper, queries, acc, den)
+    done = above_keys(upper, queries, acc, den)
     done, wo, high, high_1, high_2, high_3 = lax.optimization_barrier((done, wo, high, high_1, high_2, high_3))
     wo_s = swap(wo)
     done = lax.all_to_all(done, "z", 0, 0, tiled=True)
@@ -507,7 +531,9 @@
     heads = qkv_second(shards, mods, low, weights)
     own = lax.all_to_all(heads, "z", 0, 0, tiled=True)
     lower, upper = neighbours(own)
-    done = neighbour_keys(lower, upper, *own_keys(own, gains[1:2]))
+    queries, acc, den = own_keys(own, gains[1:2])
+    acc, den = below_keys(lower, queries, acc, den)
+    done = above_keys(upper, queries, acc, den)
     done = lax.all_to_all(done, "z", 0, 0, tiled=True)
     terms = project_second(done, wo1)
     terms = [terms[0]] + [from_ahead(terms[j], "y", NY, NY - j) for j in range(1, NY)]

time: 236 us -> 232 us (0.983)
  starting transfers between devices: 42.8 us -> 39.1 us
    ppermute x1, waiting for transfers between devices: 12.8 us -> 10.3 us  [per_device(): queue = lax.ppermute(leaving, ('x', 'core', 'z', 'y'), route)]
    pallas_call x2 -> x4, Pallas kernels: 11.5 us -> 11.2 us  [the longest x2 6.03 us: above_keys(): pl.pallas_call(functools.partial(above_kernel, per), out_shape=jax.ShapeD...]
  transfers between devices with their start and end apart: 32 -> 32, of which waited for: 19 -> 17; matrix products, arithmetic and copies ran while one was open for 0% -> 0% of each run, Pallas kernels for 15% -> 15%
where the time goes in v9:
time: 232 us; the launch traced here: 228 us
  waiting for transfers between devices  103 us (44%)
  Pallas kernels  39.5 us (17%)
  starting transfers between devices  39.1 us (17%)
  blocking collectives  30 us (13%)
  between operations  14.7 us (6%)
    ppermute x12, waiting for transfers between devices, from_ahead(): lax.ppermute(block, axis, [(i, (i - distance) % size) for i in range(size)])  43.3 us
    all_to_all x1, blocking collectives, per_device(): own = lax.all_to_all(heads, 'z', 0, 0, tiled=True)  16.3 us
    ppermute x12, starting transfers between devices, from_ahead(): lax.ppermute(block, axis, [(i, (i - distance) % size) for i in range(size)])  16 us
    all_to_all x1, blocking collectives, per_device(): done = lax.all_to_all(done, 'z', 0, 0, tiled=True)  13.7 us
    all_to_all x1, waiting for transfers between devices, per_device(): terms = lax.all_to_all(terms, 'y', 0, 0, tiled=True)  10.9 us
    ppermute x1, waiting for transfers between devices, per_device(): queue = lax.ppermute(leaving, ('x', 'core', 'z', 'y'), route)  10.3 us
    ppermute x4, starting transfers between devices, shifted(): return lax.ppermute(block, axis, route)  9.87 us
    all_gather x1, waiting for transfers between devices, per_device(): later = lax.all_gather(pack, 'z', axis=0, tiled=False)  9.64 us
  transfers between devices with their start and end apart: 32, of which 17 were waited for; matrix products, arithmetic and copies ran while one was open for 0% of the time, Pallas kernels for 15%

profile of v9, /device:TPU:4, one launch (start us, length us, event | category | flops | bytes accessed | tf_op | source)
XLA Modules:
  0.0 228.0 jit_solution(2569933525125922324)
XLA Ops:
  7.9 2.4 %prepare.1 = (bf16[32,3072]{1,0:T(8,128)(2,1)S(1)}, bf16[448,384]{1,0:T(8,128)(2,1)}) custom-call(s32[1,2]{1,0:T(1,128)S(1)} %copy-done.1, bf16[1,32,3072]{2,1,0:T(8,128)(2,1)} %latent.1, bf16[16,3072]{1,0:T(8,128)(2,1)} %pos.1, bf16[2,192,3072]{2,1,0:T(8,128)(2,1)} %bitcast.18), custom_call_target="tpu_custom_call" | custom-call | flops 300000 | bytes 800000 | tf_op jit(solution)/shard_map/prepare/pallas_call | solution.py:93
  10.3 2.0 shares.1
  12.4 3.1 %collective-permute-start = (bf16[192,1536]{1,0:T(8,128)(2,1)}, bf16[192,1536]{1,0:T(8,128)(2,1)S(1)}, u32[]{:S(2)}, u32[]{:S(2)}) collective-permute-start(bf16[192,1536]{1,0:T(8,128)(2,1)} %get-tuple-element.48), channel_id=1, source_target_pairs={{0,3},{1,0},{2,1},{3,2},{4,7},{5,4},{6,5},{7,6},{8,11},{9,8},{10,9... | collective-permute-start | bytes 1769480 | tf_op jit(solution)/shard_map/ppermute | solution.py:476
  16.2 1.0 collective-permute-start.2
  17.1 23.9 %collective-permute-done.refs_0_ = bf16[192,1536]{1,0:T(8,128)(2,1)S(1)} collective-permute-done((bf16[192,1536]{1,0:T(8,128)(2,1)}, bf16[192,1536]{1,0:T(8,128)(2,1)S(1)}, u32[]{:S(2)}, u32[]{:S(2)}) %collective-permute-start) | collective-permute-done | bytes 589856 | tf_op jit(solution)/shard_map/ppermute | solution.py:476
  41.6 3.1 %collective-permute-done.2.refs_2_ = bf16[192,1536]{1,0:T(8,128)(2,1)S(1)} collective-permute-done((bf16[192,1536]{1,0:T(8,128)(2,1)}, bf16[192,1536]{1,0:T(8,128)(2,1)S(1)}, u32[]{:S(2)}, u32[]{:S(2)}) %collective-permute-start.2) | collective-permute-done | bytes 589856 | tf_op jit(solution)/shard_map/ppermute | solution.py:476
  45.5 0.8 dynamic-slice_convert_fusion
  46.8 9.6 %all-gather.9.cloned.1.call-done = bf16[3584,384]{1,0:T(8,128)(2,1)} async-done(((bf16[448,384]{1,0:T(8,128)(2,1)}), bf16[3584,384]{1,0:T(8,128)(2,1)}) %all-gather.9.cloned.1.call-update) | async-done | bytes 2752528 | tf_op jit(solution)/shard_map/all_gather | solution.py:498
  56.5 5.3 %qkv_first.1 = (bf16[4,192,256]{2,1,0:T(8,128)(2,1)}, bf16[5,192,384]{2,1,0:T(8,128)(2,1)}, bf16[3,192,384]{2,1,0:T(8,128)(2,1)}) custom-call(bf16[8,448,384]{2,1,0:T(8,128)(2,1)} %bitcast.23, f32[6,3072]{1,0:T(8,128)S(1)} %reshape.15.mods, bf16[2,192,3072]{2,1,0:T(8,128)(2,1)} %bitcast.20, bf16[192,1536]{1,0:T(8,128)(2,1)S(1)} %collective-permute-done.refs_0_, ...), custom_call_target="tpu_custom_call" | custom-call | flops 1200000000 | bytes 14000000 | tf_op jit(solution)/shard_map/qkv_first/pallas_call | solution.py:174
  62.4 1.5 collective-permute-start.7
  63.8 4.3 %all-to-all-start = ((bf16[4,192,256]{2,1,0:T(8,128)(2,1)}), bf16[4,192,256]{2,1,0:T(8,128)(2,1)S(1)}, u32[]{:S(2)}, u32[]{:S(2)}) async-start(bf16[4,192,256]{2,1,0:T(8,128)(2,1)} %get-tuple-element.49), calls=%async_computation | async-start | bytes 786432 | tf_op jit(solution)/shard_map/all_to_all | solution.py:510
  68.1 7.4 %all-to-all-done.own = bf16[4,192,256]{2,1,0:T(8,128)(2,1)S(1)} async-done(((bf16[4,192,256]{2,1,0:T(8,128)(2,1)}), bf16[4,192,256]{2,1,0:T(8,128)(2,1)S(1)}, u32[]{:S(2)}, u32[]{:S(2)}) %all-to-all-start) | async-done | bytes 393248 | tf_op jit(solution)/shard_map/all_to_all | solution.py:510
  75.5 1.9 collective-permute-start.8
  77.4 2.4 %collective-permute-start.9 = (bf16[4,192,256]{2,1,0:T(8,128)(2,1)S(1)}, bf16[4,192,256]{2,1,0:T(8,128)(2,1)S(1)}, u32[]{:S(2)}, u32[]{:S(2)}) collective-permute-start(bf16[4,192,256]{2,1,0:T(8,128)(2,1)S(1)} %all-to-all-done.own), channel_id=1, source_target_pairs={{0,32},{32,64},{64,96},{96,128},{128,160},{160,192},{192,224},{1,3... | collective-permute-start | bytes 1179656 | tf_op jit(solution)/shard_map/ppermute | solution.py:486
  79.9 2.2 own_1.1
  82.0 4.5 %collective-permute-done.9.lower = bf16[4,192,256]{2,1,0:T(8,128)(2,1)S(1)} collective-permute-done((bf16[4,192,256]{2,1,0:T(8,128)(2,1)S(1)}, bf16[4,192,256]{2,1,0:T(8,128)(2,1)S(1)}, u32[]{:S(2)}, u32[]{:S(2)}) %collective-permute-start.9) | collective-permute-done | bytes 393248 | tf_op jit(solution)/shard_map/ppermute | solution.py:486
  87.1 2.6 %below_1.1 = (f32[4,64,256]{2,1,0:T(8,128)S(1)}, f32[4,1,256]{2,1,0:T(1,128)S(1)}) custom-call(bf16[4,192,256]{2,1,0:T(8,128)(2,1)S(1)} %collective-permute-done.9.lower, bf16[4,64,256]{2,1,0:T(8,128)(2,1)S(1)} %get-tuple-element.56.queries, f32[4,64,256]{2,1,0:T(8,128)S(1)} %get-tuple-element.58.acc_in, f32[4,1,256]{2,1,0:T(1,128)S(1)} %get-tuple-element.59.den_in), custom_call_target="tpu_custom_call" | custom-call | flops 3000000000 | bytes 1000000 | tf_op jit(solution)/shard_map/below_1/pallas_call | solution.py:322
  89.7 2.8 %above_1.1 = bf16[8,64,128]{2,1,0:T(8,128)(2,1)S(1)} custom-call(bf16[4,192,256]{2,1,0:T(8,128)(2,1)S(1)} %collective-permute-done.8.upper, bf16[4,64,256]{2,1,0:T(8,128)(2,1)S(1)} %get-tuple-element.56.queries, f32[4,64,256]{2,1,0:T(8,128)S(1)} %get-tuple-element.60.acc_in, f32[4,1,256]{2,1,0:T(1,128)S(1)} %get-tuple-element.61.den_in), custom_call_target="tpu_custom_call" | custom-call | flops 3000000000 | bytes 1000000 | tf_op jit(solution)/shard_map/above_1/pallas_call | solution.py:336
  92.4 5.2 %all-gather.11.cloned.1.call-done = bf16[2560,384]{1,0:T(8,128)(2,1)} async-done(((bf16[320,384]{1,0:T(8,128)(2,1)}), bf16[2560,384]{1,0:T(8,128)(2,1)}) %all-gather.11.cloned.1.call-update) | async-done | bytes 1966096 | tf_op jit(solution)/shard_map/all_gather | solution.py:499
  97.7 0.9 collective-permute-done.10.refs_2_
  98.6 13.7 %all_to_all.25.o = bf16[8,64,128]{2,1,0:T(8,128)(2,1)S(1)} all-to-all(bf16[8,64,128]{2,1,0:T(8,128)(2,1)S(1)} %above_1.1), channel_id=1, replica_groups=mesh['x'=4,'core'=2,'z'=8,'y'=4] {'z'}, dimensions={0} | all-to-all | bytes 262144 | tf_op jit(solution)/shard_map/all_to_all | solution.py:521
  112.3 4.3 %project_first.1 = (bf16[128,3072]{1,0:T(8,128)(2,1)}, bf16[8,64,384]{2,1,0:T(8,128)(2,1)}) custom-call(bf16[8,64,128]{2,1,0:T(8,128)(2,1)S(1)} %all_to_all.25.o, bf16[8,320,384]{2,1,0:T(8,128)(2,1)} %bitcast.25, bf16[8,320,384]{2,1,0:T(8,128)(2,1)S(1)} %collective-permute-done.11.other), custom_call_target="tpu_custom_call" | custom-call | flops 420000000 | bytes 4000000 | tf_op jit(solution)/shard_map/project_first/pallas_call | solution.py:383
  116.6 3.5 %all-to-all-start.2 = ((bf16[4,32,3072]{2,1,0:T(8,128)(2,1)}), bf16[4,32,3072]{2,1,0:T(8,128)(2,1)S(1)}, u32[]{:S(2)}, u32[]{:S(2)}) async-start(bf16[4,32,3072]{2,1,0:T(8,128)(2,1)} %bitcast.7), calls=%async_computation.2 | async-start | bytes 1572864 | tf_op jit(solution)/shard_map/all_to_all | solution.py:527
  121.3 10.9 %all-to-all-done.2.terms = bf16[4,32,3072]{2,1,0:T(8,128)(2,1)S(1)} async-done(((bf16[4,32,3072]{2,1,0:T(8,128)(2,1)}), bf16[4,32,3072]{2,1,0:T(8,128)(2,1)S(1)}, u32[]{:S(2)}, u32[]{:S(2)}) %all-to-all-start.2) | async-done | bytes 786464 | tf_op jit(solution)/shard_map/all_to_all | solution.py:527
  132.3 1.2 collective-permute-start.12
  133.5 1.5 collective-permute-start.13
  135.0 4.6 %collective-permute-done.12.x1 = bf16[32,3072]{1,0:T(8,128)(2,1)S(1)} collective-permute-done((bf16[32,3072]{1,0:T(8,128)(2,1)S(1)}, bf16[32,3072]{1,0:T(8,128)(2,1)S(1)}, u32[]{:S(2)}, u32[]{:S(2)}) %collective-permute-start.12) | collective-permute-done | bytes 196640 | tf_op jit(solution)/shard_map/ppermute | solution.py:476
  139.6 2.5 %collective-permute-done.13.x2 = bf16[32,3072]{1,0:T(8,128)(2,1)S(1)} collective-permute-done((bf16[32,3072]{1,0:T(8,128)(2,1)S(1)}, bf16[32,3072]{1,0:T(8,128)(2,1)S(1)}, u32[]{:S(2)}, u32[]{:S(2)}) %collective-permute-start.13) | collective-permute-done | bytes 196640 | tf_op jit(solution)/shard_map/ppermute | solution.py:476
  142.1 2.0 collective-permute-done.14.x3
  144.1 6.6 %qkv_second.1 = bf16[8,192,128]{2,1,0:T(8,128)(2,1)S(1)} custom-call(bf16[32,3072]{1,0:T(8,128)(2,1)S(1)} %residual.1.x0.x, bf16[32,3072]{1,0:T(8,128)(2,1)S(1)} %collective-permute-done.12.x1, bf16[32,3072]{1,0:T(8,128)(2,1)S(1)} %collective-permute-done.13.x2, bf16[32,3072]{1,0:T(8,128)(2,1)S(1)} %collective-permute-done.14.x3, ...), custom_call_target="tpu_custom_call" | custom-call | flops 1200000000 | bytes 10500000 | tf_op jit(solution)/shard_map/qkv_second/pallas_call | solution.py:220
  150.8 16.3 %all_to_all.26.own = bf16[8,192,128]{2,1,0:T(8,128)(2,1)S(1)} all-to-all(bf16[8,192,128]{2,1,0:T(8,128)(2,1)S(1)} %qkv_second.1), channel_id=1, replica_groups=mesh['x'=4,'core'=2,'z'=8,'y'=4] {'z'}, dimensions={0} | all-to-all | bytes 786432 | tf_op jit(solution)/shard_map/all_to_all | solution.py:532
  167.1 1.9 collective-permute-start.20
  169.0 3.6 %collective-permute-start.19 = (bf16[8,192,128]{2,1,0:T(8,128)(2,1)S(1)}, bf16[8,192,128]{2,1,0:T(8,128)(2,1)S(1)}, u32[]{:S(2)}, u32[]{:S(2)}) collective-permute-start(bf16[8,192,128]{2,1,0:T(8,128)(2,1)S(1)} %all_to_all.26.own), channel_id=1, source_target_pairs={{32,0},{64,32},{96,64},{128,96},{160,128},{192,160},{224,192},{33,... | collective-permute-start | bytes 1179656 | tf_op jit(solution)/shard_map/ppermute | solution.py:486
  172.7 2.2 own_2.1
  174.8 1.3 collective-permute-done.20.lower
  176.2 2.6 %below_2.1 = (f32[4,64,256]{2,1,0:T(8,128)S(1)}, f32[4,1,256]{2,1,0:T(1,128)S(1)}) custom-call(bf16[8,192,128]{2,1,0:T(8,128)(2,1)S(1)} %collective-permute-done.20.lower, bf16[4,64,256]{2,1,0:T(8,128)(2,1)S(1)} %get-tuple-element.80.queries, f32[4,64,256]{2,1,0:T(8,128)S(1)} %get-tuple-element.81.acc_in, f32[4,1,256]{2,1,0:T(1,128)S(1)} %get-tuple-element.82.den_in), custom_call_target="tpu_custom_call" | custom-call | flops 3000000000 | bytes 1000000 | tf_op jit(solution)/shard_map/below_2/pallas_call | solution.py:322
  178.8 3.3 %above_2.1 = bf16[8,64,128]{2,1,0:T(8,128)(2,1)} custom-call(bf16[8,192,128]{2,1,0:T(8,128)(2,1)S(1)} %collective-permute-done.19.upper, bf16[4,64,256]{2,1,0:T(8,128)(2,1)S(1)} %get-tuple-element.80.queries, f32[4,64,256]{2,1,0:T(8,128)S(1)} %get-tuple-element.83.acc_in, f32[4,1,256]{2,1,0:T(1,128)S(1)} %get-tuple-element.84.den_in), custom_call_target="tpu_custom_call" | custom-call | flops 3000000000 | bytes 1000000 | tf_op jit(solution)/shard_map/above_2/pallas_call | solution.py:336
  182.0 3.4 %all-to-all-start.4 = ((bf16[8,64,128]{2,1,0:T(8,128)(2,1)}), bf16[8,64,128]{2,1,0:T(8,128)(2,1)S(1)}, u32[]{:S(2)}, u32[]{:S(2)}) async-start(bf16[8,64,128]{2,1,0:T(8,128)(2,1)} %above_2.1), calls=%async_computation.4 | async-start | bytes 262144 | tf_op jit(solution)/shard_map/all_to_all | solution.py:537
  185.4 9.4 %all-to-all-done.4.o = bf16[8,64,128]{2,1,0:T(8,128)(2,1)S(1)} async-done(((bf16[8,64,128]{2,1,0:T(8,128)(2,1)}), bf16[8,64,128]{2,1,0:T(8,128)(2,1)S(1)}, u32[]{:S(2)}, u32[]{:S(2)}) %all-to-all-start.4) | async-done | bytes 131104 | tf_op jit(solution)/shard_map/all_to_all | solution.py:537
  194.8 2.4 %project_second.1 = (bf16[32,3072]{1,0:T(8,128)(2,1)S(1)}, bf16[32,3072]{1,0:T(8,128)(2,1)S(1)}, bf16[32,3072]{1,0:T(8,128)(2,1)S(1)}, bf16[32,3072]{1,0:T(8,128)(2,1)S(1)}) custom-call(bf16[8,64,128]{2,1,0:T(8,128)(2,1)S(1)} %all-to-all-done.4.o, bf16[8,8,64,384]{3,2,1,0:T(8,128)(2,1)} %bitcast.22), custom_call_target="tpu_custom_call" | custom-call | flops 420000000 | bytes 4000000 | tf_op jit(solution)/shard_map/project_second/pallas_call | solution.py:409
  197.2 1.8 collective-permute-start.21
  199.0 2.7 %collective-permute-start.22 = (bf16[32,3072]{1,0:T(8,128)(2,1)S(1)}, bf16[32,3072]{1,0:T(8,128)(2,1)S(1)}, u32[]{:S(2)}, u32[]{:S(2)}) collective-permute-start(bf16[32,3072]{1,0:T(8,128)(2,1)S(1)} %get-tuple-element.88), channel_id=1, source_target_pairs={{0,2},{1,3},{2,0},{3,1},{4,6},{5,7},{6,4},{7,5},{8,10},{9,11},{10,... | collective-permute-start | bytes 589832 | tf_op jit(solution)/shard_map/ppermute | solution.py:476
  201.8 1.4 collective-permute-start.23
  203.2 2.9 %collective-permute-done.21.t1 = bf16[32,3072]{1,0:T(8,128)(2,1)S(1)} collective-permute-done((bf16[32,3072]{1,0:T(8,128)(2,1)S(1)}, bf16[32,3072]{1,0:T(8,128)(2,1)S(1)}, u32[]{:S(2)}, u32[]{:S(2)}) %collective-permute-start.21) | collective-permute-done | bytes 196640 | tf_op jit(solution)/shard_map/ppermute | solution.py:476
  206.1 3.3 %collective-permute-done.22.t2 = bf16[32,3072]{1,0:T(8,128)(2,1)S(1)} collective-permute-done((bf16[32,3072]{1,0:T(8,128)(2,1)S(1)}, bf16[32,3072]{1,0:T(8,128)(2,1)S(1)}, u32[]{:S(2)}, u32[]{:S(2)}) %collective-permute-start.22) | collective-permute-done | bytes 196640 | tf_op jit(solution)/shard_map/ppermute | solution.py:476
  209.4 0.8 last.1
  210.4 10.3 %collective-permute-done.24 = bf16[32,3072]{1,0:T(8,128)(2,1)S(1)} collective-permute-done((bf16[32,3072]{1,0:T(8,128)(2,1)S(1)}, bf16[32,3072]{1,0:T(8,128)(2,1)S(1)}, u32[]{:S(2)}, u32[]{:S(2)}) %collective-permute-start.24) | collective-permute-done | bytes 196640 | tf_op jit(solution)/shard_map/ppermute | solution.py:544
  220.8 0.7 copy.16
  (48 shorter events, 5.3 us)
Async XLA Ops:
  7.2 49.3 %all-gather.9.cloned.1.call-start = ((), (), s32[]{:S(2)}) async-start(), calls=%async_computation.5 | async-start | bytes 3096576 | tf_op jit(solution)/shard_map/all_gather | solution.py:498
  7.2 0.7 copy-start.1
  10.3 87.4 %all-gather.11.cloned.1.call-start = ((), (), s32[]{:S(2)}) async-start(), calls=%async_computation.6 | async-start | bytes 2211840 | tf_op jit(solution)/shard_map/all_gather | solution.py:499
  12.4 131.8 %all-gather.13.cloned.1.call-start = ((), (), s32[]{:S(2)}) async-start(), calls=%async_computation.7 | async-start | bytes 6635520 | tf_op jit(solution)/shard_map/all_gather | solution.py:508
  12.4 28.6 %collective-permute-start = (bf16[192,1536]{1,0:T(8,128)(2,1)}, bf16[192,1536]{1,0:T(8,128)(2,1)S(1)}, u32[]{:S(2)}, u32[]{:S(2)}) collective-permute-start(bf16[192,1536]{1,0:T(8,128)(2,1)} %get-tuple-element.48), channel_id=1, source_target_pairs={{0,3},{1,0},{2,1},{3,2},{4,7},{5,4},{6,5},{7,6},{8,11},{9,8},{10,9... | collective-permute-start | bytes 1769480 | tf_op jit(solution)/shard_map/ppermute | solution.py:476
  15.5 25.5 %collective-permute-start.1 = (bf16[192,1536]{1,0:T(8,128)(2,1)}, bf16[192,1536]{1,0:T(8,128)(2,1)S(1)}, u32[]{:S(2)}, u32[]{:S(2)}) collective-permute-start(bf16[192,1536]{1,0:T(8,128)(2,1)} %get-tuple-element.48), channel_id=1, source_target_pairs={{0,2},{1,3},{2,0},{3,1},{4,6},{5,7},{6,4},{7,5},{8,10},{9,11},{10,... | collective-permute-start | bytes 1769480 | tf_op jit(solution)/shard_map/ppermute | solution.py:476
  16.2 28.5 %collective-permute-start.2 = (bf16[192,1536]{1,0:T(8,128)(2,1)}, bf16[192,1536]{1,0:T(8,128)(2,1)S(1)}, u32[]{:S(2)}, u32[]{:S(2)}) collective-permute-start(bf16[192,1536]{1,0:T(8,128)(2,1)} %get-tuple-element.48), channel_id=1, source_target_pairs={{0,1},{1,2},{2,3},{3,0},{4,5},{5,6},{6,7},{7,4},{8,9},{9,10},{10,1... | collective-permute-start | bytes 1769480 | tf_op jit(solution)/shard_map/ppermute | solution.py:476
  41.1 5.3 %collective-permute-start.3 = (bf16[192,1536]{1,0:T(8,128)(2,1)S(1)}, bf16[192,1536]{1,0:T(8,128)(2,1)S(1)}, u32[]{:S(2)}, u32[]{:S(2)}) collective-permute-start(bf16[192,1536]{1,0:T(8,128)(2,1)S(1)} %collective-permute-done.refs_0_), channel_id=1, source_target_pairs={{0,32},{32,0},{1,33},{33,1},{2,34},{34,2},{3,35},{35,3},{4,36},{36... | collective-permute-start | bytes 1769480 | tf_op jit(solution)/shard_map/ppermute | solution.py:480
  41.1 5.3 %collective-permute-start.4 = (bf16[192,1536]{1,0:T(8,128)(2,1)S(1)}, bf16[192,1536]{1,0:T(8,128)(2,1)S(1)}, u32[]{:S(2)}, u32[]{:S(2)}) collective-permute-start(bf16[192,1536]{1,0:T(8,128)(2,1)S(1)} %collective-permute-done.1.refs_1_), channel_id=1, source_target_pairs={{0,32},{32,0},{1,33},{33,1},{2,34},{34,2},{3,35},{35,3},{4,36},{36... | collective-permute-start | bytes 1769480 | tf_op jit(solution)/shard_map/ppermute | solution.py:480
  44.7 2.1 collective-permute-start.5
  56.4 11.7 %copy-start.2 = (bf16[2,1,128]{2,0,1:T(2,128)(2,1)S(1)}, bf16[2,1,128]{2,0,1:T(2,128)(2,1)}, u32[]{:S(2)}) copy-start(bf16[2,1,128]{2,0,1:T(2,128)(2,1)} %param.16) | copy-start | bytes 1540
  61.7 13.8 %collective-permute-start.6 = (bf16[3,192,384]{2,1,0:T(8,128)(2,1)}, bf16[3,192,384]{2,1,0:T(8,128)(2,1)S(1)}, u32[]{:S(2)}, u32[]{:S(2)}) collective-permute-start(bf16[3,192,384]{2,1,0:T(8,128)(2,1)} %get-tuple-element.76.refs_0_), channel_id=1, source_target_pairs={{0,192},{64,0},{128,64},{192,128},{1,193},{65,1},{129,65},{193,129... | collective-permute-start | bytes 1327112 | tf_op jit(solution)/shard_map/ppermute | solution.py:476
  62.4 13.1 %collective-permute-start.7 = (bf16[3,192,384]{2,1,0:T(8,128)(2,1)}, bf16[3,192,384]{2,1,0:T(8,128)(2,1)S(1)}, u32[]{:S(2)}, u32[]{:S(2)}) collective-permute-start(bf16[3,192,384]{2,1,0:T(8,128)(2,1)} %get-tuple-element.76.refs_0_), channel_id=1, source_target_pairs={{0,64},{64,128},{128,192},{192,0},{1,65},{65,129},{129,193},{193,1... | collective-permute-start | bytes 1327112 | tf_op jit(solution)/shard_map/ppermute | solution.py:476
  63.8 11.7 %all-to-all-start = ((bf16[4,192,256]{2,1,0:T(8,128)(2,1)}), bf16[4,192,256]{2,1,0:T(8,128)(2,1)S(1)}, u32[]{:S(2)}, u32[]{:S(2)}) async-start(bf16[4,192,256]{2,1,0:T(8,128)(2,1)} %get-tuple-element.49), calls=%async_computation | async-start | bytes 786432 | tf_op jit(solution)/shard_map/all_to_all | solution.py:510
  68.1 117.3 %all-gather.15.cloned.1.call-start = ((), (), s32[]{:S(2)}) async-start(), calls=%async_computation.8 | async-start | bytes 3538944 | tf_op jit(solution)/shard_map/all_gather | solution.py:526
  75.5 11.0 %collective-permute-start.8 = (bf16[4,192,256]{2,1,0:T(8,128)(2,1)S(1)}, bf16[4,192,256]{2,1,0:T(8,128)(2,1)S(1)}, u32[]{:S(2)}, u32[]{:S(2)}) collective-permute-start(bf16[4,192,256]{2,1,0:T(8,128)(2,1)S(1)} %all-to-all-done.own), channel_id=1, source_target_pairs={{32,0},{64,32},{96,64},{128,96},{160,128},{192,160},{224,192},{33,... | collective-permute-start | bytes 1179656 | tf_op jit(solution)/shard_map/ppermute | solution.py:486
  77.4 9.1 %collective-permute-start.9 = (bf16[4,192,256]{2,1,0:T(8,128)(2,1)S(1)}, bf16[4,192,256]{2,1,0:T(8,128)(2,1)S(1)}, u32[]{:S(2)}, u32[]{:S(2)}) collective-permute-start(bf16[4,192,256]{2,1,0:T(8,128)(2,1)S(1)} %all-to-all-done.own), channel_id=1, source_target_pairs={{0,32},{32,64},{64,96},{96,128},{128,160},{160,192},{192,224},{1,3... | collective-permute-start | bytes 1179656 | tf_op jit(solution)/shard_map/ppermute | solution.py:486
  86.5 12.1 %collective-permute-start.10 = (bf16[3,192,384]{2,1,0:T(8,128)(2,1)S(1)}, bf16[3,192,384]{2,1,0:T(8,128)(2,1)S(1)}, u32[]{:S(2)}, u32[]{:S(2)}) collective-permute-start(bf16[3,192,384]{2,1,0:T(8,128)(2,1)S(1)} %collective-permute-done.6.refs_1_), channel_id=1, source_target_pairs={{0,192},{64,0},{128,64},{192,128},{1,193},{65,1},{129,65},{193,129... | collective-permute-start | bytes 1327112 | tf_op jit(solution)/shard_map/ppermute | solution.py:476
  98.6 13.7 %collective-permute-start.11 = (bf16[8,320,384]{2,1,0:T(8,128)(2,1)}, bf16[8,320,384]{2,1,0:T(8,128)(2,1)S(1)}, u32[]{:S(2)}, u32[]{:S(2)}) collective-permute-start(bf16[8,320,384]{2,1,0:T(8,128)(2,1)} %bitcast.24), channel_id=1, source_target_pairs={{0,32},{32,0},{1,33},{33,1},{2,34},{34,2},{3,35},{35,3},{4,36},{36... | collective-permute-start | bytes 5898248 | tf_op jit(solution)/shard_map/ppermute | solution.py:480
  112.3 7.8 %copy-start = (bf16[3,192,384]{2,1,0:T(8,128)(2,1)S(1)}, bf16[3,192,384]{2,1,0:T(8,128)(2,1)}, u32[]{:S(2)}) copy-start(bf16[3,192,384]{2,1,0:T(8,128)(2,1)} %get-tuple-element.76.refs_0_) | copy-start | bytes 1327108
  116.6 15.5 %all-to-all-start.2 = ((bf16[4,32,3072]{2,1,0:T(8,128)(2,1)}), bf16[4,32,3072]{2,1,0:T(8,128)(2,1)S(1)}, u32[]{:S(2)}, u32[]{:S(2)}) async-start(bf16[4,32,3072]{2,1,0:T(8,128)(2,1)} %bitcast.7), calls=%async_computation.2 | async-start | bytes 1572864 | tf_op jit(solution)/shard_map/all_to_all | solution.py:527
  120.1 13.4 %collective-permute-start.15 = (bf16[3,192,384]{2,1,0:T(8,128)(2,1)S(1)}, bf16[3,192,384]{2,1,0:T(8,128)(2,1)S(1)}, u32[]{:S(2)}, u32[]{:S(2)}) collective-permute-start(bf16[3,192,384]{2,1,0:T(8,128)(2,1)S(1)} %copy-done), channel_id=1, source_target_pairs={{0,32},{32,0},{1,33},{33,1},{2,34},{34,2},{3,35},{35,3},{4,36},{36... | collective-permute-start | bytes 1327112 | tf_op jit(solution)/shard_map/ppermute | solution.py:480
  120.2 14.7 %collective-permute-start.16 = (bf16[3,192,384]{2,1,0:T(8,128)(2,1)S(1)}, bf16[3,192,384]{2,1,0:T(8,128)(2,1)}, u32[]{:S(2)}, u32[]{:S(2)}) collective-permute-start(bf16[3,192,384]{2,1,0:T(8,128)(2,1)S(1)} %collective-permute-done.6.refs_1_), channel_id=1, source_target_pairs={{0,32},{32,0},{1,33},{33,1},{2,34},{34,2},{3,35},{35,3},{4,36},{36... | collective-permute-start | bytes 1327112 | tf_op jit(solution)/shard_map/ppermute | solution.py:480
  120.7 14.3 %collective-permute-start.17 = (bf16[3,192,384]{2,1,0:T(8,128)(2,1)S(1)}, bf16[3,192,384]{2,1,0:T(8,128)(2,1)}, u32[]{:S(2)}, u32[]{:S(2)}) collective-permute-start(bf16[3,192,384]{2,1,0:T(8,128)(2,1)S(1)} %collective-permute-done.10.refs_2_), channel_id=1, source_target_pairs={{0,32},{32,0},{1,33},{33,1},{2,34},{34,2},{3,35},{35,3},{4,36},{36... | collective-permute-start | bytes 1327112 | tf_op jit(solution)/shard_map/ppermute | solution.py:480
  120.8 14.2 %collective-permute-start.18 = (bf16[3,192,384]{2,1,0:T(8,128)(2,1)S(1)}, bf16[3,192,384]{2,1,0:T(8,128)(2,1)}, u32[]{:S(2)}, u32[]{:S(2)}) collective-permute-start(bf16[3,192,384]{2,1,0:T(8,128)(2,1)S(1)} %collective-permute-done.7.refs_3_), channel_id=1, source_target_pairs={{0,32},{32,0},{1,33},{33,1},{2,34},{34,2},{3,35},{35,3},{4,36},{36... | collective-permute-start | bytes 1327112 | tf_op jit(solution)/shard_map/ppermute | solution.py:480
  132.3 7.4 %collective-permute-start.12 = (bf16[32,3072]{1,0:T(8,128)(2,1)S(1)}, bf16[32,3072]{1,0:T(8,128)(2,1)S(1)}, u32[]{:S(2)}, u32[]{:S(2)}) collective-permute-start(bf16[32,3072]{1,0:T(8,128)(2,1)S(1)} %residual.1.x0.x), channel_id=1, source_target_pairs={{0,3},{1,0},{2,1},{3,2},{4,7},{5,4},{6,5},{7,6},{8,11},{9,8},{10,9... | collective-permute-start | bytes 589832 | tf_op jit(solution)/shard_map/ppermute | solution.py:476
  133.5 8.6 %collective-permute-start.13 = (bf16[32,3072]{1,0:T(8,128)(2,1)S(1)}, bf16[32,3072]{1,0:T(8,128)(2,1)S(1)}, u32[]{:S(2)}, u32[]{:S(2)}) collective-permute-start(bf16[32,3072]{1,0:T(8,128)(2,1)S(1)} %residual.1.x0.x), channel_id=1, source_target_pairs={{0,2},{1,3},{2,0},{3,1},{4,6},{5,7},{6,4},{7,5},{8,10},{9,11},{10,... | collective-permute-start | bytes 589832 | tf_op jit(solution)/shard_map/ppermute | solution.py:476
  135.0 9.1 %collective-permute-start.14 = (bf16[32,3072]{1,0:T(8,128)(2,1)S(1)}, bf16[32,3072]{1,0:T(8,128)(2,1)S(1)}, u32[]{:S(2)}, u32[]{:S(2)}) collective-permute-start(bf16[32,3072]{1,0:T(8,128)(2,1)S(1)} %residual.1.x0.x), channel_id=1, source_target_pairs={{0,1},{1,2},{2,3},{3,0},{4,5},{5,6},{6,7},{7,4},{8,9},{9,10},{10,1... | collective-permute-start | bytes 589832 | tf_op jit(solution)/shard_map/ppermute | solution.py:476
  167.1 9.1 %collective-permute-start.20 = (bf16[8,192,128]{2,1,0:T(8,128)(2,1)S(1)}, bf16[8,192,128]{2,1,0:T(8,128)(2,1)S(1)}, u32[]{:S(2)}, u32[]{:S(2)}) collective-permute-start(bf16[8,192,128]{2,1,0:T(8,128)(2,1)S(1)} %all_to_all.26.own), channel_id=1, source_target_pairs={{0,32},{32,64},{64,96},{96,128},{128,160},{160,192},{192,224},{1,3... | collective-permute-start | bytes 1179656 | tf_op jit(solution)/shard_map/ppermute | solution.py:486
  169.0 9.7 %collective-permute-start.19 = (bf16[8,192,128]{2,1,0:T(8,128)(2,1)S(1)}, bf16[8,192,128]{2,1,0:T(8,128)(2,1)S(1)}, u32[]{:S(2)}, u32[]{:S(2)}) collective-permute-start(bf16[8,192,128]{2,1,0:T(8,128)(2,1)S(1)} %all_to_all.26.own), channel_id=1, source_target_pairs={{32,0},{64,32},{96,64},{128,96},{160,128},{192,160},{224,192},{33,... | collective-permute-start | bytes 1179656 | tf_op jit(solution)/shard_map/ppermute | solution.py:486
  182.0 12.8 %all-to-all-start.4 = ((bf16[8,64,128]{2,1,0:T(8,128)(2,1)}), bf16[8,64,128]{2,1,0:T(8,128)(2,1)S(1)}, u32[]{:S(2)}, u32[]{:S(2)}) async-start(bf16[8,64,128]{2,1,0:T(8,128)(2,1)} %above_2.1), calls=%async_computation.4 | async-start | bytes 262144 | tf_op jit(solution)/shard_map/all_to_all | solution.py:537
  197.2 8.8 %collective-permute-start.21 = (bf16[32,3072]{1,0:T(8,128)(2,1)S(1)}, bf16[32,3072]{1,0:T(8,128)(2,1)S(1)}, u32[]{:S(2)}, u32[]{:S(2)}) collective-permute-start(bf16[32,3072]{1,0:T(8,128)(2,1)S(1)} %get-tuple-element.87), channel_id=1, source_target_pairs={{0,1},{1,2},{2,3},{3,0},{4,5},{5,6},{6,7},{7,4},{8,9},{9,10},{10,1... | collective-permute-start | bytes 589832 | tf_op jit(solution)/shard_map/ppermute | solution.py:476
  199.0 10.4 %collective-permute-start.22 = (bf16[32,3072]{1,0:T(8,128)(2,1)S(1)}, bf16[32,3072]{1,0:T(8,128)(2,1)S(1)}, u32[]{:S(2)}, u32[]{:S(2)}) collective-permute-start(bf16[32,3072]{1,0:T(8,128)(2,1)S(1)} %get-tuple-element.88), channel_id=1, source_target_pairs={{0,2},{1,3},{2,0},{3,1},{4,6},{5,7},{6,4},{7,5},{8,10},{9,11},{10,... | collective-permute-start | bytes 589832 | tf_op jit(solution)/shard_map/ppermute | solution.py:476
  201.8 7.6 %collective-permute-start.23 = (bf16[32,3072]{1,0:T(8,128)(2,1)S(1)}, bf16[32,3072]{1,0:T(8,128)(2,1)S(1)}, u32[]{:S(2)}, u32[]{:S(2)}) collective-permute-start(bf16[32,3072]{1,0:T(8,128)(2,1)S(1)} %get-tuple-element.89), channel_id=1, source_target_pairs={{0,3},{1,0},{2,1},{3,2},{4,7},{5,4},{6,5},{7,6},{8,11},{9,8},{10,9... | collective-permute-start | bytes 589832 | tf_op jit(solution)/shard_map/ppermute | solution.py:476
  210.2 10.5 %collective-permute-start.24 = (bf16[32,3072]{1,0:T(8,128)(2,1)S(1)}, bf16[32,3072]{1,0:T(8,128)(2,1)S(1)}, u32[]{:S(2)}, u32[]{:S(2)}) collective-permute-start(bf16[32,3072]{1,0:T(8,128)(2,1)S(1)} %get-tuple-element.91), channel_id=1, source_target_pairs={{0,240},{1,241},{2,242},{3,243},{4,244},{5,245},{6,246},{7,247},{8... | collective-permute-start | bytes 589832 | tf_op jit(solution)/shard_map/ppermute | solution.py:544
Sparse Core Ops, SparseCore 0:
  10.4 46.0 all-gather.8
  58.2 39.4 all-gather.10
  99.5 38.9 all-gather.12
  140.2 30.3 all-gather.14

commit v10 on v9

--- a/solution.py
+++ b/solution.py
@@ -201,14 +201,14 @@
         start = (lax.rem(x_pos + n % NX, NX) * NC + side) * EIGHTH
         target = weights.at[LOW:, :, pl.ds(pl.multiple_of(start, 128), EIGHTH)]
         copies.append(pltpu.make_async_copy(weight, target, sems.at[8 + n]))
-    for copy in copies:
+    for copy in copies[8:] + copies[:8]:
         copy.start()
     for j, x in enumerate((x0, x1, x2, x3)):
         (norm,) = normalized([x[...].astype(F32)])
         part = norm * (1.0 + mods[4:5, :]) + mods[3:4, :]
         h[lax.rem(y + j, NY)] = part.astype(BF)
     tokens = h[...].reshape(NY * ROWS, D)
-    for part, (begin, end) in enumerate(((0, LOW), (LOW, NZ))):
+    for part, begin, end in ((1, LOW, NZ), (0, 0, LOW)):
         for copy in copies[8 * part : 8 * part + 8]:
             copy.wait()
         result = jnp.transpose(times(tokens, weights[begin:end].reshape((end - begin) * 3 * HD, D)))

time: 232 us -> 231 us (level)
  no operation moved by 1% of the time
where the time goes in v10:
time: 231 us; the launch traced here: 228 us
  waiting for transfers between devices  102 us (44%)
  Pallas kernels  39.2 us (17%)
  starting transfers between devices  39.1 us (17%)
  blocking collectives  30 us (13%)
  between operations  14.7 us (6%)
    ppermute x12, waiting for transfers between devices, from_ahead(): lax.ppermute(block, axis, [(i, (i - distance) % size) for i in range(size)])  43 us
    all_to_all x1, blocking collectives, per_device(): own = lax.all_to_all(heads, 'z', 0, 0, tiled=True)  16.3 us
    ppermute x12, starting transfers between devices, from_ahead(): lax.ppermute(block, axis, [(i, (i - distance) % size) for i in range(size)])  16 us
    all_to_all x1, blocking collectives, per_device(): done = lax.all_to_all(done, 'z', 0, 0, tiled=True)  13.7 us
    all_to_all x1, waiting for transfers between devices, per_device(): terms = lax.all_to_all(terms, 'y', 0, 0, tiled=True)  10.9 us
    ppermute x1, waiting for transfers between devices, per_device(): queue = lax.ppermute(leaving, ('x', 'core', 'z', 'y'), route)  10.7 us
    ppermute x4, starting transfers between devices, shifted(): return lax.ppermute(block, axis, route)  9.87 us
    all_gather x1, waiting for transfers between devices, per_device(): later = lax.all_gather(pack, 'z', axis=0, tiled=False)  9.64 us
  transfers between devices with their start and end apart: 32, of which 17 were waited for; matrix products, arithmetic and copies ran while one was open for 0% of the time, Pallas kernels for 15%

profile of v10, /device:TPU:4, one launch (start us, length us, event | category | flops | bytes accessed | tf_op | source)
XLA Modules:
  0.0 227.6 jit_solution(8295105426271565851)
XLA Ops:
  7.9 2.4 %prepare.1 = (bf16[32,3072]{1,0:T(8,128)(2,1)S(1)}, bf16[448,384]{1,0:T(8,128)(2,1)}) custom-call(s32[1,2]{1,0:T(1,128)S(1)} %copy-done.1, bf16[1,32,3072]{2,1,0:T(8,128)(2,1)} %latent.1, bf16[16,3072]{1,0:T(8,128)(2,1)} %pos.1, bf16[2,192,3072]{2,1,0:T(8,128)(2,1)} %bitcast.18), custom_call_target="tpu_custom_call" | custom-call | flops 300000 | bytes 800000 | tf_op jit(solution)/shard_map/prepare/pallas_call | solution.py:93
  10.3 2.0 shares.1
  12.4 3.1 %collective-permute-start = (bf16[192,1536]{1,0:T(8,128)(2,1)}, bf16[192,1536]{1,0:T(8,128)(2,1)S(1)}, u32[]{:S(2)}, u32[]{:S(2)}) collective-permute-start(bf16[192,1536]{1,0:T(8,128)(2,1)} %get-tuple-element.48), channel_id=1, source_target_pairs={{0,3},{1,0},{2,1},{3,2},{4,7},{5,4},{6,5},{7,6},{8,11},{9,8},{10,9... | collective-permute-start | bytes 1769480 | tf_op jit(solution)/shard_map/ppermute | solution.py:476
  16.2 1.0 collective-permute-start.2
  17.1 23.9 %collective-permute-done.refs_0_ = bf16[192,1536]{1,0:T(8,128)(2,1)S(1)} collective-permute-done((bf16[192,1536]{1,0:T(8,128)(2,1)}, bf16[192,1536]{1,0:T(8,128)(2,1)S(1)}, u32[]{:S(2)}, u32[]{:S(2)}) %collective-permute-start) | collective-permute-done | bytes 589856 | tf_op jit(solution)/shard_map/ppermute | solution.py:476
  41.6 3.1 %collective-permute-done.2.refs_2_ = bf16[192,1536]{1,0:T(8,128)(2,1)S(1)} collective-permute-done((bf16[192,1536]{1,0:T(8,128)(2,1)}, bf16[192,1536]{1,0:T(8,128)(2,1)S(1)}, u32[]{:S(2)}, u32[]{:S(2)}) %collective-permute-start.2) | collective-permute-done | bytes 589856 | tf_op jit(solution)/shard_map/ppermute | solution.py:476
  45.5 0.8 dynamic-slice_convert_fusion
  46.8 9.6 %all-gather.9.cloned.1.call-done = bf16[3584,384]{1,0:T(8,128)(2,1)} async-done(((bf16[448,384]{1,0:T(8,128)(2,1)}), bf16[3584,384]{1,0:T(8,128)(2,1)}) %all-gather.9.cloned.1.call-update) | async-done | bytes 2752528 | tf_op jit(solution)/shard_map/all_gather | solution.py:498
  56.5 5.3 %qkv_first.1 = (bf16[4,192,256]{2,1,0:T(8,128)(2,1)}, bf16[5,192,384]{2,1,0:T(8,128)(2,1)}, bf16[3,192,384]{2,1,0:T(8,128)(2,1)}) custom-call(bf16[8,448,384]{2,1,0:T(8,128)(2,1)} %bitcast.23, f32[6,3072]{1,0:T(8,128)S(1)} %reshape.15.mods, bf16[2,192,3072]{2,1,0:T(8,128)(2,1)} %bitcast.20, bf16[192,1536]{1,0:T(8,128)(2,1)S(1)} %collective-permute-done.refs_0_, ...), custom_call_target="tpu_custom_call" | custom-call | flops 1200000000 | bytes 14000000 | tf_op jit(solution)/shard_map/qkv_first/pallas_call | solution.py:174
  62.4 1.5 collective-permute-start.7
  63.8 4.3 %all-to-all-start = ((bf16[4,192,256]{2,1,0:T(8,128)(2,1)}), bf16[4,192,256]{2,1,0:T(8,128)(2,1)S(1)}, u32[]{:S(2)}, u32[]{:S(2)}) async-start(bf16[4,192,256]{2,1,0:T(8,128)(2,1)} %get-tuple-element.49), calls=%async_computation | async-start | bytes 786432 | tf_op jit(solution)/shard_map/all_to_all | solution.py:510
  68.1 7.4 %all-to-all-done.own = bf16[4,192,256]{2,1,0:T(8,128)(2,1)S(1)} async-done(((bf16[4,192,256]{2,1,0:T(8,128)(2,1)}), bf16[4,192,256]{2,1,0:T(8,128)(2,1)S(1)}, u32[]{:S(2)}, u32[]{:S(2)}) %all-to-all-start) | async-done | bytes 393248 | tf_op jit(solution)/shard_map/all_to_all | solution.py:510
  75.5 1.9 collective-permute-start.8
  77.4 2.4 %collective-permute-start.9 = (bf16[4,192,256]{2,1,0:T(8,128)(2,1)S(1)}, bf16[4,192,256]{2,1,0:T(8,128)(2,1)S(1)}, u32[]{:S(2)}, u32[]{:S(2)}) collective-permute-start(bf16[4,192,256]{2,1,0:T(8,128)(2,1)S(1)} %all-to-all-done.own), channel_id=1, source_target_pairs={{0,32},{32,64},{64,96},{96,128},{128,160},{160,192},{192,224},{1,3... | collective-permute-start | bytes 1179656 | tf_op jit(solution)/shard_map/ppermute | solution.py:486
  79.9 2.2 own_1.1
  82.0 4.5 %collective-permute-done.9.lower = bf16[4,192,256]{2,1,0:T(8,128)(2,1)S(1)} collective-permute-done((bf16[4,192,256]{2,1,0:T(8,128)(2,1)S(1)}, bf16[4,192,256]{2,1,0:T(8,128)(2,1)S(1)}, u32[]{:S(2)}, u32[]{:S(2)}) %collective-permute-start.9) | collective-permute-done | bytes 393248 | tf_op jit(solution)/shard_map/ppermute | solution.py:486
  87.1 2.6 %below_1.1 = (f32[4,64,256]{2,1,0:T(8,128)S(1)}, f32[4,1,256]{2,1,0:T(1,128)S(1)}) custom-call(bf16[4,192,256]{2,1,0:T(8,128)(2,1)S(1)} %collective-permute-done.9.lower, bf16[4,64,256]{2,1,0:T(8,128)(2,1)S(1)} %get-tuple-element.56.queries, f32[4,64,256]{2,1,0:T(8,128)S(1)} %get-tuple-element.58.acc_in, f32[4,1,256]{2,1,0:T(1,128)S(1)} %get-tuple-element.59.den_in), custom_call_target="tpu_custom_call" | custom-call | flops 3000000000 | bytes 1000000 | tf_op jit(solution)/shard_map/below_1/pallas_call | solution.py:322
  89.7 2.8 %above_1.1 = bf16[8,64,128]{2,1,0:T(8,128)(2,1)S(1)} custom-call(bf16[4,192,256]{2,1,0:T(8,128)(2,1)S(1)} %collective-permute-done.8.upper, bf16[4,64,256]{2,1,0:T(8,128)(2,1)S(1)} %get-tuple-element.56.queries, f32[4,64,256]{2,1,0:T(8,128)S(1)} %get-tuple-element.60.acc_in, f32[4,1,256]{2,1,0:T(1,128)S(1)} %get-tuple-element.61.den_in), custom_call_target="tpu_custom_call" | custom-call | flops 3000000000 | bytes 1000000 | tf_op jit(solution)/shard_map/above_1/pallas_call | solution.py:336
  92.4 5.2 %all-gather.11.cloned.1.call-done = bf16[2560,384]{1,0:T(8,128)(2,1)} async-done(((bf16[320,384]{1,0:T(8,128)(2,1)}), bf16[2560,384]{1,0:T(8,128)(2,1)}) %all-gather.11.cloned.1.call-update) | async-done | bytes 1966096 | tf_op jit(solution)/shard_map/all_gather | solution.py:499
  97.7 0.9 collective-permute-done.10.refs_2_
  98.6 13.7 %all_to_all.25.o = bf16[8,64,128]{2,1,0:T(8,128)(2,1)S(1)} all-to-all(bf16[8,64,128]{2,1,0:T(8,128)(2,1)S(1)} %above_1.1), channel_id=1, replica_groups=mesh['x'=4,'core'=2,'z'=8,'y'=4] {'z'}, dimensions={0} | all-to-all | bytes 262144 | tf_op jit(solution)/shard_map/all_to_all | solution.py:521
  112.3 4.3 %project_first.1 = (bf16[128,3072]{1,0:T(8,128)(2,1)}, bf16[8,64,384]{2,1,0:T(8,128)(2,1)}) custom-call(bf16[8,64,128]{2,1,0:T(8,128)(2,1)S(1)} %all_to_all.25.o, bf16[8,320,384]{2,1,0:T(8,128)(2,1)} %bitcast.25, bf16[8,320,384]{2,1,0:T(8,128)(2,1)S(1)} %collective-permute-done.11.other), custom_call_target="tpu_custom_call" | custom-call | flops 420000000 | bytes 4000000 | tf_op jit(solution)/shard_map/project_first/pallas_call | solution.py:383
  116.6 3.5 %all-to-all-start.2 = ((bf16[4,32,3072]{2,1,0:T(8,128)(2,1)}), bf16[4,32,3072]{2,1,0:T(8,128)(2,1)S(1)}, u32[]{:S(2)}, u32[]{:S(2)}) async-start(bf16[4,32,3072]{2,1,0:T(8,128)(2,1)} %bitcast.7), calls=%async_computation.2 | async-start | bytes 1572864 | tf_op jit(solution)/shard_map/all_to_all | solution.py:527
  121.3 10.9 %all-to-all-done.2.terms = bf16[4,32,3072]{2,1,0:T(8,128)(2,1)S(1)} async-done(((bf16[4,32,3072]{2,1,0:T(8,128)(2,1)}), bf16[4,32,3072]{2,1,0:T(8,128)(2,1)S(1)}, u32[]{:S(2)}, u32[]{:S(2)}) %all-to-all-start.2) | async-done | bytes 786464 | tf_op jit(solution)/shard_map/all_to_all | solution.py:527
  132.3 1.2 collective-permute-start.12
  133.5 1.5 collective-permute-start.13
  135.0 4.6 %collective-permute-done.12.x1 = bf16[32,3072]{1,0:T(8,128)(2,1)S(1)} collective-permute-done((bf16[32,3072]{1,0:T(8,128)(2,1)S(1)}, bf16[32,3072]{1,0:T(8,128)(2,1)S(1)}, u32[]{:S(2)}, u32[]{:S(2)}) %collective-permute-start.12) | collective-permute-done | bytes 196640 | tf_op jit(solution)/shard_map/ppermute | solution.py:476
  139.6 2.5 %collective-permute-done.13.x2 = bf16[32,3072]{1,0:T(8,128)(2,1)S(1)} collective-permute-done((bf16[32,3072]{1,0:T(8,128)(2,1)S(1)}, bf16[32,3072]{1,0:T(8,128)(2,1)S(1)}, u32[]{:S(2)}, u32[]{:S(2)}) %collective-permute-start.13) | collective-permute-done | bytes 196640 | tf_op jit(solution)/shard_map/ppermute | solution.py:476
  142.1 2.0 collective-permute-done.14.x3
  144.1 6.3 %qkv_second.1 = bf16[8,192,128]{2,1,0:T(8,128)(2,1)S(1)} custom-call(bf16[32,3072]{1,0:T(8,128)(2,1)S(1)} %residual.1.x0.x, bf16[32,3072]{1,0:T(8,128)(2,1)S(1)} %collective-permute-done.12.x1, bf16[32,3072]{1,0:T(8,128)(2,1)S(1)} %collective-permute-done.13.x2, bf16[32,3072]{1,0:T(8,128)(2,1)S(1)} %collective-permute-done.14.x3, ...), custom_call_target="tpu_custom_call" | custom-call | flops 1200000000 | bytes 10500000 | tf_op jit(solution)/shard_map/qkv_second/pallas_call | solution.py:220
  150.4 16.3 %all_to_all.26.own = bf16[8,192,128]{2,1,0:T(8,128)(2,1)S(1)} all-to-all(bf16[8,192,128]{2,1,0:T(8,128)(2,1)S(1)} %qkv_second.1), channel_id=1, replica_groups=mesh['x'=4,'core'=2,'z'=8,'y'=4] {'z'}, dimensions={0} | all-to-all | bytes 786432 | tf_op jit(solution)/shard_map/all_to_all | solution.py:532
  166.8 1.9 collective-permute-start.20
  168.7 3.6 %collective-permute-start.19 = (bf16[8,192,128]{2,1,0:T(8,128)(2,1)S(1)}, bf16[8,192,128]{2,1,0:T(8,128)(2,1)S(1)}, u32[]{:S(2)}, u32[]{:S(2)}) collective-permute-start(bf16[8,192,128]{2,1,0:T(8,128)(2,1)S(1)} %all_to_all.26.own), channel_id=1, source_target_pairs={{32,0},{64,32},{96,64},{128,96},{160,128},{192,160},{224,192},{33,... | collective-permute-start | bytes 1179656 | tf_op jit(solution)/shard_map/ppermute | solution.py:486
  172.3 2.2 own_2.1
  174.5 1.3 collective-permute-done.20.lower
  175.8 2.6 %below_2.1 = (f32[4,64,256]{2,1,0:T(8,128)S(1)}, f32[4,1,256]{2,1,0:T(1,128)S(1)}) custom-call(bf16[8,192,128]{2,1,0:T(8,128)(2,1)S(1)} %collective-permute-done.20.lower, bf16[4,64,256]{2,1,0:T(8,128)(2,1)S(1)} %get-tuple-element.80.queries, f32[4,64,256]{2,1,0:T(8,128)S(1)} %get-tuple-element.81.acc_in, f32[4,1,256]{2,1,0:T(1,128)S(1)} %get-tuple-element.82.den_in), custom_call_target="tpu_custom_call" | custom-call | flops 3000000000 | bytes 1000000 | tf_op jit(solution)/shard_map/below_2/pallas_call | solution.py:322
  178.4 3.3 %above_2.1 = bf16[8,64,128]{2,1,0:T(8,128)(2,1)} custom-call(bf16[8,192,128]{2,1,0:T(8,128)(2,1)S(1)} %collective-permute-done.19.upper, bf16[4,64,256]{2,1,0:T(8,128)(2,1)S(1)} %get-tuple-element.80.queries, f32[4,64,256]{2,1,0:T(8,128)S(1)} %get-tuple-element.83.acc_in, f32[4,1,256]{2,1,0:T(1,128)S(1)} %get-tuple-element.84.den_in), custom_call_target="tpu_custom_call" | custom-call | flops 3000000000 | bytes 1000000 | tf_op jit(solution)/shard_map/above_2/pallas_call | solution.py:336
  181.7 3.5 %all-to-all-start.4 = ((bf16[8,64,128]{2,1,0:T(8,128)(2,1)}), bf16[8,64,128]{2,1,0:T(8,128)(2,1)S(1)}, u32[]{:S(2)}, u32[]{:S(2)}) async-start(bf16[8,64,128]{2,1,0:T(8,128)(2,1)} %above_2.1), calls=%async_computation.4 | async-start | bytes 262144 | tf_op jit(solution)/shard_map/all_to_all | solution.py:537
  185.2 9.3 %all-to-all-done.4.o = bf16[8,64,128]{2,1,0:T(8,128)(2,1)S(1)} async-done(((bf16[8,64,128]{2,1,0:T(8,128)(2,1)}), bf16[8,64,128]{2,1,0:T(8,128)(2,1)S(1)}, u32[]{:S(2)}, u32[]{:S(2)}) %all-to-all-start.4) | async-done | bytes 131104 | tf_op jit(solution)/shard_map/all_to_all | solution.py:537
  194.5 2.4 %project_second.1 = (bf16[32,3072]{1,0:T(8,128)(2,1)S(1)}, bf16[32,3072]{1,0:T(8,128)(2,1)S(1)}, bf16[32,3072]{1,0:T(8,128)(2,1)S(1)}, bf16[32,3072]{1,0:T(8,128)(2,1)S(1)}) custom-call(bf16[8,64,128]{2,1,0:T(8,128)(2,1)S(1)} %all-to-all-done.4.o, bf16[8,8,64,384]{3,2,1,0:T(8,128)(2,1)} %bitcast.22), custom_call_target="tpu_custom_call" | custom-call | flops 420000000 | bytes 4000000 | tf_op jit(solution)/shard_map/project_second/pallas_call | solution.py:409
  196.9 1.8 collective-permute-start.21
  198.7 2.8 %collective-permute-start.22 = (bf16[32,3072]{1,0:T(8,128)(2,1)S(1)}, bf16[32,3072]{1,0:T(8,128)(2,1)S(1)}, u32[]{:S(2)}, u32[]{:S(2)}) collective-permute-start(bf16[32,3072]{1,0:T(8,128)(2,1)S(1)} %get-tuple-element.88), channel_id=1, source_target_pairs={{0,2},{1,3},{2,0},{3,1},{4,6},{5,7},{6,4},{7,5},{8,10},{9,11},{10,... | collective-permute-start | bytes 589832 | tf_op jit(solution)/shard_map/ppermute | solution.py:476
  201.4 1.4 collective-permute-start.23
  202.9 3.3 %collective-permute-done.21.t1 = bf16[32,3072]{1,0:T(8,128)(2,1)S(1)} collective-permute-done((bf16[32,3072]{1,0:T(8,128)(2,1)S(1)}, bf16[32,3072]{1,0:T(8,128)(2,1)S(1)}, u32[]{:S(2)}, u32[]{:S(2)}) %collective-permute-start.21) | collective-permute-done | bytes 196640 | tf_op jit(solution)/shard_map/ppermute | solution.py:476
  206.2 2.6 %collective-permute-done.22.t2 = bf16[32,3072]{1,0:T(8,128)(2,1)S(1)} collective-permute-done((bf16[32,3072]{1,0:T(8,128)(2,1)S(1)}, bf16[32,3072]{1,0:T(8,128)(2,1)S(1)}, u32[]{:S(2)}, u32[]{:S(2)}) %collective-permute-start.22) | collective-permute-done | bytes 196640 | tf_op jit(solution)/shard_map/ppermute | solution.py:476
  208.7 0.8 last.1
  209.7 10.7 %collective-permute-done.24 = bf16[32,3072]{1,0:T(8,128)(2,1)S(1)} collective-permute-done((bf16[32,3072]{1,0:T(8,128)(2,1)S(1)}, bf16[32,3072]{1,0:T(8,128)(2,1)S(1)}, u32[]{:S(2)}, u32[]{:S(2)}) %collective-permute-start.24) | collective-permute-done | bytes 196640 | tf_op jit(solution)/shard_map/ppermute | solution.py:544
  220.4 0.7 copy.16
  (48 shorter events, 5.2 us)
Async XLA Ops:
  7.2 49.3 %all-gather.9.cloned.1.call-start = ((), (), s32[]{:S(2)}) async-start(), calls=%async_computation.5 | async-start | bytes 3096576 | tf_op jit(solution)/shard_map/all_gather | solution.py:498
  7.2 0.7 copy-start.1
  10.3 87.4 %all-gather.11.cloned.1.call-start = ((), (), s32[]{:S(2)}) async-start(), calls=%async_computation.6 | async-start | bytes 2211840 | tf_op jit(solution)/shard_map/all_gather | solution.py:499
  12.4 131.8 %all-gather.13.cloned.1.call-start = ((), (), s32[]{:S(2)}) async-start(), calls=%async_computation.7 | async-start | bytes 6635520 | tf_op jit(solution)/shard_map/all_gather | solution.py:508
  12.4 28.6 %collective-permute-start = (bf16[192,1536]{1,0:T(8,128)(2,1)}, bf16[192,1536]{1,0:T(8,128)(2,1)S(1)}, u32[]{:S(2)}, u32[]{:S(2)}) collective-permute-start(bf16[192,1536]{1,0:T(8,128)(2,1)} %get-tuple-element.48), channel_id=1, source_target_pairs={{0,3},{1,0},{2,1},{3,2},{4,7},{5,4},{6,5},{7,6},{8,11},{9,8},{10,9... | collective-permute-start | bytes 1769480 | tf_op jit(solution)/shard_map/ppermute | solution.py:476
  15.5 25.5 %collective-permute-start.1 = (bf16[192,1536]{1,0:T(8,128)(2,1)}, bf16[192,1536]{1,0:T(8,128)(2,1)S(1)}, u32[]{:S(2)}, u32[]{:S(2)}) collective-permute-start(bf16[192,1536]{1,0:T(8,128)(2,1)} %get-tuple-element.48), channel_id=1, source_target_pairs={{0,2},{1,3},{2,0},{3,1},{4,6},{5,7},{6,4},{7,5},{8,10},{9,11},{10,... | collective-permute-start | bytes 1769480 | tf_op jit(solution)/shard_map/ppermute | solution.py:476
  16.2 28.5 %collective-permute-start.2 = (bf16[192,1536]{1,0:T(8,128)(2,1)}, bf16[192,1536]{1,0:T(8,128)(2,1)S(1)}, u32[]{:S(2)}, u32[]{:S(2)}) collective-permute-start(bf16[192,1536]{1,0:T(8,128)(2,1)} %get-tuple-element.48), channel_id=1, source_target_pairs={{0,1},{1,2},{2,3},{3,0},{4,5},{5,6},{6,7},{7,4},{8,9},{9,10},{10,1... | collective-permute-start | bytes 1769480 | tf_op jit(solution)/shard_map/ppermute | solution.py:476
  41.1 5.3 %collective-permute-start.3 = (bf16[192,1536]{1,0:T(8,128)(2,1)S(1)}, bf16[192,1536]{1,0:T(8,128)(2,1)S(1)}, u32[]{:S(2)}, u32[]{:S(2)}) collective-permute-start(bf16[192,1536]{1,0:T(8,128)(2,1)S(1)} %collective-permute-done.refs_0_), channel_id=1, source_target_pairs={{0,32},{32,0},{1,33},{33,1},{2,34},{34,2},{3,35},{35,3},{4,36},{36... | collective-permute-start | bytes 1769480 | tf_op jit(solution)/shard_map/ppermute | solution.py:480
  41.1 5.3 %collective-permute-start.4 = (bf16[192,1536]{1,0:T(8,128)(2,1)S(1)}, bf16[192,1536]{1,0:T(8,128)(2,1)S(1)}, u32[]{:S(2)}, u32[]{:S(2)}) collective-permute-start(bf16[192,1536]{1,0:T(8,128)(2,1)S(1)} %collective-permute-done.1.refs_1_), channel_id=1, source_target_pairs={{0,32},{32,0},{1,33},{33,1},{2,34},{34,2},{3,35},{35,3},{4,36},{36... | collective-permute-start | bytes 1769480 | tf_op jit(solution)/shard_map/ppermute | solution.py:480
  44.7 2.1 collective-permute-start.5
  56.4 11.7 %copy-start.2 = (bf16[2,1,128]{2,0,1:T(2,128)(2,1)S(1)}, bf16[2,1,128]{2,0,1:T(2,128)(2,1)}, u32[]{:S(2)}) copy-start(bf16[2,1,128]{2,0,1:T(2,128)(2,1)} %param.16) | copy-start | bytes 1540
  61.7 13.8 %collective-permute-start.6 = (bf16[3,192,384]{2,1,0:T(8,128)(2,1)}, bf16[3,192,384]{2,1,0:T(8,128)(2,1)S(1)}, u32[]{:S(2)}, u32[]{:S(2)}) collective-permute-start(bf16[3,192,384]{2,1,0:T(8,128)(2,1)} %get-tuple-element.76.refs_0_), channel_id=1, source_target_pairs={{0,192},{64,0},{128,64},{192,128},{1,193},{65,1},{129,65},{193,129... | collective-permute-start | bytes 1327112 | tf_op jit(solution)/shard_map/ppermute | solution.py:476
  62.4 13.1 %collective-permute-start.7 = (bf16[3,192,384]{2,1,0:T(8,128)(2,1)}, bf16[3,192,384]{2,1,0:T(8,128)(2,1)S(1)}, u32[]{:S(2)}, u32[]{:S(2)}) collective-permute-start(bf16[3,192,384]{2,1,0:T(8,128)(2,1)} %get-tuple-element.76.refs_0_), channel_id=1, source_target_pairs={{0,64},{64,128},{128,192},{192,0},{1,65},{65,129},{129,193},{193,1... | collective-permute-start | bytes 1327112 | tf_op jit(solution)/shard_map/ppermute | solution.py:476
  63.8 11.7 %all-to-all-start = ((bf16[4,192,256]{2,1,0:T(8,128)(2,1)}), bf16[4,192,256]{2,1,0:T(8,128)(2,1)S(1)}, u32[]{:S(2)}, u32[]{:S(2)}) async-start(bf16[4,192,256]{2,1,0:T(8,128)(2,1)} %get-tuple-element.49), calls=%async_computation | async-start | bytes 786432 | tf_op jit(solution)/shard_map/all_to_all | solution.py:510
  68.1 117.1 %all-gather.15.cloned.1.call-start = ((), (), s32[]{:S(2)}) async-start(), calls=%async_computation.8 | async-start | bytes 3538944 | tf_op jit(solution)/shard_map/all_gather | solution.py:526
  75.5 11.0 %collective-permute-start.8 = (bf16[4,192,256]{2,1,0:T(8,128)(2,1)S(1)}, bf16[4,192,256]{2,1,0:T(8,128)(2,1)S(1)}, u32[]{:S(2)}, u32[]{:S(2)}) collective-permute-start(bf16[4,192,256]{2,1,0:T(8,128)(2,1)S(1)} %all-to-all-done.own), channel_id=1, source_target_pairs={{32,0},{64,32},{96,64},{128,96},{160,128},{192,160},{224,192},{33,... | collective-permute-start | bytes 1179656 | tf_op jit(solution)/shard_map/ppermute | solution.py:486
  77.4 9.1 %collective-permute-start.9 = (bf16[4,192,256]{2,1,0:T(8,128)(2,1)S(1)}, bf16[4,192,256]{2,1,0:T(8,128)(2,1)S(1)}, u32[]{:S(2)}, u32[]{:S(2)}) collective-permute-start(bf16[4,192,256]{2,1,0:T(8,128)(2,1)S(1)} %all-to-all-done.own), channel_id=1, source_target_pairs={{0,32},{32,64},{64,96},{96,128},{128,160},{160,192},{192,224},{1,3... | collective-permute-start | bytes 1179656 | tf_op jit(solution)/shard_map/ppermute | solution.py:486
  86.5 12.1 %collective-permute-start.10 = (bf16[3,192,384]{2,1,0:T(8,128)(2,1)S(1)}, bf16[3,192,384]{2,1,0:T(8,128)(2,1)S(1)}, u32[]{:S(2)}, u32[]{:S(2)}) collective-permute-start(bf16[3,192,384]{2,1,0:T(8,128)(2,1)S(1)} %collective-permute-done.6.refs_1_), channel_id=1, source_target_pairs={{0,192},{64,0},{128,64},{192,128},{1,193},{65,1},{129,65},{193,129... | collective-permute-start | bytes 1327112 | tf_op jit(solution)/shard_map/ppermute | solution.py:476
  98.6 13.7 %collective-permute-start.11 = (bf16[8,320,384]{2,1,0:T(8,128)(2,1)}, bf16[8,320,384]{2,1,0:T(8,128)(2,1)S(1)}, u32[]{:S(2)}, u32[]{:S(2)}) collective-permute-start(bf16[8,320,384]{2,1,0:T(8,128)(2,1)} %bitcast.24), channel_id=1, source_target_pairs={{0,32},{32,0},{1,33},{33,1},{2,34},{34,2},{3,35},{35,3},{4,36},{36... | collective-permute-start | bytes 5898248 | tf_op jit(solution)/shard_map/ppermute | solution.py:480
  112.3 7.8 %copy-start = (bf16[3,192,384]{2,1,0:T(8,128)(2,1)S(1)}, bf16[3,192,384]{2,1,0:T(8,128)(2,1)}, u32[]{:S(2)}) copy-start(bf16[3,192,384]{2,1,0:T(8,128)(2,1)} %get-tuple-element.76.refs_0_) | copy-start | bytes 1327108
  116.6 15.5 %all-to-all-start.2 = ((bf16[4,32,3072]{2,1,0:T(8,128)(2,1)}), bf16[4,32,3072]{2,1,0:T(8,128)(2,1)S(1)}, u32[]{:S(2)}, u32[]{:S(2)}) async-start(bf16[4,32,3072]{2,1,0:T(8,128)(2,1)} %bitcast.7), calls=%async_computation.2 | async-start | bytes 1572864 | tf_op jit(solution)/shard_map/all_to_all | solution.py:527
  120.1 13.4 %collective-permute-start.15 = (bf16[3,192,384]{2,1,0:T(8,128)(2,1)S(1)}, bf16[3,192,384]{2,1,0:T(8,128)(2,1)S(1)}, u32[]{:S(2)}, u32[]{:S(2)}) collective-permute-start(bf16[3,192,384]{2,1,0:T(8,128)(2,1)S(1)} %copy-done), channel_id=1, source_target_pairs={{0,32},{32,0},{1,33},{33,1},{2,34},{34,2},{3,35},{35,3},{4,36},{36... | collective-permute-start | bytes 1327112 | tf_op jit(solution)/shard_map/ppermute | solution.py:480
  120.2 14.7 %collective-permute-start.16 = (bf16[3,192,384]{2,1,0:T(8,128)(2,1)S(1)}, bf16[3,192,384]{2,1,0:T(8,128)(2,1)}, u32[]{:S(2)}, u32[]{:S(2)}) collective-permute-start(bf16[3,192,384]{2,1,0:T(8,128)(2,1)S(1)} %collective-permute-done.6.refs_1_), channel_id=1, source_target_pairs={{0,32},{32,0},{1,33},{33,1},{2,34},{34,2},{3,35},{35,3},{4,36},{36... | collective-permute-start | bytes 1327112 | tf_op jit(solution)/shard_map/ppermute | solution.py:480
  120.7 14.3 %collective-permute-start.17 = (bf16[3,192,384]{2,1,0:T(8,128)(2,1)S(1)}, bf16[3,192,384]{2,1,0:T(8,128)(2,1)}, u32[]{:S(2)}, u32[]{:S(2)}) collective-permute-start(bf16[3,192,384]{2,1,0:T(8,128)(2,1)S(1)} %collective-permute-done.10.refs_2_), channel_id=1, source_target_pairs={{0,32},{32,0},{1,33},{33,1},{2,34},{34,2},{3,35},{35,3},{4,36},{36... | collective-permute-start | bytes 1327112 | tf_op jit(solution)/shard_map/ppermute | solution.py:480
  120.8 14.2 %collective-permute-start.18 = (bf16[3,192,384]{2,1,0:T(8,128)(2,1)S(1)}, bf16[3,192,384]{2,1,0:T(8,128)(2,1)}, u32[]{:S(2)}, u32[]{:S(2)}) collective-permute-start(bf16[3,192,384]{2,1,0:T(8,128)(2,1)S(1)} %collective-permute-done.7.refs_3_), channel_id=1, source_target_pairs={{0,32},{32,0},{1,33},{33,1},{2,34},{34,2},{3,35},{35,3},{4,36},{36... | collective-permute-start | bytes 1327112 | tf_op jit(solution)/shard_map/ppermute | solution.py:480
  132.3 7.4 %collective-permute-start.12 = (bf16[32,3072]{1,0:T(8,128)(2,1)S(1)}, bf16[32,3072]{1,0:T(8,128)(2,1)S(1)}, u32[]{:S(2)}, u32[]{:S(2)}) collective-permute-start(bf16[32,3072]{1,0:T(8,128)(2,1)S(1)} %residual.1.x0.x), channel_id=1, source_target_pairs={{0,3},{1,0},{2,1},{3,2},{4,7},{5,4},{6,5},{7,6},{8,11},{9,8},{10,9... | collective-permute-start | bytes 589832 | tf_op jit(solution)/shard_map/ppermute | solution.py:476
  133.5 8.6 %collective-permute-start.13 = (bf16[32,3072]{1,0:T(8,128)(2,1)S(1)}, bf16[32,3072]{1,0:T(8,128)(2,1)S(1)}, u32[]{:S(2)}, u32[]{:S(2)}) collective-permute-start(bf16[32,3072]{1,0:T(8,128)(2,1)S(1)} %residual.1.x0.x), channel_id=1, source_target_pairs={{0,2},{1,3},{2,0},{3,1},{4,6},{5,7},{6,4},{7,5},{8,10},{9,11},{10,... | collective-permute-start | bytes 589832 | tf_op jit(solution)/shard_map/ppermute | solution.py:476
  135.0 9.1 %collective-permute-start.14 = (bf16[32,3072]{1,0:T(8,128)(2,1)S(1)}, bf16[32,3072]{1,0:T(8,128)(2,1)S(1)}, u32[]{:S(2)}, u32[]{:S(2)}) collective-permute-start(bf16[32,3072]{1,0:T(8,128)(2,1)S(1)} %residual.1.x0.x), channel_id=1, source_target_pairs={{0,1},{1,2},{2,3},{3,0},{4,5},{5,6},{6,7},{7,4},{8,9},{9,10},{10,1... | collective-permute-start | bytes 589832 | tf_op jit(solution)/shard_map/ppermute | solution.py:476
  166.8 9.1 %collective-permute-start.20 = (bf16[8,192,128]{2,1,0:T(8,128)(2,1)S(1)}, bf16[8,192,128]{2,1,0:T(8,128)(2,1)S(1)}, u32[]{:S(2)}, u32[]{:S(2)}) collective-permute-start(bf16[8,192,128]{2,1,0:T(8,128)(2,1)S(1)} %all_to_all.26.own), channel_id=1, source_target_pairs={{0,32},{32,64},{64,96},{96,128},{128,160},{160,192},{192,224},{1,3... | collective-permute-start | bytes 1179656 | tf_op jit(solution)/shard_map/ppermute | solution.py:486
  168.7 9.8 %collective-permute-start.19 = (bf16[8,192,128]{2,1,0:T(8,128)(2,1)S(1)}, bf16[8,192,128]{2,1,0:T(8,128)(2,1)S(1)}, u32[]{:S(2)}, u32[]{:S(2)}) collective-permute-start(bf16[8,192,128]{2,1,0:T(8,128)(2,1)S(1)} %all_to_all.26.own), channel_id=1, source_target_pairs={{32,0},{64,32},{96,64},{128,96},{160,128},{192,160},{224,192},{33,... | collective-permute-start | bytes 1179656 | tf_op jit(solution)/shard_map/ppermute | solution.py:486
  181.7 12.8 %all-to-all-start.4 = ((bf16[8,64,128]{2,1,0:T(8,128)(2,1)}), bf16[8,64,128]{2,1,0:T(8,128)(2,1)S(1)}, u32[]{:S(2)}, u32[]{:S(2)}) async-start(bf16[8,64,128]{2,1,0:T(8,128)(2,1)} %above_2.1), calls=%async_computation.4 | async-start | bytes 262144 | tf_op jit(solution)/shard_map/all_to_all | solution.py:537
  196.9 9.3 %collective-permute-start.21 = (bf16[32,3072]{1,0:T(8,128)(2,1)S(1)}, bf16[32,3072]{1,0:T(8,128)(2,1)S(1)}, u32[]{:S(2)}, u32[]{:S(2)}) collective-permute-start(bf16[32,3072]{1,0:T(8,128)(2,1)S(1)} %get-tuple-element.87), channel_id=1, source_target_pairs={{0,1},{1,2},{2,3},{3,0},{4,5},{5,6},{6,7},{7,4},{8,9},{9,10},{10,1... | collective-permute-start | bytes 589832 | tf_op jit(solution)/shard_map/ppermute | solution.py:476
  198.7 10.1 %collective-permute-start.22 = (bf16[32,3072]{1,0:T(8,128)(2,1)S(1)}, bf16[32,3072]{1,0:T(8,128)(2,1)S(1)}, u32[]{:S(2)}, u32[]{:S(2)}) collective-permute-start(bf16[32,3072]{1,0:T(8,128)(2,1)S(1)} %get-tuple-element.88), channel_id=1, source_target_pairs={{0,2},{1,3},{2,0},{3,1},{4,6},{5,7},{6,4},{7,5},{8,10},{9,11},{10,... | collective-permute-start | bytes 589832 | tf_op jit(solution)/shard_map/ppermute | solution.py:476
  201.4 7.3 %collective-permute-start.23 = (bf16[32,3072]{1,0:T(8,128)(2,1)S(1)}, bf16[32,3072]{1,0:T(8,128)(2,1)S(1)}, u32[]{:S(2)}, u32[]{:S(2)}) collective-permute-start(bf16[32,3072]{1,0:T(8,128)(2,1)S(1)} %get-tuple-element.89), channel_id=1, source_target_pairs={{0,3},{1,0},{2,1},{3,2},{4,7},{5,4},{6,5},{7,6},{8,11},{9,8},{10,9... | collective-permute-start | bytes 589832 | tf_op jit(solution)/shard_map/ppermute | solution.py:476
  209.6 10.8 %collective-permute-start.24 = (bf16[32,3072]{1,0:T(8,128)(2,1)S(1)}, bf16[32,3072]{1,0:T(8,128)(2,1)S(1)}, u32[]{:S(2)}, u32[]{:S(2)}) collective-permute-start(bf16[32,3072]{1,0:T(8,128)(2,1)S(1)} %get-tuple-element.91), channel_id=1, source_target_pairs={{0,240},{1,241},{2,242},{3,243},{4,244},{5,245},{6,246},{7,247},{8... | collective-permute-start | bytes 589832 | tf_op jit(solution)/shard_map/ppermute | solution.py:544
Sparse Core Ops, SparseCore 0:
  10.4 46.0 all-gather.8
  58.2 39.4 all-gather.10
  99.5 38.9 all-gather.12
  140.2 30.3 all-gather.14
